TPU v7x, 32 devices: a whole 2x2x4 slice. The times are simulated.
32 devices in a mesh: scene: 2 (over x), tok: 16 (over z, y, core).
Axes of the slice: x: 2, y: 2, z: 4, core: 2. Of those that a mesh axis runs over, the one named last changes fastest.
Arguments:
- tokens: bfloat16 [16384, 768], P(('scene', 'tok')), parts along dimension 0, may hold values from -6 to 6
- qkv_weight: bfloat16 [768, 2304], replicated, may hold values from -0.21875 to 0.21875
- w_gate: float32 [4, 192, 384], replicated, may hold values from -0.4375 to 0.4375
- w_up: float32 [4, 192, 384], replicated, may hold values from -0.4375 to 0.4375
- w_down: float32 [4, 384, 192], replicated, may hold values from -0.3125 to 0.3125
- view_kind: int32 [32], P('scene'), parts along dimension 0, may hold values from 0 to 1, as said below
Outputs:
- mixed: bfloat16 [16384, 768], P(('scene', 'tok')), parts along dimension 0
There are 2 independent parts, one for each index of `scene`. A program takes and returns all parts, laid end to end along the dimension named above; an argument that names none is the same for every part. Nothing has to cross between parts.
Inputs may be any that keep to these rules, and one draw needn't show every extreme that they name: `view_kind`: exactly 12 of the 16 views are input views.
All inputs are finite; a program needn't handle non-finite values.
Results may differ from a plain program's by a relative error of at most 0.03.
Values may be sent and summed in bfloat16 or wider, within the bound.
No kernel may reach another device: no remote copies, remote signals or barrier semaphores. Data moves between devices by JAX's collectives and lax.ppermute only.
A program may use at most 64 MiB of HBM per device.

v0:
```python
import jax
import jax.numpy as jnp
from jax import lax
from jax.sharding import PartitionSpec as P

VIEWS = 16
NS_STEPS = 5


coef_a = 3.4445
coef_b = -4.775
coef_c = 2.0315
step_size = 0.8


def newton(start):
    iterate = start
    for step in range(NS_STEPS):
        gram = jnp.einsum(
            "mik,mjk->mij", iterate, iterate, preferred_element_type=jnp.float32
        ).astype(jnp.bfloat16)
        square = jnp.einsum("mij,mjk->mik", gram, gram, preferred_element_type=jnp.float32)
        mixer = (coef_b * gram.astype(jnp.float32) + coef_c * square).astype(jnp.bfloat16)
        moved = jnp.einsum("mij,mjk->mik", mixer, iterate, preferred_element_type=jnp.float32)
        iterate = (coef_a * iterate.astype(jnp.float32) + moved).astype(jnp.bfloat16)
    return iterate


def shards(tokens, qkv_weight, w_gate, w_up, w_down, view_kind):
    rows, width = tokens.shape
    heads, head_dim, hidden_dim = w_gate.shape
    groups = lax.axis_size("tok")
    place = lax.axis_index("tok")
    view_rows = rows * groups // VIEWS
    owner = place * rows // view_rows
    flag = jnp.sum(jnp.where(jnp.arange(VIEWS, dtype=jnp.int32) == owner, view_kind, 0))
    proj = jnp.dot(tokens, qkv_weight, preferred_element_type=jnp.float32).astype(jnp.bfloat16)
    query = proj[:, :width].reshape(rows, heads, head_dim)
    keys = proj[:, width : 2 * width].reshape(rows, heads, head_dim)
    values = proj[:, 2 * width :].reshape(rows, heads, head_dim)
    masked = values * flag.astype(jnp.bfloat16)
    gate_b = w_gate.astype(jnp.bfloat16)
    up_b = w_up.astype(jnp.bfloat16)
    down_b = w_down.astype(jnp.bfloat16)
    gate = jnp.einsum("thd,hdf->thf", keys, gate_b, preferred_element_type=jnp.float32)
    upper = jnp.einsum("thd,hdf->thf", keys, up_b, preferred_element_type=jnp.float32)
    sig = jax.nn.sigmoid(gate)
    act = gate * sig
    hidden = (act * upper).astype(jnp.bfloat16)
    dhid = -jnp.einsum("the,hfe->thf", masked, down_b, preferred_element_type=jnp.float32)
    dgate = (dhid * upper * (sig * (1.0 + gate * (1.0 - sig)))).astype(jnp.bfloat16)
    dup = (dhid * act).astype(jnp.bfloat16)
    grad_gate = jnp.einsum("thd,thf->hdf", keys, dgate, preferred_element_type=jnp.float32)
    grad_up = jnp.einsum("thd,thf->hdf", keys, dup, preferred_element_type=jnp.float32)
    grad_down = -jnp.einsum("the,thf->hef", masked, hidden, preferred_element_type=jnp.float32)
    grads = jnp.concatenate([grad_gate, grad_up, grad_down], axis=0)
    total = lax.psum(grads, "tok")
    norms = jnp.sqrt(jnp.sum(total * total, axis=(1, 2)))
    start = (total / (norms + 1e-07)[:, None, None]).astype(jnp.bfloat16)
    ortho = newton(start)
    stacked = jnp.concatenate([w_gate, w_up, jnp.transpose(w_down, (0, 2, 1))], axis=0)
    fresh = (stacked - step_size * ortho.astype(jnp.float32)).astype(jnp.bfloat16)
    gate2 = jnp.einsum("thd,hdf->thf", query, fresh[:heads], preferred_element_type=jnp.float32)
    upper2 = jnp.einsum(
        "thd,hdf->thf", query, fresh[heads : 2 * heads], preferred_element_type=jnp.float32
    )
    hidden2 = (jax.nn.silu(gate2) * upper2).astype(jnp.bfloat16)
    result = jnp.einsum(
        "thf,hef->the", hidden2, fresh[2 * heads :], preferred_element_type=jnp.float32
    )
    return result.reshape(rows, width).astype(jnp.bfloat16)


def solution(mesh):
    placed = (P(("scene", "tok"), None), P(), P(), P(), P(), P("scene"))
    return jax.shard_map(
        shards, mesh=mesh, in_specs=placed, out_specs=P(("scene", "tok"), None), check_vma=False
    )
```

profile of v0, /device:TPU:0, one launch (start us, length us, event | category | flops | bytes accessed | tf_op | source)
XLA Modules:
  0.0 202.8 jit_solution(2150129931057547903)
XLA Ops:
  6.5 1.4 fusion.39
  8.6 3.1 %convolution_convert_fusion = bf16[512,2304]{1,0:T(8,128)(2,1)S(1)} fusion(bf16[512,768]{1,0:T(8,128)(2,1)} %param.6, bf16[768,2304]{1,0:T(8,128)(2,1)S(1)} %copy-done), kind=kOutput, calls=%fused_computation | convolution fusion | flops 1813118976 | bytes 6684672 | tf_op jit(solution)/shard_map/dot_general | solution.py:37
  11.8 1.5 fusion.53
  13.3 2.3 %copy.17 = bf16[512,768]{0,1:T(8,128)(2,1)} copy(bf16[512,768]{1,0:T(8,128)(2,1)} %get-tuple-element.6) | data formatting | bytes 1572864 | tf_op jit(solution)/shard_map/mul | solution.py:41
  15.6 2.3 %copy.16 = bf16[512,768]{0,1:T(8,128)(2,1)} copy(bf16[512,768]{1,0:T(8,128)(2,1)} %get-tuple-element.7) | data formatting | bytes 1572864 | tf_op jit(solution)/shard_map/slice | solution.py:39
  17.9 2.5 %fusion.33 = f32[4,512,384]{2,1,0:T(8,128)S(1)} fusion(bf16[512,4,192]{0,2,1:T(8,128)(2,1)} %bitcast.110, f32[4,192,384]{2,1,0:T(8,128)} %param.8), kind=kOutput, calls=%fused_computation.59 | convolution fusion | flops 302284800 | bytes 5111808 | tf_op jit(solution)/shard_map/thd,hdf->thf/dot_general | solution.py:45
  20.4 0.8 fusion.35
  21.9 0.8 fusion.37
  22.7 1.1 fusion.20
  23.9 1.9 fusion.18
  25.7 1.1 fusion.14
  26.8 2.1 %pad_maximum_fusion = f32[12,192,384]{2,1,0:T(8,128)} fusion(f32[4,192,384]{2,1,0:T(8,128)S(1)} %fusion.20, f32[4,192,384]{2,1,0:T(8,128)S(1)} %fusion.14, f32[4,192,384]{2,1,0:T(8,128)S(1)} %fusion.18), kind=kLoop, calls=%fused_computation.3 | loop fusion | flops 1769472 | bytes 7077888 | tf_op jit(solution)/shard_map/concatenate | solution.py:56
  28.9 2.3 %copy.18 = bf16[512,768]{0,1:T(8,128)(2,1)} copy(bf16[512,768]{1,0:T(8,128)(2,1)} %get-tuple-element.5) | data formatting | bytes 1572864 | tf_op jit(solution)/shard_map/slice | solution.py:38
  31.2 106.7 %all-reduce.2.cloned.1.call-done = f32[12,192,384]{2,1,0:T(8,128)} async-done(((f32[12,192,384]{2,1,0:T(8,128)}), f32[12,192,384]{2,1,0:T(8,128)}) %all-reduce.2.cloned.1.call-update) | async-done | bytes 3538960 | tf_op jit(solution)/shard_map/psum | solution.py:57
  138.0 2.5 %multiply_reduce_fusion = f32[12]{0:T(128)S(1)} fusion(f32[12,192,384]{2,1,0:T(8,128)} %all-reduce.2.cloned.1.call-done), kind=kLoop, calls=%fused_computation.10 | loop fusion | flops 1769460 | bytes 3538992 | tf_op jit(solution)/shard_map/reduce_sum | solution.py:58
  140.5 0.5 copy-done.2
  141.0 0.4 divide_convert_fusion
  141.5 1.2 copy-done.1
  142.7 1.8 convolution_convert_fusion.5
  144.5 5.5 %add_convert_fusion.4 = bf16[12,192,384]{2,1,0:T(8,128)(2,1)} fusion(bf16[12,192,384]{2,1,0:T(8,128)(2,1)} %copy-done.1, bf16[12,192,192]{2,1,0:T(8,128)(2,1)} %convolution_convert_fusion.5), kind=kOutput, calls=%fused_computation.8 | convolution fusion | flops 515358720 | bytes 4423680 | tf_op jit(solution)/shard_map/mij,mjk->mik/dot_general | solution.py:24
  150.0 3.8 %convolution_convert_fusion.4 = bf16[12,192,192]{2,1,0:T(8,128)(2,1)} fusion(bf16[12,192,384]{2,1,0:T(8,128)(2,1)} %add_convert_fusion.4), kind=kOutput, calls=%fused_computation.44 | convolution fusion | flops 340180992 | bytes 2654208 | tf_op jit(solution)/shard_map/mik,mjk->mij/dot_general | solution.py:19
  153.8 5.6 %add_convert_fusion.3 = bf16[12,192,384]{2,1,0:T(8,128)(2,1)} fusion(bf16[12,192,384]{2,1,0:T(8,128)(2,1)} %add_convert_fusion.4, bf16[12,192,192]{2,1,0:T(8,128)(2,1)} %convolution_convert_fusion.4), kind=kOutput, calls=%fused_computation.7 | convolution fusion | flops 515358720 | bytes 4423680 | tf_op jit(solution)/shard_map/mij,mjk->mik/dot_general | solution.py:24
  159.4 3.8 %convolution_convert_fusion.3 = bf16[12,192,192]{2,1,0:T(8,128)(2,1)} fusion(bf16[12,192,384]{2,1,0:T(8,128)(2,1)} %add_convert_fusion.3), kind=kOutput, calls=%fused_computation.43 | convolution fusion | flops 340180992 | bytes 2654208 | tf_op jit(solution)/shard_map/mik,mjk->mij/dot_general | solution.py:19
  163.2 5.5 %add_convert_fusion.2 = bf16[12,192,384]{2,1,0:T(8,128)(2,1)} fusion(bf16[12,192,384]{2,1,0:T(8,128)(2,1)} %add_convert_fusion.3, bf16[12,192,192]{2,1,0:T(8,128)(2,1)} %convolution_convert_fusion.3), kind=kOutput, calls=%fused_computation.6 | convolution fusion | flops 515358720 | bytes 4423680 | tf_op jit(solution)/shard_map/mij,mjk->mik/dot_general | solution.py:24
  168.7 3.8 %convolution_convert_fusion.2 = bf16[12,192,192]{2,1,0:T(8,128)(2,1)} fusion(bf16[12,192,384]{2,1,0:T(8,128)(2,1)} %add_convert_fusion.2), kind=kOutput, calls=%fused_computation.42 | convolution fusion | flops 340180992 | bytes 2654208 | tf_op jit(solution)/shard_map/mik,mjk->mij/dot_general | solution.py:19
  172.6 5.6 %add_convert_fusion.1 = bf16[12,192,384]{2,1,0:T(8,128)(2,1)} fusion(bf16[12,192,384]{2,1,0:T(8,128)(2,1)} %add_convert_fusion.2, bf16[12,192,192]{2,1,0:T(8,128)(2,1)} %convolution_convert_fusion.2), kind=kOutput, calls=%fused_computation.5 | convolution fusion | flops 515358720 | bytes 4423680 | tf_op jit(solution)/shard_map/mij,mjk->mik/dot_general | solution.py:24
  178.2 3.8 %convolution_convert_fusion.1 = bf16[12,192,192]{2,1,0:T(8,128)(2,1)} fusion(bf16[12,192,384]{2,1,0:T(8,128)(2,1)} %add_convert_fusion.1), kind=kOutput, calls=%fused_computation.41 | convolution fusion | flops 340180992 | bytes 2654208 | tf_op jit(solution)/shard_map/mik,mjk->mij/dot_general | solution.py:19
  182.0 6.7 %fusion = bf16[12,192,384]{2,1,0:T(8,128)(2,1)} fusion(f32[4,192,384]{2,1,0:T(8,128)} %bitcast.116, f32[4,192,384]{2,1,0:T(8,128)} %param.9, f32[4,192,384]{2,1,0:T(8,128)} %param.8, bf16[12,192,384]{2,1,0:T(8,128)(2,1)} %add_convert_fusion.1, bf16[12,192,192]{2,1,0:T(8,128)(2,1)} %convolution_convert_fusion.1), kind=kOutput, calls=%fused_computation.2 | convolution fusion | flops 520667136 | bytes 7962624 | tf_op jit(solution)/shard_map/mij,mjk->mik/dot_general | solution.py:24
  188.7 2.3 %fusion.54 = f32[4,384,512]{1,2,0:T(8,128)S(1)} fusion(bf16[12,192,384]{2,1,0:T(8,128)(2,1)} %fusion, bf16[512,4,192]{0,2,1:T(8,128)(2,1)} %bitcast.117), kind=kOutput, calls=%fused_computation.82 | convolution fusion | flops 301989888 | bytes 5701632 | tf_op jit(solution)/shard_map/thd,hdf->thf/dot_general | solution.py:63
  191.0 1.1 fusion.1
  192.1 1.6 convolution_convert_fusion.6
  193.7 2.3 %copy.20 = bf16[512,768]{1,0:T(8,128)(2,1)} copy(bf16[512,768]{0,1:T(8,128)(2,1)} %bitcast.119) | data formatting | bytes 1572864 | tf_op jit(solution)/shard_map/convert_element_type | solution.py:71
  (19 shorter events, 0.7 us)
Async XLA Ops:
  6.5 2.1 %copy-start = (bf16[768,2304]{1,0:T(8,128)(2,1)S(1)}, bf16[768,2304]{1,0:T(8,128)(2,1)}, u32[]{:S(2)}) copy-start(bf16[768,2304]{1,0:T(8,128)(2,1)} %param.7) | copy-start | bytes 10616836
  6.5 131.4 %all-reduce.2.cloned.1.call-start = ((), (), s32[]{:S(2)}) async-start(), calls=%async_computation | async-start | bytes 7077888 | tf_op jit(solution)/shard_map/psum | solution.py:57
  17.9 2.5 %copy-start.3 = (bf16[512,768]{0,1:T(8,128)(2,1)S(1)}, bf16[512,768]{0,1:T(8,128)(2,1)}, u32[]{:S(2)}) copy-start(bf16[512,768]{0,1:T(8,128)(2,1)} %copy.16) | copy-start | bytes 2359300
  17.9 2.5 %copy-start.6 = (f32[4,192,384]{2,1,0:T(8,128)S(1)}, f32[4,192,384]{2,1,0:T(8,128)}, u32[]{:S(2)}) copy-start(f32[4,192,384]{2,1,0:T(8,128)} %param.9) | copy-start | bytes 3538948
  20.4 1.1 copy-start.4
  20.4 1.5 copy-start.5
  138.0 3.1 %copy-start.2 = (f32[12,192,384]{2,1,0:T(8,128)S(1)}, f32[12,192,384]{2,1,0:T(8,128)}, u32[]{:S(2)}) copy-start(f32[12,192,384]{2,1,0:T(8,128)} %all-reduce.2.cloned.1.call-done) | copy-start | bytes 10616836
  141.5 1.2 copy-start.1
  188.7 2.3 %copy-start.7 = (bf16[512,768]{0,1:T(8,128)(2,1)S(1)}, bf16[512,768]{0,1:T(8,128)(2,1)}, u32[]{:S(2)}) copy-start(bf16[512,768]{0,1:T(8,128)(2,1)} %copy.18) | copy-start | bytes 2359300
  188.7 2.3 %copy-start.8 = (bf16[12,192,384]{2,1,0:T(8,128)(2,1)S(1)}, bf16[12,192,384]{2,1,0:T(8,128)(2,1)}, u32[]{:S(2)}) copy-start(bf16[12,192,384]{2,1,0:T(8,128)(2,1)} %fusion) | copy-start | bytes 5308420
Sparse Core Ops, SparseCore 0:
  29.0 108.8 all-reduce.1
where the time goes:
time: 203 us
  waiting for transfers between devices  107 us (53%)
  matrix products  62.4 us (31%)
  between operations  14.2 us (7%)
  local copies, waits for them, and re-layouts  11.6 us (6%)
  other arithmetic  7.94 us (4%)
    psum x1, waiting for transfers between devices, shards(): total = lax.psum(grads, 'tok')  107 us
    dot_general x5, matrix products, newton(): jnp.einsum('mij,mjk->mik', mixer, iterate, preferred_element_type=jnp.flo...  28.9 us
    dot_general x5, matrix products, newton(): jnp.einsum('mik,mjk->mij', iterate, iterate, preferred_element_type=jnp.f...  17.1 us
  transfers between devices with their start and end apart: 1, of which 1 were waited for; matrix products, arithmetic and copies ran while one was open for 1% of the time, Pallas kernels for 0%

commit v1 on v0

v1 whole, which is shorter than its diff:
```python
import functools

import jax
import jax.numpy as jnp
from jax import lax
from jax.experimental import pallas as pl
from jax.experimental.pallas import tpu as pltpu
from jax.sharding import PartitionSpec as P

VIEWS = 16
NS_STEPS = 5
BF16 = jnp.bfloat16
F32 = jnp.float32
VMEM_LIMIT = 40 * 1024 * 1024

coef_a = 3.4445
coef_b = -4.775
coef_c = 2.0315
step_size = 0.8


def mm(a, b, dims):
    return lax.dot_general(a, b, (dims, ((), ())), preferred_element_type=F32)


NN = ((1,), (0,))
NT = ((1,), (1,))
TN = ((0,), (0,))


def project_kernel(plain, flag_ref, tokens_ref, weight_ref, out_ref):
    head_dim = out_ref.shape[2]
    scale = jnp.where(pl.program_id(0) >= plain, flag_ref[0], 1).astype(F32)
    part = mm(tokens_ref[...], weight_ref[...], NN).astype(BF16)
    part = (part.astype(F32) * scale).astype(BF16)
    for head in range(out_ref.shape[0]):
        out_ref[head] = part[:, head * head_dim : (head + 1) * head_dim]


def project(tokens, weight, flag, first, blocks, plain, head_dim):
    rows, width = tokens.shape
    pair = 2
    return pl.pallas_call(
        functools.partial(project_kernel, plain),
        out_shape=jax.ShapeDtypeStruct((blocks * pair, rows, head_dim), BF16),
        grid_spec=pltpu.PrefetchScalarGridSpec(
            num_scalar_prefetch=1,
            grid=(blocks,),
            in_specs=[
                pl.BlockSpec((rows, width), lambda j, flag: (0, 0)),
                pl.BlockSpec((width, pair * head_dim), lambda j, flag: (0, first + j)),
            ],
            out_specs=pl.BlockSpec((pair, rows, head_dim), lambda j, flag: (j, 0, 0)),
        ),
        compiler_params=pltpu.CompilerParams(vmem_limit_bytes=VMEM_LIMIT),
        cost_estimate=pl.CostEstimate(
            flops=2 * rows * width * blocks * pair * head_dim,
            bytes_accessed=2 * width * (rows + blocks * pair * head_dim),
            transcendentals=0,
        ),
    )(flag, tokens, weight)


def grad_kernel(chunk, ids_ref, k_ref, v_ref, gate_ref, up_ref, down_ref, keep_ref, give_ref, up_out_ref):
    core = ids_ref[1]
    rows = k_ref.shape[1]
    gate_b = gate_ref[0].astype(BF16)
    up_b = up_ref[0].astype(BF16)
    down_b = down_ref[0].astype(BF16)
    totals = [None, None, None]
    for start in range(0, rows, chunk):
        k = k_ref[0, pl.ds(start, chunk), :]
        v = v_ref[0, pl.ds(start, chunk), :]
        gate = mm(k, gate_b, NN)
        upper = mm(k, up_b, NN)
        dhid = -mm(v, down_b, NT)
        sig = jax.nn.sigmoid(gate)
        act = gate * sig
        hidden = (act * upper).astype(BF16)
        dgate = (dhid * upper * (sig * (1.0 + gate * (1.0 - sig)))).astype(BF16)
        dup = (dhid * act).astype(BF16)
        parts = [mm(k, dgate, TN), mm(k, dup, TN), -mm(v, hidden, TN)]
        totals = [p if t is None else t + p for t, p in zip(totals, parts)]
    gate_g, up_g, down_g = [t.astype(BF16) for t in totals]
    up_out_ref[...] = up_g

    @pl.when(core == 0)
    def _():
        keep_ref[...] = gate_g
        give_ref[...] = down_g

    @pl.when(core != 0)
    def _():
        keep_ref[...] = down_g
        give_ref[...] = gate_g


def gradients(ids, kv, w_gate, w_up, w_down):
    heads, head_dim, hidden = w_gate.shape
    rows = kv.shape[1]
    whole = pl.BlockSpec((head_dim, hidden), lambda i, ids: (0, 0))
    shape = jax.ShapeDtypeStruct((head_dim, hidden), BF16)
    return pl.pallas_call(
        functools.partial(grad_kernel, rows // 4),
        out_shape=[shape] * 3,
        grid_spec=pltpu.PrefetchScalarGridSpec(
            num_scalar_prefetch=1,
            grid=(1,),
            in_specs=[
                pl.BlockSpec((1, rows, head_dim), lambda i, ids: (ids[0], 0, 0)),
                pl.BlockSpec((1, rows, head_dim), lambda i, ids: (heads + ids[0], 0, 0)),
                pl.BlockSpec((1, head_dim, hidden), lambda i, ids: (ids[0], 0, 0)),
                pl.BlockSpec((1, head_dim, hidden), lambda i, ids: (ids[0], 0, 0)),
                pl.BlockSpec((1, hidden, head_dim), lambda i, ids: (ids[0], 0, 0)),
            ],
            out_specs=[whole] * 3,
        ),
        compiler_params=pltpu.CompilerParams(vmem_limit_bytes=VMEM_LIMIT),
        cost_estimate=pl.CostEstimate(
            flops=12 * rows * head_dim * hidden,
            bytes_accessed=12 * head_dim * hidden + 4 * rows * head_dim,
            transcendentals=rows * hidden,
        ),
    )(ids, kv, kv, w_gate, w_up, w_down)


def newton_kernel(a0_ref, b0_ref, a1_ref, b1_ref, base_ref, out0_ref, out1_ref):
    iterates = []
    for a_ref, b_ref in ((a0_ref, b0_ref), (a1_ref, b1_ref)):
        total = a_ref[...].astype(F32) + b_ref[...].astype(F32)
        norm = jnp.sqrt(jnp.sum(total * total))
        iterates.append((total / (norm + 1e-07)).astype(BF16))
    for step in range(NS_STEPS):
        grams = [mm(x, x, NT).astype(BF16) for x in iterates]
        squares = [mm(g, g, NN) for g in grams]
        mixers = [(coef_b * g.astype(F32) + coef_c * s).astype(BF16) for g, s in zip(grams, squares)]
        moved = [mm(m, x, NN) for m, x in zip(mixers, iterates)]
        iterates = [(coef_a * x.astype(F32) + y).astype(BF16) for x, y in zip(iterates, moved)]
    for slot, (x, out_ref) in enumerate(zip(iterates, (out0_ref, out1_ref))):
        out_ref[...] = (base_ref[slot] - step_size * x.astype(F32)).astype(BF16)


def newton(a0, b0, a1, b1, base):
    head_dim, hidden = a0.shape
    shape = jax.ShapeDtypeStruct((head_dim, hidden), BF16)
    return pl.pallas_call(
        newton_kernel,
        out_shape=[shape] * 2,
        compiler_params=pltpu.CompilerParams(vmem_limit_bytes=VMEM_LIMIT),
        cost_estimate=pl.CostEstimate(
            flops=2 * NS_STEPS * 2 * head_dim * head_dim * (2 * hidden + head_dim),
            bytes_accessed=20 * head_dim * hidden,
            transcendentals=0,
        ),
    )(a0, b0, a1, b1, base)


def apply_kernel(ids_ref, q_ref, s0_ref, s1_ref, x0_ref, x1_ref, out_ref):
    even = ids_ref[1] == 0
    gate_b = jnp.where(even, s0_ref[...], x0_ref[...])
    up_b = jnp.where(even, s1_ref[...], x1_ref[...])
    down_b = jnp.where(even, x0_ref[...], s0_ref[...])
    q = q_ref[0]
    gate = mm(q, gate_b, NN)
    upper = mm(q, up_b, NN)
    hidden = (gate * jax.nn.sigmoid(gate) * upper).astype(BF16)
    out_ref[...] = mm(hidden, down_b, NT).astype(BF16)


def apply(ids, q, s0, s1, x0, x1):
    heads, rows, head_dim = q.shape
    hidden = s0.shape[1]
    whole = pl.BlockSpec((head_dim, hidden), lambda i, ids: (0, 0))
    return pl.pallas_call(
        apply_kernel,
        out_shape=jax.ShapeDtypeStruct((rows, head_dim), BF16),
        grid_spec=pltpu.PrefetchScalarGridSpec(
            num_scalar_prefetch=1,
            grid=(1,),
            in_specs=[pl.BlockSpec((1, rows, head_dim), lambda i, ids: (ids[0], 0, 0))] + [whole] * 4,
            out_specs=pl.BlockSpec((rows, head_dim), lambda i, ids: (0, 0)),
        ),
        compiler_params=pltpu.CompilerParams(vmem_limit_bytes=VMEM_LIMIT),
        cost_estimate=pl.CostEstimate(
            flops=6 * rows * head_dim * hidden,
            bytes_accessed=8 * head_dim * hidden + 4 * rows * head_dim,
            transcendentals=rows * hidden,
        ),
    )(ids, q, s0, s1, x0, x1)


def join_kernel(own_ref, *refs):
    *pieces, out_ref = refs
    own = own_ref[0]
    head_dim = pieces[0].shape[1]
    for case in range(4):

        @pl.when(own == case)
        def _():
            for head in range(4):
                out_ref[:, head * head_dim : (head + 1) * head_dim] = pieces[head ^ case][...]


def join(own, pieces):
    rows, head_dim = pieces[0].shape
    return pl.pallas_call(
        join_kernel,
        out_shape=jax.ShapeDtypeStruct((rows, 4 * head_dim), BF16),
        in_specs=[pl.BlockSpec(memory_space=pltpu.SMEM)] + [pl.BlockSpec(memory_space=pltpu.VMEM)] * 4,
        compiler_params=pltpu.CompilerParams(vmem_limit_bytes=VMEM_LIMIT),
        cost_estimate=pl.CostEstimate(flops=0, bytes_accessed=16 * rows * head_dim, transcendentals=0),
    )(own, *pieces)


def add(*arrays):
    return sum(a.astype(F32) for a in arrays).astype(BF16)


def shards(tokens, qkv_weight, w_gate, w_up, w_down, view_kind):
    rows, width = tokens.shape
    heads, head_dim, hidden = w_gate.shape
    groups = lax.axis_size("tok")
    place = lax.axis_index("tok")
    core = place % 2
    own = (place // 2) % heads
    view_rows = rows * groups // VIEWS
    owner = place * rows // view_rows
    flag = jnp.sum(jnp.where(jnp.arange(VIEWS, dtype=jnp.int32) == owner, view_kind, 0)).reshape(1)

    def exchange(x, bits, parity=None):
        pairs = [(i, i ^ bits) for i in range(groups) if parity is None or i % 2 == parity]
        return lax.ppermute(x, "tok", pairs)

    kv = project(tokens, qkv_weight, flag, 2, 4, 2, head_dim)

    sums = [[], []]
    for far in (3, 1, 2, 0):
        ids = jnp.stack([own ^ far, core]).astype(jnp.int32)
        keep, give, upper = gradients(ids, kv, w_gate, w_up, w_down)
        slot0 = add(keep, exchange(give, 1))
        slot1 = add(upper, exchange(upper, 1, 1))
        if far:
            slot0 = exchange(slot0, 2 * far)
            slot1 = exchange(slot1, 2 * far, 0)
        sums[0].append(slot0)
        sums[1].append(slot1)
    query = project(tokens, qkv_weight, flag, 0, 2, 2, head_dim)

    slot0, slot1 = add(*sums[0]), add(*sums[1])
    bits = 8
    while bits < groups // 2:
        slot0, slot1 = add(slot0, exchange(slot0, bits)), add(slot1, exchange(slot1, bits, 0))
        bits *= 2
    other0, other1 = exchange(slot0, bits), exchange(slot1, bits, 0)

    mine = lambda w: lax.dynamic_index_in_dim(w, own, 0, keepdims=False)
    base = jnp.stack([jnp.where(core == 0, mine(w_gate), mine(w_down).T), mine(w_up)])
    fresh0, fresh1 = newton(slot0, other0, slot1, other1, base)

    pieces = []
    for far in range(heads):
        here0 = exchange(fresh0, 2 * far) if far else fresh0
        here1 = exchange(fresh1, 2 * far, 0) if far else fresh1
        there0, there1 = exchange(here0, 1), exchange(here1, 1, 0)
        ids = jnp.stack([own ^ far, core]).astype(jnp.int32)
        pieces.append(apply(ids, query, here0, here1, there0, there1))
    return join(own.reshape(1).astype(jnp.int32), pieces)


def solution(mesh):
    placed = (P(("scene", "tok"), None), P(), P(), P(), P(), P("scene"))
    return jax.shard_map(
        shards, mesh=mesh, in_specs=placed, out_specs=P(("scene", "tok"), None), check_vma=False
    )
```

time: 203 us -> 105 us (0.52)
  waiting for transfers between devices: 107 us -> 7.49 us
  matrix products: 62.4 us -> 0 us
  starting transfers between devices: 0.01 us -> 52.3 us
  Pallas kernels: 0 us -> 26.4 us
  between operations: 14.2 us -> 0.57 us
    psum x1 -> x0, waiting for transfers between devices: 107 us -> none  [shards(): total = lax.psum(grads, 'tok')]
    dot_general x20 -> x0, matrix products: 62.4 us -> none  [the longest x5 28.9 us: newton(): jnp.einsum('mij,mjk->mik', mixer, iterate, preferred_element_type=jnp.flo...]
    ppermute x0 -> x30, starting transfers between devices: none -> 52.3 us  [exchange(): return lax.ppermute(x, 'tok', pairs)]
    pallas_call x0 -> x12, Pallas kernels: none -> 26.4 us  [the longest x4 11.5 us: gradients(): pl.pallas_call(functools.partial(grad_kernel, rows // 4), out_shape=[shap...]
    unnamed x18 -> x41, local copies, waits for them, and re-layouts: 2.4 us -> 10.8 us
    ppermute x0 -> x30, waiting for transfers between devices: none -> 7.49 us  [exchange(): return lax.ppermute(x, 'tok', pairs)]
    slice x2 -> x0, local copies, waits for them, and re-layouts: 4.6 us -> none  [the longest x1 2.31 us: shards(): keys = proj[:, width:2 * width].reshape(rows, heads, head_dim)]
    convert_element_type x1 -> x8, other arithmetic: 0.44 us -> 4.29 us  [add(): return sum((a.astype(F32) for a in arrays)).astype(BF16)]
  transfers between devices with their start and end apart: 1 -> 30, of which waited for: 1 -> 3; matrix products, arithmetic and copies ran while one was open for 1% -> 5% of each run, Pallas kernels for 0% -> 14%
where the time goes in v1:
time: 105 us; the launch traced here: 104 us
  starting transfers between devices  52.3 us (50%)
  Pallas kernels  26.4 us (25%)
  local copies, waits for them, and re-layouts  10.8 us (10%)
  waiting for transfers between devices  7.49 us (7%)
  other arithmetic  6.29 us (6%)
    ppermute x30, starting transfers between devices, exchange(): return lax.ppermute(x, 'tok', pairs)  52.3 us
    pallas_call x4, Pallas kernels, gradients(): pl.pallas_call(functools.partial(grad_kernel, rows // 4), out_shape=[shap...  11.5 us
    unnamed x41, local copies, waits for them, and re-layouts  10.8 us
    ppermute x30, waiting for transfers between devices, exchange(): return lax.ppermute(x, 'tok', pairs)  7.49 us
    pallas_call x2, Pallas kernels, project(): pl.pallas_call(functools.partial(project_kernel, plain), out_shape=jax.Sh...  5.74 us
    pallas_call x4, Pallas kernels, apply(): pl.pallas_call(apply_kernel, out_shape=jax.ShapeDtypeStruct((rows, head_d...  4.95 us
    convert_element_type x8, other arithmetic, add(): return sum((a.astype(F32) for a in arrays)).astype(BF16)  4.29 us
    pallas_call x1, Pallas kernels, newton(): pl.pallas_call(newton_kernel, out_shape=[shape] * 2, compiler_params=pltp...  3.06 us
  transfers between devices with their start and end apart: 30, of which 3 were waited for; matrix products, arithmetic and copies ran while one was open for 5% of the time, Pallas kernels for 14%

profile of v1, /device:TPU:0, one launch (start us, length us, event | category | flops | bytes accessed | tf_op | source)
XLA Modules:
  0.0 103.8 jit_solution(16499617804719609993)
XLA Ops:
  0.0 2.9 %copy.7.down_ref = f32[4,384,192]{2,1,0:T(8,128)} copy(f32[4,384,192]{1,2,0:T(8,128)} %param.10) | data formatting | bytes 2359296 | tf_op args[4]
  3.6 2.0 %copy-done.5 = bf16[768,2304]{1,0:T(8,128)(2,1)S(1)} copy-done((bf16[768,2304]{1,0:T(8,128)(2,1)S(1)}, bf16[768,2304]{1,0:T(8,128)(2,1)}, u32[]{:S(2)}) %copy-start.5) | copy-done | bytes 3538968
  6.7 3.7 %shard_map.65.k_ref.v_ref = bf16[8,512,192]{2,1,0:T(8,128)(2,1)S(1)} custom-call(s32[1]{0:T(128)} %bitcast.2.flag_ref, bf16[512,768]{1,0:T(8,128)(2,1)S(1)} %copy-done.7, bf16[768,2304]{1,0:T(8,128)(2,1)S(1)} %copy-done.5), custom_call_target="tpu_custom_call" | custom-call | flops 1207959552 | bytes 3145728 | tf_op jit(solution)/shard_map/pallas_call | solution.py:43
  10.5 2.9 %shard_map.67 = (bf16[192,384]{1,0:T(8,128)(2,1)S(1)}, bf16[192,384]{1,0:T(8,128)(2,1)S(1)}, bf16[192,384]{1,0:T(8,128)(2,1)}) custom-call(s32[2]{0:T(128)S(1)} %get-tuple-element.35.ids_ref, bf16[8,512,192]{2,1,0:T(8,128)(2,1)S(1)} %shard_map.65.k_ref.v_ref, bf16[8,512,192]{2,1,0:T(8,128)(2,1)S(1)} %shard_map.65.k_ref.v_ref, f32[4,192,384]{2,1,0:T(8,128)S(1)} %copy-done.3, ...), custom_call_target="tpu_custom_call" | custom-call | flops 452984832 | bytes 1277952 | tf_op jit(solution)/shard_map/pallas_call | solution.py:103
  13.3 1.3 %collective-permute-start.10 = (bf16[192,384]{1,0:T(8,128)(2,1)}, bf16[192,384]{1,0:T(8,128)(2,1)}, u32[]{:S(2)}, u32[]{:S(2)}) collective-permute-start(bf16[192,384]{1,0:T(8,128)(2,1)} %get-tuple-element.28), channel_id=1, source_target_pairs={{1,0},{3,2},{5,4},{7,6},{9,8},{11,10},{13,12},{15,14},{17,16},{19,... | collective-permute-start | bytes 442376 | tf_op jit(solution)/shard_map/ppermute | solution.py:232
  14.6 2.9 %shard_map.68 = (bf16[192,384]{1,0:T(8,128)(2,1)S(1)}, bf16[192,384]{1,0:T(8,128)(2,1)S(1)}, bf16[192,384]{1,0:T(8,128)(2,1)}) custom-call(s32[2]{0:T(128)S(1)} %get-tuple-element.36.ids_ref, bf16[8,512,192]{2,1,0:T(8,128)(2,1)S(1)} %shard_map.65.k_ref.v_ref, bf16[8,512,192]{2,1,0:T(8,128)(2,1)S(1)} %shard_map.65.k_ref.v_ref, f32[4,192,384]{2,1,0:T(8,128)S(1)} %copy-done.3, ...), custom_call_target="tpu_custom_call" | custom-call | flops 452984832 | bytes 1277952 | tf_op jit(solution)/shard_map/pallas_call | solution.py:103
  18.8 1.3 %collective-permute-start.12 = (bf16[192,384]{1,0:T(8,128)(2,1)}, bf16[192,384]{1,0:T(8,128)(2,1)}, u32[]{:S(2)}, u32[]{:S(2)}) collective-permute-start(bf16[192,384]{1,0:T(8,128)(2,1)} %get-tuple-element.29), channel_id=1, source_target_pairs={{1,0},{3,2},{5,4},{7,6},{9,8},{11,10},{13,12},{15,14},{17,16},{19,... | collective-permute-start | bytes 442376 | tf_op jit(solution)/shard_map/ppermute | solution.py:232
  20.2 1.4 %copy-done.1 = f32[4,384,192]{2,1,0:T(8,128)S(1)} copy-done((f32[4,384,192]{2,1,0:T(8,128)S(1)}, f32[4,384,192]{2,1,0:T(8,128)}, u32[]{:S(2)}) %copy-start.1) | copy-done | bytes 1179672
  21.6 1.3 %copy-done.4 = f32[4,192,384]{2,1,0:T(8,128)S(1)} copy-done((f32[4,192,384]{2,1,0:T(8,128)S(1)}, f32[4,192,384]{2,1,0:T(8,128)}, u32[]{:S(2)}) %copy-start.4) | copy-done | bytes 1179672
  22.9 2.9 %shard_map.66 = (bf16[192,384]{1,0:T(8,128)(2,1)S(1)}, bf16[192,384]{1,0:T(8,128)(2,1)}, bf16[192,384]{1,0:T(8,128)(2,1)}) custom-call(s32[2]{0:T(128)S(1)} %get-tuple-element.34.ids_ref, bf16[8,512,192]{2,1,0:T(8,128)(2,1)S(1)} %shard_map.65.k_ref.v_ref, bf16[8,512,192]{2,1,0:T(8,128)(2,1)S(1)} %shard_map.65.k_ref.v_ref, f32[4,192,384]{2,1,0:T(8,128)S(1)} %copy-done.4, ...), custom_call_target="tpu_custom_call" | custom-call | flops 452984832 | bytes 1277952 | tf_op jit(solution)/shard_map/pallas_call | solution.py:103
  25.8 1.3 %collective-permute-start.8 = (bf16[192,384]{1,0:T(8,128)(2,1)}, bf16[192,384]{1,0:T(8,128)(2,1)}, u32[]{:S(2)}, u32[]{:S(2)}) collective-permute-start(bf16[192,384]{1,0:T(8,128)(2,1)} %get-tuple-element.27), channel_id=1, source_target_pairs={{1,0},{3,2},{5,4},{7,6},{9,8},{11,10},{13,12},{15,14},{17,16},{19,... | collective-permute-start | bytes 442376 | tf_op jit(solution)/shard_map/ppermute | solution.py:232
  27.1 2.9 %shard_map.69 = (bf16[192,384]{1,0:T(8,128)(2,1)S(1)}, bf16[192,384]{1,0:T(8,128)(2,1)S(1)}, bf16[192,384]{1,0:T(8,128)(2,1)}) custom-call(s32[2]{0:T(128)S(1)} %get-tuple-element.33.ids_ref, bf16[8,512,192]{2,1,0:T(8,128)(2,1)S(1)} %shard_map.65.k_ref.v_ref, bf16[8,512,192]{2,1,0:T(8,128)(2,1)S(1)} %shard_map.65.k_ref.v_ref, f32[4,192,384]{2,1,0:T(8,128)S(1)} %copy-done.4, ...), custom_call_target="tpu_custom_call" | custom-call | flops 452984832 | bytes 1277952 | tf_op jit(solution)/shard_map/pallas_call | solution.py:103
  30.6 1.4 %collective-permute-start.14 = (bf16[192,384]{1,0:T(8,128)(2,1)}, bf16[192,384]{1,0:T(8,128)(2,1)S(1)}, u32[]{:S(2)}, u32[]{:S(2)}) collective-permute-start(bf16[192,384]{1,0:T(8,128)(2,1)} %get-tuple-element.30), channel_id=1, source_target_pairs={{1,0},{3,2},{5,4},{7,6},{9,8},{11,10},{13,12},{15,14},{17,16},{19,... | collective-permute-start | bytes 442376 | tf_op jit(solution)/shard_map/ppermute | solution.py:232
  32.0 3.1 %collective-permute-start = (bf16[192,384]{1,0:T(8,128)(2,1)}, bf16[192,384]{1,0:T(8,128)(2,1)S(1)}, u32[]{:S(2)}, u32[]{:S(2)}) collective-permute-start(bf16[192,384]{1,0:T(8,128)(2,1)} %get-tuple-element.20), channel_id=1, source_target_pairs={{0,1},{1,0},{2,3},{3,2},{4,5},{5,4},{6,7},{7,6},{8,9},{9,8},{10,11... | collective-permute-start | bytes 442376 | tf_op jit(solution)/shard_map/ppermute | solution.py:232
  39.1 4.9 %collective-permute-start.11 = (bf16[192,384]{1,0:T(8,128)(2,1)S(1)}, bf16[192,384]{1,0:T(8,128)(2,1)S(1)}, u32[]{:S(2)}, u32[]{:S(2)}) collective-permute-start(bf16[192,384]{1,0:T(8,128)(2,1)S(1)} %add_convert_fusion.3), channel_id=1, source_target_pairs={{0,2},{2,0},{4,6},{6,4},{8,10},{10,8},{12,14},{14,12},{16,18},{18,... | collective-permute-start | bytes 442376 | tf_op jit(solution)/shard_map/ppermute | solution.py:232
  44.1 3.5 %collective-permute-start.13 = (bf16[192,384]{1,0:T(8,128)(2,1)S(1)}, bf16[192,384]{1,0:T(8,128)(2,1)S(1)}, u32[]{:S(2)}, u32[]{:S(2)}) collective-permute-start(bf16[192,384]{1,0:T(8,128)(2,1)S(1)} %add_convert_fusion.2), channel_id=1, source_target_pairs={{0,4},{2,6},{4,0},{6,2},{8,12},{10,14},{12,8},{14,10},{16,20},{18,... | collective-permute-start | bytes 442376 | tf_op jit(solution)/shard_map/ppermute | solution.py:232
  47.6 1.9 %collective-permute-start.9 = (bf16[192,384]{1,0:T(8,128)(2,1)S(1)}, bf16[192,384]{1,0:T(8,128)(2,1)S(1)}, u32[]{:S(2)}, u32[]{:S(2)}) collective-permute-start(bf16[192,384]{1,0:T(8,128)(2,1)S(1)} %add_convert_fusion.4), channel_id=1, source_target_pairs={{0,6},{2,4},{4,2},{6,0},{8,14},{10,12},{12,10},{14,8},{16,22},{18,... | collective-permute-start | bytes 442376 | tf_op jit(solution)/shard_map/ppermute | solution.py:232
  49.6 3.0 %collective-permute-start.1 = (bf16[192,384]{1,0:T(8,128)(2,1)S(1)}, bf16[192,384]{1,0:T(8,128)(2,1)S(1)}, u32[]{:S(2)}, u32[]{:S(2)}) collective-permute-start(bf16[192,384]{1,0:T(8,128)(2,1)S(1)} %add_convert_fusion.9), channel_id=1, source_target_pairs={{0,6},{1,7},{2,4},{3,5},{4,2},{5,3},{6,0},{7,1},{8,14},{9,15},{10,... | collective-permute-start | bytes 442376 | tf_op jit(solution)/shard_map/ppermute | solution.py:232
  53.8 1.7 %collective-permute-done.9 = bf16[192,384]{1,0:T(8,128)(2,1)S(1)} collective-permute-done((bf16[192,384]{1,0:T(8,128)(2,1)S(1)}, bf16[192,384]{1,0:T(8,128)(2,1)S(1)}, u32[]{:S(2)}, u32[]{:S(2)}) %collective-permute-start.9) | collective-permute-done | bytes 147488 | tf_op jit(solution)/shard_map/ppermute | solution.py:232
  56.6 5.7 %collective-permute-start.15 = (bf16[192,384]{1,0:T(8,128)(2,1)S(1)}, bf16[192,384]{1,0:T(8,128)(2,1)S(1)}, u32[]{:S(2)}, u32[]{:S(2)}) collective-permute-start(bf16[192,384]{1,0:T(8,128)(2,1)S(1)} %add_convert_fusion.a1_ref), channel_id=1, source_target_pairs={{0,8},{2,10},{4,12},{6,14},{8,0},{10,2},{12,4},{14,6},{16,24},{18,... | collective-permute-start | bytes 442376 | tf_op jit(solution)/shard_map/ppermute | solution.py:232
  63.7 3.6 %collective-permute-done.15.b1_ref = bf16[192,384]{1,0:T(8,128)(2,1)S(1)} collective-permute-done((bf16[192,384]{1,0:T(8,128)(2,1)S(1)}, bf16[192,384]{1,0:T(8,128)(2,1)S(1)}, u32[]{:S(2)}, u32[]{:S(2)}) %collective-permute-start.15) | collective-permute-done | bytes 147488 | tf_op jit(solution)/shard_map/ppermute | solution.py:232
  67.3 2.1 %collective-permute-done.7.b0_ref = bf16[192,384]{1,0:T(8,128)(2,1)S(1)} collective-permute-done((bf16[192,384]{1,0:T(8,128)(2,1)S(1)}, bf16[192,384]{1,0:T(8,128)(2,1)S(1)}, u32[]{:S(2)}, u32[]{:S(2)}) %collective-permute-start.7) | collective-permute-done | bytes 147488 | tf_op jit(solution)/shard_map/ppermute | solution.py:232
  69.4 3.1 %shard_map.70 = (bf16[192,384]{1,0:T(8,128)(2,1)S(1)}, bf16[192,384]{1,0:T(8,128)(2,1)S(1)}) custom-call(bf16[192,384]{1,0:T(8,128)(2,1)S(1)} %add_convert_fusion.5.a0_ref, bf16[192,384]{1,0:T(8,128)(2,1)S(1)} %collective-permute-done.7.b0_ref, bf16[192,384]{1,0:T(8,128)(2,1)S(1)} %add_convert_fusion.a1_ref, ...), custom_call_target="tpu_custom_call" | custom-call | flops 707788800 | bytes 1474560 | tf_op jit(solution)/shard_map/pallas_call | solution.py:146
  72.6 4.8 %collective-permute-start.27 = (bf16[192,384]{1,0:T(8,128)(2,1)S(1)}, bf16[192,384]{1,0:T(8,128)(2,1)S(1)}, u32[]{:S(2)}, u32[]{:S(2)}) collective-permute-start(bf16[192,384]{1,0:T(8,128)(2,1)S(1)} %get-tuple-element.32.s1_ref), channel_id=1, source_target_pairs={{0,6},{2,4},{4,2},{6,0},{8,14},{10,12},{12,10},{14,8},{16,22},{18,... | collective-permute-start | bytes 442376 | tf_op jit(solution)/shard_map/ppermute | solution.py:232
  77.5 3.9 %collective-permute-start.23 = (bf16[192,384]{1,0:T(8,128)(2,1)S(1)}, bf16[192,384]{1,0:T(8,128)(2,1)S(1)}, u32[]{:S(2)}, u32[]{:S(2)}) collective-permute-start(bf16[192,384]{1,0:T(8,128)(2,1)S(1)} %get-tuple-element.32.s1_ref), channel_id=1, source_target_pairs={{0,4},{2,6},{4,0},{6,2},{8,12},{10,14},{12,8},{14,10},{16,20},{18,... | collective-permute-start | bytes 442376 | tf_op jit(solution)/shard_map/ppermute | solution.py:232
  82.1 3.3 %collective-permute-start.19 = (bf16[192,384]{1,0:T(8,128)(2,1)S(1)}, bf16[192,384]{1,0:T(8,128)(2,1)S(1)}, u32[]{:S(2)}, u32[]{:S(2)}) collective-permute-start(bf16[192,384]{1,0:T(8,128)(2,1)S(1)} %get-tuple-element.32.s1_ref), channel_id=1, source_target_pairs={{0,2},{2,0},{4,6},{6,4},{8,10},{10,8},{12,14},{14,12},{16,18},{18,... | collective-permute-start | bytes 442376 | tf_op jit(solution)/shard_map/ppermute | solution.py:232
  85.5 2.6 %collective-permute-start.17 = (bf16[192,384]{1,0:T(8,128)(2,1)S(1)}, bf16[192,384]{1,0:T(8,128)(2,1)S(1)}, u32[]{:S(2)}, u32[]{:S(2)}) collective-permute-start(bf16[192,384]{1,0:T(8,128)(2,1)S(1)} %get-tuple-element.32.s1_ref), channel_id=1, source_target_pairs={{0,1},{2,3},{4,5},{6,7},{8,9},{10,11},{12,13},{14,15},{16,17},{18,... | collective-permute-start | bytes 442376 | tf_op jit(solution)/shard_map/ppermute | solution.py:232
  88.2 2.4 %collective-permute-start.29 = (bf16[192,384]{1,0:T(8,128)(2,1)S(1)}, bf16[192,384]{1,0:T(8,128)(2,1)S(1)}, u32[]{:S(2)}, u32[]{:S(2)}) collective-permute-start(bf16[192,384]{1,0:T(8,128)(2,1)S(1)} %collective-permute-done.27.s1_ref), channel_id=1, source_target_pairs={{0,1},{2,3},{4,5},{6,7},{8,9},{10,11},{12,13},{14,15},{16,17},{18,... | collective-permute-start | bytes 442376 | tf_op jit(solution)/shard_map/ppermute | solution.py:232
  90.7 2.4 %collective-permute-start.25 = (bf16[192,384]{1,0:T(8,128)(2,1)S(1)}, bf16[192,384]{1,0:T(8,128)(2,1)S(1)}, u32[]{:S(2)}, u32[]{:S(2)}) collective-permute-start(bf16[192,384]{1,0:T(8,128)(2,1)S(1)} %collective-permute-done.23.s1_ref), channel_id=1, source_target_pairs={{0,1},{2,3},{4,5},{6,7},{8,9},{10,11},{12,13},{14,15},{16,17},{18,... | collective-permute-start | bytes 442376 | tf_op jit(solution)/shard_map/ppermute | solution.py:232
  93.2 2.4 %collective-permute-start.21 = (bf16[192,384]{1,0:T(8,128)(2,1)S(1)}, bf16[192,384]{1,0:T(8,128)(2,1)S(1)}, u32[]{:S(2)}, u32[]{:S(2)}) collective-permute-start(bf16[192,384]{1,0:T(8,128)(2,1)S(1)} %collective-permute-done.19.s1_ref), channel_id=1, source_target_pairs={{0,1},{2,3},{4,5},{6,7},{8,9},{10,11},{12,13},{14,15},{16,17},{18,... | collective-permute-start | bytes 442376 | tf_op jit(solution)/shard_map/ppermute | solution.py:232
  95.6 2.1 %shard_map.64.q_ref = bf16[4,512,192]{2,1,0:T(8,128)(2,1)S(1)} custom-call(s32[1]{0:T(128)} %bitcast.2.flag_ref, bf16[512,768]{1,0:T(8,128)(2,1)S(1)} %copy-done.8, bf16[768,2304]{1,0:T(8,128)(2,1)S(1)} %copy-done.6), custom_call_target="tpu_custom_call" | custom-call | flops 603979776 | bytes 1966080 | tf_op jit(solution)/shard_map/pallas_call | solution.py:43
  100.2 1.2 %shard_map.73.refs_2_ = bf16[512,192]{1,0:T(8,128)(2,1)S(1)} custom-call(s32[2]{0:T(128)S(1)} %get-tuple-element.36.ids_ref, bf16[4,512,192]{2,1,0:T(8,128)(2,1)S(1)} %shard_map.64.q_ref, bf16[192,384]{1,0:T(8,128)(2,1)S(1)} %collective-permute-done.22.s0_ref, bf16[192,384]{1,0:T(8,128)(2,1)S(1)} %collective-permute-done.23.s1_ref, ...), custom_call_target="tpu_custom_call" | custom-call | flops 226492416 | bytes 983040 | tf_op jit(solution)/shard_map/pallas_call | solution.py:174
  (95 shorter events, 17.6 us)
Async XLA Ops:
  13.3 21.9 %collective-permute-start.10 = (bf16[192,384]{1,0:T(8,128)(2,1)}, bf16[192,384]{1,0:T(8,128)(2,1)}, u32[]{:S(2)}, u32[]{:S(2)}) collective-permute-start(bf16[192,384]{1,0:T(8,128)(2,1)} %get-tuple-element.28), channel_id=1, source_target_pairs={{1,0},{3,2},{5,4},{7,6},{9,8},{11,10},{13,12},{15,14},{17,16},{19,... | collective-permute-start | bytes 442376 | tf_op jit(solution)/shard_map/ppermute | solution.py:232
  18.8 17.6 %collective-permute-start.12 = (bf16[192,384]{1,0:T(8,128)(2,1)}, bf16[192,384]{1,0:T(8,128)(2,1)}, u32[]{:S(2)}, u32[]{:S(2)}) collective-permute-start(bf16[192,384]{1,0:T(8,128)(2,1)} %get-tuple-element.29), channel_id=1, source_target_pairs={{1,0},{3,2},{5,4},{7,6},{9,8},{11,10},{13,12},{15,14},{17,16},{19,... | collective-permute-start | bytes 442376 | tf_op jit(solution)/shard_map/ppermute | solution.py:232
  25.8 12.1 %collective-permute-start.8 = (bf16[192,384]{1,0:T(8,128)(2,1)}, bf16[192,384]{1,0:T(8,128)(2,1)}, u32[]{:S(2)}, u32[]{:S(2)}) collective-permute-start(bf16[192,384]{1,0:T(8,128)(2,1)} %get-tuple-element.27), channel_id=1, source_target_pairs={{1,0},{3,2},{5,4},{7,6},{9,8},{11,10},{13,12},{15,14},{17,16},{19,... | collective-permute-start | bytes 442376 | tf_op jit(solution)/shard_map/ppermute | solution.py:232
  30.6 19.0 %collective-permute-start.14 = (bf16[192,384]{1,0:T(8,128)(2,1)}, bf16[192,384]{1,0:T(8,128)(2,1)S(1)}, u32[]{:S(2)}, u32[]{:S(2)}) collective-permute-start(bf16[192,384]{1,0:T(8,128)(2,1)} %get-tuple-element.30), channel_id=1, source_target_pairs={{1,0},{3,2},{5,4},{7,6},{9,8},{11,10},{13,12},{15,14},{17,16},{19,... | collective-permute-start | bytes 442376 | tf_op jit(solution)/shard_map/ppermute | solution.py:232
  32.0 7.0 %collective-permute-start = (bf16[192,384]{1,0:T(8,128)(2,1)}, bf16[192,384]{1,0:T(8,128)(2,1)S(1)}, u32[]{:S(2)}, u32[]{:S(2)}) collective-permute-start(bf16[192,384]{1,0:T(8,128)(2,1)} %get-tuple-element.20), channel_id=1, source_target_pairs={{0,1},{1,0},{2,3},{3,2},{4,5},{5,4},{6,7},{7,6},{8,9},{9,8},{10,11... | collective-permute-start | bytes 442376 | tf_op jit(solution)/shard_map/ppermute | solution.py:232
  35.2 8.8 %collective-permute-start.2 = (bf16[192,384]{1,0:T(8,128)(2,1)}, bf16[192,384]{1,0:T(8,128)(2,1)S(1)}, u32[]{:S(2)}, u32[]{:S(2)}) collective-permute-start(bf16[192,384]{1,0:T(8,128)(2,1)} %copy-done.18), channel_id=1, source_target_pairs={{0,1},{1,0},{2,3},{3,2},{4,5},{5,4},{6,7},{7,6},{8,9},{9,8},{10,11... | collective-permute-start | bytes 442376 | tf_op jit(solution)/shard_map/ppermute | solution.py:232
  36.4 11.2 %collective-permute-start.4 = (bf16[192,384]{1,0:T(8,128)(2,1)}, bf16[192,384]{1,0:T(8,128)(2,1)S(1)}, u32[]{:S(2)}, u32[]{:S(2)}) collective-permute-start(bf16[192,384]{1,0:T(8,128)(2,1)} %copy-done.17), channel_id=1, source_target_pairs={{0,1},{1,0},{2,3},{3,2},{4,5},{5,4},{6,7},{7,6},{8,9},{9,8},{10,11... | collective-permute-start | bytes 442376 | tf_op jit(solution)/shard_map/ppermute | solution.py:232
  38.0 24.3 %collective-permute-start.6 = (bf16[192,384]{1,0:T(8,128)(2,1)S(1)}, bf16[192,384]{1,0:T(8,128)(2,1)S(1)}, u32[]{:S(2)}, u32[]{:S(2)}) collective-permute-start(bf16[192,384]{1,0:T(8,128)(2,1)S(1)} %copy-done.16), channel_id=1, source_target_pairs={{0,1},{1,0},{2,3},{3,2},{4,5},{5,4},{6,7},{7,6},{8,9},{9,8},{10,11... | collective-permute-start | bytes 442376 | tf_op jit(solution)/shard_map/ppermute | solution.py:232
  39.1 13.5 %collective-permute-start.11 = (bf16[192,384]{1,0:T(8,128)(2,1)S(1)}, bf16[192,384]{1,0:T(8,128)(2,1)S(1)}, u32[]{:S(2)}, u32[]{:S(2)}) collective-permute-start(bf16[192,384]{1,0:T(8,128)(2,1)S(1)} %add_convert_fusion.3), channel_id=1, source_target_pairs={{0,2},{2,0},{4,6},{6,4},{8,10},{10,8},{12,14},{14,12},{16,18},{18,... | collective-permute-start | bytes 442376 | tf_op jit(solution)/shard_map/ppermute | solution.py:232
  44.1 9.1 %collective-permute-start.13 = (bf16[192,384]{1,0:T(8,128)(2,1)S(1)}, bf16[192,384]{1,0:T(8,128)(2,1)S(1)}, u32[]{:S(2)}, u32[]{:S(2)}) collective-permute-start(bf16[192,384]{1,0:T(8,128)(2,1)S(1)} %add_convert_fusion.2), channel_id=1, source_target_pairs={{0,4},{2,6},{4,0},{6,2},{8,12},{10,14},{12,8},{14,10},{16,20},{18,... | collective-permute-start | bytes 442376 | tf_op jit(solution)/shard_map/ppermute | solution.py:232
  47.6 7.9 %collective-permute-start.9 = (bf16[192,384]{1,0:T(8,128)(2,1)S(1)}, bf16[192,384]{1,0:T(8,128)(2,1)S(1)}, u32[]{:S(2)}, u32[]{:S(2)}) collective-permute-start(bf16[192,384]{1,0:T(8,128)(2,1)S(1)} %add_convert_fusion.4), channel_id=1, source_target_pairs={{0,6},{2,4},{4,2},{6,0},{8,14},{10,12},{12,10},{14,8},{16,22},{18,... | collective-permute-start | bytes 442376 | tf_op jit(solution)/shard_map/ppermute | solution.py:232
  49.6 12.6 %collective-permute-start.1 = (bf16[192,384]{1,0:T(8,128)(2,1)S(1)}, bf16[192,384]{1,0:T(8,128)(2,1)S(1)}, u32[]{:S(2)}, u32[]{:S(2)}) collective-permute-start(bf16[192,384]{1,0:T(8,128)(2,1)S(1)} %add_convert_fusion.9), channel_id=1, source_target_pairs={{0,6},{1,7},{2,4},{3,5},{4,2},{5,3},{6,0},{7,1},{8,14},{9,15},{10,... | collective-permute-start | bytes 442376 | tf_op jit(solution)/shard_map/ppermute | solution.py:232
  52.6 9.7 %collective-permute-start.3 = (bf16[192,384]{1,0:T(8,128)(2,1)S(1)}, bf16[192,384]{1,0:T(8,128)(2,1)S(1)}, u32[]{:S(2)}, u32[]{:S(2)}) collective-permute-start(bf16[192,384]{1,0:T(8,128)(2,1)S(1)} %add_convert_fusion.8), channel_id=1, source_target_pairs={{0,2},{1,3},{2,0},{3,1},{4,6},{5,7},{6,4},{7,5},{8,10},{9,11},{10,... | collective-permute-start | bytes 442376 | tf_op jit(solution)/shard_map/ppermute | solution.py:232
  53.1 9.2 %collective-permute-start.5 = (bf16[192,384]{1,0:T(8,128)(2,1)S(1)}, bf16[192,384]{1,0:T(8,128)(2,1)S(1)}, u32[]{:S(2)}, u32[]{:S(2)}) collective-permute-start(bf16[192,384]{1,0:T(8,128)(2,1)S(1)} %add_convert_fusion.7), channel_id=1, source_target_pairs={{0,4},{1,5},{2,6},{3,7},{4,0},{5,1},{6,2},{7,3},{8,12},{9,13},{10,... | collective-permute-start | bytes 442376 | tf_op jit(solution)/shard_map/ppermute | solution.py:232
  56.6 10.8 %collective-permute-start.15 = (bf16[192,384]{1,0:T(8,128)(2,1)S(1)}, bf16[192,384]{1,0:T(8,128)(2,1)S(1)}, u32[]{:S(2)}, u32[]{:S(2)}) collective-permute-start(bf16[192,384]{1,0:T(8,128)(2,1)S(1)} %add_convert_fusion.a1_ref), channel_id=1, source_target_pairs={{0,8},{2,10},{4,12},{6,14},{8,0},{10,2},{12,4},{14,6},{16,24},{18,... | collective-permute-start | bytes 442376 | tf_op jit(solution)/shard_map/ppermute | solution.py:232
  62.4 7.0 %collective-permute-start.7 = (bf16[192,384]{1,0:T(8,128)(2,1)S(1)}, bf16[192,384]{1,0:T(8,128)(2,1)S(1)}, u32[]{:S(2)}, u32[]{:S(2)}) collective-permute-start(bf16[192,384]{1,0:T(8,128)(2,1)S(1)} %add_convert_fusion.5.a0_ref), channel_id=1, source_target_pairs={{0,8},{1,9},{2,10},{3,11},{4,12},{5,13},{6,14},{7,15},{8,0},{9,1},... | collective-permute-start | bytes 442376 | tf_op jit(solution)/shard_map/ppermute | solution.py:232
  62.5 33.1 %copy-start.8 = (bf16[512,768]{1,0:T(8,128)(2,1)S(1)}, bf16[512,768]{1,0:T(8,128)(2,1)}, u32[]{:S(2)}) copy-start(bf16[512,768]{1,0:T(8,128)(2,1)} %tokens_ref.3) | copy-start | bytes 2359300
  63.6 31.9 %copy-start.6 = (bf16[768,2304]{1,0:T(8,128)(2,1)S(1)}, bf16[768,2304]{1,0:T(8,128)(2,1)}, u32[]{:S(2)}) copy-start(bf16[768,2304]{1,0:T(8,128)(2,1)} %weight_ref.3) | copy-start | bytes 10616836
  72.5 9.6 %collective-permute-start.26 = (bf16[192,384]{1,0:T(8,128)(2,1)S(1)}, bf16[192,384]{1,0:T(8,128)(2,1)S(1)}, u32[]{:S(2)}, u32[]{:S(2)}) collective-permute-start(bf16[192,384]{1,0:T(8,128)(2,1)S(1)} %get-tuple-element.31.s0_ref), channel_id=1, source_target_pairs={{0,6},{1,7},{2,4},{3,5},{4,2},{5,3},{6,0},{7,1},{8,14},{9,15},{10,... | collective-permute-start | bytes 442376 | tf_op jit(solution)/shard_map/ppermute | solution.py:232
  72.6 12.8 %collective-permute-start.27 = (bf16[192,384]{1,0:T(8,128)(2,1)S(1)}, bf16[192,384]{1,0:T(8,128)(2,1)S(1)}, u32[]{:S(2)}, u32[]{:S(2)}) collective-permute-start(bf16[192,384]{1,0:T(8,128)(2,1)S(1)} %get-tuple-element.32.s1_ref), channel_id=1, source_target_pairs={{0,6},{2,4},{4,2},{6,0},{8,14},{10,12},{12,10},{14,8},{16,22},{18,... | collective-permute-start | bytes 442376 | tf_op jit(solution)/shard_map/ppermute | solution.py:232
  77.4 8.1 %collective-permute-start.22 = (bf16[192,384]{1,0:T(8,128)(2,1)S(1)}, bf16[192,384]{1,0:T(8,128)(2,1)S(1)}, u32[]{:S(2)}, u32[]{:S(2)}) collective-permute-start(bf16[192,384]{1,0:T(8,128)(2,1)S(1)} %get-tuple-element.31.s0_ref), channel_id=1, source_target_pairs={{0,4},{1,5},{2,6},{3,7},{4,0},{5,1},{6,2},{7,3},{8,12},{9,13},{10,... | collective-permute-start | bytes 442376 | tf_op jit(solution)/shard_map/ppermute | solution.py:232
  77.5 10.6 %collective-permute-start.23 = (bf16[192,384]{1,0:T(8,128)(2,1)S(1)}, bf16[192,384]{1,0:T(8,128)(2,1)S(1)}, u32[]{:S(2)}, u32[]{:S(2)}) collective-permute-start(bf16[192,384]{1,0:T(8,128)(2,1)S(1)} %get-tuple-element.32.s1_ref), channel_id=1, source_target_pairs={{0,4},{2,6},{4,0},{6,2},{8,12},{10,14},{12,8},{14,10},{16,20},{18,... | collective-permute-start | bytes 442376 | tf_op jit(solution)/shard_map/ppermute | solution.py:232
  81.4 6.8 %collective-permute-start.18 = (bf16[192,384]{1,0:T(8,128)(2,1)S(1)}, bf16[192,384]{1,0:T(8,128)(2,1)S(1)}, u32[]{:S(2)}, u32[]{:S(2)}) collective-permute-start(bf16[192,384]{1,0:T(8,128)(2,1)S(1)} %get-tuple-element.31.s0_ref), channel_id=1, source_target_pairs={{0,2},{1,3},{2,0},{3,1},{4,6},{5,7},{6,4},{7,5},{8,10},{9,11},{10,... | collective-permute-start | bytes 442376 | tf_op jit(solution)/shard_map/ppermute | solution.py:232
  82.1 8.5 %collective-permute-start.19 = (bf16[192,384]{1,0:T(8,128)(2,1)S(1)}, bf16[192,384]{1,0:T(8,128)(2,1)S(1)}, u32[]{:S(2)}, u32[]{:S(2)}) collective-permute-start(bf16[192,384]{1,0:T(8,128)(2,1)S(1)} %get-tuple-element.32.s1_ref), channel_id=1, source_target_pairs={{0,2},{2,0},{4,6},{6,4},{8,10},{10,8},{12,14},{14,12},{16,18},{18,... | collective-permute-start | bytes 442376 | tf_op jit(solution)/shard_map/ppermute | solution.py:232
  85.4 5.3 %collective-permute-start.16 = (bf16[192,384]{1,0:T(8,128)(2,1)S(1)}, bf16[192,384]{1,0:T(8,128)(2,1)S(1)}, u32[]{:S(2)}, u32[]{:S(2)}) collective-permute-start(bf16[192,384]{1,0:T(8,128)(2,1)S(1)} %get-tuple-element.31.s0_ref), channel_id=1, source_target_pairs={{0,1},{1,0},{2,3},{3,2},{4,5},{5,4},{6,7},{7,6},{8,9},{9,8},{10,11... | collective-permute-start | bytes 442376 | tf_op jit(solution)/shard_map/ppermute | solution.py:232
  85.5 7.6 %collective-permute-start.17 = (bf16[192,384]{1,0:T(8,128)(2,1)S(1)}, bf16[192,384]{1,0:T(8,128)(2,1)S(1)}, u32[]{:S(2)}, u32[]{:S(2)}) collective-permute-start(bf16[192,384]{1,0:T(8,128)(2,1)S(1)} %get-tuple-element.32.s1_ref), channel_id=1, source_target_pairs={{0,1},{2,3},{4,5},{6,7},{8,9},{10,11},{12,13},{14,15},{16,17},{18,... | collective-permute-start | bytes 442376 | tf_op jit(solution)/shard_map/ppermute | solution.py:232
  88.1 5.1 %collective-permute-start.28 = (bf16[192,384]{1,0:T(8,128)(2,1)S(1)}, bf16[192,384]{1,0:T(8,128)(2,1)S(1)}, u32[]{:S(2)}, u32[]{:S(2)}) collective-permute-start(bf16[192,384]{1,0:T(8,128)(2,1)S(1)} %collective-permute-done.26.s0_ref), channel_id=1, source_target_pairs={{0,1},{1,0},{2,3},{3,2},{4,5},{5,4},{6,7},{7,6},{8,9},{9,8},{10,11... | collective-permute-start | bytes 442376 | tf_op jit(solution)/shard_map/ppermute | solution.py:232
  88.2 10.7 %collective-permute-start.29 = (bf16[192,384]{1,0:T(8,128)(2,1)S(1)}, bf16[192,384]{1,0:T(8,128)(2,1)S(1)}, u32[]{:S(2)}, u32[]{:S(2)}) collective-permute-start(bf16[192,384]{1,0:T(8,128)(2,1)S(1)} %collective-permute-done.27.s1_ref), channel_id=1, source_target_pairs={{0,1},{2,3},{4,5},{6,7},{8,9},{10,11},{12,13},{14,15},{16,17},{18,... | collective-permute-start | bytes 442376 | tf_op jit(solution)/shard_map/ppermute | solution.py:232
  90.6 9.6 %collective-permute-start.24 = (bf16[192,384]{1,0:T(8,128)(2,1)S(1)}, bf16[192,384]{1,0:T(8,128)(2,1)S(1)}, u32[]{:S(2)}, u32[]{:S(2)}) collective-permute-start(bf16[192,384]{1,0:T(8,128)(2,1)S(1)} %collective-permute-done.22.s0_ref), channel_id=1, source_target_pairs={{0,1},{1,0},{2,3},{3,2},{4,5},{5,4},{6,7},{7,6},{8,9},{9,8},{10,11... | collective-permute-start | bytes 442376 | tf_op jit(solution)/shard_map/ppermute | solution.py:232
  90.7 9.5 %collective-permute-start.25 = (bf16[192,384]{1,0:T(8,128)(2,1)S(1)}, bf16[192,384]{1,0:T(8,128)(2,1)S(1)}, u32[]{:S(2)}, u32[]{:S(2)}) collective-permute-start(bf16[192,384]{1,0:T(8,128)(2,1)S(1)} %collective-permute-done.23.s1_ref), channel_id=1, source_target_pairs={{0,1},{2,3},{4,5},{6,7},{8,9},{10,11},{12,13},{14,15},{16,17},{18,... | collective-permute-start | bytes 442376 | tf_op jit(solution)/shard_map/ppermute | solution.py:232
  93.1 8.4 %collective-permute-start.20 = (bf16[192,384]{1,0:T(8,128)(2,1)S(1)}, bf16[192,384]{1,0:T(8,128)(2,1)S(1)}, u32[]{:S(2)}, u32[]{:S(2)}) collective-permute-start(bf16[192,384]{1,0:T(8,128)(2,1)S(1)} %collective-permute-done.18.s0_ref), channel_id=1, source_target_pairs={{0,1},{1,0},{2,3},{3,2},{4,5},{5,4},{6,7},{7,6},{8,9},{9,8},{10,11... | collective-permute-start | bytes 442376 | tf_op jit(solution)/shard_map/ppermute | solution.py:232
  93.2 8.3 %collective-permute-start.21 = (bf16[192,384]{1,0:T(8,128)(2,1)S(1)}, bf16[192,384]{1,0:T(8,128)(2,1)S(1)}, u32[]{:S(2)}, u32[]{:S(2)}) collective-permute-start(bf16[192,384]{1,0:T(8,128)(2,1)S(1)} %collective-permute-done.19.s1_ref), channel_id=1, source_target_pairs={{0,1},{2,3},{4,5},{6,7},{8,9},{10,11},{12,13},{14,15},{16,17},{18,... | collective-permute-start | bytes 442376 | tf_op jit(solution)/shard_map/ppermute | solution.py:232
  (18 other events, 79.0 us)

commit v2 on v0

v2 whole, which is shorter than its diff:
```python
import functools

import jax
import jax.numpy as jnp
from jax import lax
from jax.experimental import pallas as pl
from jax.experimental.pallas import tpu as pltpu
from jax.sharding import PartitionSpec as P

VIEWS = 16
NS_STEPS = 5
BF16 = jnp.bfloat16
F32 = jnp.float32
K1_LIMIT = 62
SMALL_LIMIT = 24

coef_a = 3.4445
coef_b = -4.775
coef_c = 2.0315
step_size = 0.8


def mm(a, b, dims):
    return lax.dot_general(a, b, (dims, ((), ())), preferred_element_type=F32)


NN = ((1,), (0,))
NT = ((1,), (1,))
TN = ((0,), (0,))


def grad_kernel(ids_ref, view_ref, tok_hbm, qkv_hbm, gate_hbm, up_hbm, down_hbm, keep_ref, give_ref, tok, wkv, fast, kv, both_w, down_w, sems):
    own, core, owner = ids_ref[0], ids_ref[1], ids_ref[2]
    rows, width = tok.shape
    head_dim = kv.shape[3]
    hidden = down_w.shape[2]
    heads = gate_hbm.shape[0]
    span = 2 * head_dim
    pairs = heads // 2
    half = head_dim // 2
    count = iter(range(3 + 2 * pairs + 3 * heads))

    def fetch(source, target):
        copy = pltpu.make_async_copy(source, target, sems.at[next(count)])
        copy.start()
        return copy

    tok_copy = fetch(tok_hbm, tok)
    kv_copies, fast_copies = [], []
    for pair in range(pairs):
        kv_copies.append([
            fetch(qkv_hbm.at[:, (1 + which) * width + pair * span : (1 + which) * width + (pair + 1) * span], wkv.at[pair, which])
            for which in range(2)
        ])
        for head in (2 * pair, 2 * pair + 1):
            fast_copies.append([fetch(ref.at[head], fast.at[head, i]) for i, ref in enumerate((gate_hbm, up_hbm, down_hbm))])

    flag = view_ref[owner].astype(F32)
    tok_copy.wait()
    for pair in range(pairs):
        for which in range(2):
            kv_copies[pair][which].wait()
            part = mm(tok[...], wkv[pair, which], NN).astype(BF16)
            if which == 1:
                part = (part.astype(F32) * flag).astype(BF16)
            kv[which, 0] = part[:, :head_dim]
            kv[which, 1] = part[:, head_dim:]
        for inner in range(2):
            head = 2 * pair + inner
            for copy in fast_copies[head]:
                copy.wait()
            both_w[inner, :, :hidden] = fast[head, 0].astype(BF16)
            both_w[inner, :, hidden:] = fast[head, 1].astype(BF16)
            down_w[inner] = fast[head, 2].astype(BF16)
            both_sum = down_sum = None
            chunk = rows // 2
            for start in range(0, rows, chunk):
                k = kv[0, inner, start : start + chunk, :]
                v = kv[1, inner, start : start + chunk, :]
                both = mm(k, both_w[inner], NN)
                dhid = -mm(v, down_w[inner], NN)
                gate, upper = both[:, :hidden], both[:, hidden:]
                sig = jax.nn.sigmoid(gate)
                act = gate * sig
                hid = (act * upper).astype(BF16)
                dgate = (dhid * upper * (sig * (1.0 + gate * (1.0 - sig)))).astype(BF16)
                dup = (dhid * act).astype(BF16)
                both_part = mm(k, jnp.concatenate([dgate, dup], axis=1), TN)
                down_part = mm(v, hid, TN)
                both_sum = both_part if both_sum is None else both_sum + both_part
                down_sum = down_part if down_sum is None else down_sum + down_part
            gate_g = both_sum[:, :hidden].astype(BF16)
            up_g = both_sum[:, hidden:].astype(BF16)
            down_g = (-down_sum).astype(BF16)
            slot = own ^ head

            @pl.when(core == 0)
            def _():
                keep_ref[slot, :head_dim] = gate_g
                keep_ref[slot, head_dim:] = up_g[:half]
                give_ref[slot, :head_dim] = down_g
                give_ref[slot, head_dim:] = up_g[half:]

            @pl.when(core != 0)
            def _():
                keep_ref[slot, :head_dim] = down_g
                keep_ref[slot, head_dim:] = up_g[half:]
                give_ref[slot, :head_dim] = gate_g
                give_ref[slot, head_dim:] = up_g[:half]


def gradients(ids, view_kind, tokens, qkv_weight, w_gate, w_up, w_down_t):
    rows, width = tokens.shape
    heads, head_dim, hidden = w_gate.shape
    pairs = heads // 2
    smem, vmem, hbm = (pl.BlockSpec(memory_space=s) for s in (pltpu.SMEM, pltpu.VMEM, pl.ANY))
    shape = jax.ShapeDtypeStruct((heads, head_dim * 3 // 2, hidden), BF16)
    return pl.pallas_call(
        grad_kernel,
        out_shape=[shape] * 2,
        in_specs=[smem] * 2 + [hbm] * 5,
        out_specs=[vmem] * 2,
        scratch_shapes=[
            pltpu.VMEM((rows, width), BF16),
            pltpu.VMEM((pairs, 2, width, 2 * head_dim), BF16),
            pltpu.VMEM((heads, 3, head_dim, hidden), F32),
            pltpu.VMEM((2, 2, rows, head_dim), BF16),
            pltpu.VMEM((2, head_dim, 2 * hidden), BF16),
            pltpu.VMEM((2, head_dim, hidden), BF16),
            pltpu.SemaphoreType.DMA((1 + 2 * pairs + 3 * heads,)),
        ],
        compiler_params=pltpu.CompilerParams(vmem_limit_bytes=K1_LIMIT * 1024 * 1024),
        cost_estimate=pl.CostEstimate(
            flops=4 * rows * width * width + 12 * heads * rows * head_dim * hidden,
            bytes_accessed=2 * rows * width + 4 * width * width + 12 * heads * head_dim * hidden,
            transcendentals=heads * rows * hidden,
        ),
        name="gradients",
    )(ids, view_kind, tokens, qkv_weight, w_gate, w_up, w_down_t)


def small(kernel, shapes, operands, smem=0, flops=0, nbytes=0, name=None):
    specs = [pl.BlockSpec(memory_space=pltpu.SMEM)] * smem + [pl.BlockSpec(memory_space=pltpu.VMEM)] * (len(operands) - smem)
    return pl.pallas_call(
        kernel,
        out_shape=shapes,
        in_specs=specs,
        compiler_params=pltpu.CompilerParams(vmem_limit_bytes=SMALL_LIMIT * 1024 * 1024),
        cost_estimate=pl.CostEstimate(flops=flops, bytes_accessed=nbytes, transcendentals=0),
        name=name,
    )(*operands)


def query_kernel(tokens_ref, weight_ref, out_ref):
    heads, _, head_dim = out_ref.shape
    part = mm(tokens_ref[...], weight_ref[...], NN).astype(BF16)
    for head in range(heads):
        out_ref[head] = part[:, head * head_dim : (head + 1) * head_dim]


def project_query(tokens, weight, heads):
    rows, width = tokens.shape
    return pl.pallas_call(
        query_kernel,
        out_shape=jax.ShapeDtypeStruct((heads, rows, width // heads), BF16),
        grid=(1,),
        in_specs=[pl.BlockSpec((rows, width), lambda i: (0, 0)), pl.BlockSpec((width, width), lambda i: (0, 0))],
        out_specs=pl.BlockSpec((heads, rows, width // heads), lambda i: (0, 0, 0)),
        compiler_params=pltpu.CompilerParams(vmem_limit_bytes=SMALL_LIMIT * 1024 * 1024),
        cost_estimate=pl.CostEstimate(flops=2 * rows * width * width, bytes_accessed=4 * width * (rows + width), transcendentals=0),
        name="query",
    )(tokens, weight)


def pair_sum_kernel(keep_ref, got_ref, *out_refs):
    for slot, out_ref in enumerate(out_refs):
        out_ref[...] = (keep_ref[slot].astype(F32) + got_ref[slot].astype(F32)).astype(BF16)


def sum_kernel(*refs):
    *parts, out_ref = refs
    total = parts[0][...].astype(F32)
    for part in parts[1:]:
        total = total + part[...].astype(F32)
    out_ref[...] = total.astype(BF16)


def newton_kernel(core_ref, mine_ref, other_ref, half_ref, got_ref, base_ref, base_half_ref, out_ref):
    head_dim = base_ref.shape[0]
    half = half_ref.shape[0]
    even = core_ref[0] == 0
    first = mine_ref[:head_dim].astype(F32) + other_ref[:head_dim].astype(F32)
    a, b = half_ref[...], got_ref[...]
    second = jnp.concatenate([jnp.where(even, a, b), jnp.where(even, b, a)], axis=0).astype(F32)
    iterates = []
    for total in (first, second):
        norm = jnp.sqrt(jnp.sum(total * total))
        iterates.append((total / (norm + 1e-07)).astype(BF16))
    for step in range(NS_STEPS):
        grams = [mm(x, x, NT).astype(BF16) for x in iterates]
        squares = [mm(g, g, NN) for g in grams]
        mixers = [(coef_b * g.astype(F32) + coef_c * s).astype(BF16) for g, s in zip(grams, squares)]
        moved = [mm(m, x, NN) for m, x in zip(mixers, iterates)]
        iterates = [(coef_a * x.astype(F32) + y).astype(BF16) for x, y in zip(iterates, moved)]
    first, second = [x.astype(F32) for x in iterates]
    out_ref[:head_dim] = (base_ref[...] - step_size * first).astype(BF16)
    second = jnp.where(even, second[:half], second[half:])
    out_ref[head_dim:] = (base_half_ref[...] - step_size * second).astype(BF16)


def head_output(even, q, here_ref, there_ref):
    head_dim = q.shape[1]
    here, there = here_ref[...], there_ref[...]
    a, b = jnp.where(even, here, there), jnp.where(even, there, here)
    up_b = jnp.concatenate([a[head_dim:], b[head_dim:]], axis=0)
    gate = mm(q, a[:head_dim], NN)
    upper = mm(q, up_b, NN)
    hidden = (gate * jax.nn.sigmoid(gate) * upper).astype(BF16)
    return mm(hidden, b[:head_dim], NT).astype(BF16)


def apply_kernel(ids_ref, q_ref, here_ref, there_ref, out_ref):
    out_ref[...] = head_output(ids_ref[1] == 0, q_ref[ids_ref[0]], here_ref, there_ref)


def finish_kernel(ids_ref, q_ref, here_ref, there_ref, *refs):
    *pieces, out_ref = refs
    heads, _, head_dim = q_ref.shape
    last = ids_ref[0]
    own = last ^ (heads - 1)
    piece = head_output(ids_ref[1] == 0, q_ref[last], here_ref, there_ref)
    for case in range(heads):

        @pl.when(own == case)
        def _():
            for head in range(heads):
                far = head ^ case
                out_ref[:, head * head_dim : (head + 1) * head_dim] = piece if far == heads - 1 else pieces[far][...]


def shards(tokens, qkv_weight, w_gate, w_up, w_down, view_kind):
    rows, width = tokens.shape
    heads, head_dim, hidden = w_gate.shape
    groups = lax.axis_size("tok")
    place = lax.axis_index("tok")
    core = place % 2
    own = (place // 2) % heads
    view_rows = rows * groups // VIEWS
    owner = place * rows // view_rows
    w_down_t = jnp.transpose(w_down, (0, 2, 1))
    block = jax.ShapeDtypeStruct((head_dim * 3 // 2, hidden), BF16)
    half = head_dim // 2

    def exchange(x, bits):
        return lax.ppermute(x, "tok", [(i, i ^ bits) for i in range(groups)])

    ids = jnp.stack([own, core, owner]).astype(jnp.int32)
    keep, give = gradients(ids, view_kind, tokens, qkv_weight, w_gate, w_up, w_down_t)
    got = exchange(give, 1)
    sums = small(pair_sum_kernel, [block] * heads, (keep, got), name="pair_sum", nbytes=9 * keep.size)
    arrived = [exchange(sums[far], 2 * far) for far in (3, 1, 2)]
    query = project_query(tokens, qkv_weight, heads)

    mine = lambda w: lax.dynamic_index_in_dim(w, own, 0, keepdims=False)
    base = jnp.where(core == 0, mine(w_gate), mine(w_down_t))
    base_half = lax.dynamic_slice_in_dim(mine(w_up), core * half, half, 0)

    total = small(sum_kernel, block, (sums[0], *arrived), name="plane_sum", nbytes=10 * block.size)
    bits = 2 * heads
    while bits < groups // 2:
        total = small(sum_kernel, block, (total, exchange(total, bits)), name="line_sum", nbytes=6 * block.size)
        bits *= 2
    other = exchange(total, bits)
    up_half = total[head_dim:].astype(F32) + other[head_dim:].astype(F32)
    up_half = up_half.astype(BF16)
    got_half = exchange(up_half, 1)
    fresh = small(
        newton_kernel, block, (core.reshape(1), total, other, up_half, got_half, base, base_half), smem=1,
        flops=2 * NS_STEPS * 2 * head_dim * head_dim * (2 * hidden + head_dim), nbytes=12 * block.size, name="newton",
    )

    here = [fresh] + [exchange(fresh, 2 * far) for far in range(1, heads)]
    there = [exchange(h, 1) for h in here]
    pieces = []
    cost = dict(flops=6 * rows * head_dim * hidden, nbytes=4 * block.size + 4 * rows * head_dim)
    for far in range(heads):
        ids = jnp.stack([own ^ far, core]).astype(jnp.int32)
        args = (ids, query, here[far], there[far])
        if far < heads - 1:
            piece = jax.ShapeDtypeStruct((rows, head_dim), BF16)
            pieces.append(small(apply_kernel, piece, args, smem=1, name="apply", **cost))
    whole = jax.ShapeDtypeStruct((rows, width), BF16)
    return small(finish_kernel, whole, (*args, *pieces), smem=1, name="finish", **cost)


def solution(mesh):
    placed = (P(("scene", "tok"), None), P(), P(), P(), P(), P("scene"))
    return jax.shard_map(
        shards, mesh=mesh, in_specs=placed, out_specs=P(("scene", "tok"), None), check_vma=False
    )
```

time: 203 us -> 74.5 us (0.37)
  waiting for transfers between devices: 107 us -> 31.3 us
  matrix products: 62.4 us -> 0 us
  Pallas kernels: 0 us -> 25.1 us
  between operations: 14.2 us -> 0.1 us
  starting transfers between devices: 0.01 us -> 11.4 us
  local copies, waits for them, and re-layouts: 11.6 us -> 3.24 us
  other arithmetic: 7.94 us -> 2.92 us
    psum x1 -> x0, waiting for transfers between devices: 107 us -> none  [shards(): total = lax.psum(grads, 'tok')]
    dot_general x20 -> x0, matrix products: 62.4 us -> none  [the longest x5 28.9 us: newton(): jnp.einsum('mij,mjk->mik', mixer, iterate, preferred_element_type=jnp.flo...]
    ppermute x0 -> x13, waiting for transfers between devices: none -> 31.3 us  [exchange(): return lax.ppermute(x, 'tok', [(i, i ^ bits) for i in range(groups)])]
    pallas_call x0 -> x9, Pallas kernels: none -> 25.1 us  [the longest x7 13.8 us: small(): pl.pallas_call(kernel, out_shape=shapes, in_specs=specs, compiler_params=...]
    ppermute x0 -> x13, starting transfers between devices: none -> 11.4 us  [exchange(): return lax.ppermute(x, 'tok', [(i, i ^ bits) for i in range(groups)])]
    slice x2 -> x0, local copies, waits for them, and re-layouts: 4.6 us -> none  [the longest x1 2.31 us: shards(): keys = proj[:, width:2 * width].reshape(rows, heads, head_dim)]
    reduce_sum x2 -> x0, other arithmetic: 3.97 us -> none  [the longest x1 2.53 us: shards(): norms = jnp.sqrt(jnp.sum(total * total, axis=(1, 2)))]
    mul x1 -> x0, local copies, waits for them, and re-layouts: 2.3 us -> none  [shards(): masked = values * flag.astype(jnp.bfloat16)]
  transfers between devices with their start and end apart: 1 -> 13, of which waited for: 1 -> 9; matrix products, arithmetic and copies ran while one was open for 1% -> 3% of each run, Pallas kernels for 0% -> 8%
where the time goes in v2:
time: 74.5 us; the launch traced here: 74.1 us
  waiting for transfers between devices  31.3 us (42%)
  Pallas kernels  25.1 us (34%)
  starting transfers between devices  11.4 us (15%)
  local copies, waits for them, and re-layouts  3.24 us (4%)
  other arithmetic  2.92 us (4%)
    ppermute x13, waiting for transfers between devices, exchange(): return lax.ppermute(x, 'tok', [(i, i ^ bits) for i in range(groups)])  31.3 us
    pallas_call x7, Pallas kernels, small(): pl.pallas_call(kernel, out_shape=shapes, in_specs=specs, compiler_params=...  13.8 us
    ppermute x13, starting transfers between devices, exchange(): return lax.ppermute(x, 'tok', [(i, i ^ bits) for i in range(groups)])  11.4 us
    pallas_call x1, Pallas kernels, gradients(): pl.pallas_call(grad_kernel, out_shape=[shape] * 2, in_specs=[smem] * 2 +...  10.4 us
    unnamed x6, local copies, waits for them, and re-layouts  2.3 us
  transfers between devices with their start and end apart: 13, of which 9 were waited for; matrix products, arithmetic and copies ran while one was open for 3% of the time, Pallas kernels for 8%

profile of v2, /device:TPU:0, one launch (start us, length us, event | category | flops | bytes accessed | tf_op | source)
XLA Modules:
  0.0 74.1 jit_solution(16287115809022534297)
XLA Ops:
  0.0 0.6 pad_add_fusion.1.ids_ref
  0.6 10.4 %gradients.1 = (bf16[4,288,384]{2,1,0:T(8,128)(2,1)}, bf16[4,288,384]{2,1,0:T(8,128)(2,1)}) custom-call(s32[3]{0:T(128)} %pad_add_fusion.1.ids_ref, s32[16]{0:T(128)} %view_ref.1, bf16[512,768]{1,0:T(8,128)(2,1)} %tok_hbm.1, bf16[768,2304]{1,0:T(8,128)(2,1)} %qkv_hbm.1, f32[4,192,384]{2,1,0:T(8,128)} %gate_hbm.1, f32[4,192,384]{2,1,0:T(8,128)} %up_hbm.1, ...), custom_call_target="tpu_custom_call" | custom-call | flops 3019898880 | bytes 6684672 | tf_op jit(solution)/shard_map/gradients/pallas_call | solution.py:118
  11.0 0.5 collective-permute-start
  11.6 2.3 %collective-permute-done.got_ref = bf16[4,288,384]{2,1,0:T(8,128)(2,1)S(1)} collective-permute-done((bf16[4,288,384]{2,1,0:T(8,128)(2,1)}, bf16[4,288,384]{2,1,0:T(8,128)(2,1)S(1)}, u32[]{:S(2)}, u32[]{:S(2)}) %collective-permute-start) | collective-permute-done | bytes 884768 | tf_op jit(solution)/shard_map/ppermute | solution.py:255
  13.8 1.2 %copy-done.1 = bf16[4,288,384]{2,1,0:T(8,128)(2,1)S(1)} copy-done((bf16[4,288,384]{2,1,0:T(8,128)(2,1)S(1)}, bf16[4,288,384]{2,1,0:T(8,128)(2,1)}, u32[]{:S(2)}) %copy-start.1) | copy-done | bytes 884760
  15.0 0.2 pair_sum.1
  15.2 4.0 %collective-permute-start.1 = (bf16[288,384]{1,0:T(8,128)(2,1)S(1)}, bf16[288,384]{1,0:T(8,128)(2,1)S(1)}, u32[]{:S(2)}, u32[]{:S(2)}) collective-permute-start(bf16[288,384]{1,0:T(8,128)(2,1)S(1)} %get-tuple-element.14), channel_id=1, source_target_pairs={{0,6},{1,7},{2,4},{3,5},{4,2},{5,3},{6,0},{7,1},{8,14},{9,15},{10,... | collective-permute-start | bytes 663560 | tf_op jit(solution)/shard_map/ppermute | solution.py:255
  19.2 0.5 collective-permute-start.2
  19.8 5.6 %collective-permute-done.1.refs_1_ = bf16[288,384]{1,0:T(8,128)(2,1)S(1)} collective-permute-done((bf16[288,384]{1,0:T(8,128)(2,1)S(1)}, bf16[288,384]{1,0:T(8,128)(2,1)S(1)}, u32[]{:S(2)}, u32[]{:S(2)}) %collective-permute-start.1) | collective-permute-done | bytes 221216 | tf_op jit(solution)/shard_map/ppermute | solution.py:255
  25.4 4.2 %collective-permute-done.2.refs_2_ = bf16[288,384]{1,0:T(8,128)(2,1)S(1)} collective-permute-done((bf16[288,384]{1,0:T(8,128)(2,1)S(1)}, bf16[288,384]{1,0:T(8,128)(2,1)S(1)}, u32[]{:S(2)}, u32[]{:S(2)}) %collective-permute-start.2) | collective-permute-done | bytes 221216 | tf_op jit(solution)/shard_map/ppermute | solution.py:255
  29.6 0.2 collective-permute-done.3.refs_3_
  29.8 0.8 %plane_sum.1.mine_ref = bf16[288,384]{1,0:T(8,128)(2,1)} custom-call(bf16[288,384]{1,0:T(8,128)(2,1)S(1)} %get-tuple-element.13.refs_0_, bf16[288,384]{1,0:T(8,128)(2,1)S(1)} %collective-permute-done.1.refs_1_, bf16[288,384]{1,0:T(8,128)(2,1)S(1)} %collective-permute-done.2.refs_2_, bf16[288,384]{1,0:T(8,128)(2,1)S(1)} %collective-permute-done.3.refs_3_), custom_call_target="tpu_custom_call" | custom-call | bytes 1105920 | tf_op jit(solution)/shard_map/plane_sum/pallas_call | solution.py:144
  30.6 2.6 %collective-permute-start.4 = (bf16[288,384]{1,0:T(8,128)(2,1)}, bf16[288,384]{1,0:T(8,128)(2,1)}, u32[]{:S(2)}, u32[]{:S(2)}) collective-permute-start(bf16[288,384]{1,0:T(8,128)(2,1)} %plane_sum.1.mine_ref), channel_id=1, source_target_pairs={{0,8},{1,9},{2,10},{3,11},{4,12},{5,13},{6,14},{7,15},{8,0},{9,1},... | collective-permute-start | bytes 663560 | tf_op jit(solution)/shard_map/ppermute | solution.py:255
  33.2 1.2 %fusion.base_ref = f32[192,384]{1,0:T(8,128)S(1)} fusion(f32[4,384,192]{1,2,0:T(8,128)} %param.10, s32[]{:T(128)S(6)} %select_n.46, f32[4,192,384]{2,1,0:T(8,128)} %gate_hbm.1, pred[]{:T(512)S(6)} %eq.6), kind=kLoop, calls=%fused_computation.1 | loop fusion | flops 73728 | bytes 884741 | tf_op jit(solution)/shard_map/jit(_where)/select_n | solution.py:265
  34.5 9.3 %collective-permute-done.4.other_ref = bf16[288,384]{1,0:T(8,128)(2,1)} collective-permute-done((bf16[288,384]{1,0:T(8,128)(2,1)}, bf16[288,384]{1,0:T(8,128)(2,1)}, u32[]{:S(2)}, u32[]{:S(2)}) %collective-permute-start.4) | collective-permute-done | bytes 221216 | tf_op jit(solution)/shard_map/ppermute | solution.py:255
  43.8 0.9 %add_convert_fusion.half_ref = bf16[96,384]{1,0:T(8,128)(2,1)S(1)} fusion(bf16[288,384]{1,0:T(8,128)(2,1)} %collective-permute-done.4.other_ref, bf16[288,384]{1,0:T(8,128)(2,1)} %plane_sum.1.mine_ref), kind=kLoop, calls=%fused_computation.3 | loop fusion | flops 147456 | bytes 221184 | tf_op jit(solution)/shard_map/convert_element_type | solution.py:275
  44.8 0.9 %dynamic-slice_bitcast_fusion.base_half_ref = f32[96,384]{1,0:T(8,128)S(1)} fusion(f32[4,192,384]{2,1,0:T(8,128)} %up_hbm.1, s32[]{:T(128)S(6)} %select_n.49, s32[]{:T(128)S(6)} %select_n.51), kind=kLoop, calls=%fused_computation.2 | loop fusion | bytes 294920 | tf_op jit(solution)/shard_map/dynamic_slice | solution.py:266
  45.7 0.3 collective-permute-done.5.got_ref
  46.1 4.8 %newton.1.here_ref = bf16[288,384]{1,0:T(8,128)(2,1)} custom-call(s32[1]{0:T(128)} %bitcast.1.core_ref, bf16[288,384]{1,0:T(8,128)(2,1)} %plane_sum.1.mine_ref, bf16[288,384]{1,0:T(8,128)(2,1)} %collective-permute-done.4.other_ref, bf16[96,384]{1,0:T(8,128)(2,1)S(1)} %add_convert_fusion.half_ref, bf16[96,384]{1,0:T(8,128)(2,1)S(1)} %collective-permute-done.5.got_ref, ...), custom_call_target="tpu_custom_call" | custom-call | flops 707788800 | bytes 1327104 | tf_op jit(solution)/shard_map/newton/pallas_call | solution.py:144
  50.8 0.7 collective-permute-start.11
  51.6 0.4 collective-permute-start.9
  51.9 2.4 %collective-permute-start.6 = (bf16[288,384]{1,0:T(8,128)(2,1)}, bf16[288,384]{1,0:T(8,128)(2,1)}, u32[]{:S(2)}, u32[]{:S(2)}) collective-permute-start(bf16[288,384]{1,0:T(8,128)(2,1)} %newton.1.here_ref), channel_id=1, source_target_pairs={{0,6},{1,7},{2,4},{3,5},{4,2},{5,3},{6,0},{7,1},{8,14},{9,15},{10,... | collective-permute-start | bytes 663560 | tf_op jit(solution)/shard_map/ppermute | solution.py:255
  54.3 5.1 %collective-permute-done.11.here_ref = bf16[288,384]{1,0:T(8,128)(2,1)} collective-permute-done((bf16[288,384]{1,0:T(8,128)(2,1)}, bf16[288,384]{1,0:T(8,128)(2,1)}, u32[]{:S(2)}, u32[]{:S(2)}) %collective-permute-start.11) | collective-permute-done | bytes 221216 | tf_op jit(solution)/shard_map/ppermute | solution.py:255
  59.4 0.3 collective-permute-done.9.here_ref
  59.8 0.2 collective-permute-start.10
  60.0 3.9 %collective-permute-done.6.here_ref = bf16[288,384]{1,0:T(8,128)(2,1)} collective-permute-done((bf16[288,384]{1,0:T(8,128)(2,1)}, bf16[288,384]{1,0:T(8,128)(2,1)}, u32[]{:S(2)}, u32[]{:S(2)}) %collective-permute-start.6) | collective-permute-done | bytes 221216 | tf_op jit(solution)/shard_map/ppermute | solution.py:255
  64.0 1.1 %copy-done.2 = bf16[512,768]{1,0:T(8,128)(2,1)S(1)} copy-done((bf16[512,768]{1,0:T(8,128)(2,1)S(1)}, bf16[512,768]{1,0:T(8,128)(2,1)}, u32[]{:S(2)}) %copy-start.2) | copy-done | bytes 786456
  65.1 0.9 %query.1.q_ref = bf16[4,512,192]{2,1,0:T(8,128)(2,1)S(1)} custom-call(bf16[512,768]{1,0:T(8,128)(2,1)S(1)} %copy-done.2, bf16[768,2304]{1,0:T(8,128)(2,1)S(1)} %copy-done), custom_call_target="tpu_custom_call" | custom-call | flops 603979776 | bytes 3932160 | tf_op jit(solution)/shard_map/query/pallas_call | solution.py:163
  66.0 1.8 %apply.3.refs_0_ = bf16[512,192]{1,0:T(8,128)(2,1)S(1)} custom-call(s32[2]{0:T(128)S(1)} %get-tuple-element.18.ids_ref, bf16[4,512,192]{2,1,0:T(8,128)(2,1)S(1)} %query.1.q_ref, bf16[288,384]{1,0:T(8,128)(2,1)} %newton.1.here_ref, bf16[288,384]{1,0:T(8,128)(2,1)} %collective-permute-done.8.there_ref), custom_call_target="tpu_custom_call" | custom-call | flops 226492416 | bytes 835584 | tf_op jit(solution)/shard_map/apply/pallas_call | solution.py:144
  67.8 1.8 %apply.5.refs_2_ = bf16[512,192]{1,0:T(8,128)(2,1)S(1)} custom-call(s32[2]{0:T(128)S(1)} %get-tuple-element.20.ids_ref, bf16[4,512,192]{2,1,0:T(8,128)(2,1)S(1)} %query.1.q_ref, bf16[288,384]{1,0:T(8,128)(2,1)} %collective-permute-done.11.here_ref, bf16[288,384]{1,0:T(8,128)(2,1)} %collective-permute-done.12.there_ref), custom_call_target="tpu_custom_call" | custom-call | flops 226492416 | bytes 835584 | tf_op jit(solution)/shard_map/apply/pallas_call | solution.py:144
  69.6 1.8 %apply.4.refs_1_ = bf16[512,192]{1,0:T(8,128)(2,1)S(1)} custom-call(s32[2]{0:T(128)S(1)} %get-tuple-element.19.ids_ref, bf16[4,512,192]{2,1,0:T(8,128)(2,1)S(1)} %query.1.q_ref, bf16[288,384]{1,0:T(8,128)(2,1)} %collective-permute-done.9.here_ref, bf16[288,384]{1,0:T(8,128)(2,1)} %collective-permute-done.10.there_ref), custom_call_target="tpu_custom_call" | custom-call | flops 226492416 | bytes 835584 | tf_op jit(solution)/shard_map/apply/pallas_call | solution.py:144
  71.3 2.8 %finish.1 = bf16[512,768]{1,0:T(8,128)(2,1)} custom-call(s32[2]{0:T(128)S(1)} %get-tuple-element.17.ids_ref, bf16[4,512,192]{2,1,0:T(8,128)(2,1)S(1)} %query.1.q_ref, bf16[288,384]{1,0:T(8,128)(2,1)} %collective-permute-done.6.here_ref, bf16[288,384]{1,0:T(8,128)(2,1)S(1)} %collective-permute-done.7.there_ref, bf16[512,192]{1,0:T(8,128)(2,1)S(1)} %apply.3.refs_0_, ...), custom_call_target="tpu_custom_call" | custom-call | flops 226492416 | bytes 835584 | tf_op jit(solution)/shard_map/finish/pallas_call | solution.py:144
  (15 shorter events, 0.4 us)
Async XLA Ops:
  11.0 2.8 %collective-permute-start = (bf16[4,288,384]{2,1,0:T(8,128)(2,1)}, bf16[4,288,384]{2,1,0:T(8,128)(2,1)S(1)}, u32[]{:S(2)}, u32[]{:S(2)}) collective-permute-start(bf16[4,288,384]{2,1,0:T(8,128)(2,1)} %get-tuple-element.12), channel_id=1, source_target_pairs={{0,1},{1,0},{2,3},{3,2},{4,5},{5,4},{6,7},{7,6},{8,9},{9,8},{10,11... | collective-permute-start | bytes 2654216 | tf_op jit(solution)/shard_map/ppermute | solution.py:255
  13.8 1.2 %copy-start.1 = (bf16[4,288,384]{2,1,0:T(8,128)(2,1)S(1)}, bf16[4,288,384]{2,1,0:T(8,128)(2,1)}, u32[]{:S(2)}) copy-start(bf16[4,288,384]{2,1,0:T(8,128)(2,1)} %get-tuple-element.11.keep_ref) | copy-start | bytes 2654212
  15.2 10.2 %collective-permute-start.1 = (bf16[288,384]{1,0:T(8,128)(2,1)S(1)}, bf16[288,384]{1,0:T(8,128)(2,1)S(1)}, u32[]{:S(2)}, u32[]{:S(2)}) collective-permute-start(bf16[288,384]{1,0:T(8,128)(2,1)S(1)} %get-tuple-element.14), channel_id=1, source_target_pairs={{0,6},{1,7},{2,4},{3,5},{4,2},{5,3},{6,0},{7,1},{8,14},{9,15},{10,... | collective-permute-start | bytes 663560 | tf_op jit(solution)/shard_map/ppermute | solution.py:255
  19.2 10.5 %collective-permute-start.2 = (bf16[288,384]{1,0:T(8,128)(2,1)S(1)}, bf16[288,384]{1,0:T(8,128)(2,1)S(1)}, u32[]{:S(2)}, u32[]{:S(2)}) collective-permute-start(bf16[288,384]{1,0:T(8,128)(2,1)S(1)} %get-tuple-element.15), channel_id=1, source_target_pairs={{0,2},{1,3},{2,0},{3,1},{4,6},{5,7},{6,4},{7,5},{8,10},{9,11},{10,... | collective-permute-start | bytes 663560 | tf_op jit(solution)/shard_map/ppermute | solution.py:255
  19.7 10.2 %collective-permute-start.3 = (bf16[288,384]{1,0:T(8,128)(2,1)S(1)}, bf16[288,384]{1,0:T(8,128)(2,1)S(1)}, u32[]{:S(2)}, u32[]{:S(2)}) collective-permute-start(bf16[288,384]{1,0:T(8,128)(2,1)S(1)} %get-tuple-element.16), channel_id=1, source_target_pairs={{0,4},{1,5},{2,6},{3,7},{4,0},{5,1},{6,2},{7,3},{8,12},{9,13},{10,... | collective-permute-start | bytes 663560 | tf_op jit(solution)/shard_map/ppermute | solution.py:255
  30.6 13.1 %collective-permute-start.4 = (bf16[288,384]{1,0:T(8,128)(2,1)}, bf16[288,384]{1,0:T(8,128)(2,1)}, u32[]{:S(2)}, u32[]{:S(2)}) collective-permute-start(bf16[288,384]{1,0:T(8,128)(2,1)} %plane_sum.1.mine_ref), channel_id=1, source_target_pairs={{0,8},{1,9},{2,10},{3,11},{4,12},{5,13},{6,14},{7,15},{8,0},{9,1},... | collective-permute-start | bytes 663560 | tf_op jit(solution)/shard_map/ppermute | solution.py:255
  33.2 30.7 %copy-start = (bf16[768,2304]{1,0:T(8,128)(2,1)S(1)}, bf16[768,2304]{1,0:T(8,128)(2,1)}, u32[]{:S(2)}) copy-start(bf16[768,2304]{1,0:T(8,128)(2,1)} %qkv_hbm.1) | copy-start | bytes 10616836
  44.7 1.3 %collective-permute-start.5 = (bf16[96,384]{1,0:T(8,128)(2,1)S(1)}, bf16[96,384]{1,0:T(8,128)(2,1)S(1)}, u32[]{:S(2)}, u32[]{:S(2)}) collective-permute-start(bf16[96,384]{1,0:T(8,128)(2,1)S(1)} %add_convert_fusion.half_ref), channel_id=1, source_target_pairs={{0,1},{1,0},{2,3},{3,2},{4,5},{5,4},{6,7},{7,6},{8,9},{9,8},{10,11... | collective-permute-start | bytes 221192 | tf_op jit(solution)/shard_map/ppermute | solution.py:255
  50.8 8.6 %collective-permute-start.11 = (bf16[288,384]{1,0:T(8,128)(2,1)}, bf16[288,384]{1,0:T(8,128)(2,1)}, u32[]{:S(2)}, u32[]{:S(2)}) collective-permute-start(bf16[288,384]{1,0:T(8,128)(2,1)} %newton.1.here_ref), channel_id=1, source_target_pairs={{0,4},{1,5},{2,6},{3,7},{4,0},{5,1},{6,2},{7,3},{8,12},{9,13},{10,... | collective-permute-start | bytes 663560 | tf_op jit(solution)/shard_map/ppermute | solution.py:255
  51.6 8.2 %collective-permute-start.9 = (bf16[288,384]{1,0:T(8,128)(2,1)}, bf16[288,384]{1,0:T(8,128)(2,1)}, u32[]{:S(2)}, u32[]{:S(2)}) collective-permute-start(bf16[288,384]{1,0:T(8,128)(2,1)} %newton.1.here_ref), channel_id=1, source_target_pairs={{0,2},{1,3},{2,0},{3,1},{4,6},{5,7},{6,4},{7,5},{8,10},{9,11},{10,... | collective-permute-start | bytes 663560 | tf_op jit(solution)/shard_map/ppermute | solution.py:255
  51.9 12.0 %collective-permute-start.6 = (bf16[288,384]{1,0:T(8,128)(2,1)}, bf16[288,384]{1,0:T(8,128)(2,1)}, u32[]{:S(2)}, u32[]{:S(2)}) collective-permute-start(bf16[288,384]{1,0:T(8,128)(2,1)} %newton.1.here_ref), channel_id=1, source_target_pairs={{0,6},{1,7},{2,4},{3,5},{4,2},{5,3},{6,0},{7,1},{8,14},{9,15},{10,... | collective-permute-start | bytes 663560 | tf_op jit(solution)/shard_map/ppermute | solution.py:255
  54.3 11.7 %collective-permute-start.8 = (bf16[288,384]{1,0:T(8,128)(2,1)}, bf16[288,384]{1,0:T(8,128)(2,1)}, u32[]{:S(2)}, u32[]{:S(2)}) collective-permute-start(bf16[288,384]{1,0:T(8,128)(2,1)} %newton.1.here_ref), channel_id=1, source_target_pairs={{0,1},{1,0},{2,3},{3,2},{4,5},{5,4},{6,7},{7,6},{8,9},{9,8},{10,11... | collective-permute-start | bytes 663560 | tf_op jit(solution)/shard_map/ppermute | solution.py:255
  59.4 8.4 %collective-permute-start.12 = (bf16[288,384]{1,0:T(8,128)(2,1)}, bf16[288,384]{1,0:T(8,128)(2,1)}, u32[]{:S(2)}, u32[]{:S(2)}) collective-permute-start(bf16[288,384]{1,0:T(8,128)(2,1)} %collective-permute-done.11.here_ref), channel_id=1, source_target_pairs={{0,1},{1,0},{2,3},{3,2},{4,5},{5,4},{6,7},{7,6},{8,9},{9,8},{10,11... | collective-permute-start | bytes 663560 | tf_op jit(solution)/shard_map/ppermute | solution.py:255
  59.8 9.8 %collective-permute-start.10 = (bf16[288,384]{1,0:T(8,128)(2,1)}, bf16[288,384]{1,0:T(8,128)(2,1)}, u32[]{:S(2)}, u32[]{:S(2)}) collective-permute-start(bf16[288,384]{1,0:T(8,128)(2,1)} %collective-permute-done.9.here_ref), channel_id=1, source_target_pairs={{0,1},{1,0},{2,3},{3,2},{4,5},{5,4},{6,7},{7,6},{8,9},{9,8},{10,11... | collective-permute-start | bytes 663560 | tf_op jit(solution)/shard_map/ppermute | solution.py:255
  64.0 7.4 %collective-permute-start.7 = (bf16[288,384]{1,0:T(8,128)(2,1)}, bf16[288,384]{1,0:T(8,128)(2,1)S(1)}, u32[]{:S(2)}, u32[]{:S(2)}) collective-permute-start(bf16[288,384]{1,0:T(8,128)(2,1)} %collective-permute-done.6.here_ref), channel_id=1, source_target_pairs={{0,1},{1,0},{2,3},{3,2},{4,5},{5,4},{6,7},{7,6},{8,9},{9,8},{10,11... | collective-permute-start | bytes 663560 | tf_op jit(solution)/shard_map/ppermute | solution.py:255
  64.0 1.1 %copy-start.2 = (bf16[512,768]{1,0:T(8,128)(2,1)S(1)}, bf16[512,768]{1,0:T(8,128)(2,1)}, u32[]{:S(2)}) copy-start(bf16[512,768]{1,0:T(8,128)(2,1)} %tok_hbm.1) | copy-start | bytes 2359300

commit v3 on v0

v3 whole, which is shorter than its diff:
```python
import functools

import jax
import jax.numpy as jnp
from jax import lax
from jax.experimental import pallas as pl
from jax.experimental.pallas import tpu as pltpu
from jax.sharding import PartitionSpec as P

VIEWS = 16
NS_STEPS = 5
BF16 = jnp.bfloat16
F32 = jnp.float32
K1_LIMIT = 40
SMALL_LIMIT = 24

coef_a = 3.4445
coef_b = -4.775
coef_c = 2.0315
step_size = 0.8


def mm(a, b, dims):
    return lax.dot_general(a, b, (dims, ((), ())), preferred_element_type=F32)


NN = ((1,), (0,))
NT = ((1,), (1,))
TN = ((0,), (0,))


def position(heads):
    place = lax.axis_index("tok")
    return lax.rem(lax.div(place, 2), heads), lax.rem(place, 2)


def grad_kernel(
    view_hbm, tok_hbm, qkv_hbm, gate_hbm, up_hbm, down_hbm, keep_ref, give_ref, view, tok, wkv, fast, kv, both_w, down_w, sems
):
    rows, width = tok.shape
    heads, head_dim = kv.shape[1], kv.shape[3]
    hidden = down_w.shape[2]
    half = head_dim // 2
    own, core = position(heads)
    owner = lax.div(lax.axis_index("tok") * rows, rows * lax.axis_size("tok") // VIEWS)
    count = iter(range(4 + 3 * heads))

    def fetch(source, target):
        copy = pltpu.make_async_copy(source, target, sems.at[next(count)])
        copy.start()
        return copy

    tok_copy = fetch(tok_hbm, tok)
    kv_copies = [fetch(qkv_hbm.at[:, (1 + which) * width : (2 + which) * width], wkv.at[which]) for which in range(2)]
    view_copy = fetch(view_hbm, view)
    fast_copies = [
        fetch(ref.at[head], fast.at[head, i]) for head in range(heads) for i, ref in enumerate((gate_hbm, up_hbm, down_hbm))
    ]
    tok_copy.wait()
    view_copy.wait()
    flag = view[owner].astype(F32)
    for which in range(2):
        kv_copies[which].wait()
        for pair in range(heads // 2):
            columns = slice(2 * pair * head_dim, (2 * pair + 2) * head_dim)
            part = mm(tok[...], wkv[which, :, columns], NN).astype(BF16)
            if which == 1:
                part = (part.astype(F32) * flag).astype(BF16)
            kv[which, 2 * pair] = part[:, :head_dim]
            kv[which, 2 * pair + 1] = part[:, head_dim:]
    for copy in fast_copies:
        copy.wait()
    for head in range(heads):
        both_w[head, :, :hidden] = fast[head, 0].astype(BF16)
        both_w[head, :, hidden:] = fast[head, 1].astype(BF16)
        down_w[head] = fast[head, 2].astype(BF16)
    even = core == 0
    chunk = rows // 2
    for head in range(heads):
        both_sum = down_sum = None
        for start in range(0, rows, chunk):
            k = kv[0, head, start : start + chunk, :]
            v = kv[1, head, start : start + chunk, :]
            both = mm(k, both_w[head], NN)
            dhid = -mm(v, down_w[head], NN)
            gate, upper = both[:, :hidden], both[:, hidden:]
            sig = jax.nn.sigmoid(gate)
            act = gate * sig
            hid = (act * upper).astype(BF16)
            dgate = (dhid * upper * (sig * (1.0 + gate * (1.0 - sig)))).astype(BF16)
            dup = (dhid * act).astype(BF16)
            both_part = mm(k, jnp.concatenate([dgate, dup], axis=1), TN)
            down_part = mm(v, hid, TN)
            both_sum = both_part if both_sum is None else both_sum + both_part
            down_sum = down_part if down_sum is None else down_sum + down_part
        gate_g = both_sum[:, :hidden].astype(BF16)
        up_g = both_sum[:, hidden:].astype(BF16)
        down_g = (-down_sum).astype(BF16)
        slot = own ^ head
        keep_ref[slot, :head_dim] = jnp.where(even, gate_g, down_g)
        give_ref[slot, :head_dim] = jnp.where(even, down_g, gate_g)
        keep_ref[slot, head_dim:] = jnp.where(even, up_g[:half], up_g[half:])
        give_ref[slot, head_dim:] = jnp.where(even, up_g[half:], up_g[:half])


def gradients(view_kind, tokens, qkv_weight, w_gate, w_up, w_down_t):
    rows, width = tokens.shape
    heads, head_dim, hidden = w_gate.shape
    args = [pltpu.with_memory_space_constraint(x, pltpu.HBM) for x in (view_kind, tokens, qkv_weight, w_gate, w_up, w_down_t)]
    shape = pltpu.VMEM((heads, head_dim * 3 // 2, hidden), BF16)
    return pl.pallas_call(
        grad_kernel,
        out_shape=[shape] * 2,
        in_specs=[pl.BlockSpec(memory_space=pl.ANY)] * 6,
        out_specs=[pl.BlockSpec(memory_space=pltpu.VMEM)] * 2,
        scratch_shapes=[
            pltpu.SMEM(view_kind.shape, jnp.int32),
            pltpu.VMEM((rows, width), BF16),
            pltpu.VMEM((2, width, width), BF16),
            pltpu.VMEM((heads, 3, head_dim, hidden), F32),
            pltpu.VMEM((2, heads, rows, head_dim), BF16),
            pltpu.VMEM((heads, head_dim, 2 * hidden), BF16),
            pltpu.VMEM((heads, head_dim, hidden), BF16),
            pltpu.SemaphoreType.DMA((4 + 3 * heads,)),
        ],
        compiler_params=pltpu.CompilerParams(vmem_limit_bytes=K1_LIMIT * 1024 * 1024),
        cost_estimate=pl.CostEstimate(
            flops=4 * rows * width * width + 12 * heads * rows * head_dim * hidden,
            bytes_accessed=2 * rows * width + 4 * width * width + 12 * heads * head_dim * hidden,
            transcendentals=heads * rows * hidden,
        ),
        name="gradients",
    )(*args)


def small(kernel, shapes, operands, nbytes, name):
    specs = [pl.BlockSpec(memory_space=pltpu.VMEM)] * len(operands)
    operands = [pltpu.with_memory_space_constraint(x, pltpu.VMEM) for x in operands]
    return pl.pallas_call(
        kernel,
        out_shape=shapes,
        in_specs=specs,
        compiler_params=pltpu.CompilerParams(vmem_limit_bytes=SMALL_LIMIT * 1024 * 1024),
        cost_estimate=pl.CostEstimate(flops=0, bytes_accessed=nbytes, transcendentals=0),
        name=name,
    )(*operands)


def query_kernel(tokens_ref, weight_ref, out_ref):
    heads, _, head_dim = out_ref.shape
    part = mm(tokens_ref[...], weight_ref[...], NN).astype(BF16)
    for head in range(heads):
        out_ref[head] = part[:, head * head_dim : (head + 1) * head_dim]


def project_query(tokens, weight, heads):
    rows, width = tokens.shape
    return pl.pallas_call(
        query_kernel,
        out_shape=pltpu.VMEM((heads, rows, width // heads), BF16),
        grid=(1,),
        in_specs=[pl.BlockSpec((rows, width), lambda i: (0, 0)), pl.BlockSpec((width, width), lambda i: (0, 0))],
        out_specs=pl.BlockSpec((heads, rows, width // heads), lambda i: (0, 0, 0)),
        compiler_params=pltpu.CompilerParams(vmem_limit_bytes=SMALL_LIMIT * 1024 * 1024),
        cost_estimate=pl.CostEstimate(flops=2 * rows * width * width, bytes_accessed=4 * width * (rows + width), transcendentals=0),
        name="query",
    )(*(pltpu.with_memory_space_constraint(x, pltpu.HBM) for x in (tokens, weight)))


def pair_sum_kernel(keep_ref, got_ref, *out_refs):
    heads = len(out_refs) // 2
    main = out_refs[0].shape[0]
    for slot in range(heads):
        total = (keep_ref[slot].astype(F32) + got_ref[slot].astype(F32)).astype(BF16)
        out_refs[slot][...] = total[:main]
        out_refs[heads + slot][...] = total[main:]


def sum_kernel(*refs):
    *parts, out_ref = refs
    total = parts[0][...].astype(F32)
    for part in parts[1:]:
        total = total + part[...].astype(F32)
    out_ref[...] = total.astype(BF16)


def stepped(total, base):
    norm = jnp.sqrt(jnp.sum(total * total))
    x = (total / (norm + 1e-07)).astype(BF16)
    for step in range(NS_STEPS):
        gram = mm(x, x, NT).astype(BF16)
        square = mm(gram, gram, NN)
        mixer = (coef_b * gram.astype(F32) + coef_c * square).astype(BF16)
        x = (coef_a * x.astype(F32) + mm(mixer, x, NN)).astype(BF16)
    return (base - step_size * x.astype(F32)).astype(BF16)


def newton_kernel(mine_ref, other_ref, base_ref, out_ref):
    out_ref[...] = stepped(mine_ref[...].astype(F32) + other_ref[...].astype(F32), base_ref[...])


def newton_up_kernel(heads, mine_ref, got_ref, base_ref, out_ref, half_ref):
    half = mine_ref.shape[0]
    even = position(heads)[1] == 0
    a, b = mine_ref[...], got_ref[...]
    total = jnp.concatenate([jnp.where(even, a, b), jnp.where(even, b, a)], axis=0).astype(F32)
    fresh = stepped(total, base_ref[...])
    out_ref[...] = fresh
    half_ref[...] = jnp.where(even, fresh[:half], fresh[half:])


def head_output(even, q, main_ref, main_there_ref, up_refs):
    here, there = main_ref[...], main_there_ref[...]
    gate_b, down_b = jnp.where(even, here, there), jnp.where(even, there, here)
    if len(up_refs) == 1:
        up_b = up_refs[0][...]
    else:
        a, b = up_refs[0][...], up_refs[1][...]
        up_b = jnp.concatenate([jnp.where(even, a, b), jnp.where(even, b, a)], axis=0)
    gate = mm(q, gate_b, NN)
    upper = mm(q, up_b, NN)
    hidden = (gate * jax.nn.sigmoid(gate) * upper).astype(BF16)
    return mm(hidden, down_b, NT).astype(BF16)


def apply_kernel(far, q_ref, main_ref, main_there_ref, *refs):
    *up_refs, out_ref = refs
    own, core = position(q_ref.shape[0])
    out_ref[...] = head_output(core == 0, q_ref[own ^ far], main_ref, main_there_ref, up_refs)


def finish_kernel(q_ref, main_ref, main_there_ref, up_ref, up_there_ref, *refs):
    *pieces, out_ref = refs
    heads, _, head_dim = q_ref.shape
    own, core = position(heads)
    piece = head_output(core == 0, q_ref[own ^ (heads - 1)], main_ref, main_there_ref, (up_ref, up_there_ref))
    for case in range(heads):

        @pl.when(own == case)
        def _():
            for head in range(heads):
                far = head ^ case
                out_ref[:, head * head_dim : (head + 1) * head_dim] = piece if far == heads - 1 else pieces[far][...]


def shards(tokens, qkv_weight, w_gate, w_up, w_down, view_kind):
    rows, width = tokens.shape
    heads, head_dim, hidden = w_gate.shape
    groups = lax.axis_size("tok")
    own, core = position(heads)
    w_down_t = jnp.transpose(w_down, (0, 2, 1))
    half = head_dim // 2
    shape = lambda *dims: pltpu.VMEM(dims, BF16)
    size = head_dim * hidden
    main_block, half_block = shape(head_dim, hidden), shape(half, hidden)
    size = head_dim * hidden

    def exchange(x, bits):
        return lax.ppermute(x, "tok", [(i, i ^ bits) for i in range(groups)])

    keep, give = gradients(view_kind, tokens, qkv_weight, w_gate, w_up, w_down_t)
    got = exchange(give, 1)
    sums = small(pair_sum_kernel, [main_block] * heads + [half_block] * heads, (keep, got), 9 * keep.size, "pair_sum")
    mains, ups = sums[:heads], sums[heads:]
    ups_in = [exchange(ups[far], 2 * far) for far in (1, 2, 3)]
    mains_in = [exchange(mains[far], 2 * far) for far in (1, 2, 3)]
    query = project_query(tokens, qkv_weight, heads)
    base = jnp.where(core == 0, lax.dynamic_index_in_dim(w_gate, own, 0, False), lax.dynamic_index_in_dim(w_down_t, own, 0, False))
    base_up = lax.dynamic_index_in_dim(w_up, own, 0, False)
    mains_in, query, base, base_up = lax.optimization_barrier((mains_in, query, base, base_up))

    def over_line(total, name):
        bits = 2 * heads
        while bits < groups // 2:
            total = small(sum_kernel, shape(*total.shape), (total, exchange(total, bits)), 6 * total.size, name)
            bits *= 2
        return total, exchange(total, bits)

    up_total = small(sum_kernel, half_block, (ups[0], *ups_in), 10 * size, "plane_sum_up")
    up_total, up_other = over_line(up_total, "line_sum_up")
    main_total = small(sum_kernel, main_block, (mains[0], *mains_in), 10 * size, "plane_sum")
    main_total, main_other = over_line(main_total, "line_sum")
    up_half = small(sum_kernel, half_block, (up_total, up_other), 10 * size, "up_sum")
    up_got = exchange(up_half, 1)
    up_fresh, up_out = small(
        functools.partial(newton_up_kernel, heads), [main_block, half_block], (up_half, up_got, base_up), 30 * size, "newton_up"
    )
    ups_here = [exchange(up_out, 2 * far) for far in range(1, heads)]
    ups_there = [exchange(x, 1) for x in ups_here]
    fresh = small(newton_kernel, main_block, (main_total, main_other, base), 30 * size, "newton")

    def apply(far, *args):
        return small(functools.partial(apply_kernel, far), shape(rows, head_dim), (query, *args), 20 * rows * head_dim, "apply")

    here = [exchange(fresh, 2 * far) for far in range(1, heads)]
    pieces = [apply(0, fresh, exchange(fresh, 1), up_fresh)]
    here, pieces = lax.optimization_barrier((here, pieces))
    there = [exchange(x, 1) for x in here]
    for far in range(1, heads - 1):
        pieces.append(apply(far, here[far - 1], there[far - 1], ups_here[far - 1], ups_there[far - 1]))
    args = (query, here[-1], there[-1], ups_here[-1], ups_there[-1], *pieces)
    return small(finish_kernel, jax.ShapeDtypeStruct((rows, width), BF16), args, 20 * rows * head_dim, "finish")


def solution(mesh):
    placed = (P(("scene", "tok"), None), P(), P(), P(), P(), P("scene"))
    return jax.shard_map(
        shards, mesh=mesh, in_specs=placed, out_specs=P(("scene", "tok"), None), check_vma=False
    )
```

time: 203 us -> 57.7 us (0.28)
  waiting for transfers between devices: 107 us -> 16.2 us
  matrix products: 62.4 us -> 0 us
  starting transfers between devices: 0.01 us -> 20.1 us
  Pallas kernels: 0 us -> 19.9 us
  between operations: 14.2 us -> 0.15 us
  local copies, waits for them, and re-layouts: 11.6 us -> 0 us
  other arithmetic: 7.94 us -> 1.2 us
    psum x1 -> x0, waiting for transfers between devices: 107 us -> none  [shards(): total = lax.psum(grads, 'tok')]
    dot_general x20 -> x0, matrix products: 62.4 us -> none  [the longest x5 28.9 us: newton(): jnp.einsum('mij,mjk->mik', mixer, iterate, preferred_element_type=jnp.flo...]
    ppermute x0 -> x23, starting transfers between devices: none -> 20.1 us  [exchange(): return lax.ppermute(x, 'tok', [(i, i ^ bits) for i in range(groups)])]
    pallas_call x0 -> x12, Pallas kernels: none -> 19.9 us  [the longest x10 10.1 us: small(): pl.pallas_call(kernel, out_shape=shapes, in_specs=specs, compiler_params=...]
    ppermute x0 -> x23, waiting for transfers between devices: none -> 16.2 us  [exchange(): return lax.ppermute(x, 'tok', [(i, i ^ bits) for i in range(groups)])]
    slice x2 -> x0, local copies, waits for them, and re-layouts: 4.6 us -> none  [the longest x1 2.31 us: shards(): keys = proj[:, width:2 * width].reshape(rows, heads, head_dim)]
    reduce_sum x2 -> x0, other arithmetic: 3.97 us -> none  [the longest x1 2.53 us: shards(): norms = jnp.sqrt(jnp.sum(total * total, axis=(1, 2)))]
    unnamed x18 -> x0, local copies, waits for them, and re-layouts: 2.4 us -> none
  transfers between devices with their start and end apart: 1 -> 23, of which waited for: 1 -> 11; matrix products, arithmetic and copies ran while one was open for 1% -> 2% of each run, Pallas kernels for 0% -> 18%
where the time goes in v3:
time: 57.7 us; the launch traced here: 57.5 us
  starting transfers between devices  20.1 us (35%)
  Pallas kernels  19.9 us (34%)
  waiting for transfers between devices  16.2 us (28%)
  other arithmetic  1.2 us (2%)
    ppermute x23, starting transfers between devices, exchange(): return lax.ppermute(x, 'tok', [(i, i ^ bits) for i in range(groups)])  20.1 us
    ppermute x23, waiting for transfers between devices, exchange(): return lax.ppermute(x, 'tok', [(i, i ^ bits) for i in range(groups)])  16.2 us
    pallas_call x10, Pallas kernels, small(): pl.pallas_call(kernel, out_shape=shapes, in_specs=specs, compiler_params=...  10.1 us
    pallas_call x1, Pallas kernels, gradients(): pl.pallas_call(grad_kernel, out_shape=[shape] * 2, in_specs=[pl.BlockSpec...  7.45 us
    pallas_call x1, Pallas kernels, project_query(): pl.pallas_call(query_kernel, out_shape=pltpu.VMEM((heads, rows, width //...  2.36 us
    select_n x1, other arithmetic, shards(): jnp.where(core == 0, lax.dynamic_index_in_dim(w_gate, own, 0, False), lax...  1.2 us
  transfers between devices with their start and end apart: 23, of which 11 were waited for; matrix products, arithmetic and copies ran while one was open for 2% of the time, Pallas kernels for 18%

profile of v3, /device:TPU:0, one launch (start us, length us, event | category | flops | bytes accessed | tf_op | source)
XLA Modules:
  0.0 57.5 jit_solution(16205093954342288979)
XLA Ops:
  0.0 7.5 %gradients.1 = (bf16[4,288,384]{2,1,0:T(8,128)(2,1)S(1)}, bf16[4,288,384]{2,1,0:T(8,128)(2,1)S(1)}) custom-call(s32[16]{0:T(128)} %view_hbm.1, bf16[512,768]{1,0:T(8,128)(2,1)} %tokens_ref.1, bf16[768,2304]{1,0:T(8,128)(2,1)} %weight_ref.1, f32[4,192,384]{2,1,0:T(8,128)} %gate_hbm.1, f32[4,192,384]{2,1,0:T(8,128)} %up_hbm.1, f32[4,192,384]{2,1,0:T(8,128)} %bitcast.9), custom_call_target="tpu_custom_call" | custom-call | flops 3019898880 | bytes 6684672 | tf_op jit(solution)/shard_map/gradients/pallas_call | solution.py:111
  7.5 0.5 collective-permute-start
  8.0 2.1 %collective-permute-done.got_ref = bf16[4,288,384]{2,1,0:T(8,128)(2,1)S(1)} collective-permute-done((bf16[4,288,384]{2,1,0:T(8,128)(2,1)S(1)}, bf16[4,288,384]{2,1,0:T(8,128)(2,1)S(1)}, u32[]{:S(2)}, u32[]{:S(2)}) %collective-permute-start) | collective-permute-done | bytes 884768 | tf_op jit(solution)/shard_map/ppermute | solution.py:259
  10.2 3.0 %collective-permute-start.1 = (bf16[192,384]{1,0:T(8,128)(2,1)S(1)}, bf16[192,384]{1,0:T(8,128)(2,1)S(1)}, u32[]{:S(2)}, u32[]{:S(2)}) collective-permute-start(bf16[192,384]{1,0:T(8,128)(2,1)S(1)} %get-tuple-element.29), channel_id=1, source_target_pairs={{0,2},{1,3},{2,0},{3,1},{4,6},{5,7},{6,4},{7,5},{8,10},{9,11},{10,... | collective-permute-start | bytes 442376 | tf_op jit(solution)/shard_map/ppermute | solution.py:259
  13.2 1.6 %collective-permute-start.2 = (bf16[192,384]{1,0:T(8,128)(2,1)S(1)}, bf16[192,384]{1,0:T(8,128)(2,1)S(1)}, u32[]{:S(2)}, u32[]{:S(2)}) collective-permute-start(bf16[192,384]{1,0:T(8,128)(2,1)S(1)} %get-tuple-element.30), channel_id=1, source_target_pairs={{0,4},{1,5},{2,6},{3,7},{4,0},{5,1},{6,2},{7,3},{8,12},{9,13},{10,... | collective-permute-start | bytes 442376 | tf_op jit(solution)/shard_map/ppermute | solution.py:259
  14.8 2.4 %query.1.q_ref = bf16[4,512,192]{2,1,0:T(8,128)(2,1)S(1)} custom-call(bf16[512,768]{1,0:T(8,128)(2,1)} %tokens_ref.1, bf16[768,2304]{1,0:T(8,128)(2,1)} %weight_ref.1), custom_call_target="tpu_custom_call" | custom-call | flops 603979776 | bytes 3932160 | tf_op jit(solution)/shard_map/query/pallas_call | solution.py:158
  17.2 1.2 %fusion = (f32[192,384]{1,0:T(8,128)S(1)}, f32[192,384]{1,0:T(8,128)S(1)}) fusion(f32[4,384,192]{1,2,0:T(8,128)} %param.10, s32[]{:T(128)S(6)} %select_n.18, f32[4,192,384]{2,1,0:T(8,128)} %gate_hbm.1, pred[]{:T(512)S(6)} %eq.3, f32[4,192,384]{2,1,0:T(8,128)} %up_hbm.1), kind=kLoop, calls=%fused_computation.1 | loop fusion | flops 73728 | bytes 1474565 | tf_op jit(solution)/shard_map/jit(_where)/select_n | solution.py:268
  18.4 1.6 %collective-permute-done.2.refs_2_ = bf16[192,384]{1,0:T(8,128)(2,1)S(1)} collective-permute-done((bf16[192,384]{1,0:T(8,128)(2,1)S(1)}, bf16[192,384]{1,0:T(8,128)(2,1)S(1)}, u32[]{:S(2)}, u32[]{:S(2)}) %collective-permute-start.2) | collective-permute-done | bytes 147488 | tf_op jit(solution)/shard_map/ppermute | solution.py:259
  19.9 1.8 %collective-permute-done.3.refs_3_ = bf16[192,384]{1,0:T(8,128)(2,1)S(1)} collective-permute-done((bf16[192,384]{1,0:T(8,128)(2,1)S(1)}, bf16[192,384]{1,0:T(8,128)(2,1)S(1)}, u32[]{:S(2)}, u32[]{:S(2)}) %collective-permute-start.3) | collective-permute-done | bytes 147488 | tf_op jit(solution)/shard_map/ppermute | solution.py:259
  21.8 2.8 %collective-permute-start.4 = (bf16[192,384]{1,0:T(8,128)(2,1)S(1)}, bf16[192,384]{1,0:T(8,128)(2,1)S(1)}, u32[]{:S(2)}, u32[]{:S(2)}) collective-permute-start(bf16[192,384]{1,0:T(8,128)(2,1)S(1)} %plane_sum.1.mine_ref), channel_id=1, source_target_pairs={{0,8},{1,9},{2,10},{3,11},{4,12},{5,13},{6,14},{7,15},{8,0},{9,1},... | collective-permute-start | bytes 442376 | tf_op jit(solution)/shard_map/ppermute | solution.py:259
  24.6 1.5 %collective-permute-start.9 = (bf16[96,384]{1,0:T(8,128)(2,1)S(1)}, bf16[96,384]{1,0:T(8,128)(2,1)S(1)}, u32[]{:S(2)}, u32[]{:S(2)}) collective-permute-start(bf16[96,384]{1,0:T(8,128)(2,1)S(1)} %get-tuple-element.39), channel_id=1, source_target_pairs={{0,2},{1,3},{2,0},{3,1},{4,6},{5,7},{6,4},{7,5},{8,10},{9,11},{10,... | collective-permute-start | bytes 221192 | tf_op jit(solution)/shard_map/ppermute | solution.py:259
  26.2 1.6 %collective-permute-start.10 = (bf16[96,384]{1,0:T(8,128)(2,1)S(1)}, bf16[96,384]{1,0:T(8,128)(2,1)S(1)}, u32[]{:S(2)}, u32[]{:S(2)}) collective-permute-start(bf16[96,384]{1,0:T(8,128)(2,1)S(1)} %get-tuple-element.40), channel_id=1, source_target_pairs={{0,4},{1,5},{2,6},{3,7},{4,0},{5,1},{6,2},{7,3},{8,12},{9,13},{10,... | collective-permute-start | bytes 221192 | tf_op jit(solution)/shard_map/ppermute | solution.py:259
  28.1 0.9 %collective-permute-done.9.refs_1_ = bf16[96,384]{1,0:T(8,128)(2,1)S(1)} collective-permute-done((bf16[96,384]{1,0:T(8,128)(2,1)S(1)}, bf16[96,384]{1,0:T(8,128)(2,1)S(1)}, u32[]{:S(2)}, u32[]{:S(2)}) %collective-permute-start.9) | collective-permute-done | bytes 73760 | tf_op jit(solution)/shard_map/ppermute | solution.py:259
  29.0 2.9 %collective-permute-done.10.refs_2_ = bf16[96,384]{1,0:T(8,128)(2,1)S(1)} collective-permute-done((bf16[96,384]{1,0:T(8,128)(2,1)S(1)}, bf16[96,384]{1,0:T(8,128)(2,1)S(1)}, u32[]{:S(2)}, u32[]{:S(2)}) %collective-permute-start.10) | collective-permute-done | bytes 73760 | tf_op jit(solution)/shard_map/ppermute | solution.py:259
  31.9 1.1 %collective-permute-done.11.refs_3_ = bf16[96,384]{1,0:T(8,128)(2,1)S(1)} collective-permute-done((bf16[96,384]{1,0:T(8,128)(2,1)S(1)}, bf16[96,384]{1,0:T(8,128)(2,1)S(1)}, u32[]{:S(2)}, u32[]{:S(2)}) %collective-permute-start.11) | collective-permute-done | bytes 73760 | tf_op jit(solution)/shard_map/ppermute | solution.py:259
  33.1 1.2 %collective-permute-start.12 = (bf16[96,384]{1,0:T(8,128)(2,1)S(1)}, bf16[96,384]{1,0:T(8,128)(2,1)S(1)}, u32[]{:S(2)}, u32[]{:S(2)}) collective-permute-start(bf16[96,384]{1,0:T(8,128)(2,1)S(1)} %plane_sum_up.1.refs_0_), channel_id=1, source_target_pairs={{0,8},{1,9},{2,10},{3,11},{4,12},{5,13},{6,14},{7,15},{8,0},{9,1},... | collective-permute-start | bytes 221192 | tf_op jit(solution)/shard_map/ppermute | solution.py:259
  34.2 2.9 %newton.1.main_ref = bf16[192,384]{1,0:T(8,128)(2,1)S(1)} custom-call(bf16[192,384]{1,0:T(8,128)(2,1)S(1)} %plane_sum.1.mine_ref, bf16[192,384]{1,0:T(8,128)(2,1)S(1)} %collective-permute-done.4.other_ref, f32[192,384]{1,0:T(8,128)S(1)} %get-tuple-element.37.base_ref), custom_call_target="tpu_custom_call" | custom-call | bytes 2211840 | tf_op jit(solution)/shard_map/newton/pallas_call | solution.py:139
  37.3 1.7 %collective-permute-done.12.refs_1_ = bf16[96,384]{1,0:T(8,128)(2,1)S(1)} collective-permute-done((bf16[96,384]{1,0:T(8,128)(2,1)S(1)}, bf16[96,384]{1,0:T(8,128)(2,1)S(1)}, u32[]{:S(2)}, u32[]{:S(2)}) %collective-permute-start.12) | collective-permute-done | bytes 73760 | tf_op jit(solution)/shard_map/ppermute | solution.py:259
  39.1 2.2 %collective-permute-start.6 = (bf16[192,384]{1,0:T(8,128)(2,1)S(1)}, bf16[192,384]{1,0:T(8,128)(2,1)S(1)}, u32[]{:S(2)}, u32[]{:S(2)}) collective-permute-start(bf16[192,384]{1,0:T(8,128)(2,1)S(1)} %newton.1.main_ref), channel_id=1, source_target_pairs={{0,4},{1,5},{2,6},{3,7},{4,0},{5,1},{6,2},{7,3},{8,12},{9,13},{10,... | collective-permute-start | bytes 442376 | tf_op jit(solution)/shard_map/ppermute | solution.py:259
  41.3 0.5 collective-permute-start.7
  41.9 1.3 %collective-permute-done.13.got_ref = bf16[96,384]{1,0:T(8,128)(2,1)S(1)} collective-permute-done((bf16[96,384]{1,0:T(8,128)(2,1)S(1)}, bf16[96,384]{1,0:T(8,128)(2,1)S(1)}, u32[]{:S(2)}, u32[]{:S(2)}) %collective-permute-start.13) | collective-permute-done | bytes 73760 | tf_op jit(solution)/shard_map/ppermute | solution.py:259
  43.1 2.9 %newton_up.1 = (bf16[192,384]{1,0:T(8,128)(2,1)S(1)}, bf16[96,384]{1,0:T(8,128)(2,1)S(1)}) custom-call(bf16[96,384]{1,0:T(8,128)(2,1)S(1)} %up_sum.1.mine_ref, bf16[96,384]{1,0:T(8,128)(2,1)S(1)} %collective-permute-done.13.got_ref, f32[192,384]{1,0:T(8,128)S(1)} %get-tuple-element.42.base_ref), custom_call_target="tpu_custom_call" | custom-call | bytes 2211840 | tf_op jit(solution)/shard_map/newton_up/pallas_call | solution.py:139
  46.1 1.1 %collective-permute-start.18 = (bf16[96,384]{1,0:T(8,128)(2,1)S(1)}, bf16[96,384]{1,0:T(8,128)(2,1)S(1)}, u32[]{:S(2)}, u32[]{:S(2)}) collective-permute-start(bf16[96,384]{1,0:T(8,128)(2,1)S(1)} %get-tuple-element.45), channel_id=1, source_target_pairs={{0,2},{1,3},{2,0},{3,1},{4,6},{5,7},{6,4},{7,5},{8,10},{9,11},{10,... | collective-permute-start | bytes 221192 | tf_op jit(solution)/shard_map/ppermute | solution.py:259
  47.1 1.5 %collective-permute-start.15 = (bf16[96,384]{1,0:T(8,128)(2,1)S(1)}, bf16[96,384]{1,0:T(8,128)(2,1)S(1)}, u32[]{:S(2)}, u32[]{:S(2)}) collective-permute-start(bf16[96,384]{1,0:T(8,128)(2,1)S(1)} %get-tuple-element.45), channel_id=1, source_target_pairs={{0,6},{1,7},{2,4},{3,5},{4,2},{5,3},{6,0},{7,1},{8,14},{9,15},{10,... | collective-permute-start | bytes 221192 | tf_op jit(solution)/shard_map/ppermute | solution.py:259
  48.6 0.7 %apply.3.refs_0_ = bf16[512,192]{1,0:T(8,128)(2,1)S(1)} custom-call(bf16[4,512,192]{2,1,0:T(8,128)(2,1)S(1)} %query.1.q_ref, bf16[192,384]{1,0:T(8,128)(2,1)S(1)} %newton.1.main_ref, bf16[192,384]{1,0:T(8,128)(2,1)S(1)} %collective-permute-done.8.main_there_ref, bf16[192,384]{1,0:T(8,128)(2,1)S(1)} %get-tuple-element.43.refs_0_), custom_call_target="tpu_custom_call" | custom-call | bytes 1966080 | tf_op jit(solution)/shard_map/apply/pallas_call | solution.py:139
  49.3 1.1 %collective-permute-start.21 = (bf16[96,384]{1,0:T(8,128)(2,1)S(1)}, bf16[96,384]{1,0:T(8,128)(2,1)S(1)}, u32[]{:S(2)}, u32[]{:S(2)}) collective-permute-start(bf16[96,384]{1,0:T(8,128)(2,1)S(1)} %get-tuple-element.45), channel_id=1, source_target_pairs={{0,4},{1,5},{2,6},{3,7},{4,0},{5,1},{6,2},{7,3},{8,12},{9,13},{10,... | collective-permute-start | bytes 221192 | tf_op jit(solution)/shard_map/ppermute | solution.py:259
  51.0 1.4 %collective-permute-done.15.up_ref = bf16[96,384]{1,0:T(8,128)(2,1)S(1)} collective-permute-done((bf16[96,384]{1,0:T(8,128)(2,1)S(1)}, bf16[96,384]{1,0:T(8,128)(2,1)S(1)}, u32[]{:S(2)}, u32[]{:S(2)}) %collective-permute-start.15) | collective-permute-done | bytes 73760 | tf_op jit(solution)/shard_map/ppermute | solution.py:259
  52.4 1.3 %collective-permute-done.21.refs_0_ = bf16[96,384]{1,0:T(8,128)(2,1)S(1)} collective-permute-done((bf16[96,384]{1,0:T(8,128)(2,1)S(1)}, bf16[96,384]{1,0:T(8,128)(2,1)S(1)}, u32[]{:S(2)}, u32[]{:S(2)}) %collective-permute-start.21) | collective-permute-done | bytes 73760 | tf_op jit(solution)/shard_map/ppermute | solution.py:259
  53.7 0.5 collective-permute-start.16
  54.2 0.7 %apply.4.refs_1_ = bf16[512,192]{1,0:T(8,128)(2,1)S(1)} custom-call(bf16[4,512,192]{2,1,0:T(8,128)(2,1)S(1)} %query.1.q_ref, bf16[192,384]{1,0:T(8,128)(2,1)S(1)} %collective-permute-done.5.main_ref, bf16[192,384]{1,0:T(8,128)(2,1)S(1)} %collective-permute-done.17.main_there_ref, bf16[96,384]{1,0:T(8,128)(2,1)S(1)} %collective-permute-done.18.refs_0_, ...), custom_call_target="tpu_custom_call" | custom-call | bytes 1966080 | tf_op jit(solution)/shard_map/apply/pallas_call | solution.py:139
  55.0 0.7 %apply.5.refs_2_ = bf16[512,192]{1,0:T(8,128)(2,1)S(1)} custom-call(bf16[4,512,192]{2,1,0:T(8,128)(2,1)S(1)} %query.1.q_ref, bf16[192,384]{1,0:T(8,128)(2,1)S(1)} %collective-permute-done.6.main_ref, bf16[192,384]{1,0:T(8,128)(2,1)S(1)} %collective-permute-done.20.main_there_ref, bf16[96,384]{1,0:T(8,128)(2,1)S(1)} %collective-permute-done.21.refs_0_, ...), custom_call_target="tpu_custom_call" | custom-call | bytes 1966080 | tf_op jit(solution)/shard_map/apply/pallas_call | solution.py:139
  55.7 1.8 %finish.1 = bf16[512,768]{1,0:T(8,128)(2,1)} custom-call(bf16[4,512,192]{2,1,0:T(8,128)(2,1)S(1)} %query.1.q_ref, bf16[192,384]{1,0:T(8,128)(2,1)S(1)} %collective-permute-done.7.main_ref, bf16[192,384]{1,0:T(8,128)(2,1)S(1)} %collective-permute-done.14.main_there_ref, bf16[96,384]{1,0:T(8,128)(2,1)S(1)} %collective-permute-done.15.up_ref, ...), custom_call_target="tpu_custom_call" | custom-call | bytes 1966080 | tf_op jit(solution)/shard_map/finish/pallas_call | solution.py:139
  (27 shorter events, 1.6 us)
Async XLA Ops:
  7.5 2.6 %collective-permute-start = (bf16[4,288,384]{2,1,0:T(8,128)(2,1)S(1)}, bf16[4,288,384]{2,1,0:T(8,128)(2,1)S(1)}, u32[]{:S(2)}, u32[]{:S(2)}) collective-permute-start(bf16[4,288,384]{2,1,0:T(8,128)(2,1)S(1)} %get-tuple-element.28), channel_id=1, source_target_pairs={{0,1},{1,0},{2,3},{3,2},{4,5},{5,4},{6,7},{7,6},{8,9},{9,8},{10,11... | collective-permute-start | bytes 2654216 | tf_op jit(solution)/shard_map/ppermute | solution.py:259
  10.2 8.1 %collective-permute-start.1 = (bf16[192,384]{1,0:T(8,128)(2,1)S(1)}, bf16[192,384]{1,0:T(8,128)(2,1)S(1)}, u32[]{:S(2)}, u32[]{:S(2)}) collective-permute-start(bf16[192,384]{1,0:T(8,128)(2,1)S(1)} %get-tuple-element.29), channel_id=1, source_target_pairs={{0,2},{1,3},{2,0},{3,1},{4,6},{5,7},{6,4},{7,5},{8,10},{9,11},{10,... | collective-permute-start | bytes 442376 | tf_op jit(solution)/shard_map/ppermute | solution.py:259
  13.2 6.7 %collective-permute-start.2 = (bf16[192,384]{1,0:T(8,128)(2,1)S(1)}, bf16[192,384]{1,0:T(8,128)(2,1)S(1)}, u32[]{:S(2)}, u32[]{:S(2)}) collective-permute-start(bf16[192,384]{1,0:T(8,128)(2,1)S(1)} %get-tuple-element.30), channel_id=1, source_target_pairs={{0,4},{1,5},{2,6},{3,7},{4,0},{5,1},{6,2},{7,3},{8,12},{9,13},{10,... | collective-permute-start | bytes 442376 | tf_op jit(solution)/shard_map/ppermute | solution.py:259
  14.8 7.0 %collective-permute-start.3 = (bf16[192,384]{1,0:T(8,128)(2,1)S(1)}, bf16[192,384]{1,0:T(8,128)(2,1)S(1)}, u32[]{:S(2)}, u32[]{:S(2)}) collective-permute-start(bf16[192,384]{1,0:T(8,128)(2,1)S(1)} %get-tuple-element.31), channel_id=1, source_target_pairs={{0,6},{1,7},{2,4},{3,5},{4,2},{5,3},{6,0},{7,1},{8,14},{9,15},{10,... | collective-permute-start | bytes 442376 | tf_op jit(solution)/shard_map/ppermute | solution.py:259
  21.8 12.4 %collective-permute-start.4 = (bf16[192,384]{1,0:T(8,128)(2,1)S(1)}, bf16[192,384]{1,0:T(8,128)(2,1)S(1)}, u32[]{:S(2)}, u32[]{:S(2)}) collective-permute-start(bf16[192,384]{1,0:T(8,128)(2,1)S(1)} %plane_sum.1.mine_ref), channel_id=1, source_target_pairs={{0,8},{1,9},{2,10},{3,11},{4,12},{5,13},{6,14},{7,15},{8,0},{9,1},... | collective-permute-start | bytes 442376 | tf_op jit(solution)/shard_map/ppermute | solution.py:259
  24.6 4.4 %collective-permute-start.9 = (bf16[96,384]{1,0:T(8,128)(2,1)S(1)}, bf16[96,384]{1,0:T(8,128)(2,1)S(1)}, u32[]{:S(2)}, u32[]{:S(2)}) collective-permute-start(bf16[96,384]{1,0:T(8,128)(2,1)S(1)} %get-tuple-element.39), channel_id=1, source_target_pairs={{0,2},{1,3},{2,0},{3,1},{4,6},{5,7},{6,4},{7,5},{8,10},{9,11},{10,... | collective-permute-start | bytes 221192 | tf_op jit(solution)/shard_map/ppermute | solution.py:259
  26.2 5.7 %collective-permute-start.10 = (bf16[96,384]{1,0:T(8,128)(2,1)S(1)}, bf16[96,384]{1,0:T(8,128)(2,1)S(1)}, u32[]{:S(2)}, u32[]{:S(2)}) collective-permute-start(bf16[96,384]{1,0:T(8,128)(2,1)S(1)} %get-tuple-element.40), channel_id=1, source_target_pairs={{0,4},{1,5},{2,6},{3,7},{4,0},{5,1},{6,2},{7,3},{8,12},{9,13},{10,... | collective-permute-start | bytes 221192 | tf_op jit(solution)/shard_map/ppermute | solution.py:259
  27.7 5.3 %collective-permute-start.11 = (bf16[96,384]{1,0:T(8,128)(2,1)S(1)}, bf16[96,384]{1,0:T(8,128)(2,1)S(1)}, u32[]{:S(2)}, u32[]{:S(2)}) collective-permute-start(bf16[96,384]{1,0:T(8,128)(2,1)S(1)} %get-tuple-element.41), channel_id=1, source_target_pairs={{0,6},{1,7},{2,4},{3,5},{4,2},{5,3},{6,0},{7,1},{8,14},{9,15},{10,... | collective-permute-start | bytes 221192 | tf_op jit(solution)/shard_map/ppermute | solution.py:259
  33.1 6.0 %collective-permute-start.12 = (bf16[96,384]{1,0:T(8,128)(2,1)S(1)}, bf16[96,384]{1,0:T(8,128)(2,1)S(1)}, u32[]{:S(2)}, u32[]{:S(2)}) collective-permute-start(bf16[96,384]{1,0:T(8,128)(2,1)S(1)} %plane_sum_up.1.refs_0_), channel_id=1, source_target_pairs={{0,8},{1,9},{2,10},{3,11},{4,12},{5,13},{6,14},{7,15},{8,0},{9,1},... | collective-permute-start | bytes 221192 | tf_op jit(solution)/shard_map/ppermute | solution.py:259
  37.1 10.0 %collective-permute-start.8 = (bf16[192,384]{1,0:T(8,128)(2,1)S(1)}, bf16[192,384]{1,0:T(8,128)(2,1)S(1)}, u32[]{:S(2)}, u32[]{:S(2)}) collective-permute-start(bf16[192,384]{1,0:T(8,128)(2,1)S(1)} %newton.1.main_ref), channel_id=1, source_target_pairs={{0,1},{1,0},{2,3},{3,2},{4,5},{5,4},{6,7},{7,6},{8,9},{9,8},{10,11... | collective-permute-start | bytes 442376 | tf_op jit(solution)/shard_map/ppermute | solution.py:259
  37.2 12.1 %collective-permute-start.5 = (bf16[192,384]{1,0:T(8,128)(2,1)S(1)}, bf16[192,384]{1,0:T(8,128)(2,1)S(1)}, u32[]{:S(2)}, u32[]{:S(2)}) collective-permute-start(bf16[192,384]{1,0:T(8,128)(2,1)S(1)} %newton.1.main_ref), channel_id=1, source_target_pairs={{0,2},{1,3},{2,0},{3,1},{4,6},{5,7},{6,4},{7,5},{8,10},{9,11},{10,... | collective-permute-start | bytes 442376 | tf_op jit(solution)/shard_map/ppermute | solution.py:259
  39.1 11.3 %collective-permute-start.6 = (bf16[192,384]{1,0:T(8,128)(2,1)S(1)}, bf16[192,384]{1,0:T(8,128)(2,1)S(1)}, u32[]{:S(2)}, u32[]{:S(2)}) collective-permute-start(bf16[192,384]{1,0:T(8,128)(2,1)S(1)} %newton.1.main_ref), channel_id=1, source_target_pairs={{0,4},{1,5},{2,6},{3,7},{4,0},{5,1},{6,2},{7,3},{8,12},{9,13},{10,... | collective-permute-start | bytes 442376 | tf_op jit(solution)/shard_map/ppermute | solution.py:259
  41.3 9.1 %collective-permute-start.7 = (bf16[192,384]{1,0:T(8,128)(2,1)S(1)}, bf16[192,384]{1,0:T(8,128)(2,1)S(1)}, u32[]{:S(2)}, u32[]{:S(2)}) collective-permute-start(bf16[192,384]{1,0:T(8,128)(2,1)S(1)} %newton.1.main_ref), channel_id=1, source_target_pairs={{0,6},{1,7},{2,4},{3,5},{4,2},{5,3},{6,0},{7,1},{8,14},{9,15},{10,... | collective-permute-start | bytes 442376 | tf_op jit(solution)/shard_map/ppermute | solution.py:259
  41.9 1.3 %collective-permute-start.13 = (bf16[96,384]{1,0:T(8,128)(2,1)S(1)}, bf16[96,384]{1,0:T(8,128)(2,1)S(1)}, u32[]{:S(2)}, u32[]{:S(2)}) collective-permute-start(bf16[96,384]{1,0:T(8,128)(2,1)S(1)} %up_sum.1.mine_ref), channel_id=1, source_target_pairs={{0,1},{1,0},{2,3},{3,2},{4,5},{5,4},{6,7},{7,6},{8,9},{9,8},{10,11... | collective-permute-start | bytes 221192 | tf_op jit(solution)/shard_map/ppermute | solution.py:259
  46.1 4.4 %collective-permute-start.18 = (bf16[96,384]{1,0:T(8,128)(2,1)S(1)}, bf16[96,384]{1,0:T(8,128)(2,1)S(1)}, u32[]{:S(2)}, u32[]{:S(2)}) collective-permute-start(bf16[96,384]{1,0:T(8,128)(2,1)S(1)} %get-tuple-element.45), channel_id=1, source_target_pairs={{0,2},{1,3},{2,0},{3,1},{4,6},{5,7},{6,4},{7,5},{8,10},{9,11},{10,... | collective-permute-start | bytes 221192 | tf_op jit(solution)/shard_map/ppermute | solution.py:259
  47.1 5.3 %collective-permute-start.15 = (bf16[96,384]{1,0:T(8,128)(2,1)S(1)}, bf16[96,384]{1,0:T(8,128)(2,1)S(1)}, u32[]{:S(2)}, u32[]{:S(2)}) collective-permute-start(bf16[96,384]{1,0:T(8,128)(2,1)S(1)} %get-tuple-element.45), channel_id=1, source_target_pairs={{0,6},{1,7},{2,4},{3,5},{4,2},{5,3},{6,0},{7,1},{8,14},{9,15},{10,... | collective-permute-start | bytes 221192 | tf_op jit(solution)/shard_map/ppermute | solution.py:259
  49.3 4.4 %collective-permute-start.21 = (bf16[96,384]{1,0:T(8,128)(2,1)S(1)}, bf16[96,384]{1,0:T(8,128)(2,1)S(1)}, u32[]{:S(2)}, u32[]{:S(2)}) collective-permute-start(bf16[96,384]{1,0:T(8,128)(2,1)S(1)} %get-tuple-element.45), channel_id=1, source_target_pairs={{0,4},{1,5},{2,6},{3,7},{4,0},{5,1},{6,2},{7,3},{8,12},{9,13},{10,... | collective-permute-start | bytes 221192 | tf_op jit(solution)/shard_map/ppermute | solution.py:259
  50.4 3.9 %collective-permute-start.17 = (bf16[192,384]{1,0:T(8,128)(2,1)S(1)}, bf16[192,384]{1,0:T(8,128)(2,1)S(1)}, u32[]{:S(2)}, u32[]{:S(2)}) collective-permute-start(bf16[192,384]{1,0:T(8,128)(2,1)S(1)} %collective-permute-done.5.main_ref), channel_id=1, source_target_pairs={{0,1},{1,0},{2,3},{3,2},{4,5},{5,4},{6,7},{7,6},{8,9},{9,8},{10,11... | collective-permute-start | bytes 442376 | tf_op jit(solution)/shard_map/ppermute | solution.py:259
  50.5 3.3 %collective-permute-start.19 = (bf16[96,384]{1,0:T(8,128)(2,1)S(1)}, bf16[96,384]{1,0:T(8,128)(2,1)S(1)}, u32[]{:S(2)}, u32[]{:S(2)}) collective-permute-start(bf16[96,384]{1,0:T(8,128)(2,1)S(1)} %collective-permute-done.18.refs_0_), channel_id=1, source_target_pairs={{0,1},{1,0},{2,3},{3,2},{4,5},{5,4},{6,7},{7,6},{8,9},{9,8},{10,11... | collective-permute-start | bytes 221192 | tf_op jit(solution)/shard_map/ppermute | solution.py:259
  50.9 4.1 %collective-permute-start.20 = (bf16[192,384]{1,0:T(8,128)(2,1)S(1)}, bf16[192,384]{1,0:T(8,128)(2,1)S(1)}, u32[]{:S(2)}, u32[]{:S(2)}) collective-permute-start(bf16[192,384]{1,0:T(8,128)(2,1)S(1)} %collective-permute-done.6.main_ref), channel_id=1, source_target_pairs={{0,1},{1,0},{2,3},{3,2},{4,5},{5,4},{6,7},{7,6},{8,9},{9,8},{10,11... | collective-permute-start | bytes 442376 | tf_op jit(solution)/shard_map/ppermute | solution.py:259
  52.4 3.3 %collective-permute-start.14 = (bf16[192,384]{1,0:T(8,128)(2,1)S(1)}, bf16[192,384]{1,0:T(8,128)(2,1)S(1)}, u32[]{:S(2)}, u32[]{:S(2)}) collective-permute-start(bf16[192,384]{1,0:T(8,128)(2,1)S(1)} %collective-permute-done.7.main_ref), channel_id=1, source_target_pairs={{0,1},{1,0},{2,3},{3,2},{4,5},{5,4},{6,7},{7,6},{8,9},{9,8},{10,11... | collective-permute-start | bytes 442376 | tf_op jit(solution)/shard_map/ppermute | solution.py:259
  53.7 1.3 %collective-permute-start.22 = (bf16[96,384]{1,0:T(8,128)(2,1)S(1)}, bf16[96,384]{1,0:T(8,128)(2,1)S(1)}, u32[]{:S(2)}, u32[]{:S(2)}) collective-permute-start(bf16[96,384]{1,0:T(8,128)(2,1)S(1)} %collective-permute-done.21.refs_0_), channel_id=1, source_target_pairs={{0,1},{1,0},{2,3},{3,2},{4,5},{5,4},{6,7},{7,6},{8,9},{9,8},{10,11... | collective-permute-start | bytes 221192 | tf_op jit(solution)/shard_map/ppermute | solution.py:259
  53.7 2.0 %collective-permute-start.16 = (bf16[96,384]{1,0:T(8,128)(2,1)S(1)}, bf16[96,384]{1,0:T(8,128)(2,1)S(1)}, u32[]{:S(2)}, u32[]{:S(2)}) collective-permute-start(bf16[96,384]{1,0:T(8,128)(2,1)S(1)} %collective-permute-done.15.up_ref), channel_id=1, source_target_pairs={{0,1},{1,0},{2,3},{3,2},{4,5},{5,4},{6,7},{7,6},{8,9},{9,8},{10,11... | collective-permute-start | bytes 221192 | tf_op jit(solution)/shard_map/ppermute | solution.py:259

commit v4 on v3

--- a/solution.py
+++ b/solution.py
@@ -13,6 +13,7 @@
 F32 = jnp.float32
 K1_LIMIT = 40
 SMALL_LIMIT = 24
+FINISH_LOTS = 2
 
 coef_a = 3.4445
 coef_b = -4.775
@@ -168,12 +169,20 @@
 
 
 def pair_sum_kernel(keep_ref, got_ref, *out_refs):
-    heads = len(out_refs) // 2
-    main = out_refs[0].shape[0]
-    for slot in range(heads):
-        total = (keep_ref[slot].astype(F32) + got_ref[slot].astype(F32)).astype(BF16)
-        out_refs[slot][...] = total[:main]
-        out_refs[heads + slot][...] = total[main:]
+    rows = out_refs[0].shape[0]
+    for index, out_ref in enumerate(out_refs):
+        slot, part = index // 2, slice(index % 2 * rows, (index % 2 + 1) * rows)
+        out_ref[...] = (keep_ref[slot, part].astype(F32) + got_ref[slot, part].astype(F32)).astype(BF16)
+
+
+def plane_sum_kernel(*refs):
+    *parts, main_ref, up_ref = refs
+    main = main_ref.shape[0]
+    count = len(parts) // 2
+    total = [sum(part[...].astype(F32) for part in parts[start : start + count]).astype(BF16) for start in (0, count)]
+    total = jnp.concatenate(total, axis=0)
+    main_ref[...] = total[:main]
+    up_ref[...] = total[main:]
 
 
 def sum_kernel(*refs):
@@ -184,63 +193,85 @@
     out_ref[...] = total.astype(BF16)
 
 
-def stepped(total, base):
-    norm = jnp.sqrt(jnp.sum(total * total))
-    x = (total / (norm + 1e-07)).astype(BF16)
+def stepped(totals, bases):
+    norms = [jnp.sqrt(jnp.sum(total * total)) for total in totals]
+    iterates = [(total / (norm + 1e-07)).astype(BF16) for total, norm in zip(totals, norms)]
     for step in range(NS_STEPS):
-        gram = mm(x, x, NT).astype(BF16)
-        square = mm(gram, gram, NN)
-        mixer = (coef_b * gram.astype(F32) + coef_c * square).astype(BF16)
-        x = (coef_a * x.astype(F32) + mm(mixer, x, NN)).astype(BF16)
-    return (base - step_size * x.astype(F32)).astype(BF16)
-
-
-def newton_kernel(mine_ref, other_ref, base_ref, out_ref):
-    out_ref[...] = stepped(mine_ref[...].astype(F32) + other_ref[...].astype(F32), base_ref[...])
-
-
-def newton_up_kernel(heads, mine_ref, got_ref, base_ref, out_ref, half_ref):
-    half = mine_ref.shape[0]
+        grams = [mm(x, x, NT).astype(BF16) for x in iterates]
+        squares = [mm(g, g, NN) for g in grams]
+        mixers = [(coef_b * g.astype(F32) + coef_c * s).astype(BF16) for g, s in zip(grams, squares)]
+        moved = [mm(m, x, NN) for m, x in zip(mixers, iterates)]
+        iterates = [(coef_a * x.astype(F32) + y).astype(BF16) for x, y in zip(iterates, moved)]
+    return [(base - step_size * x.astype(F32)).astype(BF16) for base, x in zip(bases, iterates)]
+
+
+def newton_kernel(heads, mine_ref, other_ref, half_ref, got_ref, base_ref, base_up_ref, out_ref, *part_refs):
+    head_dim, half = mine_ref.shape[0], half_ref.shape[0]
     even = position(heads)[1] == 0
-    a, b = mine_ref[...], got_ref[...]
-    total = jnp.concatenate([jnp.where(even, a, b), jnp.where(even, b, a)], axis=0).astype(F32)
-    fresh = stepped(total, base_ref[...])
-    out_ref[...] = fresh
-    half_ref[...] = jnp.where(even, fresh[:half], fresh[half:])
-
-
-def head_output(even, q, main_ref, main_there_ref, up_refs):
-    here, there = main_ref[...], main_there_ref[...]
-    gate_b, down_b = jnp.where(even, here, there), jnp.where(even, there, here)
-    if len(up_refs) == 1:
-        up_b = up_refs[0][...]
-    else:
-        a, b = up_refs[0][...], up_refs[1][...]
-        up_b = jnp.concatenate([jnp.where(even, a, b), jnp.where(even, b, a)], axis=0)
-    gate = mm(q, gate_b, NN)
+    a, b = half_ref[...], got_ref[...]
+    upper = jnp.concatenate([jnp.where(even, a, b), jnp.where(even, b, a)], axis=0).astype(F32)
+    main, upper = stepped((mine_ref[...].astype(F32) + other_ref[...].astype(F32), upper), (base_ref[...], base_up_ref[...]))
+    whole = jnp.concatenate([main, jnp.where(even, upper[:half], upper[half:])], axis=0)
+    out_ref[...] = whole
+    rows = whole.shape[0] // len(part_refs)
+    for index, part_ref in enumerate(part_refs):
+        part_ref[...] = whole[index * rows : (index + 1) * rows]
+
+
+def head_output(even, q, here, there):
+    head_dim = q.shape[1]
+    here, there = (jnp.concatenate([ref[...] for ref in refs], axis=0) for refs in (here, there))
+    a, b = jnp.where(even, here, there), jnp.where(even, there, here)
+    up_b = jnp.concatenate([a[head_dim:], b[head_dim:]], axis=0)
+    gate = mm(q, a[:head_dim], NN)
     upper = mm(q, up_b, NN)
     hidden = (gate * jax.nn.sigmoid(gate) * upper).astype(BF16)
-    return mm(hidden, down_b, NT).astype(BF16)
-
-
-def apply_kernel(far, q_ref, main_ref, main_there_ref, *refs):
-    *up_refs, out_ref = refs
+    return mm(hidden, b[:head_dim], NT).astype(BF16)
+
+
+def apply_kernel(far, q_ref, *refs):
+    *block_refs, out_ref = refs
+    half = len(block_refs) // 2
     own, core = position(q_ref.shape[0])
-    out_ref[...] = head_output(core == 0, q_ref[own ^ far], main_ref, main_there_ref, up_refs)
-
-
-def finish_kernel(q_ref, main_ref, main_there_ref, up_ref, up_there_ref, *refs):
-    *pieces, out_ref = refs
-    heads, _, head_dim = q_ref.shape
+    out_ref[...] = head_output(core == 0, q_ref[own ^ far], block_refs[:half], block_refs[half:])
+
+
+def finish_kernel(q_ref, *refs):
+    *piece_refs, first_ref, second_ref, first_there_ref, second_there_ref, out_hbm, pieces, whole, sems = refs
+    heads, rows, head_dim = q_ref.shape
     own, core = position(heads)
-    piece = head_output(core == 0, q_ref[own ^ (heads - 1)], main_ref, main_there_ref, (up_ref, up_there_ref))
-    for case in range(heads):
-
-        @pl.when(own == case)
-        def _():
-            for head in range(heads):
-                far = head ^ case
-                out_ref[:, head * head_dim : (head + 1) * head_dim] = piece if far == heads - 1 else pieces[far][...]
+    lot = rows // FINISH_LOTS
+    copies = []
+    for index in range(FINISH_LOTS):
+        part = pl.ds(index * lot, lot)
+        for far, piece_ref in enumerate(piece_refs):
+            pieces[far, part] = piece_ref[part]
+        q = q_ref[own ^ (heads - 1), part]
+        pieces[heads - 1, part] = head_output(core == 0, q, (first_ref, second_ref), (first_there_ref, second_there_ref))
+        for head in range(heads):
+            whole[part, head * head_dim : (head + 1) * head_dim] = pieces[own ^ head, part]
+        copies.append(pltpu.make_async_copy(whole.at[part], out_hbm.at[part], sems.at[index]))
+        copies[-1].start()
+    for copy in copies:
+        copy.wait()
+
+
+def finish(query, pieces, blocks):
+    heads, rows, head_dim = query.shape
+    operands = [pltpu.with_memory_space_constraint(x, pltpu.VMEM) for x in (query, *pieces, *blocks)]
+    return pl.pallas_call(
+        finish_kernel,
+        out_shape=jax.ShapeDtypeStruct((rows, heads * head_dim), BF16),
+        in_specs=[pl.BlockSpec(memory_space=pltpu.VMEM)] * len(operands),
+        out_specs=pl.BlockSpec(memory_space=pl.ANY),
+        scratch_shapes=[
+            pltpu.VMEM((heads, rows, head_dim), BF16),
+            pltpu.VMEM((rows, heads * head_dim), BF16),
+            pltpu.SemaphoreType.DMA((FINISH_LOTS,)),
+        ],
+        compiler_params=pltpu.CompilerParams(vmem_limit_bytes=SMALL_LIMIT * 1024 * 1024),
+        name="finish",
+    )(*operands)
 
 
 def shards(tokens, qkv_weight, w_gate, w_up, w_down, view_kind):
@@ -260,14 +291,19 @@
 
     keep, give = gradients(view_kind, tokens, qkv_weight, w_gate, w_up, w_down_t)
     got = exchange(give, 1)
-    sums = small(pair_sum_kernel, [main_block] * heads + [half_block] * heads, (keep, got), 9 * keep.size, "pair_sum")
-    mains, ups = sums[:heads], sums[heads:]
-    ups_in = [exchange(ups[far], 2 * far) for far in (1, 2, 3)]
-    mains_in = [exchange(mains[far], 2 * far) for far in (1, 2, 3)]
+    block = shape(head_dim + half, hidden)
+    part_block = shape(block.shape[0] // 2, hidden)
+    sums = small(pair_sum_kernel, [part_block] * (2 * heads), (keep, got), 9 * keep.size, "pair_sum")
+    first, second = sums[0::2], sums[1::2]
+    first_on, second_on = exchange(first[3], 2), exchange(second[3], 4)
+    first_in, second_in = exchange(first[1], 2), exchange(second[2], 4)
+    first_on = exchange(small(sum_kernel, part_block, (first[2], first_on), 6 * size, "pass_sum"), 4)
+    second_on = exchange(small(sum_kernel, part_block, (second[1], second_on), 6 * size, "pass_sum"), 2)
+    parts = (first[0], first_in, first_on, second[0], second_in, second_on)
+    main, upper = small(plane_sum_kernel, [main_block, half_block], parts, 10 * size, "plane_sum")
     query = project_query(tokens, qkv_weight, heads)
     base = jnp.where(core == 0, lax.dynamic_index_in_dim(w_gate, own, 0, False), lax.dynamic_index_in_dim(w_down_t, own, 0, False))
     base_up = lax.dynamic_index_in_dim(w_up, own, 0, False)
-    mains_in, query, base, base_up = lax.optimization_barrier((mains_in, query, base, base_up))
 
     def over_line(total, name):
         bits = 2 * heads
@@ -276,30 +312,25 @@
             bits *= 2
         return total, exchange(total, bits)
 
-    up_total = small(sum_kernel, half_block, (ups[0], *ups_in), 10 * size, "plane_sum_up")
-    up_total, up_other = over_line(up_total, "line_sum_up")
-    main_total = small(sum_kernel, main_block, (mains[0], *mains_in), 10 * size, "plane_sum")
-    main_total, main_other = over_line(main_total, "line_sum")
-    up_half = small(sum_kernel, half_block, (up_total, up_other), 10 * size, "up_sum")
-    up_got = exchange(up_half, 1)
-    up_fresh, up_out = small(
-        functools.partial(newton_up_kernel, heads), [main_block, half_block], (up_half, up_got, base_up), 30 * size, "newton_up"
+    upper, upper_other = over_line(upper, "line_sum_up")
+    upper_other, query, base, base_up = lax.optimization_barrier((upper_other, query, base, base_up))
+    main, main_other = over_line(main, "line_sum")
+    upper = small(sum_kernel, half_block, (upper, upper_other), 10 * size, "up_sum")
+    upper_got = exchange(upper, 1)
+    fresh, first, second = small(
+        functools.partial(newton_kernel, heads), [block, part_block, part_block], (main, main_other, upper, upper_got, base, base_up), 30 * size, "newton"
     )
-    ups_here = [exchange(up_out, 2 * far) for far in range(1, heads)]
-    ups_there = [exchange(x, 1) for x in ups_here]
-    fresh = small(newton_kernel, main_block, (main_total, main_other, base), 30 * size, "newton")
 
     def apply(far, *args):
         return small(functools.partial(apply_kernel, far), shape(rows, head_dim), (query, *args), 20 * rows * head_dim, "apply")
 
-    here = [exchange(fresh, 2 * far) for far in range(1, heads)]
-    pieces = [apply(0, fresh, exchange(fresh, 1), up_fresh)]
-    here, pieces = lax.optimization_barrier((here, pieces))
-    there = [exchange(x, 1) for x in here]
-    for far in range(1, heads - 1):
-        pieces.append(apply(far, here[far - 1], there[far - 1], ups_here[far - 1], ups_there[far - 1]))
-    args = (query, here[-1], there[-1], ups_here[-1], ups_there[-1], *pieces)
-    return small(finish_kernel, jax.ShapeDtypeStruct((rows, width), BF16), args, 20 * rows * head_dim, "finish")
+    over_y, over_z = [exchange(x, 2) for x in (first, second)], [exchange(x, 4) for x in (first, second)]
+    across = [exchange(over_y[0], 4), exchange(over_z[1], 2)]
+    swapped = lambda blocks: (*blocks, *(exchange(x, 1) for x in blocks))
+    piece = apply(0, fresh, exchange(fresh, 1))
+    over_y, over_z, piece = lax.optimization_barrier((over_y, over_z, piece))
+    pieces = [piece, apply(1, *swapped(over_y)), apply(2, *swapped(over_z))]
+    return finish(query, pieces, swapped(across))
 
 
 def solution(mesh):

time: 57.7 us -> 54.5 us (0.945)
  Pallas kernels: 19.9 us -> 17.1 us
  starting transfers between devices: 20.1 us -> 19.2 us
    pallas_call x10 -> x9, Pallas kernels: 10.1 us -> 5.56 us  [small(): pl.pallas_call(kernel, out_shape=shapes, in_specs=specs, compiler_params=...]
    pallas_call x0 -> x1, Pallas kernels: none -> 1.7 us  [finish(): pl.pallas_call(finish_kernel, out_shape=jax.ShapeDtypeStruct((rows, heads...]
    ppermute x23, starting transfers between devices: 20.1 us -> 19.2 us  [exchange(): return lax.ppermute(x, 'tok', [(i, i ^ bits) for i in range(groups)])]
  transfers between devices with their start and end apart: 23 -> 23, of which waited for: 11 -> 12; matrix products, arithmetic and copies ran while one was open for 2% -> 2% of each run, Pallas kernels for 18% -> 8%
where the time goes in v4:
time: 54.5 us; the launch traced here: 54.3 us
  starting transfers between devices  19.2 us (35%)
  Pallas kernels  17.1 us (31%)
  waiting for transfers between devices  16.7 us (31%)
  other arithmetic  1.19 us (2%)
    ppermute x23, starting transfers between devices, exchange(): return lax.ppermute(x, 'tok', [(i, i ^ bits) for i in range(groups)])  19.2 us
    ppermute x23, waiting for transfers between devices, exchange(): return lax.ppermute(x, 'tok', [(i, i ^ bits) for i in range(groups)])  16.7 us
    pallas_call x1, Pallas kernels, gradients(): pl.pallas_call(grad_kernel, out_shape=[shape] * 2, in_specs=[pl.BlockSpec...  7.45 us
    pallas_call x9, Pallas kernels, small(): pl.pallas_call(kernel, out_shape=shapes, in_specs=specs, compiler_params=...  5.56 us
    pallas_call x1, Pallas kernels, project_query(): pl.pallas_call(query_kernel, out_shape=pltpu.VMEM((heads, rows, width //...  2.36 us
    pallas_call x1, Pallas kernels, finish(): pl.pallas_call(finish_kernel, out_shape=jax.ShapeDtypeStruct((rows, heads...  1.7 us
    select_n x1, other arithmetic, shards(): jnp.where(core == 0, lax.dynamic_index_in_dim(w_gate, own, 0, False), lax...  1.19 us
  transfers between devices with their start and end apart: 23, of which 12 were waited for; matrix products, arithmetic and copies ran while one was open for 2% of the time, Pallas kernels for 8%

profile of v4, /device:TPU:0, one launch (start us, length us, event | category | flops | bytes accessed | tf_op | source)
XLA Modules:
  0.0 54.3 jit_solution(11247476053251182417)
XLA Ops:
  0.0 7.5 %gradients.1 = (bf16[4,288,384]{2,1,0:T(8,128)(2,1)S(1)}, bf16[4,288,384]{2,1,0:T(8,128)(2,1)S(1)}) custom-call(s32[16]{0:T(128)} %view_hbm.1, bf16[512,768]{1,0:T(8,128)(2,1)} %tokens_ref.1, bf16[768,2304]{1,0:T(8,128)(2,1)} %weight_ref.1, f32[4,192,384]{2,1,0:T(8,128)} %gate_hbm.1, f32[4,192,384]{2,1,0:T(8,128)} %up_hbm.1, f32[4,192,384]{2,1,0:T(8,128)} %bitcast.9), custom_call_target="tpu_custom_call" | custom-call | flops 3019898880 | bytes 6684672 | tf_op jit(solution)/shard_map/gradients/pallas_call | solution.py:112
  7.5 0.5 collective-permute-start
  8.0 2.1 %collective-permute-done.got_ref = bf16[4,288,384]{2,1,0:T(8,128)(2,1)S(1)} collective-permute-done((bf16[4,288,384]{2,1,0:T(8,128)(2,1)S(1)}, bf16[4,288,384]{2,1,0:T(8,128)(2,1)S(1)}, u32[]{:S(2)}, u32[]{:S(2)}) %collective-permute-start) | collective-permute-done | bytes 884768 | tf_op jit(solution)/shard_map/ppermute | solution.py:290
  10.2 3.0 %collective-permute-start.2 = (bf16[144,384]{1,0:T(8,128)(2,1)S(1)}, bf16[144,384]{1,0:T(8,128)(2,1)S(1)}, u32[]{:S(2)}, u32[]{:S(2)}) collective-permute-start(bf16[144,384]{1,0:T(8,128)(2,1)S(1)} %get-tuple-element.34), channel_id=1, source_target_pairs={{0,2},{1,3},{2,0},{3,1},{4,6},{5,7},{6,4},{7,5},{8,10},{9,11},{10,... | collective-permute-start | bytes 331784 | tf_op jit(solution)/shard_map/ppermute | solution.py:290
  13.2 1.6 %collective-permute-start.5 = (bf16[144,384]{1,0:T(8,128)(2,1)S(1)}, bf16[144,384]{1,0:T(8,128)(2,1)S(1)}, u32[]{:S(2)}, u32[]{:S(2)}) collective-permute-start(bf16[144,384]{1,0:T(8,128)(2,1)S(1)} %get-tuple-element.38), channel_id=1, source_target_pairs={{0,4},{1,5},{2,6},{3,7},{4,0},{5,1},{6,2},{7,3},{8,12},{9,13},{10,... | collective-permute-start | bytes 331784 | tf_op jit(solution)/shard_map/ppermute | solution.py:290
  14.8 0.5 collective-permute-start.1
  15.3 1.3 %collective-permute-done.2.refs_1_ = bf16[144,384]{1,0:T(8,128)(2,1)S(1)} collective-permute-done((bf16[144,384]{1,0:T(8,128)(2,1)S(1)}, bf16[144,384]{1,0:T(8,128)(2,1)S(1)}, u32[]{:S(2)}, u32[]{:S(2)}) %collective-permute-start.2) | collective-permute-done | bytes 110624 | tf_op jit(solution)/shard_map/ppermute | solution.py:290
  16.7 2.6 %collective-permute-start.3 = (bf16[144,384]{1,0:T(8,128)(2,1)S(1)}, bf16[144,384]{1,0:T(8,128)(2,1)S(1)}, u32[]{:S(2)}, u32[]{:S(2)}) collective-permute-start(bf16[144,384]{1,0:T(8,128)(2,1)S(1)} %pass_sum.2), channel_id=1, source_target_pairs={{0,4},{1,5},{2,6},{3,7},{4,0},{5,1},{6,2},{7,3},{8,12},{9,13},{10,... | collective-permute-start | bytes 331784 | tf_op jit(solution)/shard_map/ppermute | solution.py:290
  19.3 1.6 %collective-permute-start.6 = (bf16[144,384]{1,0:T(8,128)(2,1)S(1)}, bf16[144,384]{1,0:T(8,128)(2,1)S(1)}, u32[]{:S(2)}, u32[]{:S(2)}) collective-permute-start(bf16[144,384]{1,0:T(8,128)(2,1)S(1)} %pass_sum.3), channel_id=1, source_target_pairs={{0,2},{1,3},{2,0},{3,1},{4,6},{5,7},{6,4},{7,5},{8,10},{9,11},{10,... | collective-permute-start | bytes 331784 | tf_op jit(solution)/shard_map/ppermute | solution.py:290
  21.2 1.5 %collective-permute-done.3.refs_2_ = bf16[144,384]{1,0:T(8,128)(2,1)S(1)} collective-permute-done((bf16[144,384]{1,0:T(8,128)(2,1)S(1)}, bf16[144,384]{1,0:T(8,128)(2,1)S(1)}, u32[]{:S(2)}, u32[]{:S(2)}) %collective-permute-start.3) | collective-permute-done | bytes 110624 | tf_op jit(solution)/shard_map/ppermute | solution.py:290
  22.8 1.3 %collective-permute-done.6.refs_5_ = bf16[144,384]{1,0:T(8,128)(2,1)S(1)} collective-permute-done((bf16[144,384]{1,0:T(8,128)(2,1)S(1)}, bf16[144,384]{1,0:T(8,128)(2,1)S(1)}, u32[]{:S(2)}, u32[]{:S(2)}) %collective-permute-start.6) | collective-permute-done | bytes 110624 | tf_op jit(solution)/shard_map/ppermute | solution.py:290
  24.2 2.7 %collective-permute-start.7 = (bf16[96,384]{1,0:T(8,128)(2,1)S(1)}, bf16[96,384]{1,0:T(8,128)(2,1)S(1)}, u32[]{:S(2)}, u32[]{:S(2)}) collective-permute-start(bf16[96,384]{1,0:T(8,128)(2,1)S(1)} %get-tuple-element.39.refs_0_), channel_id=1, source_target_pairs={{0,8},{1,9},{2,10},{3,11},{4,12},{5,13},{6,14},{7,15},{8,0},{9,1},... | collective-permute-start | bytes 221192 | tf_op jit(solution)/shard_map/ppermute | solution.py:290
  27.2 1.2 %fusion = (f32[192,384]{1,0:T(8,128)S(1)}, f32[192,384]{1,0:T(8,128)S(1)}) fusion(f32[4,384,192]{1,2,0:T(8,128)} %param.10, s32[]{:T(128)S(6)} %select_n.18, f32[4,192,384]{2,1,0:T(8,128)} %gate_hbm.1, pred[]{:T(512)S(6)} %eq.3, f32[4,192,384]{2,1,0:T(8,128)} %up_hbm.1), kind=kLoop, calls=%fused_computation.1 | loop fusion | flops 73728 | bytes 1474565 | tf_op jit(solution)/shard_map/jit(_where)/select_n | solution.py:305
  28.4 2.4 %query.1.q_ref = bf16[4,512,192]{2,1,0:T(8,128)(2,1)S(1)} custom-call(bf16[512,768]{1,0:T(8,128)(2,1)} %tokens_ref.1, bf16[768,2304]{1,0:T(8,128)(2,1)} %weight_ref.1), custom_call_target="tpu_custom_call" | custom-call | flops 603979776 | bytes 3932160 | tf_op jit(solution)/shard_map/query/pallas_call | solution.py:159
  30.8 3.5 %collective-permute-done.7.refs_1_ = bf16[96,384]{1,0:T(8,128)(2,1)S(1)} collective-permute-done((bf16[96,384]{1,0:T(8,128)(2,1)S(1)}, bf16[96,384]{1,0:T(8,128)(2,1)S(1)}, u32[]{:S(2)}, u32[]{:S(2)}) %collective-permute-start.7) | collective-permute-done | bytes 73760 | tf_op jit(solution)/shard_map/ppermute | solution.py:290
  34.3 1.6 %collective-permute-done.8.other_ref = bf16[192,384]{1,0:T(8,128)(2,1)S(1)} collective-permute-done((bf16[192,384]{1,0:T(8,128)(2,1)S(1)}, bf16[192,384]{1,0:T(8,128)(2,1)S(1)}, u32[]{:S(2)}, u32[]{:S(2)}) %collective-permute-start.8) | collective-permute-done | bytes 147488 | tf_op jit(solution)/shard_map/ppermute | solution.py:290
  35.9 3.1 %newton.1 = (bf16[288,384]{1,0:T(8,128)(2,1)S(1)}, bf16[144,384]{1,0:T(8,128)(2,1)S(1)}, bf16[144,384]{1,0:T(8,128)(2,1)S(1)}) custom-call(bf16[192,384]{1,0:T(8,128)(2,1)S(1)} %get-tuple-element.41.mine_ref, bf16[192,384]{1,0:T(8,128)(2,1)S(1)} %collective-permute-done.8.other_ref, bf16[96,384]{1,0:T(8,128)(2,1)S(1)} %up_sum.1.half_ref, ...), custom_call_target="tpu_custom_call" | custom-call | bytes 2211840 | tf_op jit(solution)/shard_map/newton/pallas_call | solution.py:140
  39.1 0.9 %collective-permute-start.10 = (bf16[144,384]{1,0:T(8,128)(2,1)S(1)}, bf16[144,384]{1,0:T(8,128)(2,1)S(1)}, u32[]{:S(2)}, u32[]{:S(2)}) collective-permute-start(bf16[144,384]{1,0:T(8,128)(2,1)S(1)} %get-tuple-element.45), channel_id=1, source_target_pairs={{0,2},{1,3},{2,0},{3,1},{4,6},{5,7},{6,4},{7,5},{8,10},{9,11},{10,... | collective-permute-start | bytes 331784 | tf_op jit(solution)/shard_map/ppermute | solution.py:290
  40.0 1.1 %collective-permute-start.11 = (bf16[144,384]{1,0:T(8,128)(2,1)S(1)}, bf16[144,384]{1,0:T(8,128)(2,1)S(1)}, u32[]{:S(2)}, u32[]{:S(2)}) collective-permute-start(bf16[144,384]{1,0:T(8,128)(2,1)S(1)} %get-tuple-element.46), channel_id=1, source_target_pairs={{0,2},{1,3},{2,0},{3,1},{4,6},{5,7},{6,4},{7,5},{8,10},{9,11},{10,... | collective-permute-start | bytes 331784 | tf_op jit(solution)/shard_map/ppermute | solution.py:290
  41.1 2.0 %collective-permute-start.12 = (bf16[144,384]{1,0:T(8,128)(2,1)S(1)}, bf16[144,384]{1,0:T(8,128)(2,1)S(1)}, u32[]{:S(2)}, u32[]{:S(2)}) collective-permute-start(bf16[144,384]{1,0:T(8,128)(2,1)S(1)} %get-tuple-element.45), channel_id=1, source_target_pairs={{0,4},{1,5},{2,6},{3,7},{4,0},{5,1},{6,2},{7,3},{8,12},{9,13},{10,... | collective-permute-start | bytes 331784 | tf_op jit(solution)/shard_map/ppermute | solution.py:290
  43.2 1.8 %collective-permute-done.10.refs_0_ = bf16[144,384]{1,0:T(8,128)(2,1)S(1)} collective-permute-done((bf16[144,384]{1,0:T(8,128)(2,1)S(1)}, bf16[144,384]{1,0:T(8,128)(2,1)S(1)}, u32[]{:S(2)}, u32[]{:S(2)}) %collective-permute-start.10) | collective-permute-done | bytes 110624 | tf_op jit(solution)/shard_map/ppermute | solution.py:290
  45.0 0.9 %collective-permute-done.13.refs_1_ = bf16[144,384]{1,0:T(8,128)(2,1)S(1)} collective-permute-done((bf16[144,384]{1,0:T(8,128)(2,1)S(1)}, bf16[144,384]{1,0:T(8,128)(2,1)S(1)}, u32[]{:S(2)}, u32[]{:S(2)}) %collective-permute-start.13) | collective-permute-done | bytes 110624 | tf_op jit(solution)/shard_map/ppermute | solution.py:290
  45.9 1.1 %collective-permute-start.20 = (bf16[144,384]{1,0:T(8,128)(2,1)S(1)}, bf16[144,384]{1,0:T(8,128)(2,1)S(1)}, u32[]{:S(2)}, u32[]{:S(2)}) collective-permute-start(bf16[144,384]{1,0:T(8,128)(2,1)S(1)} %collective-permute-done.13.refs_1_), channel_id=1, source_target_pairs={{0,2},{1,3},{2,0},{3,1},{4,6},{5,7},{6,4},{7,5},{8,10},{9,11},{10,... | collective-permute-start | bytes 331784 | tf_op jit(solution)/shard_map/ppermute | solution.py:290
  47.1 0.7 %apply.3.refs_0_ = bf16[512,192]{1,0:T(8,128)(2,1)S(1)} custom-call(bf16[4,512,192]{2,1,0:T(8,128)(2,1)S(1)} %query.1.q_ref, bf16[288,384]{1,0:T(8,128)(2,1)S(1)} %get-tuple-element.47.refs_0_, bf16[288,384]{1,0:T(8,128)(2,1)S(1)} %collective-permute-done.14.refs_1_), custom_call_target="tpu_custom_call" | custom-call | bytes 1966080 | tf_op jit(solution)/shard_map/apply/pallas_call | solution.py:140
  47.8 0.4 collective-permute-done.12.refs_0_
  48.1 0.5 collective-permute-start.16
  48.7 1.2 %collective-permute-done.19.refs_3_ = bf16[144,384]{1,0:T(8,128)(2,1)S(1)} collective-permute-done((bf16[144,384]{1,0:T(8,128)(2,1)S(1)}, bf16[144,384]{1,0:T(8,128)(2,1)S(1)}, u32[]{:S(2)}, u32[]{:S(2)}) %collective-permute-start.19) | collective-permute-done | bytes 110624 | tf_op jit(solution)/shard_map/ppermute | solution.py:290
  49.9 0.8 %collective-permute-done.20.refs_4_ = bf16[144,384]{1,0:T(8,128)(2,1)S(1)} collective-permute-done((bf16[144,384]{1,0:T(8,128)(2,1)S(1)}, bf16[144,384]{1,0:T(8,128)(2,1)S(1)}, u32[]{:S(2)}, u32[]{:S(2)}) %collective-permute-start.20) | collective-permute-done | bytes 110624 | tf_op jit(solution)/shard_map/ppermute | solution.py:290
  50.7 0.5 collective-permute-start.22
  51.2 0.7 %apply.4.refs_1_ = bf16[512,192]{1,0:T(8,128)(2,1)S(1)} custom-call(bf16[4,512,192]{2,1,0:T(8,128)(2,1)S(1)} %query.1.q_ref, bf16[144,384]{1,0:T(8,128)(2,1)S(1)} %collective-permute-done.10.refs_0_, bf16[144,384]{1,0:T(8,128)(2,1)S(1)} %collective-permute-done.11.refs_1_, bf16[144,384]{1,0:T(8,128)(2,1)S(1)} %collective-permute-done.15.refs_2_, ...), custom_call_target="tpu_custom_call" | custom-call | bytes 1966080 | tf_op jit(solution)/shard_map/apply/pallas_call | solution.py:140
  51.9 0.7 %apply.5.refs_2_ = bf16[512,192]{1,0:T(8,128)(2,1)S(1)} custom-call(bf16[4,512,192]{2,1,0:T(8,128)(2,1)S(1)} %query.1.q_ref, bf16[144,384]{1,0:T(8,128)(2,1)S(1)} %collective-permute-done.12.refs_0_, bf16[144,384]{1,0:T(8,128)(2,1)S(1)} %collective-permute-done.13.refs_1_, bf16[144,384]{1,0:T(8,128)(2,1)S(1)} %collective-permute-done.17.refs_2_, ...), custom_call_target="tpu_custom_call" | custom-call | bytes 1966080 | tf_op jit(solution)/shard_map/apply/pallas_call | solution.py:140
  52.6 1.7 %finish.1 = bf16[512,768]{1,0:T(8,128)(2,1)} custom-call(bf16[4,512,192]{2,1,0:T(8,128)(2,1)S(1)} %query.1.q_ref, bf16[512,192]{1,0:T(8,128)(2,1)S(1)} %apply.3.refs_0_, bf16[512,192]{1,0:T(8,128)(2,1)S(1)} %apply.4.refs_1_, bf16[512,192]{1,0:T(8,128)(2,1)S(1)} %apply.5.refs_2_, bf16[144,384]{1,0:T(8,128)(2,1)S(1)} %collective-permute-done.19.refs_3_, ...), custom_call_target="tpu_custom_call" | custom-call | tf_op jit(solution)/shard_map/finish/pallas_call | solution.py:262
  (27 shorter events, 1.3 us)
Async XLA Ops:
  7.5 2.6 %collective-permute-start = (bf16[4,288,384]{2,1,0:T(8,128)(2,1)S(1)}, bf16[4,288,384]{2,1,0:T(8,128)(2,1)S(1)}, u32[]{:S(2)}, u32[]{:S(2)}) collective-permute-start(bf16[4,288,384]{2,1,0:T(8,128)(2,1)S(1)} %get-tuple-element.30), channel_id=1, source_target_pairs={{0,1},{1,0},{2,3},{3,2},{4,5},{5,4},{6,7},{7,6},{8,9},{9,8},{10,11... | collective-permute-start | bytes 2654216 | tf_op jit(solution)/shard_map/ppermute | solution.py:290
  10.2 6.4 %collective-permute-start.2 = (bf16[144,384]{1,0:T(8,128)(2,1)S(1)}, bf16[144,384]{1,0:T(8,128)(2,1)S(1)}, u32[]{:S(2)}, u32[]{:S(2)}) collective-permute-start(bf16[144,384]{1,0:T(8,128)(2,1)S(1)} %get-tuple-element.34), channel_id=1, source_target_pairs={{0,2},{1,3},{2,0},{3,1},{4,6},{5,7},{6,4},{7,5},{8,10},{9,11},{10,... | collective-permute-start | bytes 331784 | tf_op jit(solution)/shard_map/ppermute | solution.py:290
  13.2 6.1 %collective-permute-start.5 = (bf16[144,384]{1,0:T(8,128)(2,1)S(1)}, bf16[144,384]{1,0:T(8,128)(2,1)S(1)}, u32[]{:S(2)}, u32[]{:S(2)}) collective-permute-start(bf16[144,384]{1,0:T(8,128)(2,1)S(1)} %get-tuple-element.38), channel_id=1, source_target_pairs={{0,4},{1,5},{2,6},{3,7},{4,0},{5,1},{6,2},{7,3},{8,12},{9,13},{10,... | collective-permute-start | bytes 331784 | tf_op jit(solution)/shard_map/ppermute | solution.py:290
  14.8 6.1 %collective-permute-start.1 = (bf16[144,384]{1,0:T(8,128)(2,1)S(1)}, bf16[144,384]{1,0:T(8,128)(2,1)S(1)}, u32[]{:S(2)}, u32[]{:S(2)}) collective-permute-start(bf16[144,384]{1,0:T(8,128)(2,1)S(1)} %get-tuple-element.32), channel_id=1, source_target_pairs={{0,2},{1,3},{2,0},{3,1},{4,6},{5,7},{6,4},{7,5},{8,10},{9,11},{10,... | collective-permute-start | bytes 331784 | tf_op jit(solution)/shard_map/ppermute | solution.py:290
  15.3 6.0 %collective-permute-start.4 = (bf16[144,384]{1,0:T(8,128)(2,1)S(1)}, bf16[144,384]{1,0:T(8,128)(2,1)S(1)}, u32[]{:S(2)}, u32[]{:S(2)}) collective-permute-start(bf16[144,384]{1,0:T(8,128)(2,1)S(1)} %get-tuple-element.36), channel_id=1, source_target_pairs={{0,4},{1,5},{2,6},{3,7},{4,0},{5,1},{6,2},{7,3},{8,12},{9,13},{10,... | collective-permute-start | bytes 331784 | tf_op jit(solution)/shard_map/ppermute | solution.py:290
  16.7 6.1 %collective-permute-start.3 = (bf16[144,384]{1,0:T(8,128)(2,1)S(1)}, bf16[144,384]{1,0:T(8,128)(2,1)S(1)}, u32[]{:S(2)}, u32[]{:S(2)}) collective-permute-start(bf16[144,384]{1,0:T(8,128)(2,1)S(1)} %pass_sum.2), channel_id=1, source_target_pairs={{0,4},{1,5},{2,6},{3,7},{4,0},{5,1},{6,2},{7,3},{8,12},{9,13},{10,... | collective-permute-start | bytes 331784 | tf_op jit(solution)/shard_map/ppermute | solution.py:290
  19.3 4.8 %collective-permute-start.6 = (bf16[144,384]{1,0:T(8,128)(2,1)S(1)}, bf16[144,384]{1,0:T(8,128)(2,1)S(1)}, u32[]{:S(2)}, u32[]{:S(2)}) collective-permute-start(bf16[144,384]{1,0:T(8,128)(2,1)S(1)} %pass_sum.3), channel_id=1, source_target_pairs={{0,2},{1,3},{2,0},{3,1},{4,6},{5,7},{6,4},{7,5},{8,10},{9,11},{10,... | collective-permute-start | bytes 331784 | tf_op jit(solution)/shard_map/ppermute | solution.py:290
  24.2 10.0 %collective-permute-start.7 = (bf16[96,384]{1,0:T(8,128)(2,1)S(1)}, bf16[96,384]{1,0:T(8,128)(2,1)S(1)}, u32[]{:S(2)}, u32[]{:S(2)}) collective-permute-start(bf16[96,384]{1,0:T(8,128)(2,1)S(1)} %get-tuple-element.39.refs_0_), channel_id=1, source_target_pairs={{0,8},{1,9},{2,10},{3,11},{4,12},{5,13},{6,14},{7,15},{8,0},{9,1},... | collective-permute-start | bytes 221192 | tf_op jit(solution)/shard_map/ppermute | solution.py:290
  26.9 9.0 %collective-permute-start.8 = (bf16[192,384]{1,0:T(8,128)(2,1)S(1)}, bf16[192,384]{1,0:T(8,128)(2,1)S(1)}, u32[]{:S(2)}, u32[]{:S(2)}) collective-permute-start(bf16[192,384]{1,0:T(8,128)(2,1)S(1)} %get-tuple-element.41.mine_ref), channel_id=1, source_target_pairs={{0,8},{1,9},{2,10},{3,11},{4,12},{5,13},{6,14},{7,15},{8,0},{9,1},... | collective-permute-start | bytes 442376 | tf_op jit(solution)/shard_map/ppermute | solution.py:290
  34.2 1.7 %collective-permute-start.9 = (bf16[96,384]{1,0:T(8,128)(2,1)S(1)}, bf16[96,384]{1,0:T(8,128)(2,1)S(1)}, u32[]{:S(2)}, u32[]{:S(2)}) collective-permute-start(bf16[96,384]{1,0:T(8,128)(2,1)S(1)} %up_sum.1.half_ref), channel_id=1, source_target_pairs={{0,1},{1,0},{2,3},{3,2},{4,5},{5,4},{6,7},{7,6},{8,9},{9,8},{10,11... | collective-permute-start | bytes 221192 | tf_op jit(solution)/shard_map/ppermute | solution.py:290
  39.0 8.1 %collective-permute-start.14 = (bf16[288,384]{1,0:T(8,128)(2,1)S(1)}, bf16[288,384]{1,0:T(8,128)(2,1)S(1)}, u32[]{:S(2)}, u32[]{:S(2)}) collective-permute-start(bf16[288,384]{1,0:T(8,128)(2,1)S(1)} %get-tuple-element.47.refs_0_), channel_id=1, source_target_pairs={{0,1},{1,0},{2,3},{3,2},{4,5},{5,4},{6,7},{7,6},{8,9},{9,8},{10,11... | collective-permute-start | bytes 663560 | tf_op jit(solution)/shard_map/ppermute | solution.py:290
  39.1 5.9 %collective-permute-start.10 = (bf16[144,384]{1,0:T(8,128)(2,1)S(1)}, bf16[144,384]{1,0:T(8,128)(2,1)S(1)}, u32[]{:S(2)}, u32[]{:S(2)}) collective-permute-start(bf16[144,384]{1,0:T(8,128)(2,1)S(1)} %get-tuple-element.45), channel_id=1, source_target_pairs={{0,2},{1,3},{2,0},{3,1},{4,6},{5,7},{6,4},{7,5},{8,10},{9,11},{10,... | collective-permute-start | bytes 331784 | tf_op jit(solution)/shard_map/ppermute | solution.py:290
  40.0 5.9 %collective-permute-start.13 = (bf16[144,384]{1,0:T(8,128)(2,1)S(1)}, bf16[144,384]{1,0:T(8,128)(2,1)S(1)}, u32[]{:S(2)}, u32[]{:S(2)}) collective-permute-start(bf16[144,384]{1,0:T(8,128)(2,1)S(1)} %get-tuple-element.46), channel_id=1, source_target_pairs={{0,4},{1,5},{2,6},{3,7},{4,0},{5,1},{6,2},{7,3},{8,12},{9,13},{10,... | collective-permute-start | bytes 331784 | tf_op jit(solution)/shard_map/ppermute | solution.py:290
  40.0 7.8 %collective-permute-start.11 = (bf16[144,384]{1,0:T(8,128)(2,1)S(1)}, bf16[144,384]{1,0:T(8,128)(2,1)S(1)}, u32[]{:S(2)}, u32[]{:S(2)}) collective-permute-start(bf16[144,384]{1,0:T(8,128)(2,1)S(1)} %get-tuple-element.46), channel_id=1, source_target_pairs={{0,2},{1,3},{2,0},{3,1},{4,6},{5,7},{6,4},{7,5},{8,10},{9,11},{10,... | collective-permute-start | bytes 331784 | tf_op jit(solution)/shard_map/ppermute | solution.py:290
  41.1 7.0 %collective-permute-start.12 = (bf16[144,384]{1,0:T(8,128)(2,1)S(1)}, bf16[144,384]{1,0:T(8,128)(2,1)S(1)}, u32[]{:S(2)}, u32[]{:S(2)}) collective-permute-start(bf16[144,384]{1,0:T(8,128)(2,1)S(1)} %get-tuple-element.45), channel_id=1, source_target_pairs={{0,4},{1,5},{2,6},{3,7},{4,0},{5,1},{6,2},{7,3},{8,12},{9,13},{10,... | collective-permute-start | bytes 331784 | tf_op jit(solution)/shard_map/ppermute | solution.py:290
  45.0 4.9 %collective-permute-start.19 = (bf16[144,384]{1,0:T(8,128)(2,1)S(1)}, bf16[144,384]{1,0:T(8,128)(2,1)S(1)}, u32[]{:S(2)}, u32[]{:S(2)}) collective-permute-start(bf16[144,384]{1,0:T(8,128)(2,1)S(1)} %collective-permute-done.10.refs_0_), channel_id=1, source_target_pairs={{0,4},{1,5},{2,6},{3,7},{4,0},{5,1},{6,2},{7,3},{8,12},{9,13},{10,... | collective-permute-start | bytes 331784 | tf_op jit(solution)/shard_map/ppermute | solution.py:290
  45.9 4.7 %collective-permute-start.20 = (bf16[144,384]{1,0:T(8,128)(2,1)S(1)}, bf16[144,384]{1,0:T(8,128)(2,1)S(1)}, u32[]{:S(2)}, u32[]{:S(2)}) collective-permute-start(bf16[144,384]{1,0:T(8,128)(2,1)S(1)} %collective-permute-done.13.refs_1_), channel_id=1, source_target_pairs={{0,2},{1,3},{2,0},{3,1},{4,6},{5,7},{6,4},{7,5},{8,10},{9,11},{10,... | collective-permute-start | bytes 331784 | tf_op jit(solution)/shard_map/ppermute | solution.py:290
  48.1 2.5 %collective-permute-start.15 = (bf16[144,384]{1,0:T(8,128)(2,1)S(1)}, bf16[144,384]{1,0:T(8,128)(2,1)S(1)}, u32[]{:S(2)}, u32[]{:S(2)}) collective-permute-start(bf16[144,384]{1,0:T(8,128)(2,1)S(1)} %collective-permute-done.10.refs_0_), channel_id=1, source_target_pairs={{0,1},{1,0},{2,3},{3,2},{4,5},{5,4},{6,7},{7,6},{8,9},{9,8},{10,11... | collective-permute-start | bytes 331784 | tf_op jit(solution)/shard_map/ppermute | solution.py:290
  48.1 3.0 %collective-permute-start.16 = (bf16[144,384]{1,0:T(8,128)(2,1)S(1)}, bf16[144,384]{1,0:T(8,128)(2,1)S(1)}, u32[]{:S(2)}, u32[]{:S(2)}) collective-permute-start(bf16[144,384]{1,0:T(8,128)(2,1)S(1)} %collective-permute-done.11.refs_1_), channel_id=1, source_target_pairs={{0,1},{1,0},{2,3},{3,2},{4,5},{5,4},{6,7},{7,6},{8,9},{9,8},{10,11... | collective-permute-start | bytes 331784 | tf_op jit(solution)/shard_map/ppermute | solution.py:290
  48.7 3.2 %collective-permute-start.17 = (bf16[144,384]{1,0:T(8,128)(2,1)S(1)}, bf16[144,384]{1,0:T(8,128)(2,1)S(1)}, u32[]{:S(2)}, u32[]{:S(2)}) collective-permute-start(bf16[144,384]{1,0:T(8,128)(2,1)S(1)} %collective-permute-done.12.refs_0_), channel_id=1, source_target_pairs={{0,1},{1,0},{2,3},{3,2},{4,5},{5,4},{6,7},{7,6},{8,9},{9,8},{10,11... | collective-permute-start | bytes 331784 | tf_op jit(solution)/shard_map/ppermute | solution.py:290
  49.9 2.0 %collective-permute-start.18 = (bf16[144,384]{1,0:T(8,128)(2,1)S(1)}, bf16[144,384]{1,0:T(8,128)(2,1)S(1)}, u32[]{:S(2)}, u32[]{:S(2)}) collective-permute-start(bf16[144,384]{1,0:T(8,128)(2,1)S(1)} %collective-permute-done.13.refs_1_), channel_id=1, source_target_pairs={{0,1},{1,0},{2,3},{3,2},{4,5},{5,4},{6,7},{7,6},{8,9},{9,8},{10,11... | collective-permute-start | bytes 331784 | tf_op jit(solution)/shard_map/ppermute | solution.py:290
  50.7 2.0 %collective-permute-start.21 = (bf16[144,384]{1,0:T(8,128)(2,1)S(1)}, bf16[144,384]{1,0:T(8,128)(2,1)S(1)}, u32[]{:S(2)}, u32[]{:S(2)}) collective-permute-start(bf16[144,384]{1,0:T(8,128)(2,1)S(1)} %collective-permute-done.19.refs_3_), channel_id=1, source_target_pairs={{0,1},{1,0},{2,3},{3,2},{4,5},{5,4},{6,7},{7,6},{8,9},{9,8},{10,11... | collective-permute-start | bytes 331784 | tf_op jit(solution)/shard_map/ppermute | solution.py:290
  50.7 2.0 %collective-permute-start.22 = (bf16[144,384]{1,0:T(8,128)(2,1)S(1)}, bf16[144,384]{1,0:T(8,128)(2,1)S(1)}, u32[]{:S(2)}, u32[]{:S(2)}) collective-permute-start(bf16[144,384]{1,0:T(8,128)(2,1)S(1)} %collective-permute-done.20.refs_4_), channel_id=1, source_target_pairs={{0,1},{1,0},{2,3},{3,2},{4,5},{5,4},{6,7},{7,6},{8,9},{9,8},{10,11... | collective-permute-start | bytes 331784 | tf_op jit(solution)/shard_map/ppermute | solution.py:290

commit v5 on v4

--- a/solution.py
+++ b/solution.py
@@ -98,10 +98,10 @@
         up_g = both_sum[:, hidden:].astype(BF16)
         down_g = (-down_sum).astype(BF16)
         slot = own ^ head
-        keep_ref[slot, :head_dim] = jnp.where(even, gate_g, down_g)
-        give_ref[slot, :head_dim] = jnp.where(even, down_g, gate_g)
-        keep_ref[slot, head_dim:] = jnp.where(even, up_g[:half], up_g[half:])
-        give_ref[slot, head_dim:] = jnp.where(even, up_g[half:], up_g[:half])
+        keep_ref[slot, half:] = jnp.where(even, gate_g, down_g)
+        give_ref[slot, half:] = jnp.where(even, down_g, gate_g)
+        keep_ref[slot, :half] = jnp.where(even, up_g[:half], up_g[half:])
+        give_ref[slot, :half] = jnp.where(even, up_g[half:], up_g[:half])
 
 
 def gradients(view_kind, tokens, qkv_weight, w_gate, w_up, w_down_t):
@@ -175,14 +175,9 @@
         out_ref[...] = (keep_ref[slot, part].astype(F32) + got_ref[slot, part].astype(F32)).astype(BF16)
 
 
-def plane_sum_kernel(*refs):
-    *parts, main_ref, up_ref = refs
-    main = main_ref.shape[0]
-    count = len(parts) // 2
-    total = [sum(part[...].astype(F32) for part in parts[start : start + count]).astype(BF16) for start in (0, count)]
-    total = jnp.concatenate(total, axis=0)
-    main_ref[...] = total[:main]
-    up_ref[...] = total[main:]
+def up_sum_kernel(mine_ref, other_ref, out_ref):
+    half = out_ref.shape[0]
+    out_ref[...] = (mine_ref[:half].astype(F32) + other_ref[:half].astype(F32)).astype(BF16)
 
 
 def sum_kernel(*refs):
@@ -205,13 +200,17 @@
     return [(base - step_size * x.astype(F32)).astype(BF16) for base, x in zip(bases, iterates)]
 
 
-def newton_kernel(heads, mine_ref, other_ref, half_ref, got_ref, base_ref, base_up_ref, out_ref, *part_refs):
-    head_dim, half = mine_ref.shape[0], half_ref.shape[0]
+def newton_kernel(
+    heads, first_ref, first_other_ref, second_ref, second_other_ref, half_ref, got_ref, base_ref, base_up_ref, out_ref, *part_refs
+):
+    half = half_ref.shape[0]
     even = position(heads)[1] == 0
     a, b = half_ref[...], got_ref[...]
     upper = jnp.concatenate([jnp.where(even, a, b), jnp.where(even, b, a)], axis=0).astype(F32)
-    main, upper = stepped((mine_ref[...].astype(F32) + other_ref[...].astype(F32), upper), (base_ref[...], base_up_ref[...]))
-    whole = jnp.concatenate([main, jnp.where(even, upper[:half], upper[half:])], axis=0)
+    first = first_ref[half:].astype(F32) + first_other_ref[half:].astype(F32)
+    second = second_ref[...].astype(F32) + second_other_ref[...].astype(F32)
+    main, upper = stepped((jnp.concatenate([first, second], axis=0), upper), (base_ref[...], base_up_ref[...]))
+    whole = jnp.concatenate([jnp.where(even, upper[:half], upper[half:]), main], axis=0)
     out_ref[...] = whole
     rows = whole.shape[0] // len(part_refs)
     for index, part_ref in enumerate(part_refs):
@@ -222,11 +221,12 @@
     head_dim = q.shape[1]
     here, there = (jnp.concatenate([ref[...] for ref in refs], axis=0) for refs in (here, there))
     a, b = jnp.where(even, here, there), jnp.where(even, there, here)
-    up_b = jnp.concatenate([a[head_dim:], b[head_dim:]], axis=0)
-    gate = mm(q, a[:head_dim], NN)
+    half = head_dim // 2
+    up_b = jnp.concatenate([a[:half], b[:half]], axis=0)
+    gate = mm(q, a[half:], NN)
     upper = mm(q, up_b, NN)
     hidden = (gate * jax.nn.sigmoid(gate) * upper).astype(BF16)
-    return mm(hidden, b[:head_dim], NT).astype(BF16)
+    return mm(hidden, b[half:], NT).astype(BF16)
 
 
 def apply_kernel(far, q_ref, *refs):
@@ -299,8 +299,8 @@
     first_in, second_in = exchange(first[1], 2), exchange(second[2], 4)
     first_on = exchange(small(sum_kernel, part_block, (first[2], first_on), 6 * size, "pass_sum"), 4)
     second_on = exchange(small(sum_kernel, part_block, (second[1], second_on), 6 * size, "pass_sum"), 2)
-    parts = (first[0], first_in, first_on, second[0], second_in, second_on)
-    main, upper = small(plane_sum_kernel, [main_block, half_block], parts, 10 * size, "plane_sum")
+    first = small(sum_kernel, part_block, (first[0], first_in, first_on), 8 * size, "plane_sum")
+    second = small(sum_kernel, part_block, (second[0], second_in, second_on), 8 * size, "plane_sum")
     query = project_query(tokens, qkv_weight, heads)
     base = jnp.where(core == 0, lax.dynamic_index_in_dim(w_gate, own, 0, False), lax.dynamic_index_in_dim(w_down_t, own, 0, False))
     base_up = lax.dynamic_index_in_dim(w_up, own, 0, False)
@@ -312,14 +312,13 @@
             bits *= 2
         return total, exchange(total, bits)
 
-    upper, upper_other = over_line(upper, "line_sum_up")
-    upper_other, query, base, base_up = lax.optimization_barrier((upper_other, query, base, base_up))
-    main, main_other = over_line(main, "line_sum")
-    upper = small(sum_kernel, half_block, (upper, upper_other), 10 * size, "up_sum")
-    upper_got = exchange(upper, 1)
-    fresh, first, second = small(
-        functools.partial(newton_kernel, heads), [block, part_block, part_block], (main, main_other, upper, upper_got, base, base_up), 30 * size, "newton"
-    )
+    first, first_other = over_line(first, "line_sum")
+    second, second_other = over_line(second, "line_sum")
+    first_other, query, base, base_up = lax.optimization_barrier((first_other, query, base, base_up))
+    upper = small(up_sum_kernel, half_block, (first, first_other), 6 * size, "up_sum")
+    args = (first, first_other, second, second_other, upper, exchange(upper, 1), base, base_up)
+    kernel = functools.partial(newton_kernel, heads)
+    fresh, first, second = small(kernel, [block, part_block, part_block], args, 30 * size, "newton")
 
     def apply(far, *args):
         return small(functools.partial(apply_kernel, far), shape(rows, head_dim), (query, *args), 20 * rows * head_dim, "apply")

time: 54.5 us -> 53.3 us (0.978)
  waiting for transfers between devices: 16.7 us -> 15 us
  starting transfers between devices: 19.2 us -> 19.8 us
    ppermute x23, waiting for transfers between devices: 16.7 us -> 15 us  [exchange(): return lax.ppermute(x, 'tok', [(i, i ^ bits) for i in range(groups)])]
    pallas_call x9 -> x10, Pallas kernels: 5.56 us -> 5.55 us  [small(): pl.pallas_call(kernel, out_shape=shapes, in_specs=specs, compiler_params=...]
  transfers between devices with their start and end apart: 23 -> 23, of which waited for: 12 -> 10; matrix products, arithmetic and copies ran while one was open for 2% -> 2% of each run, Pallas kernels for 8% -> 9%
where the time goes in v5:
time: 53.3 us; the launch traced here: 53.2 us
  starting transfers between devices  19.8 us (37%)
  Pallas kernels  17.1 us (32%)
  waiting for transfers between devices  15 us (28%)
  other arithmetic  1.19 us (2%)
    ppermute x23, starting transfers between devices, exchange(): return lax.ppermute(x, 'tok', [(i, i ^ bits) for i in range(groups)])  19.8 us
    ppermute x23, waiting for transfers between devices, exchange(): return lax.ppermute(x, 'tok', [(i, i ^ bits) for i in range(groups)])  15 us
    pallas_call x1, Pallas kernels, gradients(): pl.pallas_call(grad_kernel, out_shape=[shape] * 2, in_specs=[pl.BlockSpec...  7.45 us
    pallas_call x10, Pallas kernels, small(): pl.pallas_call(kernel, out_shape=shapes, in_specs=specs, compiler_params=...  5.55 us
    pallas_call x1, Pallas kernels, project_query(): pl.pallas_call(query_kernel, out_shape=pltpu.VMEM((heads, rows, width //...  2.36 us
    pallas_call x1, Pallas kernels, finish(): pl.pallas_call(finish_kernel, out_shape=jax.ShapeDtypeStruct((rows, heads...  1.71 us
    select_n x1, other arithmetic, shards(): jnp.where(core == 0, lax.dynamic_index_in_dim(w_gate, own, 0, False), lax...  1.19 us
  transfers between devices with their start and end apart: 23, of which 10 were waited for; matrix products, arithmetic and copies ran while one was open for 2% of the time, Pallas kernels for 9%

profile of v5, /device:TPU:0, one launch (start us, length us, event | category | flops | bytes accessed | tf_op | source)
XLA Modules:
  0.0 53.2 jit_solution(1635393867055911709)
XLA Ops:
  0.0 7.5 %gradients.1 = (bf16[4,288,384]{2,1,0:T(8,128)(2,1)S(1)}, bf16[4,288,384]{2,1,0:T(8,128)(2,1)S(1)}) custom-call(s32[16]{0:T(128)} %view_hbm.1, bf16[512,768]{1,0:T(8,128)(2,1)} %tokens_ref.1, bf16[768,2304]{1,0:T(8,128)(2,1)} %weight_ref.1, f32[4,192,384]{2,1,0:T(8,128)} %gate_hbm.1, f32[4,192,384]{2,1,0:T(8,128)} %up_hbm.1, f32[4,192,384]{2,1,0:T(8,128)} %bitcast.9), custom_call_target="tpu_custom_call" | custom-call | flops 3019898880 | bytes 6684672 | tf_op jit(solution)/shard_map/gradients/pallas_call | solution.py:112
  7.5 0.5 collective-permute-start
  8.0 2.1 %collective-permute-done.got_ref = bf16[4,288,384]{2,1,0:T(8,128)(2,1)S(1)} collective-permute-done((bf16[4,288,384]{2,1,0:T(8,128)(2,1)S(1)}, bf16[4,288,384]{2,1,0:T(8,128)(2,1)S(1)}, u32[]{:S(2)}, u32[]{:S(2)}) %collective-permute-start) | collective-permute-done | bytes 884768 | tf_op jit(solution)/shard_map/ppermute | solution.py:290
  10.2 3.0 %collective-permute-start.2 = (bf16[144,384]{1,0:T(8,128)(2,1)S(1)}, bf16[144,384]{1,0:T(8,128)(2,1)S(1)}, u32[]{:S(2)}, u32[]{:S(2)}) collective-permute-start(bf16[144,384]{1,0:T(8,128)(2,1)S(1)} %get-tuple-element.32), channel_id=1, source_target_pairs={{0,2},{1,3},{2,0},{3,1},{4,6},{5,7},{6,4},{7,5},{8,10},{9,11},{10,... | collective-permute-start | bytes 331784 | tf_op jit(solution)/shard_map/ppermute | solution.py:290
  13.2 1.6 %collective-permute-start.6 = (bf16[144,384]{1,0:T(8,128)(2,1)S(1)}, bf16[144,384]{1,0:T(8,128)(2,1)S(1)}, u32[]{:S(2)}, u32[]{:S(2)}) collective-permute-start(bf16[144,384]{1,0:T(8,128)(2,1)S(1)} %get-tuple-element.38), channel_id=1, source_target_pairs={{0,4},{1,5},{2,6},{3,7},{4,0},{5,1},{6,2},{7,3},{8,12},{9,13},{10,... | collective-permute-start | bytes 331784 | tf_op jit(solution)/shard_map/ppermute | solution.py:290
  14.8 0.5 collective-permute-start.1
  15.3 1.3 %collective-permute-done.2.refs_1_ = bf16[144,384]{1,0:T(8,128)(2,1)S(1)} collective-permute-done((bf16[144,384]{1,0:T(8,128)(2,1)S(1)}, bf16[144,384]{1,0:T(8,128)(2,1)S(1)}, u32[]{:S(2)}, u32[]{:S(2)}) %collective-permute-start.2) | collective-permute-done | bytes 110624 | tf_op jit(solution)/shard_map/ppermute | solution.py:290
  16.7 2.6 %collective-permute-start.3 = (bf16[144,384]{1,0:T(8,128)(2,1)S(1)}, bf16[144,384]{1,0:T(8,128)(2,1)S(1)}, u32[]{:S(2)}, u32[]{:S(2)}) collective-permute-start(bf16[144,384]{1,0:T(8,128)(2,1)S(1)} %pass_sum.2), channel_id=1, source_target_pairs={{0,4},{1,5},{2,6},{3,7},{4,0},{5,1},{6,2},{7,3},{8,12},{9,13},{10,... | collective-permute-start | bytes 331784 | tf_op jit(solution)/shard_map/ppermute | solution.py:290
  19.4 1.9 %collective-permute-start.7 = (bf16[144,384]{1,0:T(8,128)(2,1)S(1)}, bf16[144,384]{1,0:T(8,128)(2,1)S(1)}, u32[]{:S(2)}, u32[]{:S(2)}) collective-permute-start(bf16[144,384]{1,0:T(8,128)(2,1)S(1)} %pass_sum.3), channel_id=1, source_target_pairs={{0,2},{1,3},{2,0},{3,1},{4,6},{5,7},{6,4},{7,5},{8,10},{9,11},{10,... | collective-permute-start | bytes 331784 | tf_op jit(solution)/shard_map/ppermute | solution.py:290
  21.3 1.1 %collective-permute-done.3.refs_2_ = bf16[144,384]{1,0:T(8,128)(2,1)S(1)} collective-permute-done((bf16[144,384]{1,0:T(8,128)(2,1)S(1)}, bf16[144,384]{1,0:T(8,128)(2,1)S(1)}, u32[]{:S(2)}, u32[]{:S(2)}) %collective-permute-start.3) | collective-permute-done | bytes 110624 | tf_op jit(solution)/shard_map/ppermute | solution.py:290
  22.5 2.7 %collective-permute-start.4 = (bf16[144,384]{1,0:T(8,128)(2,1)S(1)}, bf16[144,384]{1,0:T(8,128)(2,1)S(1)}, u32[]{:S(2)}, u32[]{:S(2)}) collective-permute-start(bf16[144,384]{1,0:T(8,128)(2,1)S(1)} %plane_sum.2.mine_ref.first_ref), channel_id=1, source_target_pairs={{0,8},{1,9},{2,10},{3,11},{4,12},{5,13},{6,14},{7,15},{8,0},{9,1},... | collective-permute-start | bytes 331784 | tf_op jit(solution)/shard_map/ppermute | solution.py:290
  25.2 1.2 %fusion = (f32[192,384]{1,0:T(8,128)S(1)}, f32[192,384]{1,0:T(8,128)S(1)}) fusion(f32[4,384,192]{1,2,0:T(8,128)} %param.10, s32[]{:T(128)S(6)} %select_n.18, f32[4,192,384]{2,1,0:T(8,128)} %gate_hbm.1, pred[]{:T(512)S(6)} %eq.3, f32[4,192,384]{2,1,0:T(8,128)} %up_hbm.1), kind=kLoop, calls=%fused_computation.1 | loop fusion | flops 73728 | bytes 1474565 | tf_op jit(solution)/shard_map/jit(_where)/select_n | solution.py:305
  26.4 1.1 %collective-permute-start.8 = (bf16[144,384]{1,0:T(8,128)(2,1)S(1)}, bf16[144,384]{1,0:T(8,128)(2,1)S(1)}, u32[]{:S(2)}, u32[]{:S(2)}) collective-permute-start(bf16[144,384]{1,0:T(8,128)(2,1)S(1)} %plane_sum.3.second_ref), channel_id=1, source_target_pairs={{0,8},{1,9},{2,10},{3,11},{4,12},{5,13},{6,14},{7,15},{8,0},{9,1},... | collective-permute-start | bytes 331784 | tf_op jit(solution)/shard_map/ppermute | solution.py:290
  27.5 2.4 %query.1.q_ref = bf16[4,512,192]{2,1,0:T(8,128)(2,1)S(1)} custom-call(bf16[512,768]{1,0:T(8,128)(2,1)} %tokens_ref.1, bf16[768,2304]{1,0:T(8,128)(2,1)} %weight_ref.1), custom_call_target="tpu_custom_call" | custom-call | flops 603979776 | bytes 3932160 | tf_op jit(solution)/shard_map/query/pallas_call | solution.py:159
  29.9 1.9 %collective-permute-done.4.other_ref.first_other_ref = bf16[144,384]{1,0:T(8,128)(2,1)S(1)} collective-permute-done((bf16[144,384]{1,0:T(8,128)(2,1)S(1)}, bf16[144,384]{1,0:T(8,128)(2,1)S(1)}, u32[]{:S(2)}, u32[]{:S(2)}) %collective-permute-start.4) | collective-permute-done | bytes 110624 | tf_op jit(solution)/shard_map/ppermute | solution.py:290
  31.9 2.3 %collective-permute-done.8.second_other_ref = bf16[144,384]{1,0:T(8,128)(2,1)S(1)} collective-permute-done((bf16[144,384]{1,0:T(8,128)(2,1)S(1)}, bf16[144,384]{1,0:T(8,128)(2,1)S(1)}, u32[]{:S(2)}, u32[]{:S(2)}) %collective-permute-start.8) | collective-permute-done | bytes 110624 | tf_op jit(solution)/shard_map/ppermute | solution.py:290
  34.1 3.1 %newton.1 = (bf16[288,384]{1,0:T(8,128)(2,1)S(1)}, bf16[144,384]{1,0:T(8,128)(2,1)S(1)}, bf16[144,384]{1,0:T(8,128)(2,1)S(1)}) custom-call(bf16[144,384]{1,0:T(8,128)(2,1)S(1)} %plane_sum.2.mine_ref.first_ref, bf16[144,384]{1,0:T(8,128)(2,1)S(1)} %collective-permute-done.4.other_ref.first_other_ref, bf16[144,384]{1,0:T(8,128)(2,1)S(1)} %plane_sum.3.second_ref, ...), custom_call_target="tpu_custom_call" | custom-call | bytes 2211840 | tf_op jit(solution)/shard_map/newton/pallas_call | solution.py:140
  37.3 1.6 %collective-permute-start.10 = (bf16[144,384]{1,0:T(8,128)(2,1)S(1)}, bf16[144,384]{1,0:T(8,128)(2,1)S(1)}, u32[]{:S(2)}, u32[]{:S(2)}) collective-permute-start(bf16[144,384]{1,0:T(8,128)(2,1)S(1)} %get-tuple-element.41), channel_id=1, source_target_pairs={{0,2},{1,3},{2,0},{3,1},{4,6},{5,7},{6,4},{7,5},{8,10},{9,11},{10,... | collective-permute-start | bytes 331784 | tf_op jit(solution)/shard_map/ppermute | solution.py:290
  38.9 0.5 collective-permute-start.11
  39.4 2.0 %collective-permute-start.12 = (bf16[144,384]{1,0:T(8,128)(2,1)S(1)}, bf16[144,384]{1,0:T(8,128)(2,1)S(1)}, u32[]{:S(2)}, u32[]{:S(2)}) collective-permute-start(bf16[144,384]{1,0:T(8,128)(2,1)S(1)} %get-tuple-element.41), channel_id=1, source_target_pairs={{0,4},{1,5},{2,6},{3,7},{4,0},{5,1},{6,2},{7,3},{8,12},{9,13},{10,... | collective-permute-start | bytes 331784 | tf_op jit(solution)/shard_map/ppermute | solution.py:290
  41.4 1.8 %collective-permute-done.10.refs_0_ = bf16[144,384]{1,0:T(8,128)(2,1)S(1)} collective-permute-done((bf16[144,384]{1,0:T(8,128)(2,1)S(1)}, bf16[144,384]{1,0:T(8,128)(2,1)S(1)}, u32[]{:S(2)}, u32[]{:S(2)}) %collective-permute-start.10) | collective-permute-done | bytes 110624 | tf_op jit(solution)/shard_map/ppermute | solution.py:290
  43.2 1.5 %collective-permute-done.13.refs_1_ = bf16[144,384]{1,0:T(8,128)(2,1)S(1)} collective-permute-done((bf16[144,384]{1,0:T(8,128)(2,1)S(1)}, bf16[144,384]{1,0:T(8,128)(2,1)S(1)}, u32[]{:S(2)}, u32[]{:S(2)}) %collective-permute-start.13) | collective-permute-done | bytes 110624 | tf_op jit(solution)/shard_map/ppermute | solution.py:290
  44.8 0.5 collective-permute-start.20
  45.3 0.7 %apply.3.refs_0_ = bf16[512,192]{1,0:T(8,128)(2,1)S(1)} custom-call(bf16[4,512,192]{2,1,0:T(8,128)(2,1)S(1)} %query.1.q_ref, bf16[288,384]{1,0:T(8,128)(2,1)S(1)} %get-tuple-element.43.refs_0_, bf16[288,384]{1,0:T(8,128)(2,1)S(1)} %collective-permute-done.14.refs_1_), custom_call_target="tpu_custom_call" | custom-call | bytes 1966080 | tf_op jit(solution)/shard_map/apply/pallas_call | solution.py:140
  46.0 1.1 %collective-permute-done.12.refs_0_ = bf16[144,384]{1,0:T(8,128)(2,1)S(1)} collective-permute-done((bf16[144,384]{1,0:T(8,128)(2,1)S(1)}, bf16[144,384]{1,0:T(8,128)(2,1)S(1)}, u32[]{:S(2)}, u32[]{:S(2)}) %collective-permute-start.12) | collective-permute-done | bytes 110624 | tf_op jit(solution)/shard_map/ppermute | solution.py:290
  47.1 0.5 collective-permute-start.16
  47.6 1.1 %collective-permute-done.19.refs_3_ = bf16[144,384]{1,0:T(8,128)(2,1)S(1)} collective-permute-done((bf16[144,384]{1,0:T(8,128)(2,1)S(1)}, bf16[144,384]{1,0:T(8,128)(2,1)S(1)}, u32[]{:S(2)}, u32[]{:S(2)}) %collective-permute-start.19) | collective-permute-done | bytes 110624 | tf_op jit(solution)/shard_map/ppermute | solution.py:290
  48.7 0.8 %collective-permute-done.20.refs_4_ = bf16[144,384]{1,0:T(8,128)(2,1)S(1)} collective-permute-done((bf16[144,384]{1,0:T(8,128)(2,1)S(1)}, bf16[144,384]{1,0:T(8,128)(2,1)S(1)}, u32[]{:S(2)}, u32[]{:S(2)}) %collective-permute-start.20) | collective-permute-done | bytes 110624 | tf_op jit(solution)/shard_map/ppermute | solution.py:290
  49.5 0.5 collective-permute-start.22
  50.0 0.7 %apply.4.refs_1_ = bf16[512,192]{1,0:T(8,128)(2,1)S(1)} custom-call(bf16[4,512,192]{2,1,0:T(8,128)(2,1)S(1)} %query.1.q_ref, bf16[144,384]{1,0:T(8,128)(2,1)S(1)} %collective-permute-done.10.refs_0_, bf16[144,384]{1,0:T(8,128)(2,1)S(1)} %collective-permute-done.11.refs_1_, bf16[144,384]{1,0:T(8,128)(2,1)S(1)} %collective-permute-done.15.refs_2_, ...), custom_call_target="tpu_custom_call" | custom-call | bytes 1966080 | tf_op jit(solution)/shard_map/apply/pallas_call | solution.py:140
  50.8 0.7 %apply.5.refs_2_ = bf16[512,192]{1,0:T(8,128)(2,1)S(1)} custom-call(bf16[4,512,192]{2,1,0:T(8,128)(2,1)S(1)} %query.1.q_ref, bf16[144,384]{1,0:T(8,128)(2,1)S(1)} %collective-permute-done.12.refs_0_, bf16[144,384]{1,0:T(8,128)(2,1)S(1)} %collective-permute-done.13.refs_1_, bf16[144,384]{1,0:T(8,128)(2,1)S(1)} %collective-permute-done.17.refs_2_, ...), custom_call_target="tpu_custom_call" | custom-call | bytes 1966080 | tf_op jit(solution)/shard_map/apply/pallas_call | solution.py:140
  51.5 1.7 %finish.1 = bf16[512,768]{1,0:T(8,128)(2,1)} custom-call(bf16[4,512,192]{2,1,0:T(8,128)(2,1)S(1)} %query.1.q_ref, bf16[512,192]{1,0:T(8,128)(2,1)S(1)} %apply.3.refs_0_, bf16[512,192]{1,0:T(8,128)(2,1)S(1)} %apply.4.refs_1_, bf16[512,192]{1,0:T(8,128)(2,1)S(1)} %apply.5.refs_2_, bf16[144,384]{1,0:T(8,128)(2,1)S(1)} %collective-permute-done.19.refs_3_, ...), custom_call_target="tpu_custom_call" | custom-call | tf_op jit(solution)/shard_map/finish/pallas_call | solution.py:262
  (28 shorter events, 0.7 us)
Async XLA Ops:
  7.5 2.6 %collective-permute-start = (bf16[4,288,384]{2,1,0:T(8,128)(2,1)S(1)}, bf16[4,288,384]{2,1,0:T(8,128)(2,1)S(1)}, u32[]{:S(2)}, u32[]{:S(2)}) collective-permute-start(bf16[4,288,384]{2,1,0:T(8,128)(2,1)S(1)} %get-tuple-element.28), channel_id=1, source_target_pairs={{0,1},{1,0},{2,3},{3,2},{4,5},{5,4},{6,7},{7,6},{8,9},{9,8},{10,11... | collective-permute-start | bytes 2654216 | tf_op jit(solution)/shard_map/ppermute | solution.py:290
  10.2 6.4 %collective-permute-start.2 = (bf16[144,384]{1,0:T(8,128)(2,1)S(1)}, bf16[144,384]{1,0:T(8,128)(2,1)S(1)}, u32[]{:S(2)}, u32[]{:S(2)}) collective-permute-start(bf16[144,384]{1,0:T(8,128)(2,1)S(1)} %get-tuple-element.32), channel_id=1, source_target_pairs={{0,2},{1,3},{2,0},{3,1},{4,6},{5,7},{6,4},{7,5},{8,10},{9,11},{10,... | collective-permute-start | bytes 331784 | tf_op jit(solution)/shard_map/ppermute | solution.py:290
  13.2 6.2 %collective-permute-start.6 = (bf16[144,384]{1,0:T(8,128)(2,1)S(1)}, bf16[144,384]{1,0:T(8,128)(2,1)S(1)}, u32[]{:S(2)}, u32[]{:S(2)}) collective-permute-start(bf16[144,384]{1,0:T(8,128)(2,1)S(1)} %get-tuple-element.38), channel_id=1, source_target_pairs={{0,4},{1,5},{2,6},{3,7},{4,0},{5,1},{6,2},{7,3},{8,12},{9,13},{10,... | collective-permute-start | bytes 331784 | tf_op jit(solution)/shard_map/ppermute | solution.py:290
  14.8 6.5 %collective-permute-start.1 = (bf16[144,384]{1,0:T(8,128)(2,1)S(1)}, bf16[144,384]{1,0:T(8,128)(2,1)S(1)}, u32[]{:S(2)}, u32[]{:S(2)}) collective-permute-start(bf16[144,384]{1,0:T(8,128)(2,1)S(1)} %get-tuple-element.30), channel_id=1, source_target_pairs={{0,2},{1,3},{2,0},{3,1},{4,6},{5,7},{6,4},{7,5},{8,10},{9,11},{10,... | collective-permute-start | bytes 331784 | tf_op jit(solution)/shard_map/ppermute | solution.py:290
  16.7 5.8 %collective-permute-start.3 = (bf16[144,384]{1,0:T(8,128)(2,1)S(1)}, bf16[144,384]{1,0:T(8,128)(2,1)S(1)}, u32[]{:S(2)}, u32[]{:S(2)}) collective-permute-start(bf16[144,384]{1,0:T(8,128)(2,1)S(1)} %pass_sum.2), channel_id=1, source_target_pairs={{0,4},{1,5},{2,6},{3,7},{4,0},{5,1},{6,2},{7,3},{8,12},{9,13},{10,... | collective-permute-start | bytes 331784 | tf_op jit(solution)/shard_map/ppermute | solution.py:290
  19.3 7.1 %collective-permute-start.5 = (bf16[144,384]{1,0:T(8,128)(2,1)S(1)}, bf16[144,384]{1,0:T(8,128)(2,1)S(1)}, u32[]{:S(2)}, u32[]{:S(2)}) collective-permute-start(bf16[144,384]{1,0:T(8,128)(2,1)S(1)} %get-tuple-element.36), channel_id=1, source_target_pairs={{0,4},{1,5},{2,6},{3,7},{4,0},{5,1},{6,2},{7,3},{8,12},{9,13},{10,... | collective-permute-start | bytes 331784 | tf_op jit(solution)/shard_map/ppermute | solution.py:290
  19.4 7.0 %collective-permute-start.7 = (bf16[144,384]{1,0:T(8,128)(2,1)S(1)}, bf16[144,384]{1,0:T(8,128)(2,1)S(1)}, u32[]{:S(2)}, u32[]{:S(2)}) collective-permute-start(bf16[144,384]{1,0:T(8,128)(2,1)S(1)} %pass_sum.3), channel_id=1, source_target_pairs={{0,2},{1,3},{2,0},{3,1},{4,6},{5,7},{6,4},{7,5},{8,10},{9,11},{10,... | collective-permute-start | bytes 331784 | tf_op jit(solution)/shard_map/ppermute | solution.py:290
  22.5 9.3 %collective-permute-start.4 = (bf16[144,384]{1,0:T(8,128)(2,1)S(1)}, bf16[144,384]{1,0:T(8,128)(2,1)S(1)}, u32[]{:S(2)}, u32[]{:S(2)}) collective-permute-start(bf16[144,384]{1,0:T(8,128)(2,1)S(1)} %plane_sum.2.mine_ref.first_ref), channel_id=1, source_target_pairs={{0,8},{1,9},{2,10},{3,11},{4,12},{5,13},{6,14},{7,15},{8,0},{9,1},... | collective-permute-start | bytes 331784 | tf_op jit(solution)/shard_map/ppermute | solution.py:290
  26.4 7.7 %collective-permute-start.8 = (bf16[144,384]{1,0:T(8,128)(2,1)S(1)}, bf16[144,384]{1,0:T(8,128)(2,1)S(1)}, u32[]{:S(2)}, u32[]{:S(2)}) collective-permute-start(bf16[144,384]{1,0:T(8,128)(2,1)S(1)} %plane_sum.3.second_ref), channel_id=1, source_target_pairs={{0,8},{1,9},{2,10},{3,11},{4,12},{5,13},{6,14},{7,15},{8,0},{9,1},... | collective-permute-start | bytes 331784 | tf_op jit(solution)/shard_map/ppermute | solution.py:290
  31.8 2.4 %collective-permute-start.9 = (bf16[96,384]{1,0:T(8,128)(2,1)S(1)}, bf16[96,384]{1,0:T(8,128)(2,1)S(1)}, u32[]{:S(2)}, u32[]{:S(2)}) collective-permute-start(bf16[96,384]{1,0:T(8,128)(2,1)S(1)} %up_sum.1.half_ref), channel_id=1, source_target_pairs={{0,1},{1,0},{2,3},{3,2},{4,5},{5,4},{6,7},{7,6},{8,9},{9,8},{10,11... | collective-permute-start | bytes 221192 | tf_op jit(solution)/shard_map/ppermute | solution.py:290
  37.2 8.1 %collective-permute-start.14 = (bf16[288,384]{1,0:T(8,128)(2,1)S(1)}, bf16[288,384]{1,0:T(8,128)(2,1)S(1)}, u32[]{:S(2)}, u32[]{:S(2)}) collective-permute-start(bf16[288,384]{1,0:T(8,128)(2,1)S(1)} %get-tuple-element.43.refs_0_), channel_id=1, source_target_pairs={{0,1},{1,0},{2,3},{3,2},{4,5},{5,4},{6,7},{7,6},{8,9},{9,8},{10,11... | collective-permute-start | bytes 663560 | tf_op jit(solution)/shard_map/ppermute | solution.py:290
  37.3 5.9 %collective-permute-start.10 = (bf16[144,384]{1,0:T(8,128)(2,1)S(1)}, bf16[144,384]{1,0:T(8,128)(2,1)S(1)}, u32[]{:S(2)}, u32[]{:S(2)}) collective-permute-start(bf16[144,384]{1,0:T(8,128)(2,1)S(1)} %get-tuple-element.41), channel_id=1, source_target_pairs={{0,2},{1,3},{2,0},{3,1},{4,6},{5,7},{6,4},{7,5},{8,10},{9,11},{10,... | collective-permute-start | bytes 331784 | tf_op jit(solution)/shard_map/ppermute | solution.py:290
  38.9 5.9 %collective-permute-start.13 = (bf16[144,384]{1,0:T(8,128)(2,1)S(1)}, bf16[144,384]{1,0:T(8,128)(2,1)S(1)}, u32[]{:S(2)}, u32[]{:S(2)}) collective-permute-start(bf16[144,384]{1,0:T(8,128)(2,1)S(1)} %get-tuple-element.42), channel_id=1, source_target_pairs={{0,4},{1,5},{2,6},{3,7},{4,0},{5,1},{6,2},{7,3},{8,12},{9,13},{10,... | collective-permute-start | bytes 331784 | tf_op jit(solution)/shard_map/ppermute | solution.py:290
  38.9 7.1 %collective-permute-start.11 = (bf16[144,384]{1,0:T(8,128)(2,1)S(1)}, bf16[144,384]{1,0:T(8,128)(2,1)S(1)}, u32[]{:S(2)}, u32[]{:S(2)}) collective-permute-start(bf16[144,384]{1,0:T(8,128)(2,1)S(1)} %get-tuple-element.42), channel_id=1, source_target_pairs={{0,2},{1,3},{2,0},{3,1},{4,6},{5,7},{6,4},{7,5},{8,10},{9,11},{10,... | collective-permute-start | bytes 331784 | tf_op jit(solution)/shard_map/ppermute | solution.py:290
  39.4 7.8 %collective-permute-start.12 = (bf16[144,384]{1,0:T(8,128)(2,1)S(1)}, bf16[144,384]{1,0:T(8,128)(2,1)S(1)}, u32[]{:S(2)}, u32[]{:S(2)}) collective-permute-start(bf16[144,384]{1,0:T(8,128)(2,1)S(1)} %get-tuple-element.41), channel_id=1, source_target_pairs={{0,4},{1,5},{2,6},{3,7},{4,0},{5,1},{6,2},{7,3},{8,12},{9,13},{10,... | collective-permute-start | bytes 331784 | tf_op jit(solution)/shard_map/ppermute | solution.py:290
  43.2 5.5 %collective-permute-start.19 = (bf16[144,384]{1,0:T(8,128)(2,1)S(1)}, bf16[144,384]{1,0:T(8,128)(2,1)S(1)}, u32[]{:S(2)}, u32[]{:S(2)}) collective-permute-start(bf16[144,384]{1,0:T(8,128)(2,1)S(1)} %collective-permute-done.10.refs_0_), channel_id=1, source_target_pairs={{0,4},{1,5},{2,6},{3,7},{4,0},{5,1},{6,2},{7,3},{8,12},{9,13},{10,... | collective-permute-start | bytes 331784 | tf_op jit(solution)/shard_map/ppermute | solution.py:290
  44.8 4.7 %collective-permute-start.20 = (bf16[144,384]{1,0:T(8,128)(2,1)S(1)}, bf16[144,384]{1,0:T(8,128)(2,1)S(1)}, u32[]{:S(2)}, u32[]{:S(2)}) collective-permute-start(bf16[144,384]{1,0:T(8,128)(2,1)S(1)} %collective-permute-done.13.refs_1_), channel_id=1, source_target_pairs={{0,2},{1,3},{2,0},{3,1},{4,6},{5,7},{6,4},{7,5},{8,10},{9,11},{10,... | collective-permute-start | bytes 331784 | tf_op jit(solution)/shard_map/ppermute | solution.py:290
  47.1 2.4 %collective-permute-start.15 = (bf16[144,384]{1,0:T(8,128)(2,1)S(1)}, bf16[144,384]{1,0:T(8,128)(2,1)S(1)}, u32[]{:S(2)}, u32[]{:S(2)}) collective-permute-start(bf16[144,384]{1,0:T(8,128)(2,1)S(1)} %collective-permute-done.10.refs_0_), channel_id=1, source_target_pairs={{0,1},{1,0},{2,3},{3,2},{4,5},{5,4},{6,7},{7,6},{8,9},{9,8},{10,11... | collective-permute-start | bytes 331784 | tf_op jit(solution)/shard_map/ppermute | solution.py:290
  47.1 2.9 %collective-permute-start.16 = (bf16[144,384]{1,0:T(8,128)(2,1)S(1)}, bf16[144,384]{1,0:T(8,128)(2,1)S(1)}, u32[]{:S(2)}, u32[]{:S(2)}) collective-permute-start(bf16[144,384]{1,0:T(8,128)(2,1)S(1)} %collective-permute-done.11.refs_1_), channel_id=1, source_target_pairs={{0,1},{1,0},{2,3},{3,2},{4,5},{5,4},{6,7},{7,6},{8,9},{9,8},{10,11... | collective-permute-start | bytes 331784 | tf_op jit(solution)/shard_map/ppermute | solution.py:290
  47.6 3.1 %collective-permute-start.17 = (bf16[144,384]{1,0:T(8,128)(2,1)S(1)}, bf16[144,384]{1,0:T(8,128)(2,1)S(1)}, u32[]{:S(2)}, u32[]{:S(2)}) collective-permute-start(bf16[144,384]{1,0:T(8,128)(2,1)S(1)} %collective-permute-done.12.refs_0_), channel_id=1, source_target_pairs={{0,1},{1,0},{2,3},{3,2},{4,5},{5,4},{6,7},{7,6},{8,9},{9,8},{10,11... | collective-permute-start | bytes 331784 | tf_op jit(solution)/shard_map/ppermute | solution.py:290
  48.7 2.0 %collective-permute-start.18 = (bf16[144,384]{1,0:T(8,128)(2,1)S(1)}, bf16[144,384]{1,0:T(8,128)(2,1)S(1)}, u32[]{:S(2)}, u32[]{:S(2)}) collective-permute-start(bf16[144,384]{1,0:T(8,128)(2,1)S(1)} %collective-permute-done.13.refs_1_), channel_id=1, source_target_pairs={{0,1},{1,0},{2,3},{3,2},{4,5},{5,4},{6,7},{7,6},{8,9},{9,8},{10,11... | collective-permute-start | bytes 331784 | tf_op jit(solution)/shard_map/ppermute | solution.py:290
  49.5 1.9 %collective-permute-start.21 = (bf16[144,384]{1,0:T(8,128)(2,1)S(1)}, bf16[144,384]{1,0:T(8,128)(2,1)S(1)}, u32[]{:S(2)}, u32[]{:S(2)}) collective-permute-start(bf16[144,384]{1,0:T(8,128)(2,1)S(1)} %collective-permute-done.19.refs_3_), channel_id=1, source_target_pairs={{0,1},{1,0},{2,3},{3,2},{4,5},{5,4},{6,7},{7,6},{8,9},{9,8},{10,11... | collective-permute-start | bytes 331784 | tf_op jit(solution)/shard_map/ppermute | solution.py:290
  49.5 1.9 %collective-permute-start.22 = (bf16[144,384]{1,0:T(8,128)(2,1)S(1)}, bf16[144,384]{1,0:T(8,128)(2,1)S(1)}, u32[]{:S(2)}, u32[]{:S(2)}) collective-permute-start(bf16[144,384]{1,0:T(8,128)(2,1)S(1)} %collective-permute-done.20.refs_4_), channel_id=1, source_target_pairs={{0,1},{1,0},{2,3},{3,2},{4,5},{5,4},{6,7},{7,6},{8,9},{9,8},{10,11... | collective-permute-start | bytes 331784 | tf_op jit(solution)/shard_map/ppermute | solution.py:290

commit v6 on v5

--- a/solution.py
+++ b/solution.py
@@ -36,7 +36,7 @@
 
 
 def grad_kernel(
-    view_hbm, tok_hbm, qkv_hbm, gate_hbm, up_hbm, down_hbm, keep_ref, give_ref, view, tok, wkv, fast, kv, both_w, down_w, sems
+    view_hbm, tok_hbm, qkv_hbm, gate_hbm, up_hbm, down_hbm, first_keep_ref, second_keep_ref, first_give_ref, second_give_ref, view, tok, wkv, fast, kv, both_w, down_w, sems
 ):
     rows, width = tok.shape
     heads, head_dim = kv.shape[1], kv.shape[3]
@@ -98,22 +98,23 @@
         up_g = both_sum[:, hidden:].astype(BF16)
         down_g = (-down_sum).astype(BF16)
         slot = own ^ head
-        keep_ref[slot, half:] = jnp.where(even, gate_g, down_g)
-        give_ref[slot, half:] = jnp.where(even, down_g, gate_g)
-        keep_ref[slot, :half] = jnp.where(even, up_g[:half], up_g[half:])
-        give_ref[slot, :half] = jnp.where(even, up_g[half:], up_g[:half])
+        keep = jnp.concatenate([jnp.where(even, up_g[:half], up_g[half:]), jnp.where(even, gate_g, down_g)], axis=0)
+        give = jnp.concatenate([jnp.where(even, up_g[half:], up_g[:half]), jnp.where(even, down_g, gate_g)], axis=0)
+        cut = keep.shape[0] // 2
+        first_keep_ref[slot], second_keep_ref[slot] = keep[:cut], keep[cut:]
+        first_give_ref[slot], second_give_ref[slot] = give[:cut], give[cut:]
 
 
 def gradients(view_kind, tokens, qkv_weight, w_gate, w_up, w_down_t):
     rows, width = tokens.shape
     heads, head_dim, hidden = w_gate.shape
     args = [pltpu.with_memory_space_constraint(x, pltpu.HBM) for x in (view_kind, tokens, qkv_weight, w_gate, w_up, w_down_t)]
-    shape = pltpu.VMEM((heads, head_dim * 3 // 2, hidden), BF16)
+    shape = pltpu.VMEM((heads, head_dim * 3 // 4, hidden), BF16)
     return pl.pallas_call(
         grad_kernel,
-        out_shape=[shape] * 2,
+        out_shape=[shape] * 4,
         in_specs=[pl.BlockSpec(memory_space=pl.ANY)] * 6,
-        out_specs=[pl.BlockSpec(memory_space=pltpu.VMEM)] * 2,
+        out_specs=[pl.BlockSpec(memory_space=pltpu.VMEM)] * 4,
         scratch_shapes=[
             pltpu.SMEM(view_kind.shape, jnp.int32),
             pltpu.VMEM((rows, width), BF16),
@@ -169,10 +170,8 @@
 
 
 def pair_sum_kernel(keep_ref, got_ref, *out_refs):
-    rows = out_refs[0].shape[0]
-    for index, out_ref in enumerate(out_refs):
-        slot, part = index // 2, slice(index % 2 * rows, (index % 2 + 1) * rows)
-        out_ref[...] = (keep_ref[slot, part].astype(F32) + got_ref[slot, part].astype(F32)).astype(BF16)
+    for slot, out_ref in enumerate(out_refs):
+        out_ref[...] = (keep_ref[slot].astype(F32) + got_ref[slot].astype(F32)).astype(BF16)
 
 
 def up_sum_kernel(mine_ref, other_ref, out_ref):
@@ -289,12 +288,12 @@
     def exchange(x, bits):
         return lax.ppermute(x, "tok", [(i, i ^ bits) for i in range(groups)])
 
-    keep, give = gradients(view_kind, tokens, qkv_weight, w_gate, w_up, w_down_t)
-    got = exchange(give, 1)
-    block = shape(head_dim + half, hidden)
-    part_block = shape(block.shape[0] // 2, hidden)
-    sums = small(pair_sum_kernel, [part_block] * (2 * heads), (keep, got), 9 * keep.size, "pair_sum")
-    first, second = sums[0::2], sums[1::2]
+    first, second, first_give, second_give = gradients(view_kind, tokens, qkv_weight, w_gate, w_up, w_down_t)
+    block, part_block = shape(head_dim + half, hidden), shape((head_dim + half) // 2, hidden)
+    first, second = (
+        small(pair_sum_kernel, [part_block] * heads, (keep, exchange(give, 1)), 9 * keep.size, "pair_sum")
+        for keep, give in ((first, first_give), (second, second_give))
+    )
     first_on, second_on = exchange(first[3], 2), exchange(second[3], 4)
     first_in, second_in = exchange(first[1], 2), exchange(second[2], 4)
     first_on = exchange(small(sum_kernel, part_block, (first[2], first_on), 6 * size, "pass_sum"), 4)

time: 53.3 us -> 52.6 us (0.987)
  waiting for transfers between devices: 15 us -> 14.4 us
    ppermute x23 -> x24, waiting for transfers between devices: 15 us -> 14.4 us  [exchange(): return lax.ppermute(x, 'tok', [(i, i ^ bits) for i in range(groups)])]
    ppermute x23 -> x24, starting transfers between devices: 19.8 us -> 19.6 us  [exchange(): return lax.ppermute(x, 'tok', [(i, i ^ bits) for i in range(groups)])]
    pallas_call x10 -> x11, Pallas kernels: 5.55 us -> 5.56 us  [small(): pl.pallas_call(kernel, out_shape=shapes, in_specs=specs, compiler_params=...]
  transfers between devices with their start and end apart: 23 -> 24, of which waited for: 10 -> 10; matrix products, arithmetic and copies ran while one was open for 2% -> 2% of each run, Pallas kernels for 9% -> 9%
where the time goes in v6:
time: 52.6 us; the launch traced here: 52.5 us
  starting transfers between devices  19.6 us (37%)
  Pallas kernels  17.1 us (33%)
  waiting for transfers between devices  14.4 us (27%)
  other arithmetic  1.19 us (2%)
    ppermute x24, starting transfers between devices, exchange(): return lax.ppermute(x, 'tok', [(i, i ^ bits) for i in range(groups)])  19.6 us
    ppermute x24, waiting for transfers between devices, exchange(): return lax.ppermute(x, 'tok', [(i, i ^ bits) for i in range(groups)])  14.4 us
    pallas_call x1, Pallas kernels, gradients(): pl.pallas_call(grad_kernel, out_shape=[shape] * 4, in_specs=[pl.BlockSpec...  7.46 us
    pallas_call x11, Pallas kernels, small(): pl.pallas_call(kernel, out_shape=shapes, in_specs=specs, compiler_params=...  5.56 us
    pallas_call x1, Pallas kernels, project_query(): pl.pallas_call(query_kernel, out_shape=pltpu.VMEM((heads, rows, width //...  2.36 us
    pallas_call x1, Pallas kernels, finish(): pl.pallas_call(finish_kernel, out_shape=jax.ShapeDtypeStruct((rows, heads...  1.71 us
    select_n x1, other arithmetic, shards(): jnp.where(core == 0, lax.dynamic_index_in_dim(w_gate, own, 0, False), lax...  1.19 us
  transfers between devices with their start and end apart: 24, of which 10 were waited for; matrix products, arithmetic and copies ran while one was open for 2% of the time, Pallas kernels for 9%

profile of v6, /device:TPU:0, one launch (start us, length us, event | category | flops | bytes accessed | tf_op | source)
XLA Modules:
  0.0 52.5 jit_solution(5917809756552868344)
XLA Ops:
  0.0 7.5 %gradients.1 = (bf16[4,144,384]{2,1,0:T(8,128)(2,1)S(1)}, bf16[4,144,384]{2,1,0:T(8,128)(2,1)S(1)}, bf16[4,144,384]{2,1,0:T(8,128)(2,1)S(1)}, bf16[4,144,384]{2,1,0:T(8,128)(2,1)S(1)}) custom-call(s32[16]{0:T(128)} %view_hbm.1, bf16[512,768]{1,0:T(8,128)(2,1)} %tokens_ref.1, bf16[768,2304]{1,0:T(8,128)(2,1)} %weight_ref.1, f32[4,192,384]{2,1,0:T(8,128)} %gate_hbm.1, ...), custom_call_target="tpu_custom_call" | custom-call | flops 3019898880 | bytes 6684672 | tf_op jit(solution)/shard_map/gradients/pallas_call | solution.py:113
  7.5 0.5 collective-permute-start
  8.1 1.3 %collective-permute-done.got_ref = bf16[4,144,384]{2,1,0:T(8,128)(2,1)S(1)} collective-permute-done((bf16[4,144,384]{2,1,0:T(8,128)(2,1)S(1)}, bf16[4,144,384]{2,1,0:T(8,128)(2,1)S(1)}, u32[]{:S(2)}, u32[]{:S(2)}) %collective-permute-start) | collective-permute-done | bytes 442400 | tf_op jit(solution)/shard_map/ppermute | solution.py:289
  9.5 3.0 %collective-permute-start.2 = (bf16[144,384]{1,0:T(8,128)(2,1)S(1)}, bf16[144,384]{1,0:T(8,128)(2,1)S(1)}, u32[]{:S(2)}, u32[]{:S(2)}) collective-permute-start(bf16[144,384]{1,0:T(8,128)(2,1)S(1)} %get-tuple-element.34), channel_id=1, source_target_pairs={{0,2},{1,3},{2,0},{3,1},{4,6},{5,7},{6,4},{7,5},{8,10},{9,11},{10,... | collective-permute-start | bytes 331784 | tf_op jit(solution)/shard_map/ppermute | solution.py:289
  12.6 1.6 %collective-permute-start.7 = (bf16[144,384]{1,0:T(8,128)(2,1)S(1)}, bf16[144,384]{1,0:T(8,128)(2,1)S(1)}, u32[]{:S(2)}, u32[]{:S(2)}) collective-permute-start(bf16[144,384]{1,0:T(8,128)(2,1)S(1)} %get-tuple-element.42), channel_id=1, source_target_pairs={{0,4},{1,5},{2,6},{3,7},{4,0},{5,1},{6,2},{7,3},{8,12},{9,13},{10,... | collective-permute-start | bytes 331784 | tf_op jit(solution)/shard_map/ppermute | solution.py:289
  14.2 0.5 collective-permute-start.1
  14.7 1.1 %collective-permute-done.2.refs_1_ = bf16[144,384]{1,0:T(8,128)(2,1)S(1)} collective-permute-done((bf16[144,384]{1,0:T(8,128)(2,1)S(1)}, bf16[144,384]{1,0:T(8,128)(2,1)S(1)}, u32[]{:S(2)}, u32[]{:S(2)}) %collective-permute-start.2) | collective-permute-done | bytes 110624 | tf_op jit(solution)/shard_map/ppermute | solution.py:289
  15.9 2.7 %collective-permute-start.3 = (bf16[144,384]{1,0:T(8,128)(2,1)S(1)}, bf16[144,384]{1,0:T(8,128)(2,1)S(1)}, u32[]{:S(2)}, u32[]{:S(2)}) collective-permute-start(bf16[144,384]{1,0:T(8,128)(2,1)S(1)} %pass_sum.2), channel_id=1, source_target_pairs={{0,4},{1,5},{2,6},{3,7},{4,0},{5,1},{6,2},{7,3},{8,12},{9,13},{10,... | collective-permute-start | bytes 331784 | tf_op jit(solution)/shard_map/ppermute | solution.py:289
  18.7 1.6 %collective-permute-start.8 = (bf16[144,384]{1,0:T(8,128)(2,1)S(1)}, bf16[144,384]{1,0:T(8,128)(2,1)S(1)}, u32[]{:S(2)}, u32[]{:S(2)}) collective-permute-start(bf16[144,384]{1,0:T(8,128)(2,1)S(1)} %pass_sum.3), channel_id=1, source_target_pairs={{0,2},{1,3},{2,0},{3,1},{4,6},{5,7},{6,4},{7,5},{8,10},{9,11},{10,... | collective-permute-start | bytes 331784 | tf_op jit(solution)/shard_map/ppermute | solution.py:289
  20.3 1.5 %collective-permute-done.3.refs_2_ = bf16[144,384]{1,0:T(8,128)(2,1)S(1)} collective-permute-done((bf16[144,384]{1,0:T(8,128)(2,1)S(1)}, bf16[144,384]{1,0:T(8,128)(2,1)S(1)}, u32[]{:S(2)}, u32[]{:S(2)}) %collective-permute-start.3) | collective-permute-done | bytes 110624 | tf_op jit(solution)/shard_map/ppermute | solution.py:289
  21.8 2.7 %collective-permute-start.4 = (bf16[144,384]{1,0:T(8,128)(2,1)S(1)}, bf16[144,384]{1,0:T(8,128)(2,1)S(1)}, u32[]{:S(2)}, u32[]{:S(2)}) collective-permute-start(bf16[144,384]{1,0:T(8,128)(2,1)S(1)} %plane_sum.2.mine_ref.first_ref), channel_id=1, source_target_pairs={{0,8},{1,9},{2,10},{3,11},{4,12},{5,13},{6,14},{7,15},{8,0},{9,1},... | collective-permute-start | bytes 331784 | tf_op jit(solution)/shard_map/ppermute | solution.py:289
  24.4 1.2 %fusion = (f32[192,384]{1,0:T(8,128)S(1)}, f32[192,384]{1,0:T(8,128)S(1)}) fusion(f32[4,384,192]{1,2,0:T(8,128)} %param.10, s32[]{:T(128)S(6)} %select_n.18, f32[4,192,384]{2,1,0:T(8,128)} %gate_hbm.1, pred[]{:T(512)S(6)} %eq.3, f32[4,192,384]{2,1,0:T(8,128)} %up_hbm.1), kind=kLoop, calls=%fused_computation.1 | loop fusion | flops 73728 | bytes 1474565 | tf_op jit(solution)/shard_map/jit(_where)/select_n | solution.py:304
  25.7 1.1 %collective-permute-start.9 = (bf16[144,384]{1,0:T(8,128)(2,1)S(1)}, bf16[144,384]{1,0:T(8,128)(2,1)S(1)}, u32[]{:S(2)}, u32[]{:S(2)}) collective-permute-start(bf16[144,384]{1,0:T(8,128)(2,1)S(1)} %plane_sum.3.second_ref), channel_id=1, source_target_pairs={{0,8},{1,9},{2,10},{3,11},{4,12},{5,13},{6,14},{7,15},{8,0},{9,1},... | collective-permute-start | bytes 331784 | tf_op jit(solution)/shard_map/ppermute | solution.py:289
  26.8 2.4 %query.1.q_ref = bf16[4,512,192]{2,1,0:T(8,128)(2,1)S(1)} custom-call(bf16[512,768]{1,0:T(8,128)(2,1)} %tokens_ref.1, bf16[768,2304]{1,0:T(8,128)(2,1)} %weight_ref.1), custom_call_target="tpu_custom_call" | custom-call | flops 603979776 | bytes 3932160 | tf_op jit(solution)/shard_map/query/pallas_call | solution.py:160
  29.2 1.8 %collective-permute-done.4.other_ref.first_other_ref = bf16[144,384]{1,0:T(8,128)(2,1)S(1)} collective-permute-done((bf16[144,384]{1,0:T(8,128)(2,1)S(1)}, bf16[144,384]{1,0:T(8,128)(2,1)S(1)}, u32[]{:S(2)}, u32[]{:S(2)}) %collective-permute-start.4) | collective-permute-done | bytes 110624 | tf_op jit(solution)/shard_map/ppermute | solution.py:289
  31.1 2.3 %collective-permute-done.9.second_other_ref = bf16[144,384]{1,0:T(8,128)(2,1)S(1)} collective-permute-done((bf16[144,384]{1,0:T(8,128)(2,1)S(1)}, bf16[144,384]{1,0:T(8,128)(2,1)S(1)}, u32[]{:S(2)}, u32[]{:S(2)}) %collective-permute-start.9) | collective-permute-done | bytes 110624 | tf_op jit(solution)/shard_map/ppermute | solution.py:289
  33.4 3.1 %newton.1 = (bf16[288,384]{1,0:T(8,128)(2,1)S(1)}, bf16[144,384]{1,0:T(8,128)(2,1)S(1)}, bf16[144,384]{1,0:T(8,128)(2,1)S(1)}) custom-call(bf16[144,384]{1,0:T(8,128)(2,1)S(1)} %plane_sum.2.mine_ref.first_ref, bf16[144,384]{1,0:T(8,128)(2,1)S(1)} %collective-permute-done.4.other_ref.first_other_ref, bf16[144,384]{1,0:T(8,128)(2,1)S(1)} %plane_sum.3.second_ref, ...), custom_call_target="tpu_custom_call" | custom-call | bytes 2211840 | tf_op jit(solution)/shard_map/newton/pallas_call | solution.py:141
  36.6 1.6 %collective-permute-start.11 = (bf16[144,384]{1,0:T(8,128)(2,1)S(1)}, bf16[144,384]{1,0:T(8,128)(2,1)S(1)}, u32[]{:S(2)}, u32[]{:S(2)}) collective-permute-start(bf16[144,384]{1,0:T(8,128)(2,1)S(1)} %get-tuple-element.45), channel_id=1, source_target_pairs={{0,2},{1,3},{2,0},{3,1},{4,6},{5,7},{6,4},{7,5},{8,10},{9,11},{10,... | collective-permute-start | bytes 331784 | tf_op jit(solution)/shard_map/ppermute | solution.py:289
  38.2 0.5 collective-permute-start.12
  38.7 2.0 %collective-permute-start.13 = (bf16[144,384]{1,0:T(8,128)(2,1)S(1)}, bf16[144,384]{1,0:T(8,128)(2,1)S(1)}, u32[]{:S(2)}, u32[]{:S(2)}) collective-permute-start(bf16[144,384]{1,0:T(8,128)(2,1)S(1)} %get-tuple-element.45), channel_id=1, source_target_pairs={{0,4},{1,5},{2,6},{3,7},{4,0},{5,1},{6,2},{7,3},{8,12},{9,13},{10,... | collective-permute-start | bytes 331784 | tf_op jit(solution)/shard_map/ppermute | solution.py:289
  40.7 1.8 %collective-permute-done.11.refs_0_ = bf16[144,384]{1,0:T(8,128)(2,1)S(1)} collective-permute-done((bf16[144,384]{1,0:T(8,128)(2,1)S(1)}, bf16[144,384]{1,0:T(8,128)(2,1)S(1)}, u32[]{:S(2)}, u32[]{:S(2)}) %collective-permute-start.11) | collective-permute-done | bytes 110624 | tf_op jit(solution)/shard_map/ppermute | solution.py:289
  42.5 1.6 %collective-permute-done.14.refs_1_ = bf16[144,384]{1,0:T(8,128)(2,1)S(1)} collective-permute-done((bf16[144,384]{1,0:T(8,128)(2,1)S(1)}, bf16[144,384]{1,0:T(8,128)(2,1)S(1)}, u32[]{:S(2)}, u32[]{:S(2)}) %collective-permute-start.14) | collective-permute-done | bytes 110624 | tf_op jit(solution)/shard_map/ppermute | solution.py:289
  44.1 0.5 collective-permute-start.21
  44.6 0.7 %apply.3.refs_0_ = bf16[512,192]{1,0:T(8,128)(2,1)S(1)} custom-call(bf16[4,512,192]{2,1,0:T(8,128)(2,1)S(1)} %query.1.q_ref, bf16[288,384]{1,0:T(8,128)(2,1)S(1)} %get-tuple-element.47.refs_0_, bf16[288,384]{1,0:T(8,128)(2,1)S(1)} %collective-permute-done.15.refs_1_), custom_call_target="tpu_custom_call" | custom-call | bytes 1966080 | tf_op jit(solution)/shard_map/apply/pallas_call | solution.py:141
  45.3 1.1 %collective-permute-done.13.refs_0_ = bf16[144,384]{1,0:T(8,128)(2,1)S(1)} collective-permute-done((bf16[144,384]{1,0:T(8,128)(2,1)S(1)}, bf16[144,384]{1,0:T(8,128)(2,1)S(1)}, u32[]{:S(2)}, u32[]{:S(2)}) %collective-permute-start.13) | collective-permute-done | bytes 110624 | tf_op jit(solution)/shard_map/ppermute | solution.py:289
  46.4 0.5 collective-permute-start.17
  46.9 1.1 %collective-permute-done.20.refs_3_ = bf16[144,384]{1,0:T(8,128)(2,1)S(1)} collective-permute-done((bf16[144,384]{1,0:T(8,128)(2,1)S(1)}, bf16[144,384]{1,0:T(8,128)(2,1)S(1)}, u32[]{:S(2)}, u32[]{:S(2)}) %collective-permute-start.20) | collective-permute-done | bytes 110624 | tf_op jit(solution)/shard_map/ppermute | solution.py:289
  48.0 0.8 %collective-permute-done.21.refs_4_ = bf16[144,384]{1,0:T(8,128)(2,1)S(1)} collective-permute-done((bf16[144,384]{1,0:T(8,128)(2,1)S(1)}, bf16[144,384]{1,0:T(8,128)(2,1)S(1)}, u32[]{:S(2)}, u32[]{:S(2)}) %collective-permute-start.21) | collective-permute-done | bytes 110624 | tf_op jit(solution)/shard_map/ppermute | solution.py:289
  48.8 0.5 collective-permute-start.23
  49.3 0.7 %apply.4.refs_1_ = bf16[512,192]{1,0:T(8,128)(2,1)S(1)} custom-call(bf16[4,512,192]{2,1,0:T(8,128)(2,1)S(1)} %query.1.q_ref, bf16[144,384]{1,0:T(8,128)(2,1)S(1)} %collective-permute-done.11.refs_0_, bf16[144,384]{1,0:T(8,128)(2,1)S(1)} %collective-permute-done.12.refs_1_, bf16[144,384]{1,0:T(8,128)(2,1)S(1)} %collective-permute-done.16.refs_2_, ...), custom_call_target="tpu_custom_call" | custom-call | bytes 1966080 | tf_op jit(solution)/shard_map/apply/pallas_call | solution.py:141
  50.0 0.7 %apply.5.refs_2_ = bf16[512,192]{1,0:T(8,128)(2,1)S(1)} custom-call(bf16[4,512,192]{2,1,0:T(8,128)(2,1)S(1)} %query.1.q_ref, bf16[144,384]{1,0:T(8,128)(2,1)S(1)} %collective-permute-done.13.refs_0_, bf16[144,384]{1,0:T(8,128)(2,1)S(1)} %collective-permute-done.14.refs_1_, bf16[144,384]{1,0:T(8,128)(2,1)S(1)} %collective-permute-done.18.refs_2_, ...), custom_call_target="tpu_custom_call" | custom-call | bytes 1966080 | tf_op jit(solution)/shard_map/apply/pallas_call | solution.py:141
  50.8 1.7 %finish.1 = bf16[512,768]{1,0:T(8,128)(2,1)} custom-call(bf16[4,512,192]{2,1,0:T(8,128)(2,1)S(1)} %query.1.q_ref, bf16[512,192]{1,0:T(8,128)(2,1)S(1)} %apply.3.refs_0_, bf16[512,192]{1,0:T(8,128)(2,1)S(1)} %apply.4.refs_1_, bf16[512,192]{1,0:T(8,128)(2,1)S(1)} %apply.5.refs_2_, bf16[144,384]{1,0:T(8,128)(2,1)S(1)} %collective-permute-done.20.refs_3_, ...), custom_call_target="tpu_custom_call" | custom-call | tf_op jit(solution)/shard_map/finish/pallas_call | solution.py:261
  (31 shorter events, 0.8 us)
Async XLA Ops:
  7.5 1.9 %collective-permute-start = (bf16[4,144,384]{2,1,0:T(8,128)(2,1)S(1)}, bf16[4,144,384]{2,1,0:T(8,128)(2,1)S(1)}, u32[]{:S(2)}, u32[]{:S(2)}) collective-permute-start(bf16[4,144,384]{2,1,0:T(8,128)(2,1)S(1)} %get-tuple-element.30), channel_id=1, source_target_pairs={{0,1},{1,0},{2,3},{3,2},{4,5},{5,4},{6,7},{7,6},{8,9},{9,8},{10,11... | collective-permute-start | bytes 1327112 | tf_op jit(solution)/shard_map/ppermute | solution.py:289
  8.0 4.5 %collective-permute-start.5 = (bf16[4,144,384]{2,1,0:T(8,128)(2,1)S(1)}, bf16[4,144,384]{2,1,0:T(8,128)(2,1)S(1)}, u32[]{:S(2)}, u32[]{:S(2)}) collective-permute-start(bf16[4,144,384]{2,1,0:T(8,128)(2,1)S(1)} %get-tuple-element.38), channel_id=1, source_target_pairs={{0,1},{1,0},{2,3},{3,2},{4,5},{5,4},{6,7},{7,6},{8,9},{9,8},{10,11... | collective-permute-start | bytes 1327112 | tf_op jit(solution)/shard_map/ppermute | solution.py:289
  9.5 6.3 %collective-permute-start.2 = (bf16[144,384]{1,0:T(8,128)(2,1)S(1)}, bf16[144,384]{1,0:T(8,128)(2,1)S(1)}, u32[]{:S(2)}, u32[]{:S(2)}) collective-permute-start(bf16[144,384]{1,0:T(8,128)(2,1)S(1)} %get-tuple-element.34), channel_id=1, source_target_pairs={{0,2},{1,3},{2,0},{3,1},{4,6},{5,7},{6,4},{7,5},{8,10},{9,11},{10,... | collective-permute-start | bytes 331784 | tf_op jit(solution)/shard_map/ppermute | solution.py:289
  12.6 6.1 %collective-permute-start.7 = (bf16[144,384]{1,0:T(8,128)(2,1)S(1)}, bf16[144,384]{1,0:T(8,128)(2,1)S(1)}, u32[]{:S(2)}, u32[]{:S(2)}) collective-permute-start(bf16[144,384]{1,0:T(8,128)(2,1)S(1)} %get-tuple-element.42), channel_id=1, source_target_pairs={{0,4},{1,5},{2,6},{3,7},{4,0},{5,1},{6,2},{7,3},{8,12},{9,13},{10,... | collective-permute-start | bytes 331784 | tf_op jit(solution)/shard_map/ppermute | solution.py:289
  14.2 6.0 %collective-permute-start.1 = (bf16[144,384]{1,0:T(8,128)(2,1)S(1)}, bf16[144,384]{1,0:T(8,128)(2,1)S(1)}, u32[]{:S(2)}, u32[]{:S(2)}) collective-permute-start(bf16[144,384]{1,0:T(8,128)(2,1)S(1)} %get-tuple-element.32), channel_id=1, source_target_pairs={{0,2},{1,3},{2,0},{3,1},{4,6},{5,7},{6,4},{7,5},{8,10},{9,11},{10,... | collective-permute-start | bytes 331784 | tf_op jit(solution)/shard_map/ppermute | solution.py:289
  15.9 5.9 %collective-permute-start.3 = (bf16[144,384]{1,0:T(8,128)(2,1)S(1)}, bf16[144,384]{1,0:T(8,128)(2,1)S(1)}, u32[]{:S(2)}, u32[]{:S(2)}) collective-permute-start(bf16[144,384]{1,0:T(8,128)(2,1)S(1)} %pass_sum.2), channel_id=1, source_target_pairs={{0,4},{1,5},{2,6},{3,7},{4,0},{5,1},{6,2},{7,3},{8,12},{9,13},{10,... | collective-permute-start | bytes 331784 | tf_op jit(solution)/shard_map/ppermute | solution.py:289
  18.5 7.1 %collective-permute-start.6 = (bf16[144,384]{1,0:T(8,128)(2,1)S(1)}, bf16[144,384]{1,0:T(8,128)(2,1)S(1)}, u32[]{:S(2)}, u32[]{:S(2)}) collective-permute-start(bf16[144,384]{1,0:T(8,128)(2,1)S(1)} %get-tuple-element.40), channel_id=1, source_target_pairs={{0,4},{1,5},{2,6},{3,7},{4,0},{5,1},{6,2},{7,3},{8,12},{9,13},{10,... | collective-permute-start | bytes 331784 | tf_op jit(solution)/shard_map/ppermute | solution.py:289
  18.7 7.0 %collective-permute-start.8 = (bf16[144,384]{1,0:T(8,128)(2,1)S(1)}, bf16[144,384]{1,0:T(8,128)(2,1)S(1)}, u32[]{:S(2)}, u32[]{:S(2)}) collective-permute-start(bf16[144,384]{1,0:T(8,128)(2,1)S(1)} %pass_sum.3), channel_id=1, source_target_pairs={{0,2},{1,3},{2,0},{3,1},{4,6},{5,7},{6,4},{7,5},{8,10},{9,11},{10,... | collective-permute-start | bytes 331784 | tf_op jit(solution)/shard_map/ppermute | solution.py:289
  21.8 9.2 %collective-permute-start.4 = (bf16[144,384]{1,0:T(8,128)(2,1)S(1)}, bf16[144,384]{1,0:T(8,128)(2,1)S(1)}, u32[]{:S(2)}, u32[]{:S(2)}) collective-permute-start(bf16[144,384]{1,0:T(8,128)(2,1)S(1)} %plane_sum.2.mine_ref.first_ref), channel_id=1, source_target_pairs={{0,8},{1,9},{2,10},{3,11},{4,12},{5,13},{6,14},{7,15},{8,0},{9,1},... | collective-permute-start | bytes 331784 | tf_op jit(solution)/shard_map/ppermute | solution.py:289
  25.7 7.7 %collective-permute-start.9 = (bf16[144,384]{1,0:T(8,128)(2,1)S(1)}, bf16[144,384]{1,0:T(8,128)(2,1)S(1)}, u32[]{:S(2)}, u32[]{:S(2)}) collective-permute-start(bf16[144,384]{1,0:T(8,128)(2,1)S(1)} %plane_sum.3.second_ref), channel_id=1, source_target_pairs={{0,8},{1,9},{2,10},{3,11},{4,12},{5,13},{6,14},{7,15},{8,0},{9,1},... | collective-permute-start | bytes 331784 | tf_op jit(solution)/shard_map/ppermute | solution.py:289
  31.0 2.4 %collective-permute-start.10 = (bf16[96,384]{1,0:T(8,128)(2,1)S(1)}, bf16[96,384]{1,0:T(8,128)(2,1)S(1)}, u32[]{:S(2)}, u32[]{:S(2)}) collective-permute-start(bf16[96,384]{1,0:T(8,128)(2,1)S(1)} %up_sum.1.half_ref), channel_id=1, source_target_pairs={{0,1},{1,0},{2,3},{3,2},{4,5},{5,4},{6,7},{7,6},{8,9},{9,8},{10,11... | collective-permute-start | bytes 221192 | tf_op jit(solution)/shard_map/ppermute | solution.py:289
  36.5 8.1 %collective-permute-start.15 = (bf16[288,384]{1,0:T(8,128)(2,1)S(1)}, bf16[288,384]{1,0:T(8,128)(2,1)S(1)}, u32[]{:S(2)}, u32[]{:S(2)}) collective-permute-start(bf16[288,384]{1,0:T(8,128)(2,1)S(1)} %get-tuple-element.47.refs_0_), channel_id=1, source_target_pairs={{0,1},{1,0},{2,3},{3,2},{4,5},{5,4},{6,7},{7,6},{8,9},{9,8},{10,11... | collective-permute-start | bytes 663560 | tf_op jit(solution)/shard_map/ppermute | solution.py:289
  36.6 5.9 %collective-permute-start.11 = (bf16[144,384]{1,0:T(8,128)(2,1)S(1)}, bf16[144,384]{1,0:T(8,128)(2,1)S(1)}, u32[]{:S(2)}, u32[]{:S(2)}) collective-permute-start(bf16[144,384]{1,0:T(8,128)(2,1)S(1)} %get-tuple-element.45), channel_id=1, source_target_pairs={{0,2},{1,3},{2,0},{3,1},{4,6},{5,7},{6,4},{7,5},{8,10},{9,11},{10,... | collective-permute-start | bytes 331784 | tf_op jit(solution)/shard_map/ppermute | solution.py:289
  38.2 5.9 %collective-permute-start.14 = (bf16[144,384]{1,0:T(8,128)(2,1)S(1)}, bf16[144,384]{1,0:T(8,128)(2,1)S(1)}, u32[]{:S(2)}, u32[]{:S(2)}) collective-permute-start(bf16[144,384]{1,0:T(8,128)(2,1)S(1)} %get-tuple-element.46), channel_id=1, source_target_pairs={{0,4},{1,5},{2,6},{3,7},{4,0},{5,1},{6,2},{7,3},{8,12},{9,13},{10,... | collective-permute-start | bytes 331784 | tf_op jit(solution)/shard_map/ppermute | solution.py:289
  38.2 7.1 %collective-permute-start.12 = (bf16[144,384]{1,0:T(8,128)(2,1)S(1)}, bf16[144,384]{1,0:T(8,128)(2,1)S(1)}, u32[]{:S(2)}, u32[]{:S(2)}) collective-permute-start(bf16[144,384]{1,0:T(8,128)(2,1)S(1)} %get-tuple-element.46), channel_id=1, source_target_pairs={{0,2},{1,3},{2,0},{3,1},{4,6},{5,7},{6,4},{7,5},{8,10},{9,11},{10,... | collective-permute-start | bytes 331784 | tf_op jit(solution)/shard_map/ppermute | solution.py:289
  38.7 7.8 %collective-permute-start.13 = (bf16[144,384]{1,0:T(8,128)(2,1)S(1)}, bf16[144,384]{1,0:T(8,128)(2,1)S(1)}, u32[]{:S(2)}, u32[]{:S(2)}) collective-permute-start(bf16[144,384]{1,0:T(8,128)(2,1)S(1)} %get-tuple-element.45), channel_id=1, source_target_pairs={{0,4},{1,5},{2,6},{3,7},{4,0},{5,1},{6,2},{7,3},{8,12},{9,13},{10,... | collective-permute-start | bytes 331784 | tf_op jit(solution)/shard_map/ppermute | solution.py:289
  42.5 5.5 %collective-permute-start.20 = (bf16[144,384]{1,0:T(8,128)(2,1)S(1)}, bf16[144,384]{1,0:T(8,128)(2,1)S(1)}, u32[]{:S(2)}, u32[]{:S(2)}) collective-permute-start(bf16[144,384]{1,0:T(8,128)(2,1)S(1)} %collective-permute-done.11.refs_0_), channel_id=1, source_target_pairs={{0,4},{1,5},{2,6},{3,7},{4,0},{5,1},{6,2},{7,3},{8,12},{9,13},{10,... | collective-permute-start | bytes 331784 | tf_op jit(solution)/shard_map/ppermute | solution.py:289
  44.1 4.7 %collective-permute-start.21 = (bf16[144,384]{1,0:T(8,128)(2,1)S(1)}, bf16[144,384]{1,0:T(8,128)(2,1)S(1)}, u32[]{:S(2)}, u32[]{:S(2)}) collective-permute-start(bf16[144,384]{1,0:T(8,128)(2,1)S(1)} %collective-permute-done.14.refs_1_), channel_id=1, source_target_pairs={{0,2},{1,3},{2,0},{3,1},{4,6},{5,7},{6,4},{7,5},{8,10},{9,11},{10,... | collective-permute-start | bytes 331784 | tf_op jit(solution)/shard_map/ppermute | solution.py:289
  46.4 2.4 %collective-permute-start.16 = (bf16[144,384]{1,0:T(8,128)(2,1)S(1)}, bf16[144,384]{1,0:T(8,128)(2,1)S(1)}, u32[]{:S(2)}, u32[]{:S(2)}) collective-permute-start(bf16[144,384]{1,0:T(8,128)(2,1)S(1)} %collective-permute-done.11.refs_0_), channel_id=1, source_target_pairs={{0,1},{1,0},{2,3},{3,2},{4,5},{5,4},{6,7},{7,6},{8,9},{9,8},{10,11... | collective-permute-start | bytes 331784 | tf_op jit(solution)/shard_map/ppermute | solution.py:289
  46.4 2.9 %collective-permute-start.17 = (bf16[144,384]{1,0:T(8,128)(2,1)S(1)}, bf16[144,384]{1,0:T(8,128)(2,1)S(1)}, u32[]{:S(2)}, u32[]{:S(2)}) collective-permute-start(bf16[144,384]{1,0:T(8,128)(2,1)S(1)} %collective-permute-done.12.refs_1_), channel_id=1, source_target_pairs={{0,1},{1,0},{2,3},{3,2},{4,5},{5,4},{6,7},{7,6},{8,9},{9,8},{10,11... | collective-permute-start | bytes 331784 | tf_op jit(solution)/shard_map/ppermute | solution.py:289
  46.9 3.1 %collective-permute-start.18 = (bf16[144,384]{1,0:T(8,128)(2,1)S(1)}, bf16[144,384]{1,0:T(8,128)(2,1)S(1)}, u32[]{:S(2)}, u32[]{:S(2)}) collective-permute-start(bf16[144,384]{1,0:T(8,128)(2,1)S(1)} %collective-permute-done.13.refs_0_), channel_id=1, source_target_pairs={{0,1},{1,0},{2,3},{3,2},{4,5},{5,4},{6,7},{7,6},{8,9},{9,8},{10,11... | collective-permute-start | bytes 331784 | tf_op jit(solution)/shard_map/ppermute | solution.py:289
  48.0 2.0 %collective-permute-start.19 = (bf16[144,384]{1,0:T(8,128)(2,1)S(1)}, bf16[144,384]{1,0:T(8,128)(2,1)S(1)}, u32[]{:S(2)}, u32[]{:S(2)}) collective-permute-start(bf16[144,384]{1,0:T(8,128)(2,1)S(1)} %collective-permute-done.14.refs_1_), channel_id=1, source_target_pairs={{0,1},{1,0},{2,3},{3,2},{4,5},{5,4},{6,7},{7,6},{8,9},{9,8},{10,11... | collective-permute-start | bytes 331784 | tf_op jit(solution)/shard_map/ppermute | solution.py:289
  48.8 1.9 %collective-permute-start.22 = (bf16[144,384]{1,0:T(8,128)(2,1)S(1)}, bf16[144,384]{1,0:T(8,128)(2,1)S(1)}, u32[]{:S(2)}, u32[]{:S(2)}) collective-permute-start(bf16[144,384]{1,0:T(8,128)(2,1)S(1)} %collective-permute-done.20.refs_3_), channel_id=1, source_target_pairs={{0,1},{1,0},{2,3},{3,2},{4,5},{5,4},{6,7},{7,6},{8,9},{9,8},{10,11... | collective-permute-start | bytes 331784 | tf_op jit(solution)/shard_map/ppermute | solution.py:289
  48.8 2.0 %collective-permute-start.23 = (bf16[144,384]{1,0:T(8,128)(2,1)S(1)}, bf16[144,384]{1,0:T(8,128)(2,1)S(1)}, u32[]{:S(2)}, u32[]{:S(2)}) collective-permute-start(bf16[144,384]{1,0:T(8,128)(2,1)S(1)} %collective-permute-done.21.refs_4_), channel_id=1, source_target_pairs={{0,1},{1,0},{2,3},{3,2},{4,5},{5,4},{6,7},{7,6},{8,9},{9,8},{10,11... | collective-permute-start | bytes 331784 | tf_op jit(solution)/shard_map/ppermute | solution.py:289

commit v7 on v6

--- a/solution.py
+++ b/solution.py
@@ -76,7 +76,7 @@
         both_w[head, :, hidden:] = fast[head, 1].astype(BF16)
         down_w[head] = fast[head, 2].astype(BF16)
     even = core == 0
-    chunk = rows // 2
+    chunk = rows
     for head in range(heads):
         both_sum = down_sum = None
         for start in range(0, rows, chunk):

time: 52.6 us -> 52.6 us (level)
  no operation moved by 1% of the time
where the time goes in v7:
time: 52.6 us; the launch traced here: 52.4 us
  starting transfers between devices  19.6 us (37%)
  Pallas kernels  17 us (32%)
  waiting for transfers between devices  14.5 us (28%)
  other arithmetic  1.19 us (2%)
    ppermute x24, starting transfers between devices, exchange(): return lax.ppermute(x, 'tok', [(i, i ^ bits) for i in range(groups)])  19.6 us
    ppermute x24, waiting for transfers between devices, exchange(): return lax.ppermute(x, 'tok', [(i, i ^ bits) for i in range(groups)])  14.5 us
    pallas_call x1, Pallas kernels, gradients(): pl.pallas_call(grad_kernel, out_shape=[shape] * 4, in_specs=[pl.BlockSpec...  7.4 us
    pallas_call x11, Pallas kernels, small(): pl.pallas_call(kernel, out_shape=shapes, in_specs=specs, compiler_params=...  5.56 us
    pallas_call x1, Pallas kernels, project_query(): pl.pallas_call(query_kernel, out_shape=pltpu.VMEM((heads, rows, width //...  2.36 us
    pallas_call x1, Pallas kernels, finish(): pl.pallas_call(finish_kernel, out_shape=jax.ShapeDtypeStruct((rows, heads...  1.71 us
    select_n x1, other arithmetic, shards(): jnp.where(core == 0, lax.dynamic_index_in_dim(w_gate, own, 0, False), lax...  1.19 us
  transfers between devices with their start and end apart: 24, of which 10 were waited for; matrix products, arithmetic and copies ran while one was open for 2% of the time, Pallas kernels for 9%

profile of v7, /device:TPU:0, one launch (start us, length us, event | category | flops | bytes accessed | tf_op | source)
XLA Modules:
  0.0 52.4 jit_solution(8528673025222575173)
XLA Ops:
  0.0 7.4 %gradients.1 = (bf16[4,144,384]{2,1,0:T(8,128)(2,1)S(1)}, bf16[4,144,384]{2,1,0:T(8,128)(2,1)S(1)}, bf16[4,144,384]{2,1,0:T(8,128)(2,1)S(1)}, bf16[4,144,384]{2,1,0:T(8,128)(2,1)S(1)}) custom-call(s32[16]{0:T(128)} %view_hbm.1, bf16[512,768]{1,0:T(8,128)(2,1)} %tokens_ref.1, bf16[768,2304]{1,0:T(8,128)(2,1)} %weight_ref.1, f32[4,192,384]{2,1,0:T(8,128)} %gate_hbm.1, ...), custom_call_target="tpu_custom_call" | custom-call | flops 3019898880 | bytes 6684672 | tf_op jit(solution)/shard_map/gradients/pallas_call | solution.py:113
  7.4 0.5 collective-permute-start
  8.0 1.3 %collective-permute-done.got_ref = bf16[4,144,384]{2,1,0:T(8,128)(2,1)S(1)} collective-permute-done((bf16[4,144,384]{2,1,0:T(8,128)(2,1)S(1)}, bf16[4,144,384]{2,1,0:T(8,128)(2,1)S(1)}, u32[]{:S(2)}, u32[]{:S(2)}) %collective-permute-start) | collective-permute-done | bytes 442400 | tf_op jit(solution)/shard_map/ppermute | solution.py:289
  9.4 3.0 %collective-permute-start.2 = (bf16[144,384]{1,0:T(8,128)(2,1)S(1)}, bf16[144,384]{1,0:T(8,128)(2,1)S(1)}, u32[]{:S(2)}, u32[]{:S(2)}) collective-permute-start(bf16[144,384]{1,0:T(8,128)(2,1)S(1)} %get-tuple-element.34), channel_id=1, source_target_pairs={{0,2},{1,3},{2,0},{3,1},{4,6},{5,7},{6,4},{7,5},{8,10},{9,11},{10,... | collective-permute-start | bytes 331784 | tf_op jit(solution)/shard_map/ppermute | solution.py:289
  12.5 1.7 %collective-permute-start.7 = (bf16[144,384]{1,0:T(8,128)(2,1)S(1)}, bf16[144,384]{1,0:T(8,128)(2,1)S(1)}, u32[]{:S(2)}, u32[]{:S(2)}) collective-permute-start(bf16[144,384]{1,0:T(8,128)(2,1)S(1)} %get-tuple-element.42), channel_id=1, source_target_pairs={{0,4},{1,5},{2,6},{3,7},{4,0},{5,1},{6,2},{7,3},{8,12},{9,13},{10,... | collective-permute-start | bytes 331784 | tf_op jit(solution)/shard_map/ppermute | solution.py:289
  14.2 0.5 collective-permute-start.1
  14.7 1.1 %collective-permute-done.2.refs_1_ = bf16[144,384]{1,0:T(8,128)(2,1)S(1)} collective-permute-done((bf16[144,384]{1,0:T(8,128)(2,1)S(1)}, bf16[144,384]{1,0:T(8,128)(2,1)S(1)}, u32[]{:S(2)}, u32[]{:S(2)}) %collective-permute-start.2) | collective-permute-done | bytes 110624 | tf_op jit(solution)/shard_map/ppermute | solution.py:289
  15.8 2.7 %collective-permute-start.3 = (bf16[144,384]{1,0:T(8,128)(2,1)S(1)}, bf16[144,384]{1,0:T(8,128)(2,1)S(1)}, u32[]{:S(2)}, u32[]{:S(2)}) collective-permute-start(bf16[144,384]{1,0:T(8,128)(2,1)S(1)} %pass_sum.2), channel_id=1, source_target_pairs={{0,4},{1,5},{2,6},{3,7},{4,0},{5,1},{6,2},{7,3},{8,12},{9,13},{10,... | collective-permute-start | bytes 331784 | tf_op jit(solution)/shard_map/ppermute | solution.py:289
  18.6 1.6 %collective-permute-start.8 = (bf16[144,384]{1,0:T(8,128)(2,1)S(1)}, bf16[144,384]{1,0:T(8,128)(2,1)S(1)}, u32[]{:S(2)}, u32[]{:S(2)}) collective-permute-start(bf16[144,384]{1,0:T(8,128)(2,1)S(1)} %pass_sum.3), channel_id=1, source_target_pairs={{0,2},{1,3},{2,0},{3,1},{4,6},{5,7},{6,4},{7,5},{8,10},{9,11},{10,... | collective-permute-start | bytes 331784 | tf_op jit(solution)/shard_map/ppermute | solution.py:289
  20.2 1.5 %collective-permute-done.3.refs_2_ = bf16[144,384]{1,0:T(8,128)(2,1)S(1)} collective-permute-done((bf16[144,384]{1,0:T(8,128)(2,1)S(1)}, bf16[144,384]{1,0:T(8,128)(2,1)S(1)}, u32[]{:S(2)}, u32[]{:S(2)}) %collective-permute-start.3) | collective-permute-done | bytes 110624 | tf_op jit(solution)/shard_map/ppermute | solution.py:289
  21.7 2.7 %collective-permute-start.4 = (bf16[144,384]{1,0:T(8,128)(2,1)S(1)}, bf16[144,384]{1,0:T(8,128)(2,1)S(1)}, u32[]{:S(2)}, u32[]{:S(2)}) collective-permute-start(bf16[144,384]{1,0:T(8,128)(2,1)S(1)} %plane_sum.2.mine_ref.first_ref), channel_id=1, source_target_pairs={{0,8},{1,9},{2,10},{3,11},{4,12},{5,13},{6,14},{7,15},{8,0},{9,1},... | collective-permute-start | bytes 331784 | tf_op jit(solution)/shard_map/ppermute | solution.py:289
  24.4 1.2 %fusion = (f32[192,384]{1,0:T(8,128)S(1)}, f32[192,384]{1,0:T(8,128)S(1)}) fusion(f32[4,384,192]{1,2,0:T(8,128)} %param.10, s32[]{:T(128)S(6)} %select_n.18, f32[4,192,384]{2,1,0:T(8,128)} %gate_hbm.1, pred[]{:T(512)S(6)} %eq.3, f32[4,192,384]{2,1,0:T(8,128)} %up_hbm.1), kind=kLoop, calls=%fused_computation.1 | loop fusion | flops 73728 | bytes 1474565 | tf_op jit(solution)/shard_map/jit(_where)/select_n | solution.py:304
  25.7 1.1 %collective-permute-start.9 = (bf16[144,384]{1,0:T(8,128)(2,1)S(1)}, bf16[144,384]{1,0:T(8,128)(2,1)S(1)}, u32[]{:S(2)}, u32[]{:S(2)}) collective-permute-start(bf16[144,384]{1,0:T(8,128)(2,1)S(1)} %plane_sum.3.second_ref), channel_id=1, source_target_pairs={{0,8},{1,9},{2,10},{3,11},{4,12},{5,13},{6,14},{7,15},{8,0},{9,1},... | collective-permute-start | bytes 331784 | tf_op jit(solution)/shard_map/ppermute | solution.py:289
  26.7 2.4 %query.1.q_ref = bf16[4,512,192]{2,1,0:T(8,128)(2,1)S(1)} custom-call(bf16[512,768]{1,0:T(8,128)(2,1)} %tokens_ref.1, bf16[768,2304]{1,0:T(8,128)(2,1)} %weight_ref.1), custom_call_target="tpu_custom_call" | custom-call | flops 603979776 | bytes 3932160 | tf_op jit(solution)/shard_map/query/pallas_call | solution.py:160
  29.1 1.8 %collective-permute-done.4.other_ref.first_other_ref = bf16[144,384]{1,0:T(8,128)(2,1)S(1)} collective-permute-done((bf16[144,384]{1,0:T(8,128)(2,1)S(1)}, bf16[144,384]{1,0:T(8,128)(2,1)S(1)}, u32[]{:S(2)}, u32[]{:S(2)}) %collective-permute-start.4) | collective-permute-done | bytes 110624 | tf_op jit(solution)/shard_map/ppermute | solution.py:289
  31.0 2.3 %collective-permute-done.9.second_other_ref = bf16[144,384]{1,0:T(8,128)(2,1)S(1)} collective-permute-done((bf16[144,384]{1,0:T(8,128)(2,1)S(1)}, bf16[144,384]{1,0:T(8,128)(2,1)S(1)}, u32[]{:S(2)}, u32[]{:S(2)}) %collective-permute-start.9) | collective-permute-done | bytes 110624 | tf_op jit(solution)/shard_map/ppermute | solution.py:289
  33.3 3.1 %newton.1 = (bf16[288,384]{1,0:T(8,128)(2,1)S(1)}, bf16[144,384]{1,0:T(8,128)(2,1)S(1)}, bf16[144,384]{1,0:T(8,128)(2,1)S(1)}) custom-call(bf16[144,384]{1,0:T(8,128)(2,1)S(1)} %plane_sum.2.mine_ref.first_ref, bf16[144,384]{1,0:T(8,128)(2,1)S(1)} %collective-permute-done.4.other_ref.first_other_ref, bf16[144,384]{1,0:T(8,128)(2,1)S(1)} %plane_sum.3.second_ref, ...), custom_call_target="tpu_custom_call" | custom-call | bytes 2211840 | tf_op jit(solution)/shard_map/newton/pallas_call | solution.py:141
  36.5 1.6 %collective-permute-start.11 = (bf16[144,384]{1,0:T(8,128)(2,1)S(1)}, bf16[144,384]{1,0:T(8,128)(2,1)S(1)}, u32[]{:S(2)}, u32[]{:S(2)}) collective-permute-start(bf16[144,384]{1,0:T(8,128)(2,1)S(1)} %get-tuple-element.45), channel_id=1, source_target_pairs={{0,2},{1,3},{2,0},{3,1},{4,6},{5,7},{6,4},{7,5},{8,10},{9,11},{10,... | collective-permute-start | bytes 331784 | tf_op jit(solution)/shard_map/ppermute | solution.py:289
  38.1 0.5 collective-permute-start.12
  38.6 2.0 %collective-permute-start.13 = (bf16[144,384]{1,0:T(8,128)(2,1)S(1)}, bf16[144,384]{1,0:T(8,128)(2,1)S(1)}, u32[]{:S(2)}, u32[]{:S(2)}) collective-permute-start(bf16[144,384]{1,0:T(8,128)(2,1)S(1)} %get-tuple-element.45), channel_id=1, source_target_pairs={{0,4},{1,5},{2,6},{3,7},{4,0},{5,1},{6,2},{7,3},{8,12},{9,13},{10,... | collective-permute-start | bytes 331784 | tf_op jit(solution)/shard_map/ppermute | solution.py:289
  40.6 1.8 %collective-permute-done.11.refs_0_ = bf16[144,384]{1,0:T(8,128)(2,1)S(1)} collective-permute-done((bf16[144,384]{1,0:T(8,128)(2,1)S(1)}, bf16[144,384]{1,0:T(8,128)(2,1)S(1)}, u32[]{:S(2)}, u32[]{:S(2)}) %collective-permute-start.11) | collective-permute-done | bytes 110624 | tf_op jit(solution)/shard_map/ppermute | solution.py:289
  42.4 1.6 %collective-permute-done.14.refs_1_ = bf16[144,384]{1,0:T(8,128)(2,1)S(1)} collective-permute-done((bf16[144,384]{1,0:T(8,128)(2,1)S(1)}, bf16[144,384]{1,0:T(8,128)(2,1)S(1)}, u32[]{:S(2)}, u32[]{:S(2)}) %collective-permute-start.14) | collective-permute-done | bytes 110624 | tf_op jit(solution)/shard_map/ppermute | solution.py:289
  44.0 0.5 collective-permute-start.21
  44.5 0.7 %apply.3.refs_0_ = bf16[512,192]{1,0:T(8,128)(2,1)S(1)} custom-call(bf16[4,512,192]{2,1,0:T(8,128)(2,1)S(1)} %query.1.q_ref, bf16[288,384]{1,0:T(8,128)(2,1)S(1)} %get-tuple-element.47.refs_0_, bf16[288,384]{1,0:T(8,128)(2,1)S(1)} %collective-permute-done.15.refs_1_), custom_call_target="tpu_custom_call" | custom-call | bytes 1966080 | tf_op jit(solution)/shard_map/apply/pallas_call | solution.py:141
  45.2 1.2 %collective-permute-done.13.refs_0_ = bf16[144,384]{1,0:T(8,128)(2,1)S(1)} collective-permute-done((bf16[144,384]{1,0:T(8,128)(2,1)S(1)}, bf16[144,384]{1,0:T(8,128)(2,1)S(1)}, u32[]{:S(2)}, u32[]{:S(2)}) %collective-permute-start.13) | collective-permute-done | bytes 110624 | tf_op jit(solution)/shard_map/ppermute | solution.py:289
  46.4 0.5 collective-permute-start.17
  46.9 1.1 %collective-permute-done.20.refs_3_ = bf16[144,384]{1,0:T(8,128)(2,1)S(1)} collective-permute-done((bf16[144,384]{1,0:T(8,128)(2,1)S(1)}, bf16[144,384]{1,0:T(8,128)(2,1)S(1)}, u32[]{:S(2)}, u32[]{:S(2)}) %collective-permute-start.20) | collective-permute-done | bytes 110624 | tf_op jit(solution)/shard_map/ppermute | solution.py:289
  48.0 0.8 %collective-permute-done.21.refs_4_ = bf16[144,384]{1,0:T(8,128)(2,1)S(1)} collective-permute-done((bf16[144,384]{1,0:T(8,128)(2,1)S(1)}, bf16[144,384]{1,0:T(8,128)(2,1)S(1)}, u32[]{:S(2)}, u32[]{:S(2)}) %collective-permute-start.21) | collective-permute-done | bytes 110624 | tf_op jit(solution)/shard_map/ppermute | solution.py:289
  48.8 0.5 collective-permute-start.23
  49.3 0.7 %apply.4.refs_1_ = bf16[512,192]{1,0:T(8,128)(2,1)S(1)} custom-call(bf16[4,512,192]{2,1,0:T(8,128)(2,1)S(1)} %query.1.q_ref, bf16[144,384]{1,0:T(8,128)(2,1)S(1)} %collective-permute-done.11.refs_0_, bf16[144,384]{1,0:T(8,128)(2,1)S(1)} %collective-permute-done.12.refs_1_, bf16[144,384]{1,0:T(8,128)(2,1)S(1)} %collective-permute-done.16.refs_2_, ...), custom_call_target="tpu_custom_call" | custom-call | bytes 1966080 | tf_op jit(solution)/shard_map/apply/pallas_call | solution.py:141
  50.0 0.7 %apply.5.refs_2_ = bf16[512,192]{1,0:T(8,128)(2,1)S(1)} custom-call(bf16[4,512,192]{2,1,0:T(8,128)(2,1)S(1)} %query.1.q_ref, bf16[144,384]{1,0:T(8,128)(2,1)S(1)} %collective-permute-done.13.refs_0_, bf16[144,384]{1,0:T(8,128)(2,1)S(1)} %collective-permute-done.14.refs_1_, bf16[144,384]{1,0:T(8,128)(2,1)S(1)} %collective-permute-done.18.refs_2_, ...), custom_call_target="tpu_custom_call" | custom-call | bytes 1966080 | tf_op jit(solution)/shard_map/apply/pallas_call | solution.py:141
  50.7 1.7 %finish.1 = bf16[512,768]{1,0:T(8,128)(2,1)} custom-call(bf16[4,512,192]{2,1,0:T(8,128)(2,1)S(1)} %query.1.q_ref, bf16[512,192]{1,0:T(8,128)(2,1)S(1)} %apply.3.refs_0_, bf16[512,192]{1,0:T(8,128)(2,1)S(1)} %apply.4.refs_1_, bf16[512,192]{1,0:T(8,128)(2,1)S(1)} %apply.5.refs_2_, bf16[144,384]{1,0:T(8,128)(2,1)S(1)} %collective-permute-done.20.refs_3_, ...), custom_call_target="tpu_custom_call" | custom-call | tf_op jit(solution)/shard_map/finish/pallas_call | solution.py:261
  (31 shorter events, 0.8 us)
Async XLA Ops:
  7.4 1.9 %collective-permute-start = (bf16[4,144,384]{2,1,0:T(8,128)(2,1)S(1)}, bf16[4,144,384]{2,1,0:T(8,128)(2,1)S(1)}, u32[]{:S(2)}, u32[]{:S(2)}) collective-permute-start(bf16[4,144,384]{2,1,0:T(8,128)(2,1)S(1)} %get-tuple-element.30), channel_id=1, source_target_pairs={{0,1},{1,0},{2,3},{3,2},{4,5},{5,4},{6,7},{7,6},{8,9},{9,8},{10,11... | collective-permute-start | bytes 1327112 | tf_op jit(solution)/shard_map/ppermute | solution.py:289
  7.9 4.5 %collective-permute-start.5 = (bf16[4,144,384]{2,1,0:T(8,128)(2,1)S(1)}, bf16[4,144,384]{2,1,0:T(8,128)(2,1)S(1)}, u32[]{:S(2)}, u32[]{:S(2)}) collective-permute-start(bf16[4,144,384]{2,1,0:T(8,128)(2,1)S(1)} %get-tuple-element.38), channel_id=1, source_target_pairs={{0,1},{1,0},{2,3},{3,2},{4,5},{5,4},{6,7},{7,6},{8,9},{9,8},{10,11... | collective-permute-start | bytes 1327112 | tf_op jit(solution)/shard_map/ppermute | solution.py:289
  9.4 6.3 %collective-permute-start.2 = (bf16[144,384]{1,0:T(8,128)(2,1)S(1)}, bf16[144,384]{1,0:T(8,128)(2,1)S(1)}, u32[]{:S(2)}, u32[]{:S(2)}) collective-permute-start(bf16[144,384]{1,0:T(8,128)(2,1)S(1)} %get-tuple-element.34), channel_id=1, source_target_pairs={{0,2},{1,3},{2,0},{3,1},{4,6},{5,7},{6,4},{7,5},{8,10},{9,11},{10,... | collective-permute-start | bytes 331784 | tf_op jit(solution)/shard_map/ppermute | solution.py:289
  12.5 6.0 %collective-permute-start.7 = (bf16[144,384]{1,0:T(8,128)(2,1)S(1)}, bf16[144,384]{1,0:T(8,128)(2,1)S(1)}, u32[]{:S(2)}, u32[]{:S(2)}) collective-permute-start(bf16[144,384]{1,0:T(8,128)(2,1)S(1)} %get-tuple-element.42), channel_id=1, source_target_pairs={{0,4},{1,5},{2,6},{3,7},{4,0},{5,1},{6,2},{7,3},{8,12},{9,13},{10,... | collective-permute-start | bytes 331784 | tf_op jit(solution)/shard_map/ppermute | solution.py:289
  14.2 6.0 %collective-permute-start.1 = (bf16[144,384]{1,0:T(8,128)(2,1)S(1)}, bf16[144,384]{1,0:T(8,128)(2,1)S(1)}, u32[]{:S(2)}, u32[]{:S(2)}) collective-permute-start(bf16[144,384]{1,0:T(8,128)(2,1)S(1)} %get-tuple-element.32), channel_id=1, source_target_pairs={{0,2},{1,3},{2,0},{3,1},{4,6},{5,7},{6,4},{7,5},{8,10},{9,11},{10,... | collective-permute-start | bytes 331784 | tf_op jit(solution)/shard_map/ppermute | solution.py:289
  15.8 5.8 %collective-permute-start.3 = (bf16[144,384]{1,0:T(8,128)(2,1)S(1)}, bf16[144,384]{1,0:T(8,128)(2,1)S(1)}, u32[]{:S(2)}, u32[]{:S(2)}) collective-permute-start(bf16[144,384]{1,0:T(8,128)(2,1)S(1)} %pass_sum.2), channel_id=1, source_target_pairs={{0,4},{1,5},{2,6},{3,7},{4,0},{5,1},{6,2},{7,3},{8,12},{9,13},{10,... | collective-permute-start | bytes 331784 | tf_op jit(solution)/shard_map/ppermute | solution.py:289
  18.5 7.1 %collective-permute-start.6 = (bf16[144,384]{1,0:T(8,128)(2,1)S(1)}, bf16[144,384]{1,0:T(8,128)(2,1)S(1)}, u32[]{:S(2)}, u32[]{:S(2)}) collective-permute-start(bf16[144,384]{1,0:T(8,128)(2,1)S(1)} %get-tuple-element.40), channel_id=1, source_target_pairs={{0,4},{1,5},{2,6},{3,7},{4,0},{5,1},{6,2},{7,3},{8,12},{9,13},{10,... | collective-permute-start | bytes 331784 | tf_op jit(solution)/shard_map/ppermute | solution.py:289
  18.6 7.0 %collective-permute-start.8 = (bf16[144,384]{1,0:T(8,128)(2,1)S(1)}, bf16[144,384]{1,0:T(8,128)(2,1)S(1)}, u32[]{:S(2)}, u32[]{:S(2)}) collective-permute-start(bf16[144,384]{1,0:T(8,128)(2,1)S(1)} %pass_sum.3), channel_id=1, source_target_pairs={{0,2},{1,3},{2,0},{3,1},{4,6},{5,7},{6,4},{7,5},{8,10},{9,11},{10,... | collective-permute-start | bytes 331784 | tf_op jit(solution)/shard_map/ppermute | solution.py:289
  21.7 9.2 %collective-permute-start.4 = (bf16[144,384]{1,0:T(8,128)(2,1)S(1)}, bf16[144,384]{1,0:T(8,128)(2,1)S(1)}, u32[]{:S(2)}, u32[]{:S(2)}) collective-permute-start(bf16[144,384]{1,0:T(8,128)(2,1)S(1)} %plane_sum.2.mine_ref.first_ref), channel_id=1, source_target_pairs={{0,8},{1,9},{2,10},{3,11},{4,12},{5,13},{6,14},{7,15},{8,0},{9,1},... | collective-permute-start | bytes 331784 | tf_op jit(solution)/shard_map/ppermute | solution.py:289
  25.7 7.7 %collective-permute-start.9 = (bf16[144,384]{1,0:T(8,128)(2,1)S(1)}, bf16[144,384]{1,0:T(8,128)(2,1)S(1)}, u32[]{:S(2)}, u32[]{:S(2)}) collective-permute-start(bf16[144,384]{1,0:T(8,128)(2,1)S(1)} %plane_sum.3.second_ref), channel_id=1, source_target_pairs={{0,8},{1,9},{2,10},{3,11},{4,12},{5,13},{6,14},{7,15},{8,0},{9,1},... | collective-permute-start | bytes 331784 | tf_op jit(solution)/shard_map/ppermute | solution.py:289
  30.9 2.4 %collective-permute-start.10 = (bf16[96,384]{1,0:T(8,128)(2,1)S(1)}, bf16[96,384]{1,0:T(8,128)(2,1)S(1)}, u32[]{:S(2)}, u32[]{:S(2)}) collective-permute-start(bf16[96,384]{1,0:T(8,128)(2,1)S(1)} %up_sum.1.half_ref), channel_id=1, source_target_pairs={{0,1},{1,0},{2,3},{3,2},{4,5},{5,4},{6,7},{7,6},{8,9},{9,8},{10,11... | collective-permute-start | bytes 221192 | tf_op jit(solution)/shard_map/ppermute | solution.py:289
  36.4 8.1 %collective-permute-start.15 = (bf16[288,384]{1,0:T(8,128)(2,1)S(1)}, bf16[288,384]{1,0:T(8,128)(2,1)S(1)}, u32[]{:S(2)}, u32[]{:S(2)}) collective-permute-start(bf16[288,384]{1,0:T(8,128)(2,1)S(1)} %get-tuple-element.47.refs_0_), channel_id=1, source_target_pairs={{0,1},{1,0},{2,3},{3,2},{4,5},{5,4},{6,7},{7,6},{8,9},{9,8},{10,11... | collective-permute-start | bytes 663560 | tf_op jit(solution)/shard_map/ppermute | solution.py:289
  36.5 5.9 %collective-permute-start.11 = (bf16[144,384]{1,0:T(8,128)(2,1)S(1)}, bf16[144,384]{1,0:T(8,128)(2,1)S(1)}, u32[]{:S(2)}, u32[]{:S(2)}) collective-permute-start(bf16[144,384]{1,0:T(8,128)(2,1)S(1)} %get-tuple-element.45), channel_id=1, source_target_pairs={{0,2},{1,3},{2,0},{3,1},{4,6},{5,7},{6,4},{7,5},{8,10},{9,11},{10,... | collective-permute-start | bytes 331784 | tf_op jit(solution)/shard_map/ppermute | solution.py:289
  38.1 5.9 %collective-permute-start.14 = (bf16[144,384]{1,0:T(8,128)(2,1)S(1)}, bf16[144,384]{1,0:T(8,128)(2,1)S(1)}, u32[]{:S(2)}, u32[]{:S(2)}) collective-permute-start(bf16[144,384]{1,0:T(8,128)(2,1)S(1)} %get-tuple-element.46), channel_id=1, source_target_pairs={{0,4},{1,5},{2,6},{3,7},{4,0},{5,1},{6,2},{7,3},{8,12},{9,13},{10,... | collective-permute-start | bytes 331784 | tf_op jit(solution)/shard_map/ppermute | solution.py:289
  38.1 7.1 %collective-permute-start.12 = (bf16[144,384]{1,0:T(8,128)(2,1)S(1)}, bf16[144,384]{1,0:T(8,128)(2,1)S(1)}, u32[]{:S(2)}, u32[]{:S(2)}) collective-permute-start(bf16[144,384]{1,0:T(8,128)(2,1)S(1)} %get-tuple-element.46), channel_id=1, source_target_pairs={{0,2},{1,3},{2,0},{3,1},{4,6},{5,7},{6,4},{7,5},{8,10},{9,11},{10,... | collective-permute-start | bytes 331784 | tf_op jit(solution)/shard_map/ppermute | solution.py:289
  38.6 7.8 %collective-permute-start.13 = (bf16[144,384]{1,0:T(8,128)(2,1)S(1)}, bf16[144,384]{1,0:T(8,128)(2,1)S(1)}, u32[]{:S(2)}, u32[]{:S(2)}) collective-permute-start(bf16[144,384]{1,0:T(8,128)(2,1)S(1)} %get-tuple-element.45), channel_id=1, source_target_pairs={{0,4},{1,5},{2,6},{3,7},{4,0},{5,1},{6,2},{7,3},{8,12},{9,13},{10,... | collective-permute-start | bytes 331784 | tf_op jit(solution)/shard_map/ppermute | solution.py:289
  42.4 5.5 %collective-permute-start.20 = (bf16[144,384]{1,0:T(8,128)(2,1)S(1)}, bf16[144,384]{1,0:T(8,128)(2,1)S(1)}, u32[]{:S(2)}, u32[]{:S(2)}) collective-permute-start(bf16[144,384]{1,0:T(8,128)(2,1)S(1)} %collective-permute-done.11.refs_0_), channel_id=1, source_target_pairs={{0,4},{1,5},{2,6},{3,7},{4,0},{5,1},{6,2},{7,3},{8,12},{9,13},{10,... | collective-permute-start | bytes 331784 | tf_op jit(solution)/shard_map/ppermute | solution.py:289
  44.0 4.7 %collective-permute-start.21 = (bf16[144,384]{1,0:T(8,128)(2,1)S(1)}, bf16[144,384]{1,0:T(8,128)(2,1)S(1)}, u32[]{:S(2)}, u32[]{:S(2)}) collective-permute-start(bf16[144,384]{1,0:T(8,128)(2,1)S(1)} %collective-permute-done.14.refs_1_), channel_id=1, source_target_pairs={{0,2},{1,3},{2,0},{3,1},{4,6},{5,7},{6,4},{7,5},{8,10},{9,11},{10,... | collective-permute-start | bytes 331784 | tf_op jit(solution)/shard_map/ppermute | solution.py:289
  46.4 2.4 %collective-permute-start.16 = (bf16[144,384]{1,0:T(8,128)(2,1)S(1)}, bf16[144,384]{1,0:T(8,128)(2,1)S(1)}, u32[]{:S(2)}, u32[]{:S(2)}) collective-permute-start(bf16[144,384]{1,0:T(8,128)(2,1)S(1)} %collective-permute-done.11.refs_0_), channel_id=1, source_target_pairs={{0,1},{1,0},{2,3},{3,2},{4,5},{5,4},{6,7},{7,6},{8,9},{9,8},{10,11... | collective-permute-start | bytes 331784 | tf_op jit(solution)/shard_map/ppermute | solution.py:289
  46.4 2.9 %collective-permute-start.17 = (bf16[144,384]{1,0:T(8,128)(2,1)S(1)}, bf16[144,384]{1,0:T(8,128)(2,1)S(1)}, u32[]{:S(2)}, u32[]{:S(2)}) collective-permute-start(bf16[144,384]{1,0:T(8,128)(2,1)S(1)} %collective-permute-done.12.refs_1_), channel_id=1, source_target_pairs={{0,1},{1,0},{2,3},{3,2},{4,5},{5,4},{6,7},{7,6},{8,9},{9,8},{10,11... | collective-permute-start | bytes 331784 | tf_op jit(solution)/shard_map/ppermute | solution.py:289
  46.9 3.1 %collective-permute-start.18 = (bf16[144,384]{1,0:T(8,128)(2,1)S(1)}, bf16[144,384]{1,0:T(8,128)(2,1)S(1)}, u32[]{:S(2)}, u32[]{:S(2)}) collective-permute-start(bf16[144,384]{1,0:T(8,128)(2,1)S(1)} %collective-permute-done.13.refs_0_), channel_id=1, source_target_pairs={{0,1},{1,0},{2,3},{3,2},{4,5},{5,4},{6,7},{7,6},{8,9},{9,8},{10,11... | collective-permute-start | bytes 331784 | tf_op jit(solution)/shard_map/ppermute | solution.py:289
  48.0 2.0 %collective-permute-start.19 = (bf16[144,384]{1,0:T(8,128)(2,1)S(1)}, bf16[144,384]{1,0:T(8,128)(2,1)S(1)}, u32[]{:S(2)}, u32[]{:S(2)}) collective-permute-start(bf16[144,384]{1,0:T(8,128)(2,1)S(1)} %collective-permute-done.14.refs_1_), channel_id=1, source_target_pairs={{0,1},{1,0},{2,3},{3,2},{4,5},{5,4},{6,7},{7,6},{8,9},{9,8},{10,11... | collective-permute-start | bytes 331784 | tf_op jit(solution)/shard_map/ppermute | solution.py:289
  48.8 1.9 %collective-permute-start.22 = (bf16[144,384]{1,0:T(8,128)(2,1)S(1)}, bf16[144,384]{1,0:T(8,128)(2,1)S(1)}, u32[]{:S(2)}, u32[]{:S(2)}) collective-permute-start(bf16[144,384]{1,0:T(8,128)(2,1)S(1)} %collective-permute-done.20.refs_3_), channel_id=1, source_target_pairs={{0,1},{1,0},{2,3},{3,2},{4,5},{5,4},{6,7},{7,6},{8,9},{9,8},{10,11... | collective-permute-start | bytes 331784 | tf_op jit(solution)/shard_map/ppermute | solution.py:289
  48.8 2.0 %collective-permute-start.23 = (bf16[144,384]{1,0:T(8,128)(2,1)S(1)}, bf16[144,384]{1,0:T(8,128)(2,1)S(1)}, u32[]{:S(2)}, u32[]{:S(2)}) collective-permute-start(bf16[144,384]{1,0:T(8,128)(2,1)S(1)} %collective-permute-done.21.refs_4_), channel_id=1, source_target_pairs={{0,1},{1,0},{2,3},{3,2},{4,5},{5,4},{6,7},{7,6},{8,9},{9,8},{10,11... | collective-permute-start | bytes 331784 | tf_op jit(solution)/shard_map/ppermute | solution.py:289

commit v8 on v7

--- a/solution.py
+++ b/solution.py
@@ -64,9 +64,8 @@
         kv_copies[which].wait()
         for pair in range(heads // 2):
             columns = slice(2 * pair * head_dim, (2 * pair + 2) * head_dim)
-            part = mm(tok[...], wkv[which, :, columns], NN).astype(BF16)
-            if which == 1:
-                part = (part.astype(F32) * flag).astype(BF16)
+            part = mm(tok[...], wkv[which, :, columns], NN)
+            part = (part * flag if which == 1 else part).astype(BF16)
             kv[which, 2 * pair] = part[:, :head_dim]
             kv[which, 2 * pair + 1] = part[:, head_dim:]
     for copy in fast_copies:
@@ -74,7 +73,7 @@
     for head in range(heads):
         both_w[head, :, :hidden] = fast[head, 0].astype(BF16)
         both_w[head, :, hidden:] = fast[head, 1].astype(BF16)
-        down_w[head] = fast[head, 2].astype(BF16)
+        down_w[head] = (-fast[head, 2]).astype(BF16)
     even = core == 0
     chunk = rows
     for head in range(heads):
@@ -83,12 +82,12 @@
             k = kv[0, head, start : start + chunk, :]
             v = kv[1, head, start : start + chunk, :]
             both = mm(k, both_w[head], NN)
-            dhid = -mm(v, down_w[head], NN)
+            dhid = mm(v, down_w[head], NN)
             gate, upper = both[:, :hidden], both[:, hidden:]
             sig = jax.nn.sigmoid(gate)
             act = gate * sig
             hid = (act * upper).astype(BF16)
-            dgate = (dhid * upper * (sig * (1.0 + gate * (1.0 - sig)))).astype(BF16)
+            dgate = (dhid * upper * (sig + act * (1.0 - sig))).astype(BF16)
             dup = (dhid * act).astype(BF16)
             both_part = mm(k, jnp.concatenate([dgate, dup], axis=1), TN)
             down_part = mm(v, hid, TN)
@@ -235,6 +234,15 @@
     out_ref[...] = head_output(core == 0, q_ref[own ^ far], block_refs[:half], block_refs[half:])
 
 
+def apply_two_kernel(q_ref, *refs):
+    *block_refs, near_ref, far_ref = refs
+    count = len(block_refs) // 4
+    own, core = position(q_ref.shape[0])
+    lots = [block_refs[i * count : (i + 1) * count] for i in range(4)]
+    near_ref[...] = head_output(core == 0, q_ref[own ^ 1], lots[0], lots[1])
+    far_ref[...] = head_output(core == 0, q_ref[own ^ 2], lots[2], lots[3])
+
+
 def finish_kernel(q_ref, *refs):
     *piece_refs, first_ref, second_ref, first_there_ref, second_there_ref, out_hbm, pieces, whole, sems = refs
     heads, rows, head_dim = q_ref.shape
@@ -327,7 +335,8 @@
     swapped = lambda blocks: (*blocks, *(exchange(x, 1) for x in blocks))
     piece = apply(0, fresh, exchange(fresh, 1))
     over_y, over_z, piece = lax.optimization_barrier((over_y, over_z, piece))
-    pieces = [piece, apply(1, *swapped(over_y)), apply(2, *swapped(over_z))]
+    args = (query, *swapped(over_y), *swapped(over_z))
+    pieces = [piece, *small(apply_two_kernel, [shape(rows, head_dim)] * 2, args, 40 * rows * head_dim, "apply_two")]
     return finish(query, pieces, swapped(across))
 
 

time: 52.6 us -> 52.1 us (level)
    pallas_call x11 -> x10, Pallas kernels: 5.56 us -> 5.27 us  [small(): pl.pallas_call(kernel, out_shape=shapes, in_specs=specs, compiler_params=...]
where the time goes in v8:
time: 52.1 us; the launch traced here: 51.9 us
  starting transfers between devices  19.6 us (38%)
  Pallas kernels  16.5 us (32%)
  waiting for transfers between devices  14.5 us (28%)
  other arithmetic  1.19 us (2%)
    ppermute x24, starting transfers between devices, exchange(): return lax.ppermute(x, 'tok', [(i, i ^ bits) for i in range(groups)])  19.6 us
    ppermute x24, waiting for transfers between devices, exchange(): return lax.ppermute(x, 'tok', [(i, i ^ bits) for i in range(groups)])  14.5 us
    pallas_call x1, Pallas kernels, gradients(): pl.pallas_call(grad_kernel, out_shape=[shape] * 4, in_specs=[pl.BlockSpec...  7.21 us
    pallas_call x10, Pallas kernels, small(): pl.pallas_call(kernel, out_shape=shapes, in_specs=specs, compiler_params=...  5.27 us
    pallas_call x1, Pallas kernels, project_query(): pl.pallas_call(query_kernel, out_shape=pltpu.VMEM((heads, rows, width //...  2.36 us
    pallas_call x1, Pallas kernels, finish(): pl.pallas_call(finish_kernel, out_shape=jax.ShapeDtypeStruct((rows, heads...  1.7 us
    select_n x1, other arithmetic, shards(): jnp.where(core == 0, lax.dynamic_index_in_dim(w_gate, own, 0, False), lax...  1.19 us
  transfers between devices with their start and end apart: 24, of which 10 were waited for; matrix products, arithmetic and copies ran while one was open for 2% of the time, Pallas kernels for 9%

profile of v8, /device:TPU:0, one launch (start us, length us, event | category | flops | bytes accessed | tf_op | source)
XLA Modules:
  0.0 51.9 jit_solution(5801732561473447508)
XLA Ops:
  0.0 7.2 %gradients.1 = (bf16[4,144,384]{2,1,0:T(8,128)(2,1)S(1)}, bf16[4,144,384]{2,1,0:T(8,128)(2,1)S(1)}, bf16[4,144,384]{2,1,0:T(8,128)(2,1)S(1)}, bf16[4,144,384]{2,1,0:T(8,128)(2,1)S(1)}) custom-call(s32[16]{0:T(128)} %view_hbm.1, bf16[512,768]{1,0:T(8,128)(2,1)} %tokens_ref.1, bf16[768,2304]{1,0:T(8,128)(2,1)} %weight_ref.1, f32[4,192,384]{2,1,0:T(8,128)} %gate_hbm.1, ...), custom_call_target="tpu_custom_call" | custom-call | flops 3019898880 | bytes 6684672 | tf_op jit(solution)/shard_map/gradients/pallas_call | solution.py:112
  7.2 0.5 collective-permute-start
  7.8 1.3 %collective-permute-done.got_ref = bf16[4,144,384]{2,1,0:T(8,128)(2,1)S(1)} collective-permute-done((bf16[4,144,384]{2,1,0:T(8,128)(2,1)S(1)}, bf16[4,144,384]{2,1,0:T(8,128)(2,1)S(1)}, u32[]{:S(2)}, u32[]{:S(2)}) %collective-permute-start) | collective-permute-done | bytes 442400 | tf_op jit(solution)/shard_map/ppermute | solution.py:297
  9.3 3.0 %collective-permute-start.2 = (bf16[144,384]{1,0:T(8,128)(2,1)S(1)}, bf16[144,384]{1,0:T(8,128)(2,1)S(1)}, u32[]{:S(2)}, u32[]{:S(2)}) collective-permute-start(bf16[144,384]{1,0:T(8,128)(2,1)S(1)} %get-tuple-element.36), channel_id=1, source_target_pairs={{0,2},{1,3},{2,0},{3,1},{4,6},{5,7},{6,4},{7,5},{8,10},{9,11},{10,... | collective-permute-start | bytes 331784 | tf_op jit(solution)/shard_map/ppermute | solution.py:297
  12.2 0.1 pair_sum.3
  12.3 1.6 %collective-permute-start.7 = (bf16[144,384]{1,0:T(8,128)(2,1)S(1)}, bf16[144,384]{1,0:T(8,128)(2,1)S(1)}, u32[]{:S(2)}, u32[]{:S(2)}) collective-permute-start(bf16[144,384]{1,0:T(8,128)(2,1)S(1)} %get-tuple-element.44), channel_id=1, source_target_pairs={{0,4},{1,5},{2,6},{3,7},{4,0},{5,1},{6,2},{7,3},{8,12},{9,13},{10,... | collective-permute-start | bytes 331784 | tf_op jit(solution)/shard_map/ppermute | solution.py:297
  14.0 0.5 collective-permute-start.1
  14.5 1.1 %collective-permute-done.2.refs_1_ = bf16[144,384]{1,0:T(8,128)(2,1)S(1)} collective-permute-done((bf16[144,384]{1,0:T(8,128)(2,1)S(1)}, bf16[144,384]{1,0:T(8,128)(2,1)S(1)}, u32[]{:S(2)}, u32[]{:S(2)}) %collective-permute-start.2) | collective-permute-done | bytes 110624 | tf_op jit(solution)/shard_map/ppermute | solution.py:297
  15.6 2.7 %collective-permute-start.3 = (bf16[144,384]{1,0:T(8,128)(2,1)S(1)}, bf16[144,384]{1,0:T(8,128)(2,1)S(1)}, u32[]{:S(2)}, u32[]{:S(2)}) collective-permute-start(bf16[144,384]{1,0:T(8,128)(2,1)S(1)} %pass_sum.2), channel_id=1, source_target_pairs={{0,4},{1,5},{2,6},{3,7},{4,0},{5,1},{6,2},{7,3},{8,12},{9,13},{10,... | collective-permute-start | bytes 331784 | tf_op jit(solution)/shard_map/ppermute | solution.py:297
  18.4 1.6 %collective-permute-start.8 = (bf16[144,384]{1,0:T(8,128)(2,1)S(1)}, bf16[144,384]{1,0:T(8,128)(2,1)S(1)}, u32[]{:S(2)}, u32[]{:S(2)}) collective-permute-start(bf16[144,384]{1,0:T(8,128)(2,1)S(1)} %pass_sum.3), channel_id=1, source_target_pairs={{0,2},{1,3},{2,0},{3,1},{4,6},{5,7},{6,4},{7,5},{8,10},{9,11},{10,... | collective-permute-start | bytes 331784 | tf_op jit(solution)/shard_map/ppermute | solution.py:297
  20.0 1.5 %collective-permute-done.3.refs_2_ = bf16[144,384]{1,0:T(8,128)(2,1)S(1)} collective-permute-done((bf16[144,384]{1,0:T(8,128)(2,1)S(1)}, bf16[144,384]{1,0:T(8,128)(2,1)S(1)}, u32[]{:S(2)}, u32[]{:S(2)}) %collective-permute-start.3) | collective-permute-done | bytes 110624 | tf_op jit(solution)/shard_map/ppermute | solution.py:297
  21.5 2.6 %collective-permute-start.4 = (bf16[144,384]{1,0:T(8,128)(2,1)S(1)}, bf16[144,384]{1,0:T(8,128)(2,1)S(1)}, u32[]{:S(2)}, u32[]{:S(2)}) collective-permute-start(bf16[144,384]{1,0:T(8,128)(2,1)S(1)} %plane_sum.2.mine_ref.first_ref), channel_id=1, source_target_pairs={{0,8},{1,9},{2,10},{3,11},{4,12},{5,13},{6,14},{7,15},{8,0},{9,1},... | collective-permute-start | bytes 331784 | tf_op jit(solution)/shard_map/ppermute | solution.py:297
  24.2 1.2 %fusion = (f32[192,384]{1,0:T(8,128)S(1)}, f32[192,384]{1,0:T(8,128)S(1)}) fusion(f32[4,384,192]{1,2,0:T(8,128)} %param.10, s32[]{:T(128)S(6)} %select_n.18, f32[4,192,384]{2,1,0:T(8,128)} %gate_hbm.1, pred[]{:T(512)S(6)} %eq.3, f32[4,192,384]{2,1,0:T(8,128)} %up_hbm.1), kind=kLoop, calls=%fused_computation.1 | loop fusion | flops 73728 | bytes 1474565 | tf_op jit(solution)/shard_map/jit(_where)/select_n | solution.py:312
  25.4 1.1 %collective-permute-start.9 = (bf16[144,384]{1,0:T(8,128)(2,1)S(1)}, bf16[144,384]{1,0:T(8,128)(2,1)S(1)}, u32[]{:S(2)}, u32[]{:S(2)}) collective-permute-start(bf16[144,384]{1,0:T(8,128)(2,1)S(1)} %plane_sum.3.second_ref), channel_id=1, source_target_pairs={{0,8},{1,9},{2,10},{3,11},{4,12},{5,13},{6,14},{7,15},{8,0},{9,1},... | collective-permute-start | bytes 331784 | tf_op jit(solution)/shard_map/ppermute | solution.py:297
  26.5 2.4 %query.1.q_ref = bf16[4,512,192]{2,1,0:T(8,128)(2,1)S(1)} custom-call(bf16[512,768]{1,0:T(8,128)(2,1)} %tokens_ref.1, bf16[768,2304]{1,0:T(8,128)(2,1)} %weight_ref.1), custom_call_target="tpu_custom_call" | custom-call | flops 603979776 | bytes 3932160 | tf_op jit(solution)/shard_map/query/pallas_call | solution.py:159
  28.9 1.8 %collective-permute-done.4.other_ref.first_other_ref = bf16[144,384]{1,0:T(8,128)(2,1)S(1)} collective-permute-done((bf16[144,384]{1,0:T(8,128)(2,1)S(1)}, bf16[144,384]{1,0:T(8,128)(2,1)S(1)}, u32[]{:S(2)}, u32[]{:S(2)}) %collective-permute-start.4) | collective-permute-done | bytes 110624 | tf_op jit(solution)/shard_map/ppermute | solution.py:297
  30.8 2.3 %collective-permute-done.9.second_other_ref = bf16[144,384]{1,0:T(8,128)(2,1)S(1)} collective-permute-done((bf16[144,384]{1,0:T(8,128)(2,1)S(1)}, bf16[144,384]{1,0:T(8,128)(2,1)S(1)}, u32[]{:S(2)}, u32[]{:S(2)}) %collective-permute-start.9) | collective-permute-done | bytes 110624 | tf_op jit(solution)/shard_map/ppermute | solution.py:297
  33.2 3.1 %newton.1 = (bf16[288,384]{1,0:T(8,128)(2,1)S(1)}, bf16[144,384]{1,0:T(8,128)(2,1)S(1)}, bf16[144,384]{1,0:T(8,128)(2,1)S(1)}) custom-call(bf16[144,384]{1,0:T(8,128)(2,1)S(1)} %plane_sum.2.mine_ref.first_ref, bf16[144,384]{1,0:T(8,128)(2,1)S(1)} %collective-permute-done.4.other_ref.first_other_ref, bf16[144,384]{1,0:T(8,128)(2,1)S(1)} %plane_sum.3.second_ref, ...), custom_call_target="tpu_custom_call" | custom-call | bytes 2211840 | tf_op jit(solution)/shard_map/newton/pallas_call | solution.py:140
  36.3 1.6 %collective-permute-start.11 = (bf16[144,384]{1,0:T(8,128)(2,1)S(1)}, bf16[144,384]{1,0:T(8,128)(2,1)S(1)}, u32[]{:S(2)}, u32[]{:S(2)}) collective-permute-start(bf16[144,384]{1,0:T(8,128)(2,1)S(1)} %get-tuple-element.47), channel_id=1, source_target_pairs={{0,2},{1,3},{2,0},{3,1},{4,6},{5,7},{6,4},{7,5},{8,10},{9,11},{10,... | collective-permute-start | bytes 331784 | tf_op jit(solution)/shard_map/ppermute | solution.py:297
  37.9 0.5 collective-permute-start.12
  38.4 2.0 %collective-permute-start.13 = (bf16[144,384]{1,0:T(8,128)(2,1)S(1)}, bf16[144,384]{1,0:T(8,128)(2,1)S(1)}, u32[]{:S(2)}, u32[]{:S(2)}) collective-permute-start(bf16[144,384]{1,0:T(8,128)(2,1)S(1)} %get-tuple-element.47), channel_id=1, source_target_pairs={{0,4},{1,5},{2,6},{3,7},{4,0},{5,1},{6,2},{7,3},{8,12},{9,13},{10,... | collective-permute-start | bytes 331784 | tf_op jit(solution)/shard_map/ppermute | solution.py:297
  40.4 1.8 %collective-permute-done.11.refs_0_ = bf16[144,384]{1,0:T(8,128)(2,1)S(1)} collective-permute-done((bf16[144,384]{1,0:T(8,128)(2,1)S(1)}, bf16[144,384]{1,0:T(8,128)(2,1)S(1)}, u32[]{:S(2)}, u32[]{:S(2)}) %collective-permute-start.11) | collective-permute-done | bytes 110624 | tf_op jit(solution)/shard_map/ppermute | solution.py:297
  42.2 1.6 %collective-permute-done.14.refs_5_ = bf16[144,384]{1,0:T(8,128)(2,1)S(1)} collective-permute-done((bf16[144,384]{1,0:T(8,128)(2,1)S(1)}, bf16[144,384]{1,0:T(8,128)(2,1)S(1)}, u32[]{:S(2)}, u32[]{:S(2)}) %collective-permute-start.14) | collective-permute-done | bytes 110624 | tf_op jit(solution)/shard_map/ppermute | solution.py:297
  43.8 0.5 collective-permute-start.21
  44.3 0.7 %apply.1.refs_0_ = bf16[512,192]{1,0:T(8,128)(2,1)S(1)} custom-call(bf16[4,512,192]{2,1,0:T(8,128)(2,1)S(1)} %query.1.q_ref, bf16[288,384]{1,0:T(8,128)(2,1)S(1)} %get-tuple-element.49.refs_0_, bf16[288,384]{1,0:T(8,128)(2,1)S(1)} %collective-permute-done.15.refs_1_), custom_call_target="tpu_custom_call" | custom-call | bytes 1966080 | tf_op jit(solution)/shard_map/apply/pallas_call | solution.py:140
  45.0 1.1 %collective-permute-done.13.refs_4_ = bf16[144,384]{1,0:T(8,128)(2,1)S(1)} collective-permute-done((bf16[144,384]{1,0:T(8,128)(2,1)S(1)}, bf16[144,384]{1,0:T(8,128)(2,1)S(1)}, u32[]{:S(2)}, u32[]{:S(2)}) %collective-permute-start.13) | collective-permute-done | bytes 110624 | tf_op jit(solution)/shard_map/ppermute | solution.py:297
  46.2 0.5 collective-permute-start.17
  46.7 1.1 %collective-permute-done.20.refs_3_ = bf16[144,384]{1,0:T(8,128)(2,1)S(1)} collective-permute-done((bf16[144,384]{1,0:T(8,128)(2,1)S(1)}, bf16[144,384]{1,0:T(8,128)(2,1)S(1)}, u32[]{:S(2)}, u32[]{:S(2)}) %collective-permute-start.20) | collective-permute-done | bytes 110624 | tf_op jit(solution)/shard_map/ppermute | solution.py:297
  47.8 0.8 %collective-permute-done.21.refs_4_ = bf16[144,384]{1,0:T(8,128)(2,1)S(1)} collective-permute-done((bf16[144,384]{1,0:T(8,128)(2,1)S(1)}, bf16[144,384]{1,0:T(8,128)(2,1)S(1)}, u32[]{:S(2)}, u32[]{:S(2)}) %collective-permute-start.21) | collective-permute-done | bytes 110624 | tf_op jit(solution)/shard_map/ppermute | solution.py:297
  48.6 0.5 collective-permute-start.23
  49.1 1.1 %apply_two.1 = (bf16[512,192]{1,0:T(8,128)(2,1)S(1)}, bf16[512,192]{1,0:T(8,128)(2,1)S(1)}) custom-call(bf16[4,512,192]{2,1,0:T(8,128)(2,1)S(1)} %query.1.q_ref, bf16[144,384]{1,0:T(8,128)(2,1)S(1)} %collective-permute-done.11.refs_0_, bf16[144,384]{1,0:T(8,128)(2,1)S(1)} %collective-permute-done.12.refs_1_, ...), custom_call_target="tpu_custom_call" | custom-call | bytes 3932160 | tf_op jit(solution)/shard_map/apply_two/pallas_call | solution.py:140
  50.2 1.7 %finish.1 = bf16[512,768]{1,0:T(8,128)(2,1)} custom-call(bf16[4,512,192]{2,1,0:T(8,128)(2,1)S(1)} %query.1.q_ref, bf16[512,192]{1,0:T(8,128)(2,1)S(1)} %apply.1.refs_0_, bf16[512,192]{1,0:T(8,128)(2,1)S(1)} %get-tuple-element.55.refs_1_, bf16[512,192]{1,0:T(8,128)(2,1)S(1)} %get-tuple-element.56.refs_2_, ...), custom_call_target="tpu_custom_call" | custom-call | tf_op jit(solution)/shard_map/finish/pallas_call | solution.py:269
  (30 shorter events, 0.7 us)
Async XLA Ops:
  7.2 1.9 %collective-permute-start = (bf16[4,144,384]{2,1,0:T(8,128)(2,1)S(1)}, bf16[4,144,384]{2,1,0:T(8,128)(2,1)S(1)}, u32[]{:S(2)}, u32[]{:S(2)}) collective-permute-start(bf16[4,144,384]{2,1,0:T(8,128)(2,1)S(1)} %get-tuple-element.32), channel_id=1, source_target_pairs={{0,1},{1,0},{2,3},{3,2},{4,5},{5,4},{6,7},{7,6},{8,9},{9,8},{10,11... | collective-permute-start | bytes 1327112 | tf_op jit(solution)/shard_map/ppermute | solution.py:297
  7.7 4.5 %collective-permute-start.5 = (bf16[4,144,384]{2,1,0:T(8,128)(2,1)S(1)}, bf16[4,144,384]{2,1,0:T(8,128)(2,1)S(1)}, u32[]{:S(2)}, u32[]{:S(2)}) collective-permute-start(bf16[4,144,384]{2,1,0:T(8,128)(2,1)S(1)} %get-tuple-element.40), channel_id=1, source_target_pairs={{0,1},{1,0},{2,3},{3,2},{4,5},{5,4},{6,7},{7,6},{8,9},{9,8},{10,11... | collective-permute-start | bytes 1327112 | tf_op jit(solution)/shard_map/ppermute | solution.py:297
  9.3 6.3 %collective-permute-start.2 = (bf16[144,384]{1,0:T(8,128)(2,1)S(1)}, bf16[144,384]{1,0:T(8,128)(2,1)S(1)}, u32[]{:S(2)}, u32[]{:S(2)}) collective-permute-start(bf16[144,384]{1,0:T(8,128)(2,1)S(1)} %get-tuple-element.36), channel_id=1, source_target_pairs={{0,2},{1,3},{2,0},{3,1},{4,6},{5,7},{6,4},{7,5},{8,10},{9,11},{10,... | collective-permute-start | bytes 331784 | tf_op jit(solution)/shard_map/ppermute | solution.py:297
  12.3 6.1 %collective-permute-start.7 = (bf16[144,384]{1,0:T(8,128)(2,1)S(1)}, bf16[144,384]{1,0:T(8,128)(2,1)S(1)}, u32[]{:S(2)}, u32[]{:S(2)}) collective-permute-start(bf16[144,384]{1,0:T(8,128)(2,1)S(1)} %get-tuple-element.44), channel_id=1, source_target_pairs={{0,4},{1,5},{2,6},{3,7},{4,0},{5,1},{6,2},{7,3},{8,12},{9,13},{10,... | collective-permute-start | bytes 331784 | tf_op jit(solution)/shard_map/ppermute | solution.py:297
  14.0 6.0 %collective-permute-start.1 = (bf16[144,384]{1,0:T(8,128)(2,1)S(1)}, bf16[144,384]{1,0:T(8,128)(2,1)S(1)}, u32[]{:S(2)}, u32[]{:S(2)}) collective-permute-start(bf16[144,384]{1,0:T(8,128)(2,1)S(1)} %get-tuple-element.34), channel_id=1, source_target_pairs={{0,2},{1,3},{2,0},{3,1},{4,6},{5,7},{6,4},{7,5},{8,10},{9,11},{10,... | collective-permute-start | bytes 331784 | tf_op jit(solution)/shard_map/ppermute | solution.py:297
  15.6 5.9 %collective-permute-start.3 = (bf16[144,384]{1,0:T(8,128)(2,1)S(1)}, bf16[144,384]{1,0:T(8,128)(2,1)S(1)}, u32[]{:S(2)}, u32[]{:S(2)}) collective-permute-start(bf16[144,384]{1,0:T(8,128)(2,1)S(1)} %pass_sum.2), channel_id=1, source_target_pairs={{0,4},{1,5},{2,6},{3,7},{4,0},{5,1},{6,2},{7,3},{8,12},{9,13},{10,... | collective-permute-start | bytes 331784 | tf_op jit(solution)/shard_map/ppermute | solution.py:297
  18.3 7.1 %collective-permute-start.6 = (bf16[144,384]{1,0:T(8,128)(2,1)S(1)}, bf16[144,384]{1,0:T(8,128)(2,1)S(1)}, u32[]{:S(2)}, u32[]{:S(2)}) collective-permute-start(bf16[144,384]{1,0:T(8,128)(2,1)S(1)} %get-tuple-element.42), channel_id=1, source_target_pairs={{0,4},{1,5},{2,6},{3,7},{4,0},{5,1},{6,2},{7,3},{8,12},{9,13},{10,... | collective-permute-start | bytes 331784 | tf_op jit(solution)/shard_map/ppermute | solution.py:297
  18.4 6.9 %collective-permute-start.8 = (bf16[144,384]{1,0:T(8,128)(2,1)S(1)}, bf16[144,384]{1,0:T(8,128)(2,1)S(1)}, u32[]{:S(2)}, u32[]{:S(2)}) collective-permute-start(bf16[144,384]{1,0:T(8,128)(2,1)S(1)} %pass_sum.3), channel_id=1, source_target_pairs={{0,2},{1,3},{2,0},{3,1},{4,6},{5,7},{6,4},{7,5},{8,10},{9,11},{10,... | collective-permute-start | bytes 331784 | tf_op jit(solution)/shard_map/ppermute | solution.py:297
  21.5 9.2 %collective-permute-start.4 = (bf16[144,384]{1,0:T(8,128)(2,1)S(1)}, bf16[144,384]{1,0:T(8,128)(2,1)S(1)}, u32[]{:S(2)}, u32[]{:S(2)}) collective-permute-start(bf16[144,384]{1,0:T(8,128)(2,1)S(1)} %plane_sum.2.mine_ref.first_ref), channel_id=1, source_target_pairs={{0,8},{1,9},{2,10},{3,11},{4,12},{5,13},{6,14},{7,15},{8,0},{9,1},... | collective-permute-start | bytes 331784 | tf_op jit(solution)/shard_map/ppermute | solution.py:297
  25.4 7.7 %collective-permute-start.9 = (bf16[144,384]{1,0:T(8,128)(2,1)S(1)}, bf16[144,384]{1,0:T(8,128)(2,1)S(1)}, u32[]{:S(2)}, u32[]{:S(2)}) collective-permute-start(bf16[144,384]{1,0:T(8,128)(2,1)S(1)} %plane_sum.3.second_ref), channel_id=1, source_target_pairs={{0,8},{1,9},{2,10},{3,11},{4,12},{5,13},{6,14},{7,15},{8,0},{9,1},... | collective-permute-start | bytes 331784 | tf_op jit(solution)/shard_map/ppermute | solution.py:297
  30.8 2.4 %collective-permute-start.10 = (bf16[96,384]{1,0:T(8,128)(2,1)S(1)}, bf16[96,384]{1,0:T(8,128)(2,1)S(1)}, u32[]{:S(2)}, u32[]{:S(2)}) collective-permute-start(bf16[96,384]{1,0:T(8,128)(2,1)S(1)} %up_sum.1.half_ref), channel_id=1, source_target_pairs={{0,1},{1,0},{2,3},{3,2},{4,5},{5,4},{6,7},{7,6},{8,9},{9,8},{10,11... | collective-permute-start | bytes 221192 | tf_op jit(solution)/shard_map/ppermute | solution.py:297
  36.2 8.1 %collective-permute-start.15 = (bf16[288,384]{1,0:T(8,128)(2,1)S(1)}, bf16[288,384]{1,0:T(8,128)(2,1)S(1)}, u32[]{:S(2)}, u32[]{:S(2)}) collective-permute-start(bf16[288,384]{1,0:T(8,128)(2,1)S(1)} %get-tuple-element.49.refs_0_), channel_id=1, source_target_pairs={{0,1},{1,0},{2,3},{3,2},{4,5},{5,4},{6,7},{7,6},{8,9},{9,8},{10,11... | collective-permute-start | bytes 663560 | tf_op jit(solution)/shard_map/ppermute | solution.py:297
  36.3 5.9 %collective-permute-start.11 = (bf16[144,384]{1,0:T(8,128)(2,1)S(1)}, bf16[144,384]{1,0:T(8,128)(2,1)S(1)}, u32[]{:S(2)}, u32[]{:S(2)}) collective-permute-start(bf16[144,384]{1,0:T(8,128)(2,1)S(1)} %get-tuple-element.47), channel_id=1, source_target_pairs={{0,2},{1,3},{2,0},{3,1},{4,6},{5,7},{6,4},{7,5},{8,10},{9,11},{10,... | collective-permute-start | bytes 331784 | tf_op jit(solution)/shard_map/ppermute | solution.py:297
  37.9 5.9 %collective-permute-start.14 = (bf16[144,384]{1,0:T(8,128)(2,1)S(1)}, bf16[144,384]{1,0:T(8,128)(2,1)S(1)}, u32[]{:S(2)}, u32[]{:S(2)}) collective-permute-start(bf16[144,384]{1,0:T(8,128)(2,1)S(1)} %get-tuple-element.48), channel_id=1, source_target_pairs={{0,4},{1,5},{2,6},{3,7},{4,0},{5,1},{6,2},{7,3},{8,12},{9,13},{10,... | collective-permute-start | bytes 331784 | tf_op jit(solution)/shard_map/ppermute | solution.py:297
  37.9 7.1 %collective-permute-start.12 = (bf16[144,384]{1,0:T(8,128)(2,1)S(1)}, bf16[144,384]{1,0:T(8,128)(2,1)S(1)}, u32[]{:S(2)}, u32[]{:S(2)}) collective-permute-start(bf16[144,384]{1,0:T(8,128)(2,1)S(1)} %get-tuple-element.48), channel_id=1, source_target_pairs={{0,2},{1,3},{2,0},{3,1},{4,6},{5,7},{6,4},{7,5},{8,10},{9,11},{10,... | collective-permute-start | bytes 331784 | tf_op jit(solution)/shard_map/ppermute | solution.py:297
  38.4 7.8 %collective-permute-start.13 = (bf16[144,384]{1,0:T(8,128)(2,1)S(1)}, bf16[144,384]{1,0:T(8,128)(2,1)S(1)}, u32[]{:S(2)}, u32[]{:S(2)}) collective-permute-start(bf16[144,384]{1,0:T(8,128)(2,1)S(1)} %get-tuple-element.47), channel_id=1, source_target_pairs={{0,4},{1,5},{2,6},{3,7},{4,0},{5,1},{6,2},{7,3},{8,12},{9,13},{10,... | collective-permute-start | bytes 331784 | tf_op jit(solution)/shard_map/ppermute | solution.py:297
  42.2 5.5 %collective-permute-start.20 = (bf16[144,384]{1,0:T(8,128)(2,1)S(1)}, bf16[144,384]{1,0:T(8,128)(2,1)S(1)}, u32[]{:S(2)}, u32[]{:S(2)}) collective-permute-start(bf16[144,384]{1,0:T(8,128)(2,1)S(1)} %collective-permute-done.11.refs_0_), channel_id=1, source_target_pairs={{0,4},{1,5},{2,6},{3,7},{4,0},{5,1},{6,2},{7,3},{8,12},{9,13},{10,... | collective-permute-start | bytes 331784 | tf_op jit(solution)/shard_map/ppermute | solution.py:297
  43.8 4.7 %collective-permute-start.21 = (bf16[144,384]{1,0:T(8,128)(2,1)S(1)}, bf16[144,384]{1,0:T(8,128)(2,1)S(1)}, u32[]{:S(2)}, u32[]{:S(2)}) collective-permute-start(bf16[144,384]{1,0:T(8,128)(2,1)S(1)} %collective-permute-done.14.refs_5_), channel_id=1, source_target_pairs={{0,2},{1,3},{2,0},{3,1},{4,6},{5,7},{6,4},{7,5},{8,10},{9,11},{10,... | collective-permute-start | bytes 331784 | tf_op jit(solution)/shard_map/ppermute | solution.py:297
  46.2 2.4 %collective-permute-start.16 = (bf16[144,384]{1,0:T(8,128)(2,1)S(1)}, bf16[144,384]{1,0:T(8,128)(2,1)S(1)}, u32[]{:S(2)}, u32[]{:S(2)}) collective-permute-start(bf16[144,384]{1,0:T(8,128)(2,1)S(1)} %collective-permute-done.11.refs_0_), channel_id=1, source_target_pairs={{0,1},{1,0},{2,3},{3,2},{4,5},{5,4},{6,7},{7,6},{8,9},{9,8},{10,11... | collective-permute-start | bytes 331784 | tf_op jit(solution)/shard_map/ppermute | solution.py:297
  46.2 2.9 %collective-permute-start.17 = (bf16[144,384]{1,0:T(8,128)(2,1)S(1)}, bf16[144,384]{1,0:T(8,128)(2,1)S(1)}, u32[]{:S(2)}, u32[]{:S(2)}) collective-permute-start(bf16[144,384]{1,0:T(8,128)(2,1)S(1)} %collective-permute-done.12.refs_1_), channel_id=1, source_target_pairs={{0,1},{1,0},{2,3},{3,2},{4,5},{5,4},{6,7},{7,6},{8,9},{9,8},{10,11... | collective-permute-start | bytes 331784 | tf_op jit(solution)/shard_map/ppermute | solution.py:297
  46.7 2.4 %collective-permute-start.18 = (bf16[144,384]{1,0:T(8,128)(2,1)S(1)}, bf16[144,384]{1,0:T(8,128)(2,1)S(1)}, u32[]{:S(2)}, u32[]{:S(2)}) collective-permute-start(bf16[144,384]{1,0:T(8,128)(2,1)S(1)} %collective-permute-done.13.refs_4_), channel_id=1, source_target_pairs={{0,1},{1,0},{2,3},{3,2},{4,5},{5,4},{6,7},{7,6},{8,9},{9,8},{10,11... | collective-permute-start | bytes 331784 | tf_op jit(solution)/shard_map/ppermute | solution.py:297
  47.8 1.3 %collective-permute-start.19 = (bf16[144,384]{1,0:T(8,128)(2,1)S(1)}, bf16[144,384]{1,0:T(8,128)(2,1)S(1)}, u32[]{:S(2)}, u32[]{:S(2)}) collective-permute-start(bf16[144,384]{1,0:T(8,128)(2,1)S(1)} %collective-permute-done.14.refs_5_), channel_id=1, source_target_pairs={{0,1},{1,0},{2,3},{3,2},{4,5},{5,4},{6,7},{7,6},{8,9},{9,8},{10,11... | collective-permute-start | bytes 331784 | tf_op jit(solution)/shard_map/ppermute | solution.py:297
  48.6 1.6 %collective-permute-start.22 = (bf16[144,384]{1,0:T(8,128)(2,1)S(1)}, bf16[144,384]{1,0:T(8,128)(2,1)S(1)}, u32[]{:S(2)}, u32[]{:S(2)}) collective-permute-start(bf16[144,384]{1,0:T(8,128)(2,1)S(1)} %collective-permute-done.20.refs_3_), channel_id=1, source_target_pairs={{0,1},{1,0},{2,3},{3,2},{4,5},{5,4},{6,7},{7,6},{8,9},{9,8},{10,11... | collective-permute-start | bytes 331784 | tf_op jit(solution)/shard_map/ppermute | solution.py:297
  48.6 1.7 %collective-permute-start.23 = (bf16[144,384]{1,0:T(8,128)(2,1)S(1)}, bf16[144,384]{1,0:T(8,128)(2,1)S(1)}, u32[]{:S(2)}, u32[]{:S(2)}) collective-permute-start(bf16[144,384]{1,0:T(8,128)(2,1)S(1)} %collective-permute-done.21.refs_4_), channel_id=1, source_target_pairs={{0,1},{1,0},{2,3},{3,2},{4,5},{5,4},{6,7},{7,6},{8,9},{9,8},{10,11... | collective-permute-start | bytes 331784 | tf_op jit(solution)/shard_map/ppermute | solution.py:297

commit v9 on v8

--- a/solution.py
+++ b/solution.py
@@ -234,30 +234,34 @@
     out_ref[...] = head_output(core == 0, q_ref[own ^ far], block_refs[:half], block_refs[half:])
 
 
-def apply_two_kernel(q_ref, *refs):
-    *block_refs, near_ref, far_ref = refs
+def beside(even_head, a, b):
+    return jnp.concatenate([jnp.where(even_head, a, b), jnp.where(even_head, b, a)], axis=1)
+
+
+def apply_two_kernel(q_ref, piece_ref, *refs):
+    *block_refs, pair_ref, far_ref = refs
     count = len(block_refs) // 4
     own, core = position(q_ref.shape[0])
     lots = [block_refs[i * count : (i + 1) * count] for i in range(4)]
-    near_ref[...] = head_output(core == 0, q_ref[own ^ 1], lots[0], lots[1])
+    near = head_output(core == 0, q_ref[own ^ 1], lots[0], lots[1])
+    pair_ref[...] = beside(lax.rem(own, 2) == 0, piece_ref[...], near)
     far_ref[...] = head_output(core == 0, q_ref[own ^ 2], lots[2], lots[3])
 
 
-def finish_kernel(q_ref, *refs):
-    *piece_refs, first_ref, second_ref, first_there_ref, second_there_ref, out_hbm, pieces, whole, sems = refs
+def finish_kernel(q_ref, pair_ref, far_ref, first_ref, second_ref, first_there_ref, second_there_ref, out_hbm, other, sems):
     heads, rows, head_dim = q_ref.shape
     own, core = position(heads)
+    pair = lax.div(own, 2)
     lot = rows // FINISH_LOTS
-    copies = []
+    columns = [pl.ds(pl.multiple_of(p * 2 * head_dim, 128), 2 * head_dim) for p in (pair, pair ^ 1)]
+    copies = [pltpu.make_async_copy(pair_ref, out_hbm.at[:, columns[0]], sems.at[FINISH_LOTS])]
+    copies[0].start()
     for index in range(FINISH_LOTS):
         part = pl.ds(index * lot, lot)
-        for far, piece_ref in enumerate(piece_refs):
-            pieces[far, part] = piece_ref[part]
         q = q_ref[own ^ (heads - 1), part]
-        pieces[heads - 1, part] = head_output(core == 0, q, (first_ref, second_ref), (first_there_ref, second_there_ref))
-        for head in range(heads):
-            whole[part, head * head_dim : (head + 1) * head_dim] = pieces[own ^ head, part]
-        copies.append(pltpu.make_async_copy(whole.at[part], out_hbm.at[part], sems.at[index]))
+        last = head_output(core == 0, q, (first_ref, second_ref), (first_there_ref, second_there_ref))
+        other[part] = beside(lax.rem(own, 2) == 0, far_ref[part], last)
+        copies.append(pltpu.make_async_copy(other.at[part], out_hbm.at[part, columns[1]], sems.at[index]))
         copies[-1].start()
     for copy in copies:
         copy.wait()
@@ -272,9 +276,8 @@
         in_specs=[pl.BlockSpec(memory_space=pltpu.VMEM)] * len(operands),
         out_specs=pl.BlockSpec(memory_space=pl.ANY),
         scratch_shapes=[
-            pltpu.VMEM((heads, rows, head_dim), BF16),
-            pltpu.VMEM((rows, heads * head_dim), BF16),
-            pltpu.SemaphoreType.DMA((FINISH_LOTS,)),
+            pltpu.VMEM((rows, 2 * head_dim), BF16),
+            pltpu.SemaphoreType.DMA((FINISH_LOTS + 1,)),
         ],
         compiler_params=pltpu.CompilerParams(vmem_limit_bytes=SMALL_LIMIT * 1024 * 1024),
         name="finish",
@@ -335,8 +338,9 @@
     swapped = lambda blocks: (*blocks, *(exchange(x, 1) for x in blocks))
     piece = apply(0, fresh, exchange(fresh, 1))
     over_y, over_z, piece = lax.optimization_barrier((over_y, over_z, piece))
-    args = (query, *swapped(over_y), *swapped(over_z))
-    pieces = [piece, *small(apply_two_kernel, [shape(rows, head_dim)] * 2, args, 40 * rows * head_dim, "apply_two")]
+    args = (query, piece, *swapped(over_y), *swapped(over_z))
+    shapes = [shape(rows, 2 * head_dim), shape(rows, head_dim)]
+    pieces = small(apply_two_kernel, shapes, args, 40 * rows * head_dim, "apply_two")
     return finish(query, pieces, swapped(across))
 
 

time: 52.1 us -> 51.9 us (level)
  no operation moved by 1% of the time
where the time goes in v9:
time: 51.9 us; the launch traced here: 51.8 us
  starting transfers between devices  19.6 us (38%)
  Pallas kernels  16.4 us (32%)
  waiting for transfers between devices  14.5 us (28%)
  other arithmetic  1.19 us (2%)
    ppermute x24, starting transfers between devices, exchange(): return lax.ppermute(x, 'tok', [(i, i ^ bits) for i in range(groups)])  19.6 us
    ppermute x24, waiting for transfers between devices, exchange(): return lax.ppermute(x, 'tok', [(i, i ^ bits) for i in range(groups)])  14.5 us
    pallas_call x1, Pallas kernels, gradients(): pl.pallas_call(grad_kernel, out_shape=[shape] * 4, in_specs=[pl.BlockSpec...  7.21 us
    pallas_call x10, Pallas kernels, small(): pl.pallas_call(kernel, out_shape=shapes, in_specs=specs, compiler_params=...  5.26 us
    pallas_call x1, Pallas kernels, project_query(): pl.pallas_call(query_kernel, out_shape=pltpu.VMEM((heads, rows, width //...  2.36 us
    pallas_call x1, Pallas kernels, finish(): pl.pallas_call(finish_kernel, out_shape=jax.ShapeDtypeStruct((rows, heads...  1.53 us
    select_n x1, other arithmetic, shards(): jnp.where(core == 0, lax.dynamic_index_in_dim(w_gate, own, 0, False), lax...  1.19 us
  transfers between devices with their start and end apart: 24, of which 10 were waited for; matrix products, arithmetic and copies ran while one was open for 2% of the time, Pallas kernels for 9%

profile of v9, /device:TPU:0, one launch (start us, length us, event | category | flops | bytes accessed | tf_op | source)
XLA Modules:
  0.0 51.8 jit_solution(4617997124273810811)
XLA Ops:
  0.0 7.2 %gradients.1 = (bf16[4,144,384]{2,1,0:T(8,128)(2,1)S(1)}, bf16[4,144,384]{2,1,0:T(8,128)(2,1)S(1)}, bf16[4,144,384]{2,1,0:T(8,128)(2,1)S(1)}, bf16[4,144,384]{2,1,0:T(8,128)(2,1)S(1)}) custom-call(s32[16]{0:T(128)} %view_hbm.1, bf16[512,768]{1,0:T(8,128)(2,1)} %tokens_ref.1, bf16[768,2304]{1,0:T(8,128)(2,1)} %weight_ref.1, f32[4,192,384]{2,1,0:T(8,128)} %gate_hbm.1, ...), custom_call_target="tpu_custom_call" | custom-call | flops 3019898880 | bytes 6684672 | tf_op jit(solution)/shard_map/gradients/pallas_call | solution.py:112
  7.2 0.5 collective-permute-start
  7.8 1.3 %collective-permute-done.got_ref = bf16[4,144,384]{2,1,0:T(8,128)(2,1)S(1)} collective-permute-done((bf16[4,144,384]{2,1,0:T(8,128)(2,1)S(1)}, bf16[4,144,384]{2,1,0:T(8,128)(2,1)S(1)}, u32[]{:S(2)}, u32[]{:S(2)}) %collective-permute-start) | collective-permute-done | bytes 442400 | tf_op jit(solution)/shard_map/ppermute | solution.py:300
  9.3 3.0 %collective-permute-start.2 = (bf16[144,384]{1,0:T(8,128)(2,1)S(1)}, bf16[144,384]{1,0:T(8,128)(2,1)S(1)}, u32[]{:S(2)}, u32[]{:S(2)}) collective-permute-start(bf16[144,384]{1,0:T(8,128)(2,1)S(1)} %get-tuple-element.36), channel_id=1, source_target_pairs={{0,2},{1,3},{2,0},{3,1},{4,6},{5,7},{6,4},{7,5},{8,10},{9,11},{10,... | collective-permute-start | bytes 331784 | tf_op jit(solution)/shard_map/ppermute | solution.py:300
  12.2 0.1 pair_sum.3
  12.3 1.6 %collective-permute-start.7 = (bf16[144,384]{1,0:T(8,128)(2,1)S(1)}, bf16[144,384]{1,0:T(8,128)(2,1)S(1)}, u32[]{:S(2)}, u32[]{:S(2)}) collective-permute-start(bf16[144,384]{1,0:T(8,128)(2,1)S(1)} %get-tuple-element.44), channel_id=1, source_target_pairs={{0,4},{1,5},{2,6},{3,7},{4,0},{5,1},{6,2},{7,3},{8,12},{9,13},{10,... | collective-permute-start | bytes 331784 | tf_op jit(solution)/shard_map/ppermute | solution.py:300
  14.0 0.5 collective-permute-start.1
  14.5 1.1 %collective-permute-done.2.refs_1_ = bf16[144,384]{1,0:T(8,128)(2,1)S(1)} collective-permute-done((bf16[144,384]{1,0:T(8,128)(2,1)S(1)}, bf16[144,384]{1,0:T(8,128)(2,1)S(1)}, u32[]{:S(2)}, u32[]{:S(2)}) %collective-permute-start.2) | collective-permute-done | bytes 110624 | tf_op jit(solution)/shard_map/ppermute | solution.py:300
  15.6 2.7 %collective-permute-start.3 = (bf16[144,384]{1,0:T(8,128)(2,1)S(1)}, bf16[144,384]{1,0:T(8,128)(2,1)S(1)}, u32[]{:S(2)}, u32[]{:S(2)}) collective-permute-start(bf16[144,384]{1,0:T(8,128)(2,1)S(1)} %pass_sum.2), channel_id=1, source_target_pairs={{0,4},{1,5},{2,6},{3,7},{4,0},{5,1},{6,2},{7,3},{8,12},{9,13},{10,... | collective-permute-start | bytes 331784 | tf_op jit(solution)/shard_map/ppermute | solution.py:300
  18.4 1.6 %collective-permute-start.8 = (bf16[144,384]{1,0:T(8,128)(2,1)S(1)}, bf16[144,384]{1,0:T(8,128)(2,1)S(1)}, u32[]{:S(2)}, u32[]{:S(2)}) collective-permute-start(bf16[144,384]{1,0:T(8,128)(2,1)S(1)} %pass_sum.3), channel_id=1, source_target_pairs={{0,2},{1,3},{2,0},{3,1},{4,6},{5,7},{6,4},{7,5},{8,10},{9,11},{10,... | collective-permute-start | bytes 331784 | tf_op jit(solution)/shard_map/ppermute | solution.py:300
  20.0 1.5 %collective-permute-done.3.refs_2_ = bf16[144,384]{1,0:T(8,128)(2,1)S(1)} collective-permute-done((bf16[144,384]{1,0:T(8,128)(2,1)S(1)}, bf16[144,384]{1,0:T(8,128)(2,1)S(1)}, u32[]{:S(2)}, u32[]{:S(2)}) %collective-permute-start.3) | collective-permute-done | bytes 110624 | tf_op jit(solution)/shard_map/ppermute | solution.py:300
  21.5 2.6 %collective-permute-start.4 = (bf16[144,384]{1,0:T(8,128)(2,1)S(1)}, bf16[144,384]{1,0:T(8,128)(2,1)S(1)}, u32[]{:S(2)}, u32[]{:S(2)}) collective-permute-start(bf16[144,384]{1,0:T(8,128)(2,1)S(1)} %plane_sum.2.mine_ref.first_ref), channel_id=1, source_target_pairs={{0,8},{1,9},{2,10},{3,11},{4,12},{5,13},{6,14},{7,15},{8,0},{9,1},... | collective-permute-start | bytes 331784 | tf_op jit(solution)/shard_map/ppermute | solution.py:300
  24.2 1.2 %fusion = (f32[192,384]{1,0:T(8,128)S(1)}, f32[192,384]{1,0:T(8,128)S(1)}) fusion(f32[4,384,192]{1,2,0:T(8,128)} %param.10, s32[]{:T(128)S(6)} %select_n.18, f32[4,192,384]{2,1,0:T(8,128)} %gate_hbm.1, pred[]{:T(512)S(6)} %eq.3, f32[4,192,384]{2,1,0:T(8,128)} %up_hbm.1), kind=kLoop, calls=%fused_computation.1 | loop fusion | flops 73728 | bytes 1474565 | tf_op jit(solution)/shard_map/jit(_where)/select_n | solution.py:315
  25.4 1.1 %collective-permute-start.9 = (bf16[144,384]{1,0:T(8,128)(2,1)S(1)}, bf16[144,384]{1,0:T(8,128)(2,1)S(1)}, u32[]{:S(2)}, u32[]{:S(2)}) collective-permute-start(bf16[144,384]{1,0:T(8,128)(2,1)S(1)} %plane_sum.3.second_ref), channel_id=1, source_target_pairs={{0,8},{1,9},{2,10},{3,11},{4,12},{5,13},{6,14},{7,15},{8,0},{9,1},... | collective-permute-start | bytes 331784 | tf_op jit(solution)/shard_map/ppermute | solution.py:300
  26.5 2.4 %query.1.q_ref = bf16[4,512,192]{2,1,0:T(8,128)(2,1)S(1)} custom-call(bf16[512,768]{1,0:T(8,128)(2,1)} %tokens_ref.1, bf16[768,2304]{1,0:T(8,128)(2,1)} %weight_ref.1), custom_call_target="tpu_custom_call" | custom-call | flops 603979776 | bytes 3932160 | tf_op jit(solution)/shard_map/query/pallas_call | solution.py:159
  28.9 1.8 %collective-permute-done.4.other_ref.first_other_ref = bf16[144,384]{1,0:T(8,128)(2,1)S(1)} collective-permute-done((bf16[144,384]{1,0:T(8,128)(2,1)S(1)}, bf16[144,384]{1,0:T(8,128)(2,1)S(1)}, u32[]{:S(2)}, u32[]{:S(2)}) %collective-permute-start.4) | collective-permute-done | bytes 110624 | tf_op jit(solution)/shard_map/ppermute | solution.py:300
  30.8 2.3 %collective-permute-done.9.second_other_ref = bf16[144,384]{1,0:T(8,128)(2,1)S(1)} collective-permute-done((bf16[144,384]{1,0:T(8,128)(2,1)S(1)}, bf16[144,384]{1,0:T(8,128)(2,1)S(1)}, u32[]{:S(2)}, u32[]{:S(2)}) %collective-permute-start.9) | collective-permute-done | bytes 110624 | tf_op jit(solution)/shard_map/ppermute | solution.py:300
  33.2 3.1 %newton.1 = (bf16[288,384]{1,0:T(8,128)(2,1)S(1)}, bf16[144,384]{1,0:T(8,128)(2,1)S(1)}, bf16[144,384]{1,0:T(8,128)(2,1)S(1)}) custom-call(bf16[144,384]{1,0:T(8,128)(2,1)S(1)} %plane_sum.2.mine_ref.first_ref, bf16[144,384]{1,0:T(8,128)(2,1)S(1)} %collective-permute-done.4.other_ref.first_other_ref, bf16[144,384]{1,0:T(8,128)(2,1)S(1)} %plane_sum.3.second_ref, ...), custom_call_target="tpu_custom_call" | custom-call | bytes 2211840 | tf_op jit(solution)/shard_map/newton/pallas_call | solution.py:140
  36.3 1.6 %collective-permute-start.11 = (bf16[144,384]{1,0:T(8,128)(2,1)S(1)}, bf16[144,384]{1,0:T(8,128)(2,1)S(1)}, u32[]{:S(2)}, u32[]{:S(2)}) collective-permute-start(bf16[144,384]{1,0:T(8,128)(2,1)S(1)} %get-tuple-element.47), channel_id=1, source_target_pairs={{0,2},{1,3},{2,0},{3,1},{4,6},{5,7},{6,4},{7,5},{8,10},{9,11},{10,... | collective-permute-start | bytes 331784 | tf_op jit(solution)/shard_map/ppermute | solution.py:300
  37.9 0.5 collective-permute-start.12
  38.4 2.0 %collective-permute-start.13 = (bf16[144,384]{1,0:T(8,128)(2,1)S(1)}, bf16[144,384]{1,0:T(8,128)(2,1)S(1)}, u32[]{:S(2)}, u32[]{:S(2)}) collective-permute-start(bf16[144,384]{1,0:T(8,128)(2,1)S(1)} %get-tuple-element.47), channel_id=1, source_target_pairs={{0,4},{1,5},{2,6},{3,7},{4,0},{5,1},{6,2},{7,3},{8,12},{9,13},{10,... | collective-permute-start | bytes 331784 | tf_op jit(solution)/shard_map/ppermute | solution.py:300
  40.4 1.8 %collective-permute-done.11.refs_0_ = bf16[144,384]{1,0:T(8,128)(2,1)S(1)} collective-permute-done((bf16[144,384]{1,0:T(8,128)(2,1)S(1)}, bf16[144,384]{1,0:T(8,128)(2,1)S(1)}, u32[]{:S(2)}, u32[]{:S(2)}) %collective-permute-start.11) | collective-permute-done | bytes 110624 | tf_op jit(solution)/shard_map/ppermute | solution.py:300
  42.2 1.6 %collective-permute-done.14.refs_5_ = bf16[144,384]{1,0:T(8,128)(2,1)S(1)} collective-permute-done((bf16[144,384]{1,0:T(8,128)(2,1)S(1)}, bf16[144,384]{1,0:T(8,128)(2,1)S(1)}, u32[]{:S(2)}, u32[]{:S(2)}) %collective-permute-start.14) | collective-permute-done | bytes 110624 | tf_op jit(solution)/shard_map/ppermute | solution.py:300
  43.8 0.5 collective-permute-start.21
  44.3 0.7 %apply.1.piece_ref = bf16[512,192]{1,0:T(8,128)(2,1)S(1)} custom-call(bf16[4,512,192]{2,1,0:T(8,128)(2,1)S(1)} %query.1.q_ref, bf16[288,384]{1,0:T(8,128)(2,1)S(1)} %get-tuple-element.49.refs_0_, bf16[288,384]{1,0:T(8,128)(2,1)S(1)} %collective-permute-done.15.refs_1_), custom_call_target="tpu_custom_call" | custom-call | bytes 1966080 | tf_op jit(solution)/shard_map/apply/pallas_call | solution.py:140
  45.0 1.1 %collective-permute-done.13.refs_4_ = bf16[144,384]{1,0:T(8,128)(2,1)S(1)} collective-permute-done((bf16[144,384]{1,0:T(8,128)(2,1)S(1)}, bf16[144,384]{1,0:T(8,128)(2,1)S(1)}, u32[]{:S(2)}, u32[]{:S(2)}) %collective-permute-start.13) | collective-permute-done | bytes 110624 | tf_op jit(solution)/shard_map/ppermute | solution.py:300
  46.2 0.5 collective-permute-start.17
  46.7 1.1 %collective-permute-done.20.first_ref = bf16[144,384]{1,0:T(8,128)(2,1)S(1)} collective-permute-done((bf16[144,384]{1,0:T(8,128)(2,1)S(1)}, bf16[144,384]{1,0:T(8,128)(2,1)S(1)}, u32[]{:S(2)}, u32[]{:S(2)}) %collective-permute-start.20) | collective-permute-done | bytes 110624 | tf_op jit(solution)/shard_map/ppermute | solution.py:300
  47.8 0.8 %collective-permute-done.21.second_ref = bf16[144,384]{1,0:T(8,128)(2,1)S(1)} collective-permute-done((bf16[144,384]{1,0:T(8,128)(2,1)S(1)}, bf16[144,384]{1,0:T(8,128)(2,1)S(1)}, u32[]{:S(2)}, u32[]{:S(2)}) %collective-permute-start.21) | collective-permute-done | bytes 110624 | tf_op jit(solution)/shard_map/ppermute | solution.py:300
  48.6 0.5 collective-permute-start.23
  49.1 1.1 %apply_two.1 = (bf16[512,384]{1,0:T(8,128)(2,1)S(1)}, bf16[512,192]{1,0:T(8,128)(2,1)S(1)}) custom-call(bf16[4,512,192]{2,1,0:T(8,128)(2,1)S(1)} %query.1.q_ref, bf16[512,192]{1,0:T(8,128)(2,1)S(1)} %apply.1.piece_ref, bf16[144,384]{1,0:T(8,128)(2,1)S(1)} %collective-permute-done.11.refs_0_, bf16[144,384]{1,0:T(8,128)(2,1)S(1)} %collective-permute-done.12.refs_1_, ...), custom_call_target="tpu_custom_call" | custom-call | bytes 3932160 | tf_op jit(solution)/shard_map/apply_two/pallas_call | solution.py:140
  50.2 1.5 %finish.1 = bf16[512,768]{1,0:T(8,128)(2,1)} custom-call(bf16[4,512,192]{2,1,0:T(8,128)(2,1)S(1)} %query.1.q_ref, bf16[512,384]{1,0:T(8,128)(2,1)S(1)} %get-tuple-element.55.pair_ref, bf16[512,192]{1,0:T(8,128)(2,1)S(1)} %get-tuple-element.56.far_ref, bf16[144,384]{1,0:T(8,128)(2,1)S(1)} %collective-permute-done.20.first_ref, ...), custom_call_target="tpu_custom_call" | custom-call | tf_op jit(solution)/shard_map/finish/pallas_call | solution.py:273
  (30 shorter events, 0.7 us)
Async XLA Ops:
  7.2 1.9 %collective-permute-start = (bf16[4,144,384]{2,1,0:T(8,128)(2,1)S(1)}, bf16[4,144,384]{2,1,0:T(8,128)(2,1)S(1)}, u32[]{:S(2)}, u32[]{:S(2)}) collective-permute-start(bf16[4,144,384]{2,1,0:T(8,128)(2,1)S(1)} %get-tuple-element.32), channel_id=1, source_target_pairs={{0,1},{1,0},{2,3},{3,2},{4,5},{5,4},{6,7},{7,6},{8,9},{9,8},{10,11... | collective-permute-start | bytes 1327112 | tf_op jit(solution)/shard_map/ppermute | solution.py:300
  7.7 4.5 %collective-permute-start.5 = (bf16[4,144,384]{2,1,0:T(8,128)(2,1)S(1)}, bf16[4,144,384]{2,1,0:T(8,128)(2,1)S(1)}, u32[]{:S(2)}, u32[]{:S(2)}) collective-permute-start(bf16[4,144,384]{2,1,0:T(8,128)(2,1)S(1)} %get-tuple-element.40), channel_id=1, source_target_pairs={{0,1},{1,0},{2,3},{3,2},{4,5},{5,4},{6,7},{7,6},{8,9},{9,8},{10,11... | collective-permute-start | bytes 1327112 | tf_op jit(solution)/shard_map/ppermute | solution.py:300
  9.3 6.3 %collective-permute-start.2 = (bf16[144,384]{1,0:T(8,128)(2,1)S(1)}, bf16[144,384]{1,0:T(8,128)(2,1)S(1)}, u32[]{:S(2)}, u32[]{:S(2)}) collective-permute-start(bf16[144,384]{1,0:T(8,128)(2,1)S(1)} %get-tuple-element.36), channel_id=1, source_target_pairs={{0,2},{1,3},{2,0},{3,1},{4,6},{5,7},{6,4},{7,5},{8,10},{9,11},{10,... | collective-permute-start | bytes 331784 | tf_op jit(solution)/shard_map/ppermute | solution.py:300
  12.3 6.1 %collective-permute-start.7 = (bf16[144,384]{1,0:T(8,128)(2,1)S(1)}, bf16[144,384]{1,0:T(8,128)(2,1)S(1)}, u32[]{:S(2)}, u32[]{:S(2)}) collective-permute-start(bf16[144,384]{1,0:T(8,128)(2,1)S(1)} %get-tuple-element.44), channel_id=1, source_target_pairs={{0,4},{1,5},{2,6},{3,7},{4,0},{5,1},{6,2},{7,3},{8,12},{9,13},{10,... | collective-permute-start | bytes 331784 | tf_op jit(solution)/shard_map/ppermute | solution.py:300
  14.0 6.0 %collective-permute-start.1 = (bf16[144,384]{1,0:T(8,128)(2,1)S(1)}, bf16[144,384]{1,0:T(8,128)(2,1)S(1)}, u32[]{:S(2)}, u32[]{:S(2)}) collective-permute-start(bf16[144,384]{1,0:T(8,128)(2,1)S(1)} %get-tuple-element.34), channel_id=1, source_target_pairs={{0,2},{1,3},{2,0},{3,1},{4,6},{5,7},{6,4},{7,5},{8,10},{9,11},{10,... | collective-permute-start | bytes 331784 | tf_op jit(solution)/shard_map/ppermute | solution.py:300
  15.6 5.9 %collective-permute-start.3 = (bf16[144,384]{1,0:T(8,128)(2,1)S(1)}, bf16[144,384]{1,0:T(8,128)(2,1)S(1)}, u32[]{:S(2)}, u32[]{:S(2)}) collective-permute-start(bf16[144,384]{1,0:T(8,128)(2,1)S(1)} %pass_sum.2), channel_id=1, source_target_pairs={{0,4},{1,5},{2,6},{3,7},{4,0},{5,1},{6,2},{7,3},{8,12},{9,13},{10,... | collective-permute-start | bytes 331784 | tf_op jit(solution)/shard_map/ppermute | solution.py:300
  18.3 7.1 %collective-permute-start.6 = (bf16[144,384]{1,0:T(8,128)(2,1)S(1)}, bf16[144,384]{1,0:T(8,128)(2,1)S(1)}, u32[]{:S(2)}, u32[]{:S(2)}) collective-permute-start(bf16[144,384]{1,0:T(8,128)(2,1)S(1)} %get-tuple-element.42), channel_id=1, source_target_pairs={{0,4},{1,5},{2,6},{3,7},{4,0},{5,1},{6,2},{7,3},{8,12},{9,13},{10,... | collective-permute-start | bytes 331784 | tf_op jit(solution)/shard_map/ppermute | solution.py:300
  18.4 6.9 %collective-permute-start.8 = (bf16[144,384]{1,0:T(8,128)(2,1)S(1)}, bf16[144,384]{1,0:T(8,128)(2,1)S(1)}, u32[]{:S(2)}, u32[]{:S(2)}) collective-permute-start(bf16[144,384]{1,0:T(8,128)(2,1)S(1)} %pass_sum.3), channel_id=1, source_target_pairs={{0,2},{1,3},{2,0},{3,1},{4,6},{5,7},{6,4},{7,5},{8,10},{9,11},{10,... | collective-permute-start | bytes 331784 | tf_op jit(solution)/shard_map/ppermute | solution.py:300
  21.5 9.2 %collective-permute-start.4 = (bf16[144,384]{1,0:T(8,128)(2,1)S(1)}, bf16[144,384]{1,0:T(8,128)(2,1)S(1)}, u32[]{:S(2)}, u32[]{:S(2)}) collective-permute-start(bf16[144,384]{1,0:T(8,128)(2,1)S(1)} %plane_sum.2.mine_ref.first_ref), channel_id=1, source_target_pairs={{0,8},{1,9},{2,10},{3,11},{4,12},{5,13},{6,14},{7,15},{8,0},{9,1},... | collective-permute-start | bytes 331784 | tf_op jit(solution)/shard_map/ppermute | solution.py:300
  25.4 7.7 %collective-permute-start.9 = (bf16[144,384]{1,0:T(8,128)(2,1)S(1)}, bf16[144,384]{1,0:T(8,128)(2,1)S(1)}, u32[]{:S(2)}, u32[]{:S(2)}) collective-permute-start(bf16[144,384]{1,0:T(8,128)(2,1)S(1)} %plane_sum.3.second_ref), channel_id=1, source_target_pairs={{0,8},{1,9},{2,10},{3,11},{4,12},{5,13},{6,14},{7,15},{8,0},{9,1},... | collective-permute-start | bytes 331784 | tf_op jit(solution)/shard_map/ppermute | solution.py:300
  30.8 2.4 %collective-permute-start.10 = (bf16[96,384]{1,0:T(8,128)(2,1)S(1)}, bf16[96,384]{1,0:T(8,128)(2,1)S(1)}, u32[]{:S(2)}, u32[]{:S(2)}) collective-permute-start(bf16[96,384]{1,0:T(8,128)(2,1)S(1)} %up_sum.1.half_ref), channel_id=1, source_target_pairs={{0,1},{1,0},{2,3},{3,2},{4,5},{5,4},{6,7},{7,6},{8,9},{9,8},{10,11... | collective-permute-start | bytes 221192 | tf_op jit(solution)/shard_map/ppermute | solution.py:300
  36.2 8.1 %collective-permute-start.15 = (bf16[288,384]{1,0:T(8,128)(2,1)S(1)}, bf16[288,384]{1,0:T(8,128)(2,1)S(1)}, u32[]{:S(2)}, u32[]{:S(2)}) collective-permute-start(bf16[288,384]{1,0:T(8,128)(2,1)S(1)} %get-tuple-element.49.refs_0_), channel_id=1, source_target_pairs={{0,1},{1,0},{2,3},{3,2},{4,5},{5,4},{6,7},{7,6},{8,9},{9,8},{10,11... | collective-permute-start | bytes 663560 | tf_op jit(solution)/shard_map/ppermute | solution.py:300
  36.3 5.9 %collective-permute-start.11 = (bf16[144,384]{1,0:T(8,128)(2,1)S(1)}, bf16[144,384]{1,0:T(8,128)(2,1)S(1)}, u32[]{:S(2)}, u32[]{:S(2)}) collective-permute-start(bf16[144,384]{1,0:T(8,128)(2,1)S(1)} %get-tuple-element.47), channel_id=1, source_target_pairs={{0,2},{1,3},{2,0},{3,1},{4,6},{5,7},{6,4},{7,5},{8,10},{9,11},{10,... | collective-permute-start | bytes 331784 | tf_op jit(solution)/shard_map/ppermute | solution.py:300
  37.9 5.9 %collective-permute-start.14 = (bf16[144,384]{1,0:T(8,128)(2,1)S(1)}, bf16[144,384]{1,0:T(8,128)(2,1)S(1)}, u32[]{:S(2)}, u32[]{:S(2)}) collective-permute-start(bf16[144,384]{1,0:T(8,128)(2,1)S(1)} %get-tuple-element.48), channel_id=1, source_target_pairs={{0,4},{1,5},{2,6},{3,7},{4,0},{5,1},{6,2},{7,3},{8,12},{9,13},{10,... | collective-permute-start | bytes 331784 | tf_op jit(solution)/shard_map/ppermute | solution.py:300
  37.9 7.1 %collective-permute-start.12 = (bf16[144,384]{1,0:T(8,128)(2,1)S(1)}, bf16[144,384]{1,0:T(8,128)(2,1)S(1)}, u32[]{:S(2)}, u32[]{:S(2)}) collective-permute-start(bf16[144,384]{1,0:T(8,128)(2,1)S(1)} %get-tuple-element.48), channel_id=1, source_target_pairs={{0,2},{1,3},{2,0},{3,1},{4,6},{5,7},{6,4},{7,5},{8,10},{9,11},{10,... | collective-permute-start | bytes 331784 | tf_op jit(solution)/shard_map/ppermute | solution.py:300
  38.4 7.8 %collective-permute-start.13 = (bf16[144,384]{1,0:T(8,128)(2,1)S(1)}, bf16[144,384]{1,0:T(8,128)(2,1)S(1)}, u32[]{:S(2)}, u32[]{:S(2)}) collective-permute-start(bf16[144,384]{1,0:T(8,128)(2,1)S(1)} %get-tuple-element.47), channel_id=1, source_target_pairs={{0,4},{1,5},{2,6},{3,7},{4,0},{5,1},{6,2},{7,3},{8,12},{9,13},{10,... | collective-permute-start | bytes 331784 | tf_op jit(solution)/shard_map/ppermute | solution.py:300
  42.2 5.5 %collective-permute-start.20 = (bf16[144,384]{1,0:T(8,128)(2,1)S(1)}, bf16[144,384]{1,0:T(8,128)(2,1)S(1)}, u32[]{:S(2)}, u32[]{:S(2)}) collective-permute-start(bf16[144,384]{1,0:T(8,128)(2,1)S(1)} %collective-permute-done.11.refs_0_), channel_id=1, source_target_pairs={{0,4},{1,5},{2,6},{3,7},{4,0},{5,1},{6,2},{7,3},{8,12},{9,13},{10,... | collective-permute-start | bytes 331784 | tf_op jit(solution)/shard_map/ppermute | solution.py:300
  43.8 4.7 %collective-permute-start.21 = (bf16[144,384]{1,0:T(8,128)(2,1)S(1)}, bf16[144,384]{1,0:T(8,128)(2,1)S(1)}, u32[]{:S(2)}, u32[]{:S(2)}) collective-permute-start(bf16[144,384]{1,0:T(8,128)(2,1)S(1)} %collective-permute-done.14.refs_5_), channel_id=1, source_target_pairs={{0,2},{1,3},{2,0},{3,1},{4,6},{5,7},{6,4},{7,5},{8,10},{9,11},{10,... | collective-permute-start | bytes 331784 | tf_op jit(solution)/shard_map/ppermute | solution.py:300
  46.2 2.4 %collective-permute-start.16 = (bf16[144,384]{1,0:T(8,128)(2,1)S(1)}, bf16[144,384]{1,0:T(8,128)(2,1)S(1)}, u32[]{:S(2)}, u32[]{:S(2)}) collective-permute-start(bf16[144,384]{1,0:T(8,128)(2,1)S(1)} %collective-permute-done.11.refs_0_), channel_id=1, source_target_pairs={{0,1},{1,0},{2,3},{3,2},{4,5},{5,4},{6,7},{7,6},{8,9},{9,8},{10,11... | collective-permute-start | bytes 331784 | tf_op jit(solution)/shard_map/ppermute | solution.py:300
  46.2 2.9 %collective-permute-start.17 = (bf16[144,384]{1,0:T(8,128)(2,1)S(1)}, bf16[144,384]{1,0:T(8,128)(2,1)S(1)}, u32[]{:S(2)}, u32[]{:S(2)}) collective-permute-start(bf16[144,384]{1,0:T(8,128)(2,1)S(1)} %collective-permute-done.12.refs_1_), channel_id=1, source_target_pairs={{0,1},{1,0},{2,3},{3,2},{4,5},{5,4},{6,7},{7,6},{8,9},{9,8},{10,11... | collective-permute-start | bytes 331784 | tf_op jit(solution)/shard_map/ppermute | solution.py:300
  46.7 2.4 %collective-permute-start.18 = (bf16[144,384]{1,0:T(8,128)(2,1)S(1)}, bf16[144,384]{1,0:T(8,128)(2,1)S(1)}, u32[]{:S(2)}, u32[]{:S(2)}) collective-permute-start(bf16[144,384]{1,0:T(8,128)(2,1)S(1)} %collective-permute-done.13.refs_4_), channel_id=1, source_target_pairs={{0,1},{1,0},{2,3},{3,2},{4,5},{5,4},{6,7},{7,6},{8,9},{9,8},{10,11... | collective-permute-start | bytes 331784 | tf_op jit(solution)/shard_map/ppermute | solution.py:300
  47.8 1.3 %collective-permute-start.19 = (bf16[144,384]{1,0:T(8,128)(2,1)S(1)}, bf16[144,384]{1,0:T(8,128)(2,1)S(1)}, u32[]{:S(2)}, u32[]{:S(2)}) collective-permute-start(bf16[144,384]{1,0:T(8,128)(2,1)S(1)} %collective-permute-done.14.refs_5_), channel_id=1, source_target_pairs={{0,1},{1,0},{2,3},{3,2},{4,5},{5,4},{6,7},{7,6},{8,9},{9,8},{10,11... | collective-permute-start | bytes 331784 | tf_op jit(solution)/shard_map/ppermute | solution.py:300
  48.6 1.7 %collective-permute-start.22 = (bf16[144,384]{1,0:T(8,128)(2,1)S(1)}, bf16[144,384]{1,0:T(8,128)(2,1)S(1)}, u32[]{:S(2)}, u32[]{:S(2)}) collective-permute-start(bf16[144,384]{1,0:T(8,128)(2,1)S(1)} %collective-permute-done.20.first_ref), channel_id=1, source_target_pairs={{0,1},{1,0},{2,3},{3,2},{4,5},{5,4},{6,7},{7,6},{8,9},{9,8},{10,11... | collective-permute-start | bytes 331784 | tf_op jit(solution)/shard_map/ppermute | solution.py:300
  48.6 1.7 %collective-permute-start.23 = (bf16[144,384]{1,0:T(8,128)(2,1)S(1)}, bf16[144,384]{1,0:T(8,128)(2,1)S(1)}, u32[]{:S(2)}, u32[]{:S(2)}) collective-permute-start(bf16[144,384]{1,0:T(8,128)(2,1)S(1)} %collective-permute-done.21.second_ref), channel_id=1, source_target_pairs={{0,1},{1,0},{2,3},{3,2},{4,5},{5,4},{6,7},{7,6},{8,9},{9,8},{10,11... | collective-permute-start | bytes 331784 | tf_op jit(solution)/shard_map/ppermute | solution.py:300

commit v10 on v9

--- a/solution.py
+++ b/solution.py
@@ -305,10 +305,10 @@
         small(pair_sum_kernel, [part_block] * heads, (keep, exchange(give, 1)), 9 * keep.size, "pair_sum")
         for keep, give in ((first, first_give), (second, second_give))
     )
-    first_on, second_on = exchange(first[3], 2), exchange(second[3], 4)
-    first_in, second_in = exchange(first[1], 2), exchange(second[2], 4)
-    first_on = exchange(small(sum_kernel, part_block, (first[2], first_on), 6 * size, "pass_sum"), 4)
-    second_on = exchange(small(sum_kernel, part_block, (second[1], second_on), 6 * size, "pass_sum"), 2)
+    first_on, second_on = exchange(first[3], 4), exchange(second[3], 2)
+    first_in, second_in = exchange(first[2], 4), exchange(second[1], 2)
+    first_on = exchange(small(sum_kernel, part_block, (first[1], first_on), 6 * size, "pass_sum"), 2)
+    second_on = exchange(small(sum_kernel, part_block, (second[2], second_on), 6 * size, "pass_sum"), 4)
     first = small(sum_kernel, part_block, (first[0], first_in, first_on), 8 * size, "plane_sum")
     second = small(sum_kernel, part_block, (second[0], second_in, second_on), 8 * size, "plane_sum")
     query = project_query(tokens, qkv_weight, heads)

time: 51.9 us -> 51.8 us (level)
  no operation moved by 1% of the time
where the time goes in v10:
time: 51.8 us; the launch traced here: 51.6 us
  starting transfers between devices  19.6 us (38%)
  Pallas kernels  16.4 us (32%)
  waiting for transfers between devices  14.3 us (28%)
  other arithmetic  1.19 us (2%)
    ppermute x24, starting transfers between devices, exchange(): return lax.ppermute(x, 'tok', [(i, i ^ bits) for i in range(groups)])  19.6 us
    ppermute x24, waiting for transfers between devices, exchange(): return lax.ppermute(x, 'tok', [(i, i ^ bits) for i in range(groups)])  14.3 us
    pallas_call x1, Pallas kernels, gradients(): pl.pallas_call(grad_kernel, out_shape=[shape] * 4, in_specs=[pl.BlockSpec...  7.21 us
    pallas_call x10, Pallas kernels, small(): pl.pallas_call(kernel, out_shape=shapes, in_specs=specs, compiler_params=...  5.26 us
    pallas_call x1, Pallas kernels, project_query(): pl.pallas_call(query_kernel, out_shape=pltpu.VMEM((heads, rows, width //...  2.36 us
    pallas_call x1, Pallas kernels, finish(): pl.pallas_call(finish_kernel, out_shape=jax.ShapeDtypeStruct((rows, heads...  1.53 us
    select_n x1, other arithmetic, shards(): jnp.where(core == 0, lax.dynamic_index_in_dim(w_gate, own, 0, False), lax...  1.19 us
  transfers between devices with their start and end apart: 24, of which 10 were waited for; matrix products, arithmetic and copies ran while one was open for 2% of the time, Pallas kernels for 9%

profile of v10, /device:TPU:0, one launch (start us, length us, event | category | flops | bytes accessed | tf_op | source)
XLA Modules:
  0.0 51.6 jit_solution(18174581213534102539)
XLA Ops:
  0.0 7.2 %gradients.1 = (bf16[4,144,384]{2,1,0:T(8,128)(2,1)S(1)}, bf16[4,144,384]{2,1,0:T(8,128)(2,1)S(1)}, bf16[4,144,384]{2,1,0:T(8,128)(2,1)S(1)}, bf16[4,144,384]{2,1,0:T(8,128)(2,1)S(1)}) custom-call(s32[16]{0:T(128)} %view_hbm.1, bf16[512,768]{1,0:T(8,128)(2,1)} %tokens_ref.1, bf16[768,2304]{1,0:T(8,128)(2,1)} %weight_ref.1, f32[4,192,384]{2,1,0:T(8,128)} %gate_hbm.1, ...), custom_call_target="tpu_custom_call" | custom-call | flops 3019898880 | bytes 6684672 | tf_op jit(solution)/shard_map/gradients/pallas_call | solution.py:112
  7.2 0.5 collective-permute-start
  7.8 1.3 %collective-permute-done.got_ref = bf16[4,144,384]{2,1,0:T(8,128)(2,1)S(1)} collective-permute-done((bf16[4,144,384]{2,1,0:T(8,128)(2,1)S(1)}, bf16[4,144,384]{2,1,0:T(8,128)(2,1)S(1)}, u32[]{:S(2)}, u32[]{:S(2)}) %collective-permute-start) | collective-permute-done | bytes 442400 | tf_op jit(solution)/shard_map/ppermute | solution.py:300
  9.2 0.1 pair_sum.2
  9.3 3.0 %collective-permute-start.2 = (bf16[144,384]{1,0:T(8,128)(2,1)S(1)}, bf16[144,384]{1,0:T(8,128)(2,1)S(1)}, u32[]{:S(2)}, u32[]{:S(2)}) collective-permute-start(bf16[144,384]{1,0:T(8,128)(2,1)S(1)} %get-tuple-element.36), channel_id=1, source_target_pairs={{0,4},{1,5},{2,6},{3,7},{4,0},{5,1},{6,2},{7,3},{8,12},{9,13},{10,... | collective-permute-start | bytes 331784 | tf_op jit(solution)/shard_map/ppermute | solution.py:300
  12.4 1.6 %collective-permute-start.7 = (bf16[144,384]{1,0:T(8,128)(2,1)S(1)}, bf16[144,384]{1,0:T(8,128)(2,1)S(1)}, u32[]{:S(2)}, u32[]{:S(2)}) collective-permute-start(bf16[144,384]{1,0:T(8,128)(2,1)S(1)} %get-tuple-element.44), channel_id=1, source_target_pairs={{0,2},{1,3},{2,0},{3,1},{4,6},{5,7},{6,4},{7,5},{8,10},{9,11},{10,... | collective-permute-start | bytes 331784 | tf_op jit(solution)/shard_map/ppermute | solution.py:300
  14.0 0.5 collective-permute-start.1
  14.4 1.2 %collective-permute-done.2.refs_1_ = bf16[144,384]{1,0:T(8,128)(2,1)S(1)} collective-permute-done((bf16[144,384]{1,0:T(8,128)(2,1)S(1)}, bf16[144,384]{1,0:T(8,128)(2,1)S(1)}, u32[]{:S(2)}, u32[]{:S(2)}) %collective-permute-start.2) | collective-permute-done | bytes 110624 | tf_op jit(solution)/shard_map/ppermute | solution.py:300
  15.7 2.4 %collective-permute-start.3 = (bf16[144,384]{1,0:T(8,128)(2,1)S(1)}, bf16[144,384]{1,0:T(8,128)(2,1)S(1)}, u32[]{:S(2)}, u32[]{:S(2)}) collective-permute-start(bf16[144,384]{1,0:T(8,128)(2,1)S(1)} %pass_sum.2), channel_id=1, source_target_pairs={{0,2},{1,3},{2,0},{3,1},{4,6},{5,7},{6,4},{7,5},{8,10},{9,11},{10,... | collective-permute-start | bytes 331784 | tf_op jit(solution)/shard_map/ppermute | solution.py:300
  18.2 1.9 %collective-permute-start.8 = (bf16[144,384]{1,0:T(8,128)(2,1)S(1)}, bf16[144,384]{1,0:T(8,128)(2,1)S(1)}, u32[]{:S(2)}, u32[]{:S(2)}) collective-permute-start(bf16[144,384]{1,0:T(8,128)(2,1)S(1)} %pass_sum.3), channel_id=1, source_target_pairs={{0,4},{1,5},{2,6},{3,7},{4,0},{5,1},{6,2},{7,3},{8,12},{9,13},{10,... | collective-permute-start | bytes 331784 | tf_op jit(solution)/shard_map/ppermute | solution.py:300
  20.1 1.4 %collective-permute-done.3.refs_2_ = bf16[144,384]{1,0:T(8,128)(2,1)S(1)} collective-permute-done((bf16[144,384]{1,0:T(8,128)(2,1)S(1)}, bf16[144,384]{1,0:T(8,128)(2,1)S(1)}, u32[]{:S(2)}, u32[]{:S(2)}) %collective-permute-start.3) | collective-permute-done | bytes 110624 | tf_op jit(solution)/shard_map/ppermute | solution.py:300
  21.6 2.6 %collective-permute-start.4 = (bf16[144,384]{1,0:T(8,128)(2,1)S(1)}, bf16[144,384]{1,0:T(8,128)(2,1)S(1)}, u32[]{:S(2)}, u32[]{:S(2)}) collective-permute-start(bf16[144,384]{1,0:T(8,128)(2,1)S(1)} %plane_sum.2.mine_ref.first_ref), channel_id=1, source_target_pairs={{0,8},{1,9},{2,10},{3,11},{4,12},{5,13},{6,14},{7,15},{8,0},{9,1},... | collective-permute-start | bytes 331784 | tf_op jit(solution)/shard_map/ppermute | solution.py:300
  24.1 1.2 %fusion = (f32[192,384]{1,0:T(8,128)S(1)}, f32[192,384]{1,0:T(8,128)S(1)}) fusion(f32[4,384,192]{1,2,0:T(8,128)} %param.10, s32[]{:T(128)S(6)} %select_n.18, f32[4,192,384]{2,1,0:T(8,128)} %gate_hbm.1, pred[]{:T(512)S(6)} %eq.3, f32[4,192,384]{2,1,0:T(8,128)} %up_hbm.1), kind=kLoop, calls=%fused_computation.1 | loop fusion | flops 73728 | bytes 1474565 | tf_op jit(solution)/shard_map/jit(_where)/select_n | solution.py:315
  25.4 1.1 %collective-permute-start.9 = (bf16[144,384]{1,0:T(8,128)(2,1)S(1)}, bf16[144,384]{1,0:T(8,128)(2,1)S(1)}, u32[]{:S(2)}, u32[]{:S(2)}) collective-permute-start(bf16[144,384]{1,0:T(8,128)(2,1)S(1)} %plane_sum.3.second_ref), channel_id=1, source_target_pairs={{0,8},{1,9},{2,10},{3,11},{4,12},{5,13},{6,14},{7,15},{8,0},{9,1},... | collective-permute-start | bytes 331784 | tf_op jit(solution)/shard_map/ppermute | solution.py:300
  26.5 2.4 %query.1.q_ref = bf16[4,512,192]{2,1,0:T(8,128)(2,1)S(1)} custom-call(bf16[512,768]{1,0:T(8,128)(2,1)} %tokens_ref.1, bf16[768,2304]{1,0:T(8,128)(2,1)} %weight_ref.1), custom_call_target="tpu_custom_call" | custom-call | flops 603979776 | bytes 3932160 | tf_op jit(solution)/shard_map/query/pallas_call | solution.py:159
  28.8 2.0 %collective-permute-done.4.other_ref.first_other_ref = bf16[144,384]{1,0:T(8,128)(2,1)S(1)} collective-permute-done((bf16[144,384]{1,0:T(8,128)(2,1)S(1)}, bf16[144,384]{1,0:T(8,128)(2,1)S(1)}, u32[]{:S(2)}, u32[]{:S(2)}) %collective-permute-start.4) | collective-permute-done | bytes 110624 | tf_op jit(solution)/shard_map/ppermute | solution.py:300
  30.9 2.3 %collective-permute-done.9.second_other_ref = bf16[144,384]{1,0:T(8,128)(2,1)S(1)} collective-permute-done((bf16[144,384]{1,0:T(8,128)(2,1)S(1)}, bf16[144,384]{1,0:T(8,128)(2,1)S(1)}, u32[]{:S(2)}, u32[]{:S(2)}) %collective-permute-start.9) | collective-permute-done | bytes 110624 | tf_op jit(solution)/shard_map/ppermute | solution.py:300
  33.2 3.1 %newton.1 = (bf16[288,384]{1,0:T(8,128)(2,1)S(1)}, bf16[144,384]{1,0:T(8,128)(2,1)S(1)}, bf16[144,384]{1,0:T(8,128)(2,1)S(1)}) custom-call(bf16[144,384]{1,0:T(8,128)(2,1)S(1)} %plane_sum.2.mine_ref.first_ref, bf16[144,384]{1,0:T(8,128)(2,1)S(1)} %collective-permute-done.4.other_ref.first_other_ref, bf16[144,384]{1,0:T(8,128)(2,1)S(1)} %plane_sum.3.second_ref, ...), custom_call_target="tpu_custom_call" | custom-call | bytes 2211840 | tf_op jit(solution)/shard_map/newton/pallas_call | solution.py:140
  36.4 1.4 %collective-permute-start.11 = (bf16[144,384]{1,0:T(8,128)(2,1)S(1)}, bf16[144,384]{1,0:T(8,128)(2,1)S(1)}, u32[]{:S(2)}, u32[]{:S(2)}) collective-permute-start(bf16[144,384]{1,0:T(8,128)(2,1)S(1)} %get-tuple-element.47), channel_id=1, source_target_pairs={{0,2},{1,3},{2,0},{3,1},{4,6},{5,7},{6,4},{7,5},{8,10},{9,11},{10,... | collective-permute-start | bytes 331784 | tf_op jit(solution)/shard_map/ppermute | solution.py:300
  37.8 0.7 %collective-permute-start.12 = (bf16[144,384]{1,0:T(8,128)(2,1)S(1)}, bf16[144,384]{1,0:T(8,128)(2,1)S(1)}, u32[]{:S(2)}, u32[]{:S(2)}) collective-permute-start(bf16[144,384]{1,0:T(8,128)(2,1)S(1)} %get-tuple-element.48), channel_id=1, source_target_pairs={{0,2},{1,3},{2,0},{3,1},{4,6},{5,7},{6,4},{7,5},{8,10},{9,11},{10,... | collective-permute-start | bytes 331784 | tf_op jit(solution)/shard_map/ppermute | solution.py:300
  38.5 2.0 %collective-permute-start.13 = (bf16[144,384]{1,0:T(8,128)(2,1)S(1)}, bf16[144,384]{1,0:T(8,128)(2,1)S(1)}, u32[]{:S(2)}, u32[]{:S(2)}) collective-permute-start(bf16[144,384]{1,0:T(8,128)(2,1)S(1)} %get-tuple-element.47), channel_id=1, source_target_pairs={{0,4},{1,5},{2,6},{3,7},{4,0},{5,1},{6,2},{7,3},{8,12},{9,13},{10,... | collective-permute-start | bytes 331784 | tf_op jit(solution)/shard_map/ppermute | solution.py:300
  40.5 1.8 %collective-permute-done.11.refs_0_ = bf16[144,384]{1,0:T(8,128)(2,1)S(1)} collective-permute-done((bf16[144,384]{1,0:T(8,128)(2,1)S(1)}, bf16[144,384]{1,0:T(8,128)(2,1)S(1)}, u32[]{:S(2)}, u32[]{:S(2)}) %collective-permute-start.11) | collective-permute-done | bytes 110624 | tf_op jit(solution)/shard_map/ppermute | solution.py:300
  42.3 1.4 %collective-permute-done.14.refs_5_ = bf16[144,384]{1,0:T(8,128)(2,1)S(1)} collective-permute-done((bf16[144,384]{1,0:T(8,128)(2,1)S(1)}, bf16[144,384]{1,0:T(8,128)(2,1)S(1)}, u32[]{:S(2)}, u32[]{:S(2)}) %collective-permute-start.14) | collective-permute-done | bytes 110624 | tf_op jit(solution)/shard_map/ppermute | solution.py:300
  43.7 0.7 %collective-permute-start.21 = (bf16[144,384]{1,0:T(8,128)(2,1)S(1)}, bf16[144,384]{1,0:T(8,128)(2,1)S(1)}, u32[]{:S(2)}, u32[]{:S(2)}) collective-permute-start(bf16[144,384]{1,0:T(8,128)(2,1)S(1)} %collective-permute-done.14.refs_5_), channel_id=1, source_target_pairs={{0,2},{1,3},{2,0},{3,1},{4,6},{5,7},{6,4},{7,5},{8,10},{9,11},{10,... | collective-permute-start | bytes 331784 | tf_op jit(solution)/shard_map/ppermute | solution.py:300
  44.4 0.7 %apply.1.piece_ref = bf16[512,192]{1,0:T(8,128)(2,1)S(1)} custom-call(bf16[4,512,192]{2,1,0:T(8,128)(2,1)S(1)} %query.1.q_ref, bf16[288,384]{1,0:T(8,128)(2,1)S(1)} %get-tuple-element.49.refs_0_, bf16[288,384]{1,0:T(8,128)(2,1)S(1)} %collective-permute-done.15.refs_1_), custom_call_target="tpu_custom_call" | custom-call | bytes 1966080 | tf_op jit(solution)/shard_map/apply/pallas_call | solution.py:140
  45.1 1.0 %collective-permute-done.13.refs_4_ = bf16[144,384]{1,0:T(8,128)(2,1)S(1)} collective-permute-done((bf16[144,384]{1,0:T(8,128)(2,1)S(1)}, bf16[144,384]{1,0:T(8,128)(2,1)S(1)}, u32[]{:S(2)}, u32[]{:S(2)}) %collective-permute-start.13) | collective-permute-done | bytes 110624 | tf_op jit(solution)/shard_map/ppermute | solution.py:300
  46.1 0.5 collective-permute-start.17
  46.6 1.1 %collective-permute-done.20.first_ref = bf16[144,384]{1,0:T(8,128)(2,1)S(1)} collective-permute-done((bf16[144,384]{1,0:T(8,128)(2,1)S(1)}, bf16[144,384]{1,0:T(8,128)(2,1)S(1)}, u32[]{:S(2)}, u32[]{:S(2)}) %collective-permute-start.20) | collective-permute-done | bytes 110624 | tf_op jit(solution)/shard_map/ppermute | solution.py:300
  47.7 0.8 %collective-permute-done.21.second_ref = bf16[144,384]{1,0:T(8,128)(2,1)S(1)} collective-permute-done((bf16[144,384]{1,0:T(8,128)(2,1)S(1)}, bf16[144,384]{1,0:T(8,128)(2,1)S(1)}, u32[]{:S(2)}, u32[]{:S(2)}) %collective-permute-start.21) | collective-permute-done | bytes 110624 | tf_op jit(solution)/shard_map/ppermute | solution.py:300
  48.4 0.5 collective-permute-start.23
  49.0 1.1 %apply_two.1 = (bf16[512,384]{1,0:T(8,128)(2,1)S(1)}, bf16[512,192]{1,0:T(8,128)(2,1)S(1)}) custom-call(bf16[4,512,192]{2,1,0:T(8,128)(2,1)S(1)} %query.1.q_ref, bf16[512,192]{1,0:T(8,128)(2,1)S(1)} %apply.1.piece_ref, bf16[144,384]{1,0:T(8,128)(2,1)S(1)} %collective-permute-done.11.refs_0_, bf16[144,384]{1,0:T(8,128)(2,1)S(1)} %collective-permute-done.12.refs_1_, ...), custom_call_target="tpu_custom_call" | custom-call | bytes 3932160 | tf_op jit(solution)/shard_map/apply_two/pallas_call | solution.py:140
  50.1 1.5 %finish.1 = bf16[512,768]{1,0:T(8,128)(2,1)} custom-call(bf16[4,512,192]{2,1,0:T(8,128)(2,1)S(1)} %query.1.q_ref, bf16[512,384]{1,0:T(8,128)(2,1)S(1)} %get-tuple-element.55.pair_ref, bf16[512,192]{1,0:T(8,128)(2,1)S(1)} %get-tuple-element.56.far_ref, bf16[144,384]{1,0:T(8,128)(2,1)S(1)} %collective-permute-done.20.first_ref, ...), custom_call_target="tpu_custom_call" | custom-call | tf_op jit(solution)/shard_map/finish/pallas_call | solution.py:273
  (30 shorter events, 0.7 us)
Async XLA Ops:
  7.2 1.9 %collective-permute-start = (bf16[4,144,384]{2,1,0:T(8,128)(2,1)S(1)}, bf16[4,144,384]{2,1,0:T(8,128)(2,1)S(1)}, u32[]{:S(2)}, u32[]{:S(2)}) collective-permute-start(bf16[4,144,384]{2,1,0:T(8,128)(2,1)S(1)} %get-tuple-element.32), channel_id=1, source_target_pairs={{0,1},{1,0},{2,3},{3,2},{4,5},{5,4},{6,7},{7,6},{8,9},{9,8},{10,11... | collective-permute-start | bytes 1327112 | tf_op jit(solution)/shard_map/ppermute | solution.py:300
  7.7 4.5 %collective-permute-start.5 = (bf16[4,144,384]{2,1,0:T(8,128)(2,1)S(1)}, bf16[4,144,384]{2,1,0:T(8,128)(2,1)S(1)}, u32[]{:S(2)}, u32[]{:S(2)}) collective-permute-start(bf16[4,144,384]{2,1,0:T(8,128)(2,1)S(1)} %get-tuple-element.40), channel_id=1, source_target_pairs={{0,1},{1,0},{2,3},{3,2},{4,5},{5,4},{6,7},{7,6},{8,9},{9,8},{10,11... | collective-permute-start | bytes 1327112 | tf_op jit(solution)/shard_map/ppermute | solution.py:300
  9.3 6.4 %collective-permute-start.2 = (bf16[144,384]{1,0:T(8,128)(2,1)S(1)}, bf16[144,384]{1,0:T(8,128)(2,1)S(1)}, u32[]{:S(2)}, u32[]{:S(2)}) collective-permute-start(bf16[144,384]{1,0:T(8,128)(2,1)S(1)} %get-tuple-element.36), channel_id=1, source_target_pairs={{0,4},{1,5},{2,6},{3,7},{4,0},{5,1},{6,2},{7,3},{8,12},{9,13},{10,... | collective-permute-start | bytes 331784 | tf_op jit(solution)/shard_map/ppermute | solution.py:300
  12.4 5.8 %collective-permute-start.7 = (bf16[144,384]{1,0:T(8,128)(2,1)S(1)}, bf16[144,384]{1,0:T(8,128)(2,1)S(1)}, u32[]{:S(2)}, u32[]{:S(2)}) collective-permute-start(bf16[144,384]{1,0:T(8,128)(2,1)S(1)} %get-tuple-element.44), channel_id=1, source_target_pairs={{0,2},{1,3},{2,0},{3,1},{4,6},{5,7},{6,4},{7,5},{8,10},{9,11},{10,... | collective-permute-start | bytes 331784 | tf_op jit(solution)/shard_map/ppermute | solution.py:300
  14.0 6.1 %collective-permute-start.1 = (bf16[144,384]{1,0:T(8,128)(2,1)S(1)}, bf16[144,384]{1,0:T(8,128)(2,1)S(1)}, u32[]{:S(2)}, u32[]{:S(2)}) collective-permute-start(bf16[144,384]{1,0:T(8,128)(2,1)S(1)} %get-tuple-element.34), channel_id=1, source_target_pairs={{0,4},{1,5},{2,6},{3,7},{4,0},{5,1},{6,2},{7,3},{8,12},{9,13},{10,... | collective-permute-start | bytes 331784 | tf_op jit(solution)/shard_map/ppermute | solution.py:300
  15.7 5.8 %collective-permute-start.3 = (bf16[144,384]{1,0:T(8,128)(2,1)S(1)}, bf16[144,384]{1,0:T(8,128)(2,1)S(1)}, u32[]{:S(2)}, u32[]{:S(2)}) collective-permute-start(bf16[144,384]{1,0:T(8,128)(2,1)S(1)} %pass_sum.2), channel_id=1, source_target_pairs={{0,2},{1,3},{2,0},{3,1},{4,6},{5,7},{6,4},{7,5},{8,10},{9,11},{10,... | collective-permute-start | bytes 331784 | tf_op jit(solution)/shard_map/ppermute | solution.py:300
  18.1 7.2 %collective-permute-start.6 = (bf16[144,384]{1,0:T(8,128)(2,1)S(1)}, bf16[144,384]{1,0:T(8,128)(2,1)S(1)}, u32[]{:S(2)}, u32[]{:S(2)}) collective-permute-start(bf16[144,384]{1,0:T(8,128)(2,1)S(1)} %get-tuple-element.42), channel_id=1, source_target_pairs={{0,2},{1,3},{2,0},{3,1},{4,6},{5,7},{6,4},{7,5},{8,10},{9,11},{10,... | collective-permute-start | bytes 331784 | tf_op jit(solution)/shard_map/ppermute | solution.py:300
  18.2 7.1 %collective-permute-start.8 = (bf16[144,384]{1,0:T(8,128)(2,1)S(1)}, bf16[144,384]{1,0:T(8,128)(2,1)S(1)}, u32[]{:S(2)}, u32[]{:S(2)}) collective-permute-start(bf16[144,384]{1,0:T(8,128)(2,1)S(1)} %pass_sum.3), channel_id=1, source_target_pairs={{0,4},{1,5},{2,6},{3,7},{4,0},{5,1},{6,2},{7,3},{8,12},{9,13},{10,... | collective-permute-start | bytes 331784 | tf_op jit(solution)/shard_map/ppermute | solution.py:300
  21.6 9.3 %collective-permute-start.4 = (bf16[144,384]{1,0:T(8,128)(2,1)S(1)}, bf16[144,384]{1,0:T(8,128)(2,1)S(1)}, u32[]{:S(2)}, u32[]{:S(2)}) collective-permute-start(bf16[144,384]{1,0:T(8,128)(2,1)S(1)} %plane_sum.2.mine_ref.first_ref), channel_id=1, source_target_pairs={{0,8},{1,9},{2,10},{3,11},{4,12},{5,13},{6,14},{7,15},{8,0},{9,1},... | collective-permute-start | bytes 331784 | tf_op jit(solution)/shard_map/ppermute | solution.py:300
  25.4 7.8 %collective-permute-start.9 = (bf16[144,384]{1,0:T(8,128)(2,1)S(1)}, bf16[144,384]{1,0:T(8,128)(2,1)S(1)}, u32[]{:S(2)}, u32[]{:S(2)}) collective-permute-start(bf16[144,384]{1,0:T(8,128)(2,1)S(1)} %plane_sum.3.second_ref), channel_id=1, source_target_pairs={{0,8},{1,9},{2,10},{3,11},{4,12},{5,13},{6,14},{7,15},{8,0},{9,1},... | collective-permute-start | bytes 331784 | tf_op jit(solution)/shard_map/ppermute | solution.py:300
  30.9 2.4 %collective-permute-start.10 = (bf16[96,384]{1,0:T(8,128)(2,1)S(1)}, bf16[96,384]{1,0:T(8,128)(2,1)S(1)}, u32[]{:S(2)}, u32[]{:S(2)}) collective-permute-start(bf16[96,384]{1,0:T(8,128)(2,1)S(1)} %up_sum.1.half_ref), channel_id=1, source_target_pairs={{0,1},{1,0},{2,3},{3,2},{4,5},{5,4},{6,7},{7,6},{8,9},{9,8},{10,11... | collective-permute-start | bytes 221192 | tf_op jit(solution)/shard_map/ppermute | solution.py:300
  36.3 8.1 %collective-permute-start.15 = (bf16[288,384]{1,0:T(8,128)(2,1)S(1)}, bf16[288,384]{1,0:T(8,128)(2,1)S(1)}, u32[]{:S(2)}, u32[]{:S(2)}) collective-permute-start(bf16[288,384]{1,0:T(8,128)(2,1)S(1)} %get-tuple-element.49.refs_0_), channel_id=1, source_target_pairs={{0,1},{1,0},{2,3},{3,2},{4,5},{5,4},{6,7},{7,6},{8,9},{9,8},{10,11... | collective-permute-start | bytes 663560 | tf_op jit(solution)/shard_map/ppermute | solution.py:300
  36.4 5.9 %collective-permute-start.11 = (bf16[144,384]{1,0:T(8,128)(2,1)S(1)}, bf16[144,384]{1,0:T(8,128)(2,1)S(1)}, u32[]{:S(2)}, u32[]{:S(2)}) collective-permute-start(bf16[144,384]{1,0:T(8,128)(2,1)S(1)} %get-tuple-element.47), channel_id=1, source_target_pairs={{0,2},{1,3},{2,0},{3,1},{4,6},{5,7},{6,4},{7,5},{8,10},{9,11},{10,... | collective-permute-start | bytes 331784 | tf_op jit(solution)/shard_map/ppermute | solution.py:300
  37.8 5.9 %collective-permute-start.14 = (bf16[144,384]{1,0:T(8,128)(2,1)S(1)}, bf16[144,384]{1,0:T(8,128)(2,1)S(1)}, u32[]{:S(2)}, u32[]{:S(2)}) collective-permute-start(bf16[144,384]{1,0:T(8,128)(2,1)S(1)} %get-tuple-element.48), channel_id=1, source_target_pairs={{0,4},{1,5},{2,6},{3,7},{4,0},{5,1},{6,2},{7,3},{8,12},{9,13},{10,... | collective-permute-start | bytes 331784 | tf_op jit(solution)/shard_map/ppermute | solution.py:300
  37.8 7.3 %collective-permute-start.12 = (bf16[144,384]{1,0:T(8,128)(2,1)S(1)}, bf16[144,384]{1,0:T(8,128)(2,1)S(1)}, u32[]{:S(2)}, u32[]{:S(2)}) collective-permute-start(bf16[144,384]{1,0:T(8,128)(2,1)S(1)} %get-tuple-element.48), channel_id=1, source_target_pairs={{0,2},{1,3},{2,0},{3,1},{4,6},{5,7},{6,4},{7,5},{8,10},{9,11},{10,... | collective-permute-start | bytes 331784 | tf_op jit(solution)/shard_map/ppermute | solution.py:300
  38.5 7.6 %collective-permute-start.13 = (bf16[144,384]{1,0:T(8,128)(2,1)S(1)}, bf16[144,384]{1,0:T(8,128)(2,1)S(1)}, u32[]{:S(2)}, u32[]{:S(2)}) collective-permute-start(bf16[144,384]{1,0:T(8,128)(2,1)S(1)} %get-tuple-element.47), channel_id=1, source_target_pairs={{0,4},{1,5},{2,6},{3,7},{4,0},{5,1},{6,2},{7,3},{8,12},{9,13},{10,... | collective-permute-start | bytes 331784 | tf_op jit(solution)/shard_map/ppermute | solution.py:300
  42.3 5.4 %collective-permute-start.20 = (bf16[144,384]{1,0:T(8,128)(2,1)S(1)}, bf16[144,384]{1,0:T(8,128)(2,1)S(1)}, u32[]{:S(2)}, u32[]{:S(2)}) collective-permute-start(bf16[144,384]{1,0:T(8,128)(2,1)S(1)} %collective-permute-done.11.refs_0_), channel_id=1, source_target_pairs={{0,4},{1,5},{2,6},{3,7},{4,0},{5,1},{6,2},{7,3},{8,12},{9,13},{10,... | collective-permute-start | bytes 331784 | tf_op jit(solution)/shard_map/ppermute | solution.py:300
  43.7 4.7 %collective-permute-start.21 = (bf16[144,384]{1,0:T(8,128)(2,1)S(1)}, bf16[144,384]{1,0:T(8,128)(2,1)S(1)}, u32[]{:S(2)}, u32[]{:S(2)}) collective-permute-start(bf16[144,384]{1,0:T(8,128)(2,1)S(1)} %collective-permute-done.14.refs_5_), channel_id=1, source_target_pairs={{0,2},{1,3},{2,0},{3,1},{4,6},{5,7},{6,4},{7,5},{8,10},{9,11},{10,... | collective-permute-start | bytes 331784 | tf_op jit(solution)/shard_map/ppermute | solution.py:300
  46.1 2.4 %collective-permute-start.16 = (bf16[144,384]{1,0:T(8,128)(2,1)S(1)}, bf16[144,384]{1,0:T(8,128)(2,1)S(1)}, u32[]{:S(2)}, u32[]{:S(2)}) collective-permute-start(bf16[144,384]{1,0:T(8,128)(2,1)S(1)} %collective-permute-done.11.refs_0_), channel_id=1, source_target_pairs={{0,1},{1,0},{2,3},{3,2},{4,5},{5,4},{6,7},{7,6},{8,9},{9,8},{10,11... | collective-permute-start | bytes 331784 | tf_op jit(solution)/shard_map/ppermute | solution.py:300
  46.1 2.9 %collective-permute-start.17 = (bf16[144,384]{1,0:T(8,128)(2,1)S(1)}, bf16[144,384]{1,0:T(8,128)(2,1)S(1)}, u32[]{:S(2)}, u32[]{:S(2)}) collective-permute-start(bf16[144,384]{1,0:T(8,128)(2,1)S(1)} %collective-permute-done.12.refs_1_), channel_id=1, source_target_pairs={{0,1},{1,0},{2,3},{3,2},{4,5},{5,4},{6,7},{7,6},{8,9},{9,8},{10,11... | collective-permute-start | bytes 331784 | tf_op jit(solution)/shard_map/ppermute | solution.py:300
  46.6 2.4 %collective-permute-start.18 = (bf16[144,384]{1,0:T(8,128)(2,1)S(1)}, bf16[144,384]{1,0:T(8,128)(2,1)S(1)}, u32[]{:S(2)}, u32[]{:S(2)}) collective-permute-start(bf16[144,384]{1,0:T(8,128)(2,1)S(1)} %collective-permute-done.13.refs_4_), channel_id=1, source_target_pairs={{0,1},{1,0},{2,3},{3,2},{4,5},{5,4},{6,7},{7,6},{8,9},{9,8},{10,11... | collective-permute-start | bytes 331784 | tf_op jit(solution)/shard_map/ppermute | solution.py:300
  47.7 1.3 %collective-permute-start.19 = (bf16[144,384]{1,0:T(8,128)(2,1)S(1)}, bf16[144,384]{1,0:T(8,128)(2,1)S(1)}, u32[]{:S(2)}, u32[]{:S(2)}) collective-permute-start(bf16[144,384]{1,0:T(8,128)(2,1)S(1)} %collective-permute-done.14.refs_5_), channel_id=1, source_target_pairs={{0,1},{1,0},{2,3},{3,2},{4,5},{5,4},{6,7},{7,6},{8,9},{9,8},{10,11... | collective-permute-start | bytes 331784 | tf_op jit(solution)/shard_map/ppermute | solution.py:300
  48.4 1.7 %collective-permute-start.22 = (bf16[144,384]{1,0:T(8,128)(2,1)S(1)}, bf16[144,384]{1,0:T(8,128)(2,1)S(1)}, u32[]{:S(2)}, u32[]{:S(2)}) collective-permute-start(bf16[144,384]{1,0:T(8,128)(2,1)S(1)} %collective-permute-done.20.first_ref), channel_id=1, source_target_pairs={{0,1},{1,0},{2,3},{3,2},{4,5},{5,4},{6,7},{7,6},{8,9},{9,8},{10,11... | collective-permute-start | bytes 331784 | tf_op jit(solution)/shard_map/ppermute | solution.py:300
  48.4 1.7 %collective-permute-start.23 = (bf16[144,384]{1,0:T(8,128)(2,1)S(1)}, bf16[144,384]{1,0:T(8,128)(2,1)S(1)}, u32[]{:S(2)}, u32[]{:S(2)}) collective-permute-start(bf16[144,384]{1,0:T(8,128)(2,1)S(1)} %collective-permute-done.21.second_ref), channel_id=1, source_target_pairs={{0,1},{1,0},{2,3},{3,2},{4,5},{5,4},{6,7},{7,6},{8,9},{9,8},{10,11... | collective-permute-start | bytes 331784 | tf_op jit(solution)/shard_map/ppermute | solution.py:300

commit v11 on v10

--- a/solution.py
+++ b/solution.py
@@ -334,7 +334,7 @@
         return small(functools.partial(apply_kernel, far), shape(rows, head_dim), (query, *args), 20 * rows * head_dim, "apply")
 
     over_y, over_z = [exchange(x, 2) for x in (first, second)], [exchange(x, 4) for x in (first, second)]
-    across = [exchange(over_y[0], 4), exchange(over_z[1], 2)]
+    across = [exchange(over_z[0], 2), exchange(over_y[1], 4)]
     swapped = lambda blocks: (*blocks, *(exchange(x, 1) for x in blocks))
     piece = apply(0, fresh, exchange(fresh, 1))
     over_y, over_z, piece = lax.optimization_barrier((over_y, over_z, piece))

time: 51.8 us -> 51.8 us (level)
  waiting for transfers between devices: 14.3 us -> 12.7 us
  starting transfers between devices: 19.6 us -> 21.2 us
    ppermute x24, waiting for transfers between devices: 14.3 us -> 12.7 us  [exchange(): return lax.ppermute(x, 'tok', [(i, i ^ bits) for i in range(groups)])]
    ppermute x24, starting transfers between devices: 19.6 us -> 21.2 us  [exchange(): return lax.ppermute(x, 'tok', [(i, i ^ bits) for i in range(groups)])]
  transfers between devices with their start and end apart: 24 -> 24, of which waited for: 10 -> 8; matrix products, arithmetic and copies ran while one was open for 2% -> 2% of each run, Pallas kernels for 9% -> 9%
where the time goes in v11:
time: 51.8 us; the launch traced here: 51.6 us
  starting transfers between devices  21.2 us (41%)
  Pallas kernels  16.4 us (32%)
  waiting for transfers between devices  12.7 us (25%)
  other arithmetic  1.19 us (2%)
    ppermute x24, starting transfers between devices, exchange(): return lax.ppermute(x, 'tok', [(i, i ^ bits) for i in range(groups)])  21.2 us
    ppermute x24, waiting for transfers between devices, exchange(): return lax.ppermute(x, 'tok', [(i, i ^ bits) for i in range(groups)])  12.7 us
    pallas_call x1, Pallas kernels, gradients(): pl.pallas_call(grad_kernel, out_shape=[shape] * 4, in_specs=[pl.BlockSpec...  7.21 us
    pallas_call x10, Pallas kernels, small(): pl.pallas_call(kernel, out_shape=shapes, in_specs=specs, compiler_params=...  5.26 us
    pallas_call x1, Pallas kernels, project_query(): pl.pallas_call(query_kernel, out_shape=pltpu.VMEM((heads, rows, width //...  2.36 us
    pallas_call x1, Pallas kernels, finish(): pl.pallas_call(finish_kernel, out_shape=jax.ShapeDtypeStruct((rows, heads...  1.54 us
    select_n x1, other arithmetic, shards(): jnp.where(core == 0, lax.dynamic_index_in_dim(w_gate, own, 0, False), lax...  1.19 us
  transfers between devices with their start and end apart: 24, of which 8 were waited for; matrix products, arithmetic and copies ran while one was open for 2% of the time, Pallas kernels for 9%

profile of v11, /device:TPU:0, one launch (start us, length us, event | category | flops | bytes accessed | tf_op | source)
XLA Modules:
  0.0 51.6 jit_solution(13256939482680451925)
XLA Ops:
  0.0 7.2 %gradients.1 = (bf16[4,144,384]{2,1,0:T(8,128)(2,1)S(1)}, bf16[4,144,384]{2,1,0:T(8,128)(2,1)S(1)}, bf16[4,144,384]{2,1,0:T(8,128)(2,1)S(1)}, bf16[4,144,384]{2,1,0:T(8,128)(2,1)S(1)}) custom-call(s32[16]{0:T(128)} %view_hbm.1, bf16[512,768]{1,0:T(8,128)(2,1)} %tokens_ref.1, bf16[768,2304]{1,0:T(8,128)(2,1)} %weight_ref.1, f32[4,192,384]{2,1,0:T(8,128)} %gate_hbm.1, ...), custom_call_target="tpu_custom_call" | custom-call | flops 3019898880 | bytes 6684672 | tf_op jit(solution)/shard_map/gradients/pallas_call | solution.py:112
  7.2 0.5 %collective-permute-start = (bf16[4,144,384]{2,1,0:T(8,128)(2,1)S(1)}, bf16[4,144,384]{2,1,0:T(8,128)(2,1)S(1)}, u32[]{:S(2)}, u32[]{:S(2)}) collective-permute-start(bf16[4,144,384]{2,1,0:T(8,128)(2,1)S(1)} %get-tuple-element.32), channel_id=1, source_target_pairs={{0,1},{1,0},{2,3},{3,2},{4,5},{5,4},{6,7},{7,6},{8,9},{9,8},{10,11... | collective-permute-start | bytes 1327112 | tf_op jit(solution)/shard_map/ppermute | solution.py:300
  7.8 1.3 %collective-permute-done.got_ref = bf16[4,144,384]{2,1,0:T(8,128)(2,1)S(1)} collective-permute-done((bf16[4,144,384]{2,1,0:T(8,128)(2,1)S(1)}, bf16[4,144,384]{2,1,0:T(8,128)(2,1)S(1)}, u32[]{:S(2)}, u32[]{:S(2)}) %collective-permute-start) | collective-permute-done | bytes 442400 | tf_op jit(solution)/shard_map/ppermute | solution.py:300
  9.2 0.1 pair_sum.2
  9.3 3.0 %collective-permute-start.2 = (bf16[144,384]{1,0:T(8,128)(2,1)S(1)}, bf16[144,384]{1,0:T(8,128)(2,1)S(1)}, u32[]{:S(2)}, u32[]{:S(2)}) collective-permute-start(bf16[144,384]{1,0:T(8,128)(2,1)S(1)} %get-tuple-element.36), channel_id=1, source_target_pairs={{0,4},{1,5},{2,6},{3,7},{4,0},{5,1},{6,2},{7,3},{8,12},{9,13},{10,... | collective-permute-start | bytes 331784 | tf_op jit(solution)/shard_map/ppermute | solution.py:300
  12.3 0.1 pair_sum.3
  12.4 1.6 %collective-permute-start.7 = (bf16[144,384]{1,0:T(8,128)(2,1)S(1)}, bf16[144,384]{1,0:T(8,128)(2,1)S(1)}, u32[]{:S(2)}, u32[]{:S(2)}) collective-permute-start(bf16[144,384]{1,0:T(8,128)(2,1)S(1)} %get-tuple-element.44), channel_id=1, source_target_pairs={{0,2},{1,3},{2,0},{3,1},{4,6},{5,7},{6,4},{7,5},{8,10},{9,11},{10,... | collective-permute-start | bytes 331784 | tf_op jit(solution)/shard_map/ppermute | solution.py:300
  14.0 0.5 collective-permute-start.1
  14.4 1.2 %collective-permute-done.2.refs_1_ = bf16[144,384]{1,0:T(8,128)(2,1)S(1)} collective-permute-done((bf16[144,384]{1,0:T(8,128)(2,1)S(1)}, bf16[144,384]{1,0:T(8,128)(2,1)S(1)}, u32[]{:S(2)}, u32[]{:S(2)}) %collective-permute-start.2) | collective-permute-done | bytes 110624 | tf_op jit(solution)/shard_map/ppermute | solution.py:300
  15.7 2.4 %collective-permute-start.3 = (bf16[144,384]{1,0:T(8,128)(2,1)S(1)}, bf16[144,384]{1,0:T(8,128)(2,1)S(1)}, u32[]{:S(2)}, u32[]{:S(2)}) collective-permute-start(bf16[144,384]{1,0:T(8,128)(2,1)S(1)} %pass_sum.2), channel_id=1, source_target_pairs={{0,2},{1,3},{2,0},{3,1},{4,6},{5,7},{6,4},{7,5},{8,10},{9,11},{10,... | collective-permute-start | bytes 331784 | tf_op jit(solution)/shard_map/ppermute | solution.py:300
  18.2 1.9 %collective-permute-start.8 = (bf16[144,384]{1,0:T(8,128)(2,1)S(1)}, bf16[144,384]{1,0:T(8,128)(2,1)S(1)}, u32[]{:S(2)}, u32[]{:S(2)}) collective-permute-start(bf16[144,384]{1,0:T(8,128)(2,1)S(1)} %pass_sum.3), channel_id=1, source_target_pairs={{0,4},{1,5},{2,6},{3,7},{4,0},{5,1},{6,2},{7,3},{8,12},{9,13},{10,... | collective-permute-start | bytes 331784 | tf_op jit(solution)/shard_map/ppermute | solution.py:300
  20.1 1.4 %collective-permute-done.3.refs_2_ = bf16[144,384]{1,0:T(8,128)(2,1)S(1)} collective-permute-done((bf16[144,384]{1,0:T(8,128)(2,1)S(1)}, bf16[144,384]{1,0:T(8,128)(2,1)S(1)}, u32[]{:S(2)}, u32[]{:S(2)}) %collective-permute-start.3) | collective-permute-done | bytes 110624 | tf_op jit(solution)/shard_map/ppermute | solution.py:300
  21.6 2.6 %collective-permute-start.4 = (bf16[144,384]{1,0:T(8,128)(2,1)S(1)}, bf16[144,384]{1,0:T(8,128)(2,1)S(1)}, u32[]{:S(2)}, u32[]{:S(2)}) collective-permute-start(bf16[144,384]{1,0:T(8,128)(2,1)S(1)} %plane_sum.2.mine_ref.first_ref), channel_id=1, source_target_pairs={{0,8},{1,9},{2,10},{3,11},{4,12},{5,13},{6,14},{7,15},{8,0},{9,1},... | collective-permute-start | bytes 331784 | tf_op jit(solution)/shard_map/ppermute | solution.py:300
  24.1 1.2 %fusion = (f32[192,384]{1,0:T(8,128)S(1)}, f32[192,384]{1,0:T(8,128)S(1)}) fusion(f32[4,384,192]{1,2,0:T(8,128)} %param.10, s32[]{:T(128)S(6)} %select_n.18, f32[4,192,384]{2,1,0:T(8,128)} %gate_hbm.1, pred[]{:T(512)S(6)} %eq.3, f32[4,192,384]{2,1,0:T(8,128)} %up_hbm.1), kind=kLoop, calls=%fused_computation.1 | loop fusion | flops 73728 | bytes 1474565 | tf_op jit(solution)/shard_map/jit(_where)/select_n | solution.py:315
  25.4 1.1 %collective-permute-start.9 = (bf16[144,384]{1,0:T(8,128)(2,1)S(1)}, bf16[144,384]{1,0:T(8,128)(2,1)S(1)}, u32[]{:S(2)}, u32[]{:S(2)}) collective-permute-start(bf16[144,384]{1,0:T(8,128)(2,1)S(1)} %plane_sum.3.second_ref), channel_id=1, source_target_pairs={{0,8},{1,9},{2,10},{3,11},{4,12},{5,13},{6,14},{7,15},{8,0},{9,1},... | collective-permute-start | bytes 331784 | tf_op jit(solution)/shard_map/ppermute | solution.py:300
  26.5 2.4 %query.1.q_ref = bf16[4,512,192]{2,1,0:T(8,128)(2,1)S(1)} custom-call(bf16[512,768]{1,0:T(8,128)(2,1)} %tokens_ref.1, bf16[768,2304]{1,0:T(8,128)(2,1)} %weight_ref.1), custom_call_target="tpu_custom_call" | custom-call | flops 603979776 | bytes 3932160 | tf_op jit(solution)/shard_map/query/pallas_call | solution.py:159
  28.8 2.0 %collective-permute-done.4.other_ref.first_other_ref = bf16[144,384]{1,0:T(8,128)(2,1)S(1)} collective-permute-done((bf16[144,384]{1,0:T(8,128)(2,1)S(1)}, bf16[144,384]{1,0:T(8,128)(2,1)S(1)}, u32[]{:S(2)}, u32[]{:S(2)}) %collective-permute-start.4) | collective-permute-done | bytes 110624 | tf_op jit(solution)/shard_map/ppermute | solution.py:300
  30.9 2.3 %collective-permute-done.9.second_other_ref = bf16[144,384]{1,0:T(8,128)(2,1)S(1)} collective-permute-done((bf16[144,384]{1,0:T(8,128)(2,1)S(1)}, bf16[144,384]{1,0:T(8,128)(2,1)S(1)}, u32[]{:S(2)}, u32[]{:S(2)}) %collective-permute-start.9) | collective-permute-done | bytes 110624 | tf_op jit(solution)/shard_map/ppermute | solution.py:300
  33.2 3.1 %newton.1 = (bf16[288,384]{1,0:T(8,128)(2,1)S(1)}, bf16[144,384]{1,0:T(8,128)(2,1)S(1)}, bf16[144,384]{1,0:T(8,128)(2,1)S(1)}) custom-call(bf16[144,384]{1,0:T(8,128)(2,1)S(1)} %plane_sum.2.mine_ref.first_ref, bf16[144,384]{1,0:T(8,128)(2,1)S(1)} %collective-permute-done.4.other_ref.first_other_ref, bf16[144,384]{1,0:T(8,128)(2,1)S(1)} %plane_sum.3.second_ref, ...), custom_call_target="tpu_custom_call" | custom-call | bytes 2211840 | tf_op jit(solution)/shard_map/newton/pallas_call | solution.py:140
  36.4 1.4 %collective-permute-start.12 = (bf16[144,384]{1,0:T(8,128)(2,1)S(1)}, bf16[144,384]{1,0:T(8,128)(2,1)S(1)}, u32[]{:S(2)}, u32[]{:S(2)}) collective-permute-start(bf16[144,384]{1,0:T(8,128)(2,1)S(1)} %get-tuple-element.48), channel_id=1, source_target_pairs={{0,2},{1,3},{2,0},{3,1},{4,6},{5,7},{6,4},{7,5},{8,10},{9,11},{10,... | collective-permute-start | bytes 331784 | tf_op jit(solution)/shard_map/ppermute | solution.py:300
  37.9 0.7 %collective-permute-start.11 = (bf16[144,384]{1,0:T(8,128)(2,1)S(1)}, bf16[144,384]{1,0:T(8,128)(2,1)S(1)}, u32[]{:S(2)}, u32[]{:S(2)}) collective-permute-start(bf16[144,384]{1,0:T(8,128)(2,1)S(1)} %get-tuple-element.47), channel_id=1, source_target_pairs={{0,2},{1,3},{2,0},{3,1},{4,6},{5,7},{6,4},{7,5},{8,10},{9,11},{10,... | collective-permute-start | bytes 331784 | tf_op jit(solution)/shard_map/ppermute | solution.py:300
  38.5 1.9 %collective-permute-start.14 = (bf16[144,384]{1,0:T(8,128)(2,1)S(1)}, bf16[144,384]{1,0:T(8,128)(2,1)S(1)}, u32[]{:S(2)}, u32[]{:S(2)}) collective-permute-start(bf16[144,384]{1,0:T(8,128)(2,1)S(1)} %get-tuple-element.48), channel_id=1, source_target_pairs={{0,4},{1,5},{2,6},{3,7},{4,0},{5,1},{6,2},{7,3},{8,12},{9,13},{10,... | collective-permute-start | bytes 331784 | tf_op jit(solution)/shard_map/ppermute | solution.py:300
  40.5 1.8 %collective-permute-done.13.refs_4_ = bf16[144,384]{1,0:T(8,128)(2,1)S(1)} collective-permute-done((bf16[144,384]{1,0:T(8,128)(2,1)S(1)}, bf16[144,384]{1,0:T(8,128)(2,1)S(1)}, u32[]{:S(2)}, u32[]{:S(2)}) %collective-permute-start.13) | collective-permute-done | bytes 110624 | tf_op jit(solution)/shard_map/ppermute | solution.py:300
  42.3 1.4 %collective-permute-start.20 = (bf16[144,384]{1,0:T(8,128)(2,1)S(1)}, bf16[144,384]{1,0:T(8,128)(2,1)S(1)}, u32[]{:S(2)}, u32[]{:S(2)}) collective-permute-start(bf16[144,384]{1,0:T(8,128)(2,1)S(1)} %collective-permute-done.13.refs_4_), channel_id=1, source_target_pairs={{0,2},{1,3},{2,0},{3,1},{4,6},{5,7},{6,4},{7,5},{8,10},{9,11},{10,... | collective-permute-start | bytes 331784 | tf_op jit(solution)/shard_map/ppermute | solution.py:300
  43.6 0.7 %collective-permute-start.21 = (bf16[144,384]{1,0:T(8,128)(2,1)S(1)}, bf16[144,384]{1,0:T(8,128)(2,1)S(1)}, u32[]{:S(2)}, u32[]{:S(2)}) collective-permute-start(bf16[144,384]{1,0:T(8,128)(2,1)S(1)} %collective-permute-done.12.refs_1_), channel_id=1, source_target_pairs={{0,4},{1,5},{2,6},{3,7},{4,0},{5,1},{6,2},{7,3},{8,12},{9,13},{10,... | collective-permute-start | bytes 331784 | tf_op jit(solution)/shard_map/ppermute | solution.py:300
  44.4 0.7 %apply.1.piece_ref = bf16[512,192]{1,0:T(8,128)(2,1)S(1)} custom-call(bf16[4,512,192]{2,1,0:T(8,128)(2,1)S(1)} %query.1.q_ref, bf16[288,384]{1,0:T(8,128)(2,1)S(1)} %get-tuple-element.49.refs_0_, bf16[288,384]{1,0:T(8,128)(2,1)S(1)} %collective-permute-done.15.refs_1_), custom_call_target="tpu_custom_call" | custom-call | bytes 1966080 | tf_op jit(solution)/shard_map/apply/pallas_call | solution.py:140
  45.2 0.5 collective-permute-start.17
  45.7 1.3 %collective-permute-done.20.first_ref = bf16[144,384]{1,0:T(8,128)(2,1)S(1)} collective-permute-done((bf16[144,384]{1,0:T(8,128)(2,1)S(1)}, bf16[144,384]{1,0:T(8,128)(2,1)S(1)}, u32[]{:S(2)}, u32[]{:S(2)}) %collective-permute-start.20) | collective-permute-done | bytes 110624 | tf_op jit(solution)/shard_map/ppermute | solution.py:300
  47.0 1.4 %collective-permute-done.21.second_ref = bf16[144,384]{1,0:T(8,128)(2,1)S(1)} collective-permute-done((bf16[144,384]{1,0:T(8,128)(2,1)S(1)}, bf16[144,384]{1,0:T(8,128)(2,1)S(1)}, u32[]{:S(2)}, u32[]{:S(2)}) %collective-permute-start.21) | collective-permute-done | bytes 110624 | tf_op jit(solution)/shard_map/ppermute | solution.py:300
  48.4 0.5 collective-permute-start.23
  48.9 1.1 %apply_two.1 = (bf16[512,384]{1,0:T(8,128)(2,1)S(1)}, bf16[512,192]{1,0:T(8,128)(2,1)S(1)}) custom-call(bf16[4,512,192]{2,1,0:T(8,128)(2,1)S(1)} %query.1.q_ref, bf16[512,192]{1,0:T(8,128)(2,1)S(1)} %apply.1.piece_ref, bf16[144,384]{1,0:T(8,128)(2,1)S(1)} %collective-permute-done.11.refs_0_, bf16[144,384]{1,0:T(8,128)(2,1)S(1)} %collective-permute-done.12.refs_1_, ...), custom_call_target="tpu_custom_call" | custom-call | bytes 3932160 | tf_op jit(solution)/shard_map/apply_two/pallas_call | solution.py:140
  50.1 1.5 %finish.1 = bf16[512,768]{1,0:T(8,128)(2,1)} custom-call(bf16[4,512,192]{2,1,0:T(8,128)(2,1)S(1)} %query.1.q_ref, bf16[512,384]{1,0:T(8,128)(2,1)S(1)} %get-tuple-element.55.pair_ref, bf16[512,192]{1,0:T(8,128)(2,1)S(1)} %get-tuple-element.56.far_ref, bf16[144,384]{1,0:T(8,128)(2,1)S(1)} %collective-permute-done.20.first_ref, ...), custom_call_target="tpu_custom_call" | custom-call | tf_op jit(solution)/shard_map/finish/pallas_call | solution.py:273
  (30 shorter events, 0.8 us)
Async XLA Ops:
  7.2 1.9 %collective-permute-start = (bf16[4,144,384]{2,1,0:T(8,128)(2,1)S(1)}, bf16[4,144,384]{2,1,0:T(8,128)(2,1)S(1)}, u32[]{:S(2)}, u32[]{:S(2)}) collective-permute-start(bf16[4,144,384]{2,1,0:T(8,128)(2,1)S(1)} %get-tuple-element.32), channel_id=1, source_target_pairs={{0,1},{1,0},{2,3},{3,2},{4,5},{5,4},{6,7},{7,6},{8,9},{9,8},{10,11... | collective-permute-start | bytes 1327112 | tf_op jit(solution)/shard_map/ppermute | solution.py:300
  7.7 4.5 %collective-permute-start.5 = (bf16[4,144,384]{2,1,0:T(8,128)(2,1)S(1)}, bf16[4,144,384]{2,1,0:T(8,128)(2,1)S(1)}, u32[]{:S(2)}, u32[]{:S(2)}) collective-permute-start(bf16[4,144,384]{2,1,0:T(8,128)(2,1)S(1)} %get-tuple-element.40), channel_id=1, source_target_pairs={{0,1},{1,0},{2,3},{3,2},{4,5},{5,4},{6,7},{7,6},{8,9},{9,8},{10,11... | collective-permute-start | bytes 1327112 | tf_op jit(solution)/shard_map/ppermute | solution.py:300
  9.3 6.4 %collective-permute-start.2 = (bf16[144,384]{1,0:T(8,128)(2,1)S(1)}, bf16[144,384]{1,0:T(8,128)(2,1)S(1)}, u32[]{:S(2)}, u32[]{:S(2)}) collective-permute-start(bf16[144,384]{1,0:T(8,128)(2,1)S(1)} %get-tuple-element.36), channel_id=1, source_target_pairs={{0,4},{1,5},{2,6},{3,7},{4,0},{5,1},{6,2},{7,3},{8,12},{9,13},{10,... | collective-permute-start | bytes 331784 | tf_op jit(solution)/shard_map/ppermute | solution.py:300
  12.4 5.8 %collective-permute-start.7 = (bf16[144,384]{1,0:T(8,128)(2,1)S(1)}, bf16[144,384]{1,0:T(8,128)(2,1)S(1)}, u32[]{:S(2)}, u32[]{:S(2)}) collective-permute-start(bf16[144,384]{1,0:T(8,128)(2,1)S(1)} %get-tuple-element.44), channel_id=1, source_target_pairs={{0,2},{1,3},{2,0},{3,1},{4,6},{5,7},{6,4},{7,5},{8,10},{9,11},{10,... | collective-permute-start | bytes 331784 | tf_op jit(solution)/shard_map/ppermute | solution.py:300
  14.0 6.1 %collective-permute-start.1 = (bf16[144,384]{1,0:T(8,128)(2,1)S(1)}, bf16[144,384]{1,0:T(8,128)(2,1)S(1)}, u32[]{:S(2)}, u32[]{:S(2)}) collective-permute-start(bf16[144,384]{1,0:T(8,128)(2,1)S(1)} %get-tuple-element.34), channel_id=1, source_target_pairs={{0,4},{1,5},{2,6},{3,7},{4,0},{5,1},{6,2},{7,3},{8,12},{9,13},{10,... | collective-permute-start | bytes 331784 | tf_op jit(solution)/shard_map/ppermute | solution.py:300
  15.7 5.8 %collective-permute-start.3 = (bf16[144,384]{1,0:T(8,128)(2,1)S(1)}, bf16[144,384]{1,0:T(8,128)(2,1)S(1)}, u32[]{:S(2)}, u32[]{:S(2)}) collective-permute-start(bf16[144,384]{1,0:T(8,128)(2,1)S(1)} %pass_sum.2), channel_id=1, source_target_pairs={{0,2},{1,3},{2,0},{3,1},{4,6},{5,7},{6,4},{7,5},{8,10},{9,11},{10,... | collective-permute-start | bytes 331784 | tf_op jit(solution)/shard_map/ppermute | solution.py:300
  18.1 7.2 %collective-permute-start.6 = (bf16[144,384]{1,0:T(8,128)(2,1)S(1)}, bf16[144,384]{1,0:T(8,128)(2,1)S(1)}, u32[]{:S(2)}, u32[]{:S(2)}) collective-permute-start(bf16[144,384]{1,0:T(8,128)(2,1)S(1)} %get-tuple-element.42), channel_id=1, source_target_pairs={{0,2},{1,3},{2,0},{3,1},{4,6},{5,7},{6,4},{7,5},{8,10},{9,11},{10,... | collective-permute-start | bytes 331784 | tf_op jit(solution)/shard_map/ppermute | solution.py:300
  18.2 7.1 %collective-permute-start.8 = (bf16[144,384]{1,0:T(8,128)(2,1)S(1)}, bf16[144,384]{1,0:T(8,128)(2,1)S(1)}, u32[]{:S(2)}, u32[]{:S(2)}) collective-permute-start(bf16[144,384]{1,0:T(8,128)(2,1)S(1)} %pass_sum.3), channel_id=1, source_target_pairs={{0,4},{1,5},{2,6},{3,7},{4,0},{5,1},{6,2},{7,3},{8,12},{9,13},{10,... | collective-permute-start | bytes 331784 | tf_op jit(solution)/shard_map/ppermute | solution.py:300
  21.6 9.3 %collective-permute-start.4 = (bf16[144,384]{1,0:T(8,128)(2,1)S(1)}, bf16[144,384]{1,0:T(8,128)(2,1)S(1)}, u32[]{:S(2)}, u32[]{:S(2)}) collective-permute-start(bf16[144,384]{1,0:T(8,128)(2,1)S(1)} %plane_sum.2.mine_ref.first_ref), channel_id=1, source_target_pairs={{0,8},{1,9},{2,10},{3,11},{4,12},{5,13},{6,14},{7,15},{8,0},{9,1},... | collective-permute-start | bytes 331784 | tf_op jit(solution)/shard_map/ppermute | solution.py:300
  25.4 7.8 %collective-permute-start.9 = (bf16[144,384]{1,0:T(8,128)(2,1)S(1)}, bf16[144,384]{1,0:T(8,128)(2,1)S(1)}, u32[]{:S(2)}, u32[]{:S(2)}) collective-permute-start(bf16[144,384]{1,0:T(8,128)(2,1)S(1)} %plane_sum.3.second_ref), channel_id=1, source_target_pairs={{0,8},{1,9},{2,10},{3,11},{4,12},{5,13},{6,14},{7,15},{8,0},{9,1},... | collective-permute-start | bytes 331784 | tf_op jit(solution)/shard_map/ppermute | solution.py:300
  30.9 2.4 %collective-permute-start.10 = (bf16[96,384]{1,0:T(8,128)(2,1)S(1)}, bf16[96,384]{1,0:T(8,128)(2,1)S(1)}, u32[]{:S(2)}, u32[]{:S(2)}) collective-permute-start(bf16[96,384]{1,0:T(8,128)(2,1)S(1)} %up_sum.1.half_ref), channel_id=1, source_target_pairs={{0,1},{1,0},{2,3},{3,2},{4,5},{5,4},{6,7},{7,6},{8,9},{9,8},{10,11... | collective-permute-start | bytes 221192 | tf_op jit(solution)/shard_map/ppermute | solution.py:300
  36.3 8.1 %collective-permute-start.15 = (bf16[288,384]{1,0:T(8,128)(2,1)S(1)}, bf16[288,384]{1,0:T(8,128)(2,1)S(1)}, u32[]{:S(2)}, u32[]{:S(2)}) collective-permute-start(bf16[288,384]{1,0:T(8,128)(2,1)S(1)} %get-tuple-element.49.refs_0_), channel_id=1, source_target_pairs={{0,1},{1,0},{2,3},{3,2},{4,5},{5,4},{6,7},{7,6},{8,9},{9,8},{10,11... | collective-permute-start | bytes 663560 | tf_op jit(solution)/shard_map/ppermute | solution.py:300
  36.4 5.9 %collective-permute-start.13 = (bf16[144,384]{1,0:T(8,128)(2,1)S(1)}, bf16[144,384]{1,0:T(8,128)(2,1)S(1)}, u32[]{:S(2)}, u32[]{:S(2)}) collective-permute-start(bf16[144,384]{1,0:T(8,128)(2,1)S(1)} %get-tuple-element.47), channel_id=1, source_target_pairs={{0,4},{1,5},{2,6},{3,7},{4,0},{5,1},{6,2},{7,3},{8,12},{9,13},{10,... | collective-permute-start | bytes 331784 | tf_op jit(solution)/shard_map/ppermute | solution.py:300
  36.4 7.2 %collective-permute-start.12 = (bf16[144,384]{1,0:T(8,128)(2,1)S(1)}, bf16[144,384]{1,0:T(8,128)(2,1)S(1)}, u32[]{:S(2)}, u32[]{:S(2)}) collective-permute-start(bf16[144,384]{1,0:T(8,128)(2,1)S(1)} %get-tuple-element.48), channel_id=1, source_target_pairs={{0,2},{1,3},{2,0},{3,1},{4,6},{5,7},{6,4},{7,5},{8,10},{9,11},{10,... | collective-permute-start | bytes 331784 | tf_op jit(solution)/shard_map/ppermute | solution.py:300
  37.9 7.2 %collective-permute-start.11 = (bf16[144,384]{1,0:T(8,128)(2,1)S(1)}, bf16[144,384]{1,0:T(8,128)(2,1)S(1)}, u32[]{:S(2)}, u32[]{:S(2)}) collective-permute-start(bf16[144,384]{1,0:T(8,128)(2,1)S(1)} %get-tuple-element.47), channel_id=1, source_target_pairs={{0,2},{1,3},{2,0},{3,1},{4,6},{5,7},{6,4},{7,5},{8,10},{9,11},{10,... | collective-permute-start | bytes 331784 | tf_op jit(solution)/shard_map/ppermute | solution.py:300
  38.5 6.5 %collective-permute-start.14 = (bf16[144,384]{1,0:T(8,128)(2,1)S(1)}, bf16[144,384]{1,0:T(8,128)(2,1)S(1)}, u32[]{:S(2)}, u32[]{:S(2)}) collective-permute-start(bf16[144,384]{1,0:T(8,128)(2,1)S(1)} %get-tuple-element.48), channel_id=1, source_target_pairs={{0,4},{1,5},{2,6},{3,7},{4,0},{5,1},{6,2},{7,3},{8,12},{9,13},{10,... | collective-permute-start | bytes 331784 | tf_op jit(solution)/shard_map/ppermute | solution.py:300
  42.3 4.7 %collective-permute-start.20 = (bf16[144,384]{1,0:T(8,128)(2,1)S(1)}, bf16[144,384]{1,0:T(8,128)(2,1)S(1)}, u32[]{:S(2)}, u32[]{:S(2)}) collective-permute-start(bf16[144,384]{1,0:T(8,128)(2,1)S(1)} %collective-permute-done.13.refs_4_), channel_id=1, source_target_pairs={{0,2},{1,3},{2,0},{3,1},{4,6},{5,7},{6,4},{7,5},{8,10},{9,11},{10,... | collective-permute-start | bytes 331784 | tf_op jit(solution)/shard_map/ppermute | solution.py:300
  43.6 4.7 %collective-permute-start.21 = (bf16[144,384]{1,0:T(8,128)(2,1)S(1)}, bf16[144,384]{1,0:T(8,128)(2,1)S(1)}, u32[]{:S(2)}, u32[]{:S(2)}) collective-permute-start(bf16[144,384]{1,0:T(8,128)(2,1)S(1)} %collective-permute-done.12.refs_1_), channel_id=1, source_target_pairs={{0,4},{1,5},{2,6},{3,7},{4,0},{5,1},{6,2},{7,3},{8,12},{9,13},{10,... | collective-permute-start | bytes 331784 | tf_op jit(solution)/shard_map/ppermute | solution.py:300
  45.1 3.3 %collective-permute-start.16 = (bf16[144,384]{1,0:T(8,128)(2,1)S(1)}, bf16[144,384]{1,0:T(8,128)(2,1)S(1)}, u32[]{:S(2)}, u32[]{:S(2)}) collective-permute-start(bf16[144,384]{1,0:T(8,128)(2,1)S(1)} %collective-permute-done.11.refs_0_), channel_id=1, source_target_pairs={{0,1},{1,0},{2,3},{3,2},{4,5},{5,4},{6,7},{7,6},{8,9},{9,8},{10,11... | collective-permute-start | bytes 331784 | tf_op jit(solution)/shard_map/ppermute | solution.py:300
  45.2 3.8 %collective-permute-start.17 = (bf16[144,384]{1,0:T(8,128)(2,1)S(1)}, bf16[144,384]{1,0:T(8,128)(2,1)S(1)}, u32[]{:S(2)}, u32[]{:S(2)}) collective-permute-start(bf16[144,384]{1,0:T(8,128)(2,1)S(1)} %collective-permute-done.12.refs_1_), channel_id=1, source_target_pairs={{0,1},{1,0},{2,3},{3,2},{4,5},{5,4},{6,7},{7,6},{8,9},{9,8},{10,11... | collective-permute-start | bytes 331784 | tf_op jit(solution)/shard_map/ppermute | solution.py:300
  45.7 3.3 %collective-permute-start.18 = (bf16[144,384]{1,0:T(8,128)(2,1)S(1)}, bf16[144,384]{1,0:T(8,128)(2,1)S(1)}, u32[]{:S(2)}, u32[]{:S(2)}) collective-permute-start(bf16[144,384]{1,0:T(8,128)(2,1)S(1)} %collective-permute-done.13.refs_4_), channel_id=1, source_target_pairs={{0,1},{1,0},{2,3},{3,2},{4,5},{5,4},{6,7},{7,6},{8,9},{9,8},{10,11... | collective-permute-start | bytes 331784 | tf_op jit(solution)/shard_map/ppermute | solution.py:300
  47.0 1.9 %collective-permute-start.19 = (bf16[144,384]{1,0:T(8,128)(2,1)S(1)}, bf16[144,384]{1,0:T(8,128)(2,1)S(1)}, u32[]{:S(2)}, u32[]{:S(2)}) collective-permute-start(bf16[144,384]{1,0:T(8,128)(2,1)S(1)} %collective-permute-done.14.refs_5_), channel_id=1, source_target_pairs={{0,1},{1,0},{2,3},{3,2},{4,5},{5,4},{6,7},{7,6},{8,9},{9,8},{10,11... | collective-permute-start | bytes 331784 | tf_op jit(solution)/shard_map/ppermute | solution.py:300
  48.4 1.6 %collective-permute-start.22 = (bf16[144,384]{1,0:T(8,128)(2,1)S(1)}, bf16[144,384]{1,0:T(8,128)(2,1)S(1)}, u32[]{:S(2)}, u32[]{:S(2)}) collective-permute-start(bf16[144,384]{1,0:T(8,128)(2,1)S(1)} %collective-permute-done.20.first_ref), channel_id=1, source_target_pairs={{0,1},{1,0},{2,3},{3,2},{4,5},{5,4},{6,7},{7,6},{8,9},{9,8},{10,11... | collective-permute-start | bytes 331784 | tf_op jit(solution)/shard_map/ppermute | solution.py:300
  48.4 1.7 %collective-permute-start.23 = (bf16[144,384]{1,0:T(8,128)(2,1)S(1)}, bf16[144,384]{1,0:T(8,128)(2,1)S(1)}, u32[]{:S(2)}, u32[]{:S(2)}) collective-permute-start(bf16[144,384]{1,0:T(8,128)(2,1)S(1)} %collective-permute-done.21.second_ref), channel_id=1, source_target_pairs={{0,1},{1,0},{2,3},{3,2},{4,5},{5,4},{6,7},{7,6},{8,9},{9,8},{10,11... | collective-permute-start | bytes 331784 | tf_op jit(solution)/shard_map/ppermute | solution.py:300
